TPU v7x, 512 devices: a whole 4x4x16 slice. The times are simulated.
512 devices in a mesh: group: 32 (over z, core), tensor: 16 (over y, x).
Axes of the slice: x: 4, y: 4, z: 16, core: 2. Of those that a mesh axis runs over, the one named last changes fastest.
Arguments:
- queries: bfloat16 [384, 4, 8192], P('group', None, 'tensor'), may hold values from -603 to 603
- new_entries: bfloat16 [384, 4, 2048], P('group'), may hold values from -6 to 6
- resident_cache: bfloat16 [128, 512, 2048], P('group', 'tensor'), may hold values from -6 to 6
- prefill_cache: bfloat16 [256, 512, 2048], P('group', 'tensor'), may hold values from -6 to 6
- resident_kept: int32 [128], replicated, may hold values from 256 to 512, as said below
- kept_tokens: int32 [256], replicated, may hold values from 1 to 512, as said below
- prefill_slot: int32 [256], replicated, may hold values from 0 to 255, as said below
- decode_slot: int32 [256], replicated, may hold values from 4 to 383, as said below
Outputs:
- attended: bfloat16 [384, 4, 8192], P('group', None, 'tensor')
Inputs may be any that keep to these rules, and one draw needn't show every extreme that they name: `kept_tokens`: some request keeps exactly 512 positions. `prefill_slot`: A permutation of the 256 prefill slots; slot s lies in prefill group s // 8. `decode_slot`: every slot g * 12 + l with l >= 4 is named by exactly one request; from one prefill group to one decode group go at most 1 request, and exactly 1 for some pairs. `resident_kept`: some resident request keeps exactly 512 positions.
All inputs are finite; a program needn't handle non-finite values.
Results may differ from a plain program's by a relative error of at most 0.0044.
Values may be sent and summed in bfloat16 or wider, within the bound.
No kernel may reach another device: no remote copies, remote signals or barrier semaphores. Data moves between devices by JAX's collectives and lax.ppermute only.
A program may use at most 128 MiB of HBM per device.

v0:
```python
import math

import jax
import jax.numpy as jnp
from jax import lax
from jax.sharding import PartitionSpec as P

H = 64
KVH = 8
HD = 128
STEPS = 4
MIG_DEV = 8
RES_DEV = 4


NEG_FLOOR = -1e30


def combined_all(part, axis, combine):
    gathered = jax.tree.map(lambda a: lax.all_gather(a, axis), part)

    def take(source):
        return jax.tree.map(lambda a: lax.dynamic_index_in_dim(a, source, 0, False), gathered)

    return lax.fori_loop(
        1, lax.axis_size(axis), lambda source, state: combine(state, take(source)), take(0)
    )


def routing(kept_tokens, prefill_slot, decode_slot, groups, per_pair):
    slot_count = MIG_DEV * groups
    per_group = RES_DEV + MIG_DEV
    dest_by_slot = jnp.zeros((slot_count,), jnp.int32).at[prefill_slot].set(decode_slot)
    kept_by_slot = jnp.zeros((slot_count,), jnp.int32).at[prefill_slot].set(kept_tokens)
    dest_group = (dest_by_slot // per_group).reshape(groups, MIG_DEV)
    earlier = jnp.arange(MIG_DEV)[None, :] < jnp.arange(MIG_DEV)[:, None]
    matching = dest_group[:, :, None] == dest_group[:, None, :]
    ranking = jnp.sum((matching & earlier[None]).astype(jnp.int32), axis=2)
    outgoing_row = (dest_group * per_pair + ranking).reshape(slot_count)
    source_by_dslot = jnp.zeros((groups * per_group,), jnp.int32).at[decode_slot].set(prefill_slot)
    return (kept_by_slot, ranking.reshape(slot_count), outgoing_row, source_by_dslot)


def partials(asking, stored, lengths, offset):
    row_count = stored.shape[0]
    stride = stored.shape[1]
    sharing = H // KVH
    asked_rows = asking.reshape(row_count, STEPS, KVH, sharing, HD)
    entries = stored.reshape(row_count, stride, 2, KVH, HD)
    scores = jnp.einsum(
        "rtkgd,rpkd->rtkgp", asked_rows, entries[:, :, 0], preferred_element_type=jnp.float32
    ) * (1.0 / math.sqrt(HD))
    usable = (offset + jnp.arange(stride))[None, :] < lengths[:, None]
    usable = usable[:, None, None, None, :]
    highest = jnp.max(jnp.where(usable, scores, NEG_FLOOR), axis=4)
    weights = jnp.where(usable, jnp.exp(scores - highest[..., None]), 0.0)
    totals = jnp.sum(weights, axis=4)
    blended = jnp.einsum(
        "rtkgp,rpkd->rtkgd",
        weights.astype(jnp.bfloat16),
        entries[:, :, 1],
        preferred_element_type=jnp.float32,
    )
    return (
        highest.reshape(row_count, STEPS, H),
        totals.reshape(row_count, STEPS, H),
        blended.reshape(row_count, STEPS, H, HD),
    )


def combine(earlier, later):
    highest = jnp.maximum(earlier[0], later[0])
    first_factor = jnp.exp(earlier[0] - highest)
    second_factor = jnp.exp(later[0] - highest)
    return (
        highest,
        earlier[1] * first_factor + later[1] * second_factor,
        earlier[2] * first_factor[..., None] + later[2] * second_factor[..., None],
    )


def own_heads(parts):
    shards = lax.axis_size("tensor")
    stride_heads = H // shards
    merged = combined_all(parts, "tensor", combine)
    start_head = lax.axis_index("tensor") * stride_heads
    result = tuple(
        (lax.dynamic_slice_in_dim(member, start_head, stride_heads, 2) for member in merged)
    )
    return result


def body(
    queries,
    new_entries,
    resident_cache,
    prefill_cache,
    resident_kept,
    kept_tokens,
    prefill_slot,
    decode_slot,
):
    groups = lax.axis_size("group")
    shards = lax.axis_size("tensor")
    per_pair = max(1, MIG_DEV // groups)
    per_group = RES_DEV + MIG_DEV
    stride = prefill_cache.shape[1]
    features = prefill_cache.shape[2]
    offset = lax.axis_index("tensor") * stride
    group_here = lax.axis_index("group")
    kept_by_slot, ranking, outgoing_row, source_by_dslot = routing(
        kept_tokens, prefill_slot, decode_slot, groups, per_pair
    )
    local_rows = lax.dynamic_slice_in_dim(outgoing_row, group_here * MIG_DEV, MIG_DEV)
    arriving = lax.dynamic_slice_in_dim(source_by_dslot, group_here * per_group + RES_DEV, MIG_DEV)
    arriving_rows = arriving // MIG_DEV * per_pair + ranking[arriving]
    arriving_kept = kept_by_slot[arriving]
    resident_len = lax.dynamic_slice_in_dim(resident_kept, group_here * RES_DEV, RES_DEV)
    asking = lax.all_gather(queries, "tensor", axis=2, tiled=True)
    resident_parts = partials(asking[:RES_DEV], resident_cache, resident_len, offset)
    outgoing = (
        jnp.zeros((groups * per_pair, stride, features), jnp.bfloat16)
        .at[local_rows]
        .set(prefill_cache)
    )
    arrived = lax.all_to_all(
        outgoing.reshape(groups, per_pair, stride, features),
        "group",
        split_axis=0,
        concat_axis=0,
        tiled=True,
    )
    moved_cache = arrived.reshape(groups * per_pair, stride, features)[arriving_rows]
    moved_parts = partials(asking[RES_DEV:], moved_cache, arriving_kept, offset)
    heads_parts = own_heads(
        tuple(
            (
                jnp.concatenate([former, latter], 0)
                for former, latter in zip(resident_parts, moved_parts)
            )
        )
    )
    highest, totals, blended = heads_parts
    stride_heads = H // shards
    sharing = H // KVH
    heads_here = lax.axis_index("tensor") * stride_heads + jnp.arange(stride_heads)
    pairs_here = heads_here // sharing
    asked_here = queries.reshape(per_group, STEPS, stride_heads, HD)
    newest = new_entries.reshape(per_group, STEPS, 2, KVH, HD)
    new_keys = jnp.take(newest[:, :, 0], pairs_here, axis=2)
    new_values = jnp.take(newest[:, :, 1], pairs_here, axis=2)
    scores = jnp.einsum(
        "rthd,ruhd->rthu", asked_here, new_keys, preferred_element_type=jnp.float32
    ) * (1.0 / math.sqrt(HD))
    causal = (jnp.arange(STEPS)[None, :] <= jnp.arange(STEPS)[:, None])[None, :, None, :]
    new_high = jnp.max(jnp.where(causal, scores, NEG_FLOOR), axis=3)
    overall = jnp.maximum(highest, new_high)
    weights = jnp.where(causal, jnp.exp(scores - overall[..., None]), 0.0)
    carried = jnp.exp(highest - overall)
    totals = totals * carried + jnp.sum(weights, axis=3)
    blended = blended * carried[..., None] + jnp.einsum(
        "rthu,ruhd->rthd",
        weights.astype(jnp.bfloat16),
        new_values,
        preferred_element_type=jnp.float32,
    )
    return (
        (blended / totals[..., None])
        .astype(jnp.bfloat16)
        .reshape(per_group, STEPS, stride_heads * HD)
    )


def solution(mesh):
    in_specs = (
        P("group", None, "tensor"),
        P("group", None, None),
        P("group", "tensor", None),
        P("group", "tensor", None),
        P(),
        P(),
        P(),
        P(),
    )
    out_specs = P("group", None, "tensor")
    return jax.shard_map(body, mesh=mesh, in_specs=in_specs, out_specs=out_specs, check_vma=False)
```

profile of v0, /device:TPU:1, one launch (start us, length us, event | category | flops | bytes accessed | tf_op | source)
XLA Modules:
  0.0 440.7 jit_solution(7627150290861144147)
XLA Ops:
  6.5 0.7 compare_select_fusion
  7.2 1.6 scatter_custom_fusion.2
  9.3 2.5 broadcast_in_dim.118
  11.8 2.9 scatter_fusion
  14.7 16.9 %all-to-all-start = ((bf16[32,1,32,2048]{3,2,1,0:T(8,128)(2,1)}), bf16[32,1,32,2048]{3,2,1,0:T(8,128)(2,1)}, u32[]{:S(2)}, u32[]{:S(2)}) async-start(bf16[32,1,32,2048]{3,2,1,0:T(8,128)(2,1)} %bitcast.125), calls=%async_computation | async-start | bytes 8388608 | tf_op jit(solution)/shard_map/all_to_all | solution.py:126
  31.7 22.6 %all_gather.21 = bf16[12,4,8192]{2,1,0:T(4,128)(2,1)S(1)} all-gather(bf16[12,4,512]{2,1,0:T(4,128)(2,1)S(1)} %copy-done.4), channel_id=1, replica_groups=mesh['group'=32,'tensor'=16] {'tensor'}, dimensions={2}, use_global_device_ids=true | all-gather | bytes 835584 | tf_op jit(solution)/shard_map/all_gather | solution.py:119
  54.3 0.2 slice.51
  54.6 1.7 scatter_custom_fusion.1
  56.4 0.6 gather_fusion.1
  57.0 1.6 scatter_custom_fusion
  58.6 0.6 gather_fusion
  59.3 0.5 reshape.250
  59.8 0.3 reshape.138
  60.1 0.1 copy.179
  60.5 0.4 select_reduce_fusion.1
  60.9 0.3 convolution_bitcast_fusion.1
  61.4 153.5 %all-to-all-done = bf16[32,1,32,2048]{3,2,1,0:T(8,128)(2,1)} async-done(((bf16[32,1,32,2048]{3,2,1,0:T(8,128)(2,1)}), bf16[32,1,32,2048]{3,2,1,0:T(8,128)(2,1)}, u32[]{:S(2)}, u32[]{:S(2)}) %all-to-all-start) | async-done | bytes 4194336 | tf_op jit(solution)/shard_map/all_to_all | solution.py:126
  214.9 2.8 gather_fusion.2
  217.7 0.2 copy.180
  218.0 0.2 fusion.41
  218.2 0.5 select_reduce_fusion
  218.7 0.7 convolution_bitcast_fusion
  219.4 0.1 copy.209
  219.5 1.4 pad_maximum_fusion
  220.9 0.4 fusion.17
  221.6 0.2 copy-done.3
  221.8 0.1 reshape.149
  222.1 0.6 gather_fusion.3
  222.7 0.6 gather_fusion.4
  223.3 0.7 select_bitcast_fusion
  224.1 0.2 fusion.23
  224.2 0.2 copy.155
  224.5 0.1 fusion.27
  224.6 0.1 copy.171
  224.7 0.8 fusion.10
  225.7 20.1 %all-gather.1 = f32[192,4,64]{2,1,0:T(4,128)S(1)} all-gather(f32[12,4,64]{2,1,0:T(4,128)S(1)} %copy.145), channel_id=3, replica_groups=mesh['group'=32,'tensor'=16] {'tensor'}, dimensions={0}, use_global_device_ids=true | all-gather | bytes 208896 | tf_op jit(solution)/shard_map/all_gather | solution.py:20
  245.9 21.4 %all-gather = f32[192,4,64]{2,1,0:T(4,128)S(1)} all-gather(f32[12,4,64]{2,1,0:T(4,128)S(1)} %pad_maximum_fusion.2), channel_id=2, replica_groups=mesh['group'=32,'tensor'=16] {'tensor'}, dimensions={0}, use_global_device_ids=true | all-gather | bytes 208896 | tf_op jit(solution)/shard_map/all_gather | solution.py:20
  267.3 124.1 %all-gather.5.cloned.1.call-done = f32[192,4,64,128]{3,2,1,0:T(8,128)} async-done(((f32[12,4,64,128]{3,2,1,0:T(8,128)}), f32[192,4,64,128]{3,2,1,0:T(8,128)}) %all-gather.5.cloned.1.call-update) | async-done | bytes 25165840 | tf_op jit(solution)/shard_map/all_gather | solution.py:20
  391.4 1.5 slice.56
  392.9 35.1 %while.19 = (s32[]{:T(128)}, f32[12,4,64]{2,1,0:T(4,128)S(1)}, f32[12,4,64]{2,1,0:T(4,128)S(1)}, f32[12,4,64,128]{3,2,1,0:T(8,128)S(1)}, f32[16,12,4,64]{3,2,1,0...) while((s32[]{:T(128)}, f32[12,4,64]{2,1,0:T(4,128)S(1)}, ...), condition=%wide.region_10.11_spmd, body=%wide.region_9.10_spmd.sunk | while | flops 1198085 | bytes 4841623 | solution.py:25
  393.0 2.3 fusion.49
  395.3 2.3 fusion.49
  397.7 2.3 fusion.49
  400.0 2.3 fusion.49
  402.4 2.3 fusion.49
  404.7 2.3 fusion.49
  407.0 2.3 fusion.49
  409.4 2.3 fusion.49
  411.7 2.3 fusion.49
  414.1 2.3 fusion.49
  416.4 2.3 fusion.49
  418.8 2.3 fusion.49
  421.1 2.3 fusion.49
  423.4 2.3 fusion.49
  425.8 2.3 fusion.49
  428.1 0.2 copy.151
  428.3 0.1 copy.158
  428.4 0.1 fusion.30
  428.5 0.7 copy.172
  429.2 0.9 copy.161
  430.2 1.0 copy.150
  431.2 0.2 copy.160
  431.4 0.8 multiply_add_fusion
  432.3 1.6 fusion.8
  (68 shorter events, 2.6 us)
Async XLA Ops:
  9.3 2.5 copy-start
  14.7 17.0 %copy-start.4 = (bf16[12,4,512]{2,1,0:T(4,128)(2,1)S(1)}, bf16[12,4,512]{2,1,0:T(4,128)(2,1)}, u32[]{:S(2)}) copy-start(bf16[12,4,512]{2,1,0:T(4,128)(2,1)} %param.12) | copy-start | bytes 147460
  14.7 200.2 %all-to-all-start = ((bf16[32,1,32,2048]{3,2,1,0:T(8,128)(2,1)}), bf16[32,1,32,2048]{3,2,1,0:T(8,128)(2,1)}, u32[]{:S(2)}, u32[]{:S(2)}) async-start(bf16[32,1,32,2048]{3,2,1,0:T(8,128)(2,1)} %bitcast.125), calls=%async_computation | async-start | bytes 8388608 | tf_op jit(solution)/shard_map/all_to_all | solution.py:126
  31.7 359.8 %all-gather.5.cloned.1.call-start = ((), (), s32[]{:S(2)}) async-start(), calls=%async_computation.1 | async-start | bytes 26738688 | tf_op jit(solution)/shard_map/all_gather | solution.py:20
  54.5 5.6 %copy-start.1 = (bf16[4,32,2048]{2,1,0:T(8,128)(2,1)S(1)}, bf16[4,32,2048]{2,1,0:T(8,128)(2,1)}, u32[]{:S(2)}) copy-start(bf16[4,32,2048]{2,1,0:T(8,128)(2,1)} %param.14) | copy-start | bytes 1572868
  58.6 1.6 copy-start.5
  220.9 0.9 copy-start.3
  428.3 1.9 copy-start.2
Sparse Core Ops, SparseCore 0:
  221.0 170.3 all-gather.4
where the time goes:
time: 442 us; the launch traced here: 441 us
  waiting for transfers between devices  278 us (63%)
  blocking collectives  64.1 us (15%)
  other arithmetic  40.4 us (9%)
  local copies, waits for them, and re-layouts  23.8 us (5%)
  starting transfers between devices  17 us (4%)
  between operations  13.8 us (3%)
    all_to_all x1, waiting for transfers between devices, body(): lax.all_to_all(outgoing.reshape(groups, per_pair, stride, features), 'gro...  153 us
    all_gather x1, waiting for transfers between devices, combined_all(): gathered = jax.tree.map(lambda a: lax.all_gather(a, axis), part)  124 us
    all_gather x2, blocking collectives, combined_all(): gathered = jax.tree.map(lambda a: lax.all_gather(a, axis), part)  41.5 us
    add x15, other arithmetic, combine(): earlier[2] * first_factor[..., None] + later[2] * second_factor[..., None]  34 us
    all_gather x1, blocking collectives, body(): asking = lax.all_gather(queries, 'tensor', axis=2, tiled=True)  22.6 us
    all_to_all x1, starting transfers between devices, body(): lax.all_to_all(outgoing.reshape(groups, per_pair, stride, features), 'gro...  16.9 us
  transfers between devices with their start and end apart: 2, of which 2 were waited for; matrix products, arithmetic and copies ran while one was open for 3% of the time, Pallas kernels for 0%

commit v1 on v0

v1 whole, which is shorter than its diff:
```python
import math

import jax
import jax.numpy as jnp
from jax import lax
from jax.experimental import pallas as pl
from jax.experimental.pallas import tpu as pltpu
from jax.sharding import PartitionSpec as P

H = 64
KVH = 8
HD = 128
STEPS = 4
MIG = 8
RES = 4
SLOTS = MIG + RES
GROUPS = 32
SHARDS = 16
STRIDE = 32
HEADS = H // SHARDS
QROWS = HEADS * STEPS
ROWS = SLOTS * QROWS
FEATURES = KVH * HD
CHUNK = QROWS + 2 * STEPS
PAYLOAD = ROWS + 16
FLOOR = -1e30
SCALE = 1.0 / math.sqrt(HD)
LIMIT = 48 * 1024 * 1024
BF = jnp.bfloat16
F32 = jnp.float32

VM = pl.BlockSpec(memory_space=pltpu.VMEM)
SM = pl.BlockSpec(memory_space=pltpu.SMEM)


def call(kernel, outs, specs, flops=0, moved=0, scratch=()):
    return pl.pallas_call(
        kernel,
        out_shape=outs,
        in_specs=specs,
        out_specs=jax.tree.map(lambda _: VM, outs),
        scratch_shapes=scratch,
        compiler_params=pltpu.CompilerParams(vmem_limit_bytes=LIMIT),
        cost_estimate=pl.CostEstimate(flops=flops, bytes_accessed=moved, transcendentals=0),
    )


def pack_kernel(target, where, asked, fresh, sent, kept):
    sent[...] = jnp.zeros_like(sent)
    pair = pl.multiple_of(where[0] // 2 * HD, HD)

    def chunk(slot):
        keys = fresh[slot, :, pl.ds(pair, HD)].astype(F32)
        values = fresh[slot, :, pl.ds(pair + FEATURES, HD)].astype(F32)
        entries = jnp.concatenate([keys, values], 0)
        return jnp.concatenate([asked[slot].astype(F32), entries], 0).astype(BF)

    for slot in range(RES):
        kept[slot] = chunk(slot)
    for slot in range(MIG):
        sent[target[slot]] = chunk(RES + slot)


def spread_kernel(origin, arrived, kept, asking, recent):
    recent[...] = jnp.zeros_like(recent)
    for row in range(SLOTS):
        chunk = arrived[origin[row]] if row < MIG else kept[row - MIG]
        for peer in range(SHARDS):
            asking[peer, row * QROWS : (row + 1) * QROWS, :] = chunk[:QROWS]
        recent[row * 8 : (row + 1) * 8, :] = chunk[QROWS:].astype(F32)


def scores_of(left, right):
    return lax.dot_general(left, right, (((1,), (1,)), ((), ())), preferred_element_type=F32) * SCALE


def partial_kernel(lengths, where, asking, moved, resident, payload, stats):
    stats[...] = jnp.zeros_like(stats)
    lane = lax.broadcasted_iota(jnp.int32, (QROWS, HD), 1)
    column = lax.broadcasted_iota(jnp.int32, (2 * QROWS, STRIDE), 1) + where[0] * STRIDE
    for row in range(SLOTS):
        cache = moved.at[row] if row < MIG else resident.at[row - MIG]
        usable = column < lengths[row]
        span = slice(row * QROWS, (row + 1) * QROWS)
        table = jnp.zeros((QROWS, HD), F32)
        for pair in range(KVH):
            keys = cache[:, pair * HD : (pair + 1) * HD]
            values = cache[:, FEATURES + pair * HD : FEATURES + (pair + 1) * HD]
            asked = jnp.concatenate([asking[2 * pair, span, :], asking[2 * pair + 1, span, :]], 0)
            scores = jnp.where(usable, scores_of(asked, keys), FLOOR)
            top = jnp.max(scores, axis=1, keepdims=True)
            first = top.astype(BF).astype(F32)
            second = (top - first).astype(BF).astype(F32)
            weights = jnp.where(usable, jnp.exp(scores - (first + second)), 0.0)
            total = jnp.sum(weights, axis=1, keepdims=True)
            blended = jnp.dot(weights.astype(BF), values, preferred_element_type=F32).astype(BF)
            total_first = total.astype(BF).astype(F32)
            columns = (first, total_first, second, total - total_first)
            for half in range(2):
                peer = 2 * pair + half
                rows = slice(half * QROWS, (half + 1) * QROWS)
                payload[peer, span, :] = blended[rows]
                for place, value in enumerate(columns):
                    table = jnp.where(lane == peer * 8 + place, value[rows], table)
        stats[span, :] = table
    low = stats[:HD, :].T.reshape(SHARDS, 8, HD)
    high = stats[HD:, :].T.reshape(SHARDS, 8, HD)
    payload[:, ROWS:, :] = jnp.concatenate([low, high], 1).astype(BF)


def merge_kernel(origin, gathered, asked, recent, sent, kept):
    entries = recent[...].astype(BF)
    row = lax.broadcasted_iota(jnp.int32, (ROWS, HD), 0)
    lane = lax.broadcasted_iota(jnp.int32, (ROWS, HD), 1)
    causal = (lane // 8 == row // QROWS) & (lane % 8 <= row % STEPS)
    fresh = jnp.where(causal, scores_of(asked[...], entries), FLOOR)
    fresh_top = jnp.max(fresh, axis=1, keepdims=True)

    tops = gathered[:, ROWS:, :].astype(F32)
    low = tops[:, :8, :].reshape(HD, HD).T
    high = tops[:, 8:, :].reshape(HD, HD).T[: ROWS - HD]
    pairs = jnp.concatenate([low, high], 0)
    both = pairs + pltpu.roll(pairs, HD - 2, 1)
    is_top = lane % 8 == 0
    tops = jnp.where(is_top, both, FLOOR)
    sums = pltpu.roll(both, HD - 1, 1)
    highest = jnp.maximum(jnp.max(tops, axis=1, keepdims=True), fresh_top)
    factors = jnp.where(is_top, jnp.exp(tops - highest), 0.0)
    fresh_weights = jnp.where(causal, jnp.exp(fresh - highest), 0.0)
    totals = jnp.sum(jnp.where(is_top, factors * sums, 0.0) + fresh_weights, axis=1, keepdims=True)
    blended = jnp.dot(
        pltpu.roll(fresh_weights, STEPS, 1).astype(BF), entries, preferred_element_type=F32
    )
    for peer in range(SHARDS):
        blended += factors[:, peer * 8 : peer * 8 + 1] * gathered[peer, :ROWS, :].astype(F32)
    result = (blended / totals).astype(BF)

    sent[...] = jnp.zeros_like(sent)
    for slot in range(MIG):
        sent[origin[slot]] = result[slot * QROWS : (slot + 1) * QROWS]
    for slot in range(RES):
        kept[slot] = result[(MIG + slot) * QROWS : (MIG + slot + 1) * QROWS]


def select_kernel(target, returned, kept, out):
    for slot in range(RES):
        out[slot] = kept[slot]
    for slot in range(MIG):
        out[RES + slot] = returned[target[slot]]


def body(
    queries,
    new_entries,
    resident_cache,
    prefill_cache,
    resident_kept,
    kept_tokens,
    prefill_slot,
    decode_slot,
):
    group = lax.axis_index("group")
    shard = lax.axis_index("tensor")

    def looked_up(names, first, values):
        wanted = first + jnp.arange(MIG, dtype=jnp.int32)
        return jnp.sum(jnp.where(names[None, :] == wanted[:, None], values[None, :], 0), axis=1)

    target = looked_up(decode_slot, group * SLOTS + RES, prefill_slot) // MIG
    origin = looked_up(prefill_slot, group * MIG, decode_slot) // SLOTS
    moved_len = looked_up(prefill_slot, group * MIG, kept_tokens)
    resident_len = lax.dynamic_slice_in_dim(resident_kept, group * RES, RES)
    lengths = jnp.concatenate([moved_len, resident_len])
    where = shard.reshape(1)

    asked = queries.reshape(SLOTS, STEPS, HEADS, HD).transpose(0, 2, 1, 3)
    asked = asked.reshape(SLOTS, QROWS, HD)
    shape = jax.ShapeDtypeStruct

    sent, kept = call(
        pack_kernel,
        (shape((GROUPS, CHUNK, HD), BF), shape((RES, CHUNK, HD), BF)),
        [SM, SM, VM, VM],
    )(target, where, asked, new_entries)
    arrived = lax.all_to_all(sent, "group", 0, 0, tiled=True)

    asking, recent = call(
        spread_kernel,
        (shape((SHARDS, ROWS, HD), BF), shape((HD, HD), F32)),
        [SM, VM, VM],
    )(origin, arrived, kept)
    everyone = lax.all_to_all(asking, "tensor", 0, 0, tiled=True)

    payload = call(
        partial_kernel,
        shape((SHARDS, PAYLOAD, HD), BF),
        [SM, SM, VM, VM, VM],
        flops=10**8,
        moved=3 * 2**20,
        scratch=[pltpu.VMEM((2 * HD, HD), F32)],
    )(lengths, where, everyone, prefill_cache, resident_cache)
    gathered = lax.all_to_all(payload, "tensor", 0, 0, tiled=True)

    finished, here = call(
        merge_kernel,
        (shape((GROUPS, QROWS, HD), BF), shape((RES, QROWS, HD), BF)),
        [SM, VM, VM, VM],
    )(origin, gathered, asking[0], recent)
    returned = lax.all_to_all(finished, "group", 0, 0, tiled=True)

    result = call(select_kernel, shape((SLOTS, QROWS, HD), BF), [SM, VM, VM])(target, returned, here)
    result = result.reshape(SLOTS, HEADS, STEPS, HD).transpose(0, 2, 1, 3)
    return result.reshape(SLOTS, STEPS, HEADS * HD)


def solution(mesh):
    in_specs = (
        P("group", None, "tensor"),
        P("group", None, None),
        P("group", "tensor", None),
        P("group", "tensor", None),
        P(),
        P(),
        P(),
        P(),
    )
    out_specs = P("group", None, "tensor")
    return jax.shard_map(body, mesh=mesh, in_specs=in_specs, out_specs=out_specs, check_vma=False)
```

time: 442 us -> 128 us (0.29)
  waiting for transfers between devices: 278 us -> 41.7 us
  other arithmetic: 40.4 us -> 0.31 us
  blocking collectives: 64.1 us -> 25.7 us
  Pallas kernels: 0 us -> 28.5 us
  local copies, waits for them, and re-layouts: 23.8 us -> 3.95 us
  between operations: 13.8 us -> 0.08 us
  starting transfers between devices: 17 us -> 27.4 us
    all_gather x1 -> x0, waiting for transfers between devices: 124 us -> none  [combined_all(): gathered = jax.tree.map(lambda a: lax.all_gather(a, axis), part)]
    all_to_all x1 -> x3, waiting for transfers between devices: 153 us -> 41.7 us  [the longest x1 18.6 us: body(): arrived = lax.all_to_all(sent, 'group', 0, 0, tiled=True)]
    all_gather x3 -> x0, blocking collectives: 64.1 us -> none  [the longest x2 41.5 us: combined_all(): gathered = jax.tree.map(lambda a: lax.all_gather(a, axis), part)]
    add x33 -> x1, other arithmetic: 35.5 us -> 0.01 us  [looked_up(): wanted = first + jnp.arange(MIG, dtype=jnp.int32)]
    pallas_call x0 -> x5, Pallas kernels: none -> 28.5 us  [the longest x1 22.7 us: body(): call(partial_kernel, shape((SHARDS, PAYLOAD, HD), BF), [SM, SM, VM, VM, V...]
    all_to_all x0 -> x1, blocking collectives: none -> 25.7 us  [body(): returned = lax.all_to_all(finished, 'group', 0, 0, tiled=True)]
    all_to_all x1 -> x3, starting transfers between devices: 16.9 us -> 27.4 us  [the longest x1 16.9 us: body(): arrived = lax.all_to_all(sent, 'group', 0, 0, tiled=True)]
    scatter x4 -> x0, local copies, waits for them, and re-layouts: 7.68 us -> none  [the longest x1 2.89 us: body(): outgoing = jnp.zeros((groups * per_pair, stride, features), jnp.bfloat16)...]
  transfers between devices with their start and end apart: 2 -> 3, of which waited for: 2 -> 3; matrix products, arithmetic and copies ran while one was open for 3% -> 1% of each run, Pallas kernels for 0% -> 0%
where the time goes in v1:
time: 128 us
  waiting for transfers between devices  41.7 us (33%)
  Pallas kernels  28.5 us (22%)
  starting transfers between devices  27.4 us (21%)
  blocking collectives  25.7 us (20%)
  local copies, waits for them, and re-layouts  3.95 us (3%)
    all_to_all x1, blocking collectives, body(): returned = lax.all_to_all(finished, 'group', 0, 0, tiled=True)  25.7 us
    pallas_call x1, Pallas kernels, body(): call(partial_kernel, shape((SHARDS, PAYLOAD, HD), BF), [SM, SM, VM, VM, V...  22.7 us
    all_to_all x1, waiting for transfers between devices, body(): arrived = lax.all_to_all(sent, 'group', 0, 0, tiled=True)  18.6 us
    all_to_all x1, starting transfers between devices, body(): arrived = lax.all_to_all(sent, 'group', 0, 0, tiled=True)  16.9 us
    all_to_all x1, waiting for transfers between devices, body(): everyone = lax.all_to_all(asking, 'tensor', 0, 0, tiled=True)  11.7 us
    all_to_all x1, waiting for transfers between devices, body(): gathered = lax.all_to_all(payload, 'tensor', 0, 0, tiled=True)  11.4 us
    all_to_all x1, starting transfers between devices, body(): everyone = lax.all_to_all(asking, 'tensor', 0, 0, tiled=True)  6.89 us
    all_to_all x1, starting transfers between devices, body(): gathered = lax.all_to_all(payload, 'tensor', 0, 0, tiled=True)  3.62 us
  transfers between devices with their start and end apart: 3, of which 3 were waited for; matrix products, arithmetic and copies ran while one was open for 1% of the time, Pallas kernels for 0%

profile of v1, /device:TPU:1, one launch (start us, length us, event | category | flops | bytes accessed | tf_op | source)
XLA Modules:
  0.0 127.7 jit_solution(8215029632613818909)
XLA Ops:
  0.0 0.0 copy-start.5
  0.0 0.0 copy-start.6
  0.0 0.0 copy-start.4
  0.0 0.7 copy-done.5
  0.7 0.0 copy-done.6
  0.7 0.0 copy-done.4
  0.7 0.2 fusion
  0.9 0.0 copy-start.2
  1.0 0.9 copy-done.2
  1.9 0.0 copy-start.3
  1.9 0.8 copy-done.3
  2.7 1.2 shard_map.82
  3.9 0.0 copy-start
  3.9 16.9 %all-to-all-start = ((bf16[32,24,128]{2,1,0:T(8,128)(2,1)}), bf16[32,24,128]{2,1,0:T(8,128)(2,1)S(1)}, u32[]{:S(2)}, u32[]{:S(2)}) async-start(bf16[32,24,128]{2,1,0:T(8,128)(2,1)} %get-tuple-element.11), calls=%async_computation | async-start | bytes 393216 | tf_op jit(solution)/shard_map/all_to_all | solution.py:185
  20.8 18.6 %all-to-all-done.arrived = bf16[32,24,128]{2,1,0:T(8,128)(2,1)S(1)} async-done(((bf16[32,24,128]{2,1,0:T(8,128)(2,1)}), bf16[32,24,128]{2,1,0:T(8,128)(2,1)S(1)}, u32[]{:S(2)}, u32[]{:S(2)}) %all-to-all-start) | async-done | bytes 196640 | tf_op jit(solution)/shard_map/all_to_all | solution.py:185
  39.4 1.6 %shard_map.83 = (bf16[16,192,128]{2,1,0:T(8,128)(2,1)}, f32[128,128]{1,0:T(8,128)S(1)}) custom-call(s32[8]{0:T(128)S(1)} %and_select_fusion.origin, bf16[32,24,128]{2,1,0:T(8,128)(2,1)S(1)} %all-to-all-done.arrived, bf16[4,24,128]{2,1,0:T(8,128)(2,1)S(1)} %get-tuple-element.12.kept), custom_call_target="tpu_custom_call" | custom-call | tf_op jit(solution)/shard_map/pallas_call | solution.py:187
  41.1 0.0 copy-start.1
  41.1 6.9 %all-to-all-start.1 = ((bf16[16,192,128]{2,1,0:T(8,128)(2,1)}), bf16[16,192,128]{2,1,0:T(8,128)(2,1)S(1)}, u32[]{:S(2)}, u32[]{:S(2)}) async-start(bf16[16,192,128]{2,1,0:T(8,128)(2,1)} %get-tuple-element.13), calls=%async_computation.1 | async-start | bytes 1572864 | tf_op jit(solution)/shard_map/all_to_all | solution.py:192
  48.0 0.0 copy-start.7
  48.0 0.6 copy-done.7
  48.6 0.1 dynamic_slice.3
  48.7 0.1 pad_add_fusion.lengths
  48.8 11.7 %all-to-all-done.1.asking = bf16[16,192,128]{2,1,0:T(8,128)(2,1)S(1)} async-done(((bf16[16,192,128]{2,1,0:T(8,128)(2,1)}), bf16[16,192,128]{2,1,0:T(8,128)(2,1)S(1)}, u32[]{:S(2)}, u32[]{:S(2)}) %all-to-all-start.1) | async-done | bytes 786464 | tf_op jit(solution)/shard_map/all_to_all | solution.py:192
  60.5 0.0 copy-done
  60.5 0.0 copy-done.1
  60.5 22.7 %shard_map.84 = bf16[16,208,128]{2,1,0:T(8,128)(2,1)} custom-call(s32[12]{0:T(128)S(1)} %pad_add_fusion.lengths, s32[1]{0:T(128)} %bitcast.where, bf16[16,192,128]{2,1,0:T(8,128)(2,1)S(1)} %all-to-all-done.1.asking, bf16[8,32,2048]{2,1,0:T(8,128)(2,1)S(1)} %copy-done, bf16[4,32,2048]{2,1,0:T(8,128)(2,1)S(1)} %copy-done.1), custom_call_target="tpu_custom_call" | custom-call | flops 100000000 | bytes 3145728 | tf_op jit(solution)/shard_map/pallas_call | solution.py:194
  83.2 3.6 %all-to-all-start.2 = ((bf16[16,208,128]{2,1,0:T(8,128)(2,1)}), bf16[16,208,128]{2,1,0:T(8,128)(2,1)S(1)}, u32[]{:S(2)}, u32[]{:S(2)}) async-start(bf16[16,208,128]{2,1,0:T(8,128)(2,1)} %shard_map.84), calls=%async_computation.2 | async-start | bytes 1703936 | tf_op jit(solution)/shard_map/all_to_all | solution.py:202
  86.8 0.8 slice_bitcast_fusion.asked
  87.6 11.4 %all-to-all-done.2.gathered = bf16[16,208,128]{2,1,0:T(8,128)(2,1)S(1)} async-done(((bf16[16,208,128]{2,1,0:T(8,128)(2,1)}), bf16[16,208,128]{2,1,0:T(8,128)(2,1)S(1)}, u32[]{:S(2)}, u32[]{:S(2)}) %all-to-all-start.2) | async-done | bytes 852000 | tf_op jit(solution)/shard_map/all_to_all | solution.py:202
  99.1 1.7 %shard_map.85 = (bf16[32,16,128]{2,1,0:T(8,128)(2,1)S(1)}, bf16[4,16,128]{2,1,0:T(8,128)(2,1)S(1)}) custom-call(s32[8]{0:T(128)S(1)} %and_select_fusion.origin, bf16[16,208,128]{2,1,0:T(8,128)(2,1)S(1)} %all-to-all-done.2.gathered, bf16[192,128]{1,0:T(8,128)(2,1)S(1)} %slice_bitcast_fusion.asked, f32[128,128]{1,0:T(8,128)S(1)} %get-tuple-element.14.recent), custom_call_target="tpu_custom_call" | custom-call | tf_op jit(solution)/shard_map/pallas_call | solution.py:204
  100.8 25.7 %all_to_all.20.returned = bf16[32,16,128]{2,1,0:T(8,128)(2,1)S(1)} all-to-all(bf16[32,16,128]{2,1,0:T(8,128)(2,1)S(1)} %get-tuple-element.15), channel_id=1, replica_groups=mesh['group'=32,'tensor'=16] {'group'}, dimensions={0} | all-to-all | bytes 262144 | tf_op jit(solution)/shard_map/all_to_all | solution.py:209
  126.5 1.2 shard_map.86
  (3 shorter events, 0.0 us)
Async XLA Ops:
  0.0 0.7 copy-start.5
  0.0 0.7 copy-start.6
  0.0 0.7 copy-start.4
  0.9 0.9 copy-start.2
  1.9 0.8 copy-start.3
  3.9 56.5 %copy-start = (bf16[8,32,2048]{2,1,0:T(8,128)(2,1)S(1)}, bf16[8,32,2048]{2,1,0:T(8,128)(2,1)}, u32[]{:S(2)}) copy-start(bf16[8,32,2048]{2,1,0:T(8,128)(2,1)} %moved.1) | copy-start | bytes 3145732
  3.9 35.5 %all-to-all-start = ((bf16[32,24,128]{2,1,0:T(8,128)(2,1)}), bf16[32,24,128]{2,1,0:T(8,128)(2,1)S(1)}, u32[]{:S(2)}, u32[]{:S(2)}) async-start(bf16[32,24,128]{2,1,0:T(8,128)(2,1)} %get-tuple-element.11), calls=%async_computation | async-start | bytes 393216 | tf_op jit(solution)/shard_map/all_to_all | solution.py:185
  41.1 19.4 %copy-start.1 = (bf16[4,32,2048]{2,1,0:T(8,128)(2,1)S(1)}, bf16[4,32,2048]{2,1,0:T(8,128)(2,1)}, u32[]{:S(2)}) copy-start(bf16[4,32,2048]{2,1,0:T(8,128)(2,1)} %resident.1) | copy-start | bytes 1572868
  41.1 19.4 %all-to-all-start.1 = ((bf16[16,192,128]{2,1,0:T(8,128)(2,1)}), bf16[16,192,128]{2,1,0:T(8,128)(2,1)S(1)}, u32[]{:S(2)}, u32[]{:S(2)}) async-start(bf16[16,192,128]{2,1,0:T(8,128)(2,1)} %get-tuple-element.13), calls=%async_computation.1 | async-start | bytes 1572864 | tf_op jit(solution)/shard_map/all_to_all | solution.py:192
  48.0 0.7 copy-start.7
  83.2 15.9 %all-to-all-start.2 = ((bf16[16,208,128]{2,1,0:T(8,128)(2,1)}), bf16[16,208,128]{2,1,0:T(8,128)(2,1)S(1)}, u32[]{:S(2)}, u32[]{:S(2)}) async-start(bf16[16,208,128]{2,1,0:T(8,128)(2,1)} %shard_map.84), calls=%async_computation.2 | async-start | bytes 1703936 | tf_op jit(solution)/shard_map/all_to_all | solution.py:202

commit v2 on v1

--- a/solution.py
+++ b/solution.py
@@ -16,14 +16,17 @@
 SLOTS = MIG + RES
 GROUPS = 32
 SHARDS = 16
+SIDE = 4
 STRIDE = 32
 HEADS = H // SHARDS
+PAIRS = KVH // SIDE
 QROWS = HEADS * STEPS
 ROWS = SLOTS * QROWS
 FEATURES = KVH * HD
+WIDTH = PAIRS * HD
 CHUNK = QROWS + 2 * STEPS
 PAYLOAD = ROWS + 16
-FLOOR = -1e30
+FLOOR = -(2.0**100)
 SCALE = 1.0 / math.sqrt(HD)
 LIMIT = 48 * 1024 * 1024
 BF = jnp.bfloat16
@@ -61,12 +64,25 @@
         sent[target[slot]] = chunk(RES + slot)
 
 
-def spread_kernel(origin, arrived, kept, asking, recent):
+def split_kernel(where, moved, resident, *outs):
+    along = where[0] // SIDE
+    for step, out in enumerate(outs):
+        first = pl.multiple_of((along + step) % SIDE * WIDTH, WIDTH)
+        for part in range(2):
+            lanes = pl.ds(first + part * FEATURES, WIDTH)
+            columns = slice(part * WIDTH, (part + 1) * WIDTH)
+            out[:MIG, :, columns] = moved[:, :, lanes]
+            out[MIG:, :, columns] = resident[:, :, lanes]
+
+
+def spread_kernel(origin, arrived, kept, asking, own, recent):
     recent[...] = jnp.zeros_like(recent)
     for row in range(SLOTS):
         chunk = arrived[origin[row]] if row < MIG else kept[row - MIG]
-        for peer in range(SHARDS):
-            asking[peer, row * QROWS : (row + 1) * QROWS, :] = chunk[:QROWS]
+        span = slice(row * QROWS, (row + 1) * QROWS)
+        for peer in range(SIDE):
+            asking[peer, span, :] = chunk[:QROWS]
+        own[span, :] = chunk[:QROWS]
         recent[row * 8 : (row + 1) * 8, :] = chunk[QROWS:].astype(F32)
 
 
@@ -74,38 +90,52 @@
     return lax.dot_general(left, right, (((1,), (1,)), ((), ())), preferred_element_type=F32) * SCALE
 
 
-def partial_kernel(lengths, where, asking, moved, resident, payload, stats):
-    stats[...] = jnp.zeros_like(stats)
-    lane = lax.broadcasted_iota(jnp.int32, (QROWS, HD), 1)
-    column = lax.broadcasted_iota(jnp.int32, (2 * QROWS, STRIDE), 1) + where[0] * STRIDE
+def partial_kernel(lengths, where, asking, *rest):
+    *blocks, payload, scores, weights, stats = rest
+    along, across = where[0] // SIDE, where[0] % SIDE
+    column = lax.broadcasted_iota(jnp.int32, (1, HD), 1)
+    source = ((along - column // STRIDE) & (SIDE - 1)) * SIDE + across
+    position = source * STRIDE + column % STRIDE
+
+    def stored(row, place):
+        lanes = slice(place * HD, (place + 1) * HD)
+        return jnp.concatenate([block[row, :, lanes] for block in blocks], 0)
+
     for row in range(SLOTS):
-        cache = moved.at[row] if row < MIG else resident.at[row - MIG]
-        usable = column < lengths[row]
+        usable = position < lengths[row]
         span = slice(row * QROWS, (row + 1) * QROWS)
-        table = jnp.zeros((QROWS, HD), F32)
-        for pair in range(KVH):
-            keys = cache[:, pair * HD : (pair + 1) * HD]
-            values = cache[:, FEATURES + pair * HD : FEATURES + (pair + 1) * HD]
+        for pair in range(PAIRS):
             asked = jnp.concatenate([asking[2 * pair, span, :], asking[2 * pair + 1, span, :]], 0)
-            scores = jnp.where(usable, scores_of(asked, keys), FLOOR)
-            top = jnp.max(scores, axis=1, keepdims=True)
-            first = top.astype(BF).astype(F32)
-            second = (top - first).astype(BF).astype(F32)
-            weights = jnp.where(usable, jnp.exp(scores - (first + second)), 0.0)
-            total = jnp.sum(weights, axis=1, keepdims=True)
-            blended = jnp.dot(weights.astype(BF), values, preferred_element_type=F32).astype(BF)
-            total_first = total.astype(BF).astype(F32)
-            columns = (first, total_first, second, total - total_first)
-            for half in range(2):
-                peer = 2 * pair + half
-                rows = slice(half * QROWS, (half + 1) * QROWS)
-                payload[peer, span, :] = blended[rows]
-                for place, value in enumerate(columns):
-                    table = jnp.where(lane == peer * 8 + place, value[rows], table)
-        stats[span, :] = table
-    low = stats[:HD, :].T.reshape(SHARDS, 8, HD)
-    high = stats[HD:, :].T.reshape(SHARDS, 8, HD)
-    payload[:, ROWS:, :] = jnp.concatenate([low, high], 1).astype(BF)
+            found = jnp.where(usable, scores_of(asked, stored(row, pair)), FLOOR)
+            scores[2 * pair, span, :] = found[:QROWS]
+            scores[2 * pair + 1, span, :] = found[QROWS:]
+    lane = lax.broadcasted_iota(jnp.int32, (ROWS, HD), 1)
+    table = jnp.zeros((ROWS, HD), F32)
+    for peer in range(SIDE):
+        found = scores[peer]
+        top = jnp.max(found, axis=1, keepdims=True)
+        first = top.astype(BF).astype(F32)
+        second = (top - first).astype(BF).astype(F32)
+        weight = jnp.exp(found - (first + second))
+        total = jnp.sum(weight, axis=1, keepdims=True)
+        weights[peer] = weight.astype(BF)
+        total_first = total.astype(BF).astype(F32)
+        for place, value in enumerate((first, total_first, second, total - total_first)):
+            table = jnp.where(lane == peer * 8 + place, value, table)
+    stats[:ROWS, :] = table
+    stats[ROWS:, :] = jnp.zeros((2 * HD - ROWS, HD), F32)
+    low = stats[:HD, :].T
+    high = stats[HD:, :].T
+    for peer in range(SIDE):
+        rows = slice(peer * 8, (peer + 1) * 8)
+        payload[peer, ROWS:, :] = jnp.concatenate([low[rows], high[rows]], 0).astype(BF)
+    for row in range(SLOTS):
+        span = slice(row * QROWS, (row + 1) * QROWS)
+        for pair in range(PAIRS):
+            weight = jnp.concatenate([weights[2 * pair, span, :], weights[2 * pair + 1, span, :]], 0)
+            blended = jnp.dot(weight, stored(row, PAIRS + pair), preferred_element_type=F32).astype(BF)
+            payload[2 * pair, span, :] = blended[:QROWS]
+            payload[2 * pair + 1, span, :] = blended[QROWS:]
 
 
 def merge_kernel(origin, gathered, asked, recent, sent, kept):
@@ -117,11 +147,12 @@
     fresh_top = jnp.max(fresh, axis=1, keepdims=True)
 
     tops = gathered[:, ROWS:, :].astype(F32)
-    low = tops[:, :8, :].reshape(HD, HD).T
-    high = tops[:, 8:, :].reshape(HD, HD).T[: ROWS - HD]
+    blank = jnp.zeros((HD - SIDE * 8, HD), F32)
+    low = jnp.concatenate([tops[:, :8, :].reshape(SIDE * 8, HD), blank], 0).T
+    high = jnp.concatenate([tops[:, 8:, :].reshape(SIDE * 8, HD), blank], 0).T[: ROWS - HD]
     pairs = jnp.concatenate([low, high], 0)
     both = pairs + pltpu.roll(pairs, HD - 2, 1)
-    is_top = lane % 8 == 0
+    is_top = (lane % 8 == 0) & (lane < SIDE * 8)
     tops = jnp.where(is_top, both, FLOOR)
     sums = pltpu.roll(both, HD - 1, 1)
     highest = jnp.maximum(jnp.max(tops, axis=1, keepdims=True), fresh_top)
@@ -131,7 +162,7 @@
     blended = jnp.dot(
         pltpu.roll(fresh_weights, STEPS, 1).astype(BF), entries, preferred_element_type=F32
     )
-    for peer in range(SHARDS):
+    for peer in range(SIDE):
         blended += factors[:, peer * 8 : peer * 8 + 1] * gathered[peer, :ROWS, :].astype(F32)
     result = (blended / totals).astype(BF)
 
@@ -172,6 +203,11 @@
     resident_len = lax.dynamic_slice_in_dim(resident_kept, group * RES, RES)
     lengths = jnp.concatenate([moved_len, resident_len])
     where = shard.reshape(1)
+    rings = [[SIDE * y + x for x in range(SIDE)] for y in range(SIDE)]
+
+    def across(array):
+        return lax.all_to_all(array, "tensor", 0, 0, axis_index_groups=rings, tiled=True)
+
 
     asked = queries.reshape(SLOTS, STEPS, HEADS, HD).transpose(0, 2, 1, 3)
     asked = asked.reshape(SLOTS, QROWS, HD)
@@ -184,28 +220,43 @@
     )(target, where, asked, new_entries)
     arrived = lax.all_to_all(sent, "group", 0, 0, tiled=True)
 
-    asking, recent = call(
+    split = call(
+        split_kernel,
+        (shape((SLOTS, STRIDE, 2 * WIDTH), BF),) * SIDE,
+        [SM, VM, VM],
+        moved=3 * 2**20,
+    )(where, prefill_cache, resident_cache)
+    blocks = [split[0]]
+    for step in range(1, SIDE):
+        steps = [(t, (t + step * SIDE) % SHARDS) for t in range(SHARDS)]
+        blocks.append(lax.ppermute(split[step], "tensor", steps))
+
+    asking, own, recent = call(
         spread_kernel,
-        (shape((SHARDS, ROWS, HD), BF), shape((HD, HD), F32)),
+        (shape((SIDE, ROWS, HD), BF), shape((ROWS, HD), BF), shape((HD, HD), F32)),
         [SM, VM, VM],
     )(origin, arrived, kept)
-    everyone = lax.all_to_all(asking, "tensor", 0, 0, tiled=True)
+    everyone = across(asking)
 
     payload = call(
         partial_kernel,
-        shape((SHARDS, PAYLOAD, HD), BF),
-        [SM, SM, VM, VM, VM],
+        shape((SIDE, PAYLOAD, HD), BF),
+        [SM, SM] + [VM] * (1 + SIDE),
         flops=10**8,
         moved=3 * 2**20,
-        scratch=[pltpu.VMEM((2 * HD, HD), F32)],
-    )(lengths, where, everyone, prefill_cache, resident_cache)
-    gathered = lax.all_to_all(payload, "tensor", 0, 0, tiled=True)
+        scratch=[
+            pltpu.VMEM((SIDE, ROWS, HD), F32),
+            pltpu.VMEM((SIDE, ROWS, HD), BF),
+            pltpu.VMEM((2 * HD, HD), F32),
+        ],
+    )(lengths, where, everyone, *blocks)
+    gathered = across(payload)
 
     finished, here = call(
         merge_kernel,
         (shape((GROUPS, QROWS, HD), BF), shape((RES, QROWS, HD), BF)),
         [SM, VM, VM, VM],
-    )(origin, gathered, asking[0], recent)
+    )(origin, gathered, own, recent)
     returned = lax.all_to_all(finished, "group", 0, 0, tiled=True)
 
     result = call(select_kernel, shape((SLOTS, QROWS, HD), BF), [SM, VM, VM])(target, returned, here)

time: 128 us -> 91.3 us (0.71)
  waiting for transfers between devices: 41.7 us -> 10.8 us
  Pallas kernels: 28.5 us -> 6.59 us
  blocking collectives: 25.7 us -> 36 us
  starting transfers between devices: 27.4 us -> 31.5 us
    pallas_call x2 -> x3, Pallas kernels: 24.4 us -> 2.76 us  [the longest x1 1.31 us: body(): call(partial_kernel, shape((SIDE, PAYLOAD, HD), BF), [SM, SM] + [VM] * (1...]
    all_to_all x2 -> x1, waiting for transfers between devices: 23.1 us -> 3.23 us  [across(): lax.all_to_all(array, 'tensor', 0, 0, axis_index_groups=rings, tiled=True)]
    all_to_all x1, waiting for transfers between devices: 18.6 us -> 6.42 us  [body(): arrived = lax.all_to_all(sent, 'group', 0, 0, tiled=True)]
    ppermute x0 -> x3, starting transfers between devices: none -> 10.7 us  [body(): blocks.append(lax.ppermute(split[step], 'tensor', steps))]
    all_to_all x0 -> x1, blocking collectives: none -> 7.65 us  [across(): lax.all_to_all(array, 'tensor', 0, 0, axis_index_groups=rings, tiled=True)]
    all_to_all x2 -> x1, starting transfers between devices: 10.5 us -> 4.01 us  [across(): lax.all_to_all(array, 'tensor', 0, 0, axis_index_groups=rings, tiled=True)]
    all_to_all x1, blocking collectives: 25.7 us -> 28.4 us  [body(): returned = lax.all_to_all(finished, 'group', 0, 0, tiled=True)]
    unnamed x16 -> x10, local copies, waits for them, and re-layouts: 3.08 us -> 3.6 us
  transfers between devices with their start and end apart: 3 -> 5, of which waited for: 3 -> 3; matrix products, arithmetic and copies ran while one was open for 1% -> 0% of each run, Pallas kernels for 0% -> 2%
where the time goes in v2:
time: 91.3 us; the launch traced here: 89.7 us
  blocking collectives  36 us (39%)
  starting transfers between devices  31.5 us (35%)
  waiting for transfers between devices  10.8 us (12%)
  Pallas kernels  6.59 us (7%)
  local copies, waits for them, and re-layouts  3.68 us (4%)
  other arithmetic  1.08 us (1%)
    all_to_all x1, blocking collectives, body(): returned = lax.all_to_all(finished, 'group', 0, 0, tiled=True)  28.4 us
    all_to_all x1, starting transfers between devices, body(): arrived = lax.all_to_all(sent, 'group', 0, 0, tiled=True)  16.7 us
    ppermute x3, starting transfers between devices, body(): blocks.append(lax.ppermute(split[step], 'tensor', steps))  10.7 us
    all_to_all x1, blocking collectives, across(): lax.all_to_all(array, 'tensor', 0, 0, axis_index_groups=rings, tiled=True)  7.65 us
    all_to_all x1, waiting for transfers between devices, body(): arrived = lax.all_to_all(sent, 'group', 0, 0, tiled=True)  6.42 us
    all_to_all x1, starting transfers between devices, across(): lax.all_to_all(array, 'tensor', 0, 0, axis_index_groups=rings, tiled=True)  4.01 us
    unnamed x10, local copies, waits for them, and re-layouts  3.6 us
    all_to_all x1, waiting for transfers between devices, across(): lax.all_to_all(array, 'tensor', 0, 0, axis_index_groups=rings, tiled=True)  3.23 us
  transfers between devices with their start and end apart: 5, of which 3 were waited for; matrix products, arithmetic and copies ran while one was open for 0% of the time, Pallas kernels for 2%

profile of v2, /device:TPU:1, one launch (start us, length us, event | category | flops | bytes accessed | tf_op | source)
XLA Modules:
  0.0 89.7 jit_solution(9993614710908848159)
XLA Ops:
  0.0 0.0 copy-start.1
  0.0 1.0 %fusion = (s32[8]{0:T(128)S(1)}, s32[8]{0:T(128)S(1)}, s32[8]{0:T(128)S(1)}) fusion(s32[256]{0:T(256)} %param.14, s32[256]{0:T(256)} %param.15, s32[8]{0:T(128)S(1)} %get-tuple-element.30, s32[8]{0:T(128)S(1)} %get-tuple-element.31, s32[256]{0:T(256)} %param.13), kind=kLoop, calls=%fused_computation.2 | loop fusion | flops 16360 | bytes 3232 | tf_op jit(solution)/shard_map/reduce_sum | solution.py:198
  1.0 0.0 copy-start.2
  1.0 0.9 %copy-done.2 = bf16[12,4,2048]{2,1,0:T(4,128)(2,1)S(1)} copy-done((bf16[12,4,2048]{2,1,0:T(4,128)(2,1)S(1)}, bf16[12,4,2048]{2,1,0:T(4,128)(2,1)}, u32[]{:S(2)}) %copy-start.2) | copy-done | bytes 196632
  1.9 0.0 copy-start.3
  1.9 0.8 copy-done.3
  2.7 1.2 %shard_map.82 = (bf16[32,24,128]{2,1,0:T(8,128)(2,1)}, bf16[4,24,128]{2,1,0:T(8,128)(2,1)S(1)}) custom-call(s32[8]{0:T(128)S(1)} %and_select_fusion.1.target, s32[1]{0:T(128)} %bitcast.where, bf16[12,16,128]{2,1,0:T(8,128)(2,1)S(1)} %bitcast.11, bf16[12,4,2048]{2,1,0:T(4,128)(2,1)S(1)} %copy-done.2), custom_call_target="tpu_custom_call" | custom-call | tf_op jit(solution)/shard_map/pallas_call | solution.py:216
  4.0 16.7 %all-to-all-start = ((bf16[32,24,128]{2,1,0:T(8,128)(2,1)}), bf16[32,24,128]{2,1,0:T(8,128)(2,1)S(1)}, u32[]{:S(2)}, u32[]{:S(2)}) async-start(bf16[32,24,128]{2,1,0:T(8,128)(2,1)} %get-tuple-element.16), calls=%async_computation | async-start | bytes 393216 | tf_op jit(solution)/shard_map/all_to_all | solution.py:221
  20.7 0.0 copy-done.1
  20.7 0.0 copy-start
  20.8 1.2 %copy-done = bf16[8,32,2048]{2,1,0:T(8,128)(2,1)S(1)} copy-done((bf16[8,32,2048]{2,1,0:T(8,128)(2,1)S(1)}, bf16[8,32,2048]{2,1,0:T(8,128)(2,1)}, u32[]{:S(2)}) %copy-start) | copy-done | bytes 1048600
  22.0 0.2 shard_map.84
  22.2 3.2 %collective-permute-start = (bf16[12,32,512]{2,1,0:T(8,128)(2,1)S(1)}, bf16[12,32,512]{2,1,0:T(8,128)(2,1)S(1)}, u32[]{:S(2)}, u32[]{:S(2)}) collective-permute-start(bf16[12,32,512]{2,1,0:T(8,128)(2,1)S(1)} %get-tuple-element.20), channel_id=1, source_target_pairs={{0,4},{1,5},{2,6},{3,7},{4,8},{5,9},{6,10},{7,11},{8,12},{9,13},{1... | collective-permute-start | bytes 1179656 | tf_op jit(solution)/shard_map/ppermute | solution.py:232
  25.4 4.5 %collective-permute-start.1 = (bf16[12,32,512]{2,1,0:T(8,128)(2,1)S(1)}, bf16[12,32,512]{2,1,0:T(8,128)(2,1)S(1)}, u32[]{:S(2)}, u32[]{:S(2)}) collective-permute-start(bf16[12,32,512]{2,1,0:T(8,128)(2,1)S(1)} %get-tuple-element.21), channel_id=1, source_target_pairs={{0,8},{1,9},{2,10},{3,11},{4,12},{5,13},{6,14},{7,15},{8,0},{9,1},... | collective-permute-start | bytes 1179656 | tf_op jit(solution)/shard_map/ppermute | solution.py:232
  29.9 3.0 %collective-permute-start.2 = (bf16[12,32,512]{2,1,0:T(8,128)(2,1)S(1)}, bf16[12,32,512]{2,1,0:T(8,128)(2,1)S(1)}, u32[]{:S(2)}, u32[]{:S(2)}) collective-permute-start(bf16[12,32,512]{2,1,0:T(8,128)(2,1)S(1)} %get-tuple-element.22), channel_id=1, source_target_pairs={{0,12},{1,13},{2,14},{3,15},{4,0},{5,1},{6,2},{7,3},{8,4},{9,5},{1... | collective-permute-start | bytes 1179656 | tf_op jit(solution)/shard_map/ppermute | solution.py:232
  32.9 6.4 %all-to-all-done.arrived = bf16[32,24,128]{2,1,0:T(8,128)(2,1)S(1)} async-done(((bf16[32,24,128]{2,1,0:T(8,128)(2,1)}), bf16[32,24,128]{2,1,0:T(8,128)(2,1)S(1)}, u32[]{:S(2)}, u32[]{:S(2)}) %all-to-all-start) | async-done | bytes 196640 | tf_op jit(solution)/shard_map/all_to_all | solution.py:221
  39.4 1.2 %shard_map.83 = (bf16[4,192,128]{2,1,0:T(8,128)(2,1)}, bf16[192,128]{1,0:T(8,128)(2,1)S(1)}, f32[128,128]{1,0:T(8,128)S(1)}) custom-call(s32[8]{0:T(128)S(1)} %and_select_fusion.origin, bf16[32,24,128]{2,1,0:T(8,128)(2,1)S(1)} %all-to-all-done.arrived, bf16[4,24,128]{2,1,0:T(8,128)(2,1)S(1)} %get-tuple-element.17.kept), custom_call_target="tpu_custom_call" | custom-call | tf_op jit(solution)/shard_map/pallas_call | solution.py:234
  40.6 4.0 %all-to-all-start.1 = ((bf16[4,192,128]{2,1,0:T(8,128)(2,1)}), bf16[4,192,128]{2,1,0:T(8,128)(2,1)S(1)}, u32[]{:S(2)}, u32[]{:S(2)}) async-start(bf16[4,192,128]{2,1,0:T(8,128)(2,1)} %get-tuple-element.18), calls=%async_computation.1 | async-start | bytes 393216 | tf_op jit(solution)/shard_map/all_to_all | solution.py:209
  44.6 0.0 copy-start.4
  44.6 0.7 copy-done.4
  45.3 0.1 dynamic_slice.3
  45.4 0.1 pad_add_fusion.lengths
  45.4 0.0 collective-permute-done.rest_1_
  45.4 0.0 collective-permute-done.1.rest_2_
  45.4 1.1 %collective-permute-done.2.rest_3_ = bf16[12,32,512]{2,1,0:T(8,128)(2,1)S(1)} collective-permute-done((bf16[12,32,512]{2,1,0:T(8,128)(2,1)S(1)}, bf16[12,32,512]{2,1,0:T(8,128)(2,1)S(1)}, u32[]{:S(2)}, u32[]{:S(2)}) %collective-permute-start.2) | collective-permute-done | bytes 393248 | tf_op jit(solution)/shard_map/ppermute | solution.py:232
  46.6 3.2 %all-to-all-done.1.asking = bf16[4,192,128]{2,1,0:T(8,128)(2,1)S(1)} async-done(((bf16[4,192,128]{2,1,0:T(8,128)(2,1)}), bf16[4,192,128]{2,1,0:T(8,128)(2,1)S(1)}, u32[]{:S(2)}, u32[]{:S(2)}) %all-to-all-start.1) | async-done | bytes 196640 | tf_op jit(solution)/shard_map/all_to_all | solution.py:209
  49.8 1.3 %shard_map.85 = bf16[4,208,128]{2,1,0:T(8,128)(2,1)S(1)} custom-call(s32[12]{0:T(128)S(1)} %pad_add_fusion.lengths, s32[1]{0:T(128)} %bitcast.where, bf16[4,192,128]{2,1,0:T(8,128)(2,1)S(1)} %all-to-all-done.1.asking, bf16[12,32,512]{2,1,0:T(8,128)(2,1)S(1)} %get-tuple-element.19.rest_0_, bf16[12,32,512]{2,1,0:T(8,128)(2,1)S(1)} %collective-permute-done.rest_1_, ...), custom_call_target="tpu_custom_call" | custom-call | flops 100000000 | bytes 3145728 | tf_op jit(solution)/shard_map/pallas_call | solution.py:241
  51.1 7.6 %all_to_all.20.gathered = bf16[4,208,128]{2,1,0:T(8,128)(2,1)S(1)} all-to-all(bf16[4,208,128]{2,1,0:T(8,128)(2,1)S(1)} %shard_map.85), channel_id=1, replica_groups={{0,1,2,3},{4,5,6,7},{8,9,10,11},{12,13,14,15},{16,17,18,19},{20,21,22,2..., dimensions={0} | all-to-all | bytes 425984 | tf_op jit(solution)/shard_map/all_to_all | solution.py:209
  58.8 1.4 %shard_map.86 = (bf16[32,16,128]{2,1,0:T(8,128)(2,1)S(1)}, bf16[4,16,128]{2,1,0:T(8,128)(2,1)S(1)}) custom-call(s32[8]{0:T(128)S(1)} %and_select_fusion.origin, bf16[4,208,128]{2,1,0:T(8,128)(2,1)S(1)} %all_to_all.20.gathered, bf16[192,128]{1,0:T(8,128)(2,1)S(1)} %get-tuple-element.23.asked, f32[128,128]{1,0:T(8,128)S(1)} %get-tuple-element.24.recent), custom_call_target="tpu_custom_call" | custom-call | tf_op jit(solution)/shard_map/pallas_call | solution.py:255
  60.2 28.4 %all_to_all.21.returned = bf16[32,16,128]{2,1,0:T(8,128)(2,1)S(1)} all-to-all(bf16[32,16,128]{2,1,0:T(8,128)(2,1)S(1)} %get-tuple-element.25), channel_id=1, replica_groups=mesh['group'=32,'tensor'=16] {'group'}, dimensions={0} | all-to-all | bytes 262144 | tf_op jit(solution)/shard_map/all_to_all | solution.py:260
  88.6 1.2 %shard_map.87 = bf16[12,16,128]{2,1,0:T(8,128)(2,1)} custom-call(s32[8]{0:T(128)S(1)} %and_select_fusion.1.target, bf16[32,16,128]{2,1,0:T(8,128)(2,1)S(1)} %all_to_all.21.returned, bf16[4,16,128]{2,1,0:T(8,128)(2,1)S(1)} %get-tuple-element.26.kept), custom_call_target="tpu_custom_call" | custom-call | tf_op jit(solution)/shard_map/pallas_call | solution.py:262
  (3 shorter events, 0.0 us)
Async XLA Ops:
  0.0 20.7 %copy-start.1 = (bf16[4,32,2048]{2,1,0:T(8,128)(2,1)S(1)}, bf16[4,32,2048]{2,1,0:T(8,128)(2,1)}, u32[]{:S(2)}) copy-start(bf16[4,32,2048]{2,1,0:T(8,128)(2,1)} %resident.1) | copy-start | bytes 1572868
  1.0 0.9 %copy-start.2 = (bf16[12,4,2048]{2,1,0:T(4,128)(2,1)S(1)}, bf16[12,4,2048]{2,1,0:T(4,128)(2,1)}, u32[]{:S(2)}) copy-start(bf16[12,4,2048]{2,1,0:T(4,128)(2,1)} %fresh.1) | copy-start | bytes 589828
  1.9 0.8 copy-start.3
  4.0 35.4 %all-to-all-start = ((bf16[32,24,128]{2,1,0:T(8,128)(2,1)}), bf16[32,24,128]{2,1,0:T(8,128)(2,1)S(1)}, u32[]{:S(2)}, u32[]{:S(2)}) async-start(bf16[32,24,128]{2,1,0:T(8,128)(2,1)} %get-tuple-element.16), calls=%async_computation | async-start | bytes 393216 | tf_op jit(solution)/shard_map/all_to_all | solution.py:221
  20.7 1.2 %copy-start = (bf16[8,32,2048]{2,1,0:T(8,128)(2,1)S(1)}, bf16[8,32,2048]{2,1,0:T(8,128)(2,1)}, u32[]{:S(2)}) copy-start(bf16[8,32,2048]{2,1,0:T(8,128)(2,1)} %moved.1) | copy-start | bytes 3145732
  22.2 23.2 %collective-permute-start = (bf16[12,32,512]{2,1,0:T(8,128)(2,1)S(1)}, bf16[12,32,512]{2,1,0:T(8,128)(2,1)S(1)}, u32[]{:S(2)}, u32[]{:S(2)}) collective-permute-start(bf16[12,32,512]{2,1,0:T(8,128)(2,1)S(1)} %get-tuple-element.20), channel_id=1, source_target_pairs={{0,4},{1,5},{2,6},{3,7},{4,8},{5,9},{6,10},{7,11},{8,12},{9,13},{1... | collective-permute-start | bytes 1179656 | tf_op jit(solution)/shard_map/ppermute | solution.py:232
  25.4 20.0 %collective-permute-start.1 = (bf16[12,32,512]{2,1,0:T(8,128)(2,1)S(1)}, bf16[12,32,512]{2,1,0:T(8,128)(2,1)S(1)}, u32[]{:S(2)}, u32[]{:S(2)}) collective-permute-start(bf16[12,32,512]{2,1,0:T(8,128)(2,1)S(1)} %get-tuple-element.21), channel_id=1, source_target_pairs={{0,8},{1,9},{2,10},{3,11},{4,12},{5,13},{6,14},{7,15},{8,0},{9,1},... | collective-permute-start | bytes 1179656 | tf_op jit(solution)/shard_map/ppermute | solution.py:232
  29.9 16.6 %collective-permute-start.2 = (bf16[12,32,512]{2,1,0:T(8,128)(2,1)S(1)}, bf16[12,32,512]{2,1,0:T(8,128)(2,1)S(1)}, u32[]{:S(2)}, u32[]{:S(2)}) collective-permute-start(bf16[12,32,512]{2,1,0:T(8,128)(2,1)S(1)} %get-tuple-element.22), channel_id=1, source_target_pairs={{0,12},{1,13},{2,14},{3,15},{4,0},{5,1},{6,2},{7,3},{8,4},{9,5},{1... | collective-permute-start | bytes 1179656 | tf_op jit(solution)/shard_map/ppermute | solution.py:232
  40.6 9.2 %all-to-all-start.1 = ((bf16[4,192,128]{2,1,0:T(8,128)(2,1)}), bf16[4,192,128]{2,1,0:T(8,128)(2,1)S(1)}, u32[]{:S(2)}, u32[]{:S(2)}) async-start(bf16[4,192,128]{2,1,0:T(8,128)(2,1)} %get-tuple-element.18), calls=%async_computation.1 | async-start | bytes 393216 | tf_op jit(solution)/shard_map/all_to_all | solution.py:209
  44.6 0.7 copy-start.4

commit v3 on v2

v3 whole, which is shorter than its diff:
```python
import math

import jax
import jax.numpy as jnp
from jax import lax
from jax.experimental import pallas as pl
from jax.experimental.pallas import tpu as pltpu
from jax.sharding import PartitionSpec as P

H = 64
KVH = 8
HD = 128
STEPS = 4
MIG = 8
RES = 4
SLOTS = MIG + RES
GROUPS = 32
SHARDS = 16
SIDE = 4
STRIDE = 32
HEADS = H // SHARDS
PAIRS = KVH // SIDE
QROWS = HEADS * STEPS
ROWS = SLOTS * QROWS
FEATURES = KVH * HD
TILES = HEADS + 1
ENTRIES = SLOTS * STEPS
PAYLOAD = ROWS + 16
FLOOR = -(2.0**100)
SCALE = 1.0 / math.sqrt(HD)
LIMIT = 48 * 1024 * 1024
FULL = 63 * 1024 * 1024
BF = jnp.bfloat16
F32 = jnp.float32

VM = pl.BlockSpec(memory_space=pltpu.VMEM)
SM = pl.BlockSpec(memory_space=pltpu.SMEM)
HB = pl.BlockSpec(memory_space=pltpu.HBM)


def call(kernel, outs, specs, flops=0, moved=0, scratch=(), limit=LIMIT, place=VM):
    return pl.pallas_call(
        kernel,
        out_shape=outs,
        in_specs=specs,
        out_specs=jax.tree.map(lambda _: place, outs),
        scratch_shapes=scratch,
        compiler_params=pltpu.CompilerParams(vmem_limit_bytes=limit),
        cost_estimate=pl.CostEstimate(flops=flops, bytes_accessed=moved, transcendentals=0),
    )


def swapped(step, y, x):
    return y ^ (step % 2), x ^ (step // 2 * 3)


def class_of(y, x):
    return jnp.minimum(y, 3 - y), x // 2


def place_of():
    shard = lax.axis_index("tensor")
    return shard // SIDE, shard % SIDE


def pack_kernel(named, holders, asked, fresh, sent, kept, asked_here, fresh_here, named_here, holders_here, sems):
    shard = lax.axis_index("tensor")
    first = pl.multiple_of(shard % 2 * FEATURES + shard // 2 * HD, HD)
    copies = [
        pltpu.make_async_copy(source, target, sems.at[n])
        for n, (source, target) in enumerate(
            (
                (named, named_here),
                (holders, holders_here),
                (asked, asked_here),
                (fresh.at[:, :, pl.ds(first, HD)], fresh_here),
            )
        )
    ]
    for copy in copies:
        copy.start()
    sent[...] = jnp.zeros_like(sent)
    for copy in copies:
        copy.wait()
    names = named_here[...]
    slots = holders_here[...].astype(F32)
    for slot in range(RES):
        kept[slot, :HEADS] = asked_here[slot]
        kept[slot, HEADS] = fresh_here[slot]
    groups = []
    for slot in range(RES, SLOTS):
        mine = names == lax.axis_index("group") * SLOTS + slot
        groups.append(jnp.sum(jnp.where(mine, slots, 0.0)).astype(jnp.int32) // MIG)
    for slot, group in zip(range(RES, SLOTS), groups):
        sent[group, :HEADS] = asked_here[slot]
        sent[group, HEADS] = fresh_here[slot]


def split_kernel(moved, resident, *rest):
    *outs, sems = rest
    here = place_of()
    copies = []
    for step in (*range(1, SIDE), 0):
        low, half = class_of(*swapped(step, *here))
        for place, pair in enumerate((2 * low + half, 6 - 2 * low + half)):
            for part in range(2):
                lanes = pl.ds(pl.multiple_of(pair * HD + part * FEATURES, HD), HD)
                columns = pl.ds((part * PAIRS + place) * HD, HD)
                for source, rows in ((moved, pl.ds(0, MIG)), (resident, pl.ds(MIG, RES))):
                    target = outs[step].at[rows, :, columns]
                    sem = sems.at[len(copies)]
                    copies.append(pltpu.make_async_copy(source.at[:, :, lanes], target, sem))
    for copy in copies:
        copy.start()
    for copy in copies:
        copy.wait()


def spread_kernel(origin, arrived, kept, asking):
    for row in range(SLOTS):
        chunk = arrived.at[origin[row]] if row < MIG else kept.at[row - MIG]
        for peer in range(SIDE):
            asking[peer, row * HEADS : (row + 1) * HEADS] = chunk[:HEADS]
            asking[peer, SLOTS * HEADS + row] = chunk[HEADS]


def scores_of(left, right):
    return lax.dot_general(left, right, (((1,), (1,)), ((), ())), preferred_element_type=F32) * SCALE


def partial_kernel(lengths, asking, *rest):
    *blocks, payload, scores, weights, stats = rest
    column = lax.broadcasted_iota(jnp.int32, (1, HD), 1)
    y, x = swapped(column // STRIDE, *place_of())
    position = (y * SIDE + x) * STRIDE + column % STRIDE

    def stored(row, place):
        lanes = slice(place * HD, (place + 1) * HD)
        return jnp.concatenate([block[row, :, lanes] for block in blocks], 0)

    for row in range(SLOTS):
        usable = position < lengths[row]
        span = slice(row * QROWS, (row + 1) * QROWS)
        for pair in range(PAIRS):
            asked = jnp.concatenate([asking[2 * pair, span, :], asking[2 * pair + 1, span, :]], 0)
            found = jnp.where(usable, scores_of(asked, stored(row, pair)), FLOOR)
            scores[2 * pair, span, :] = found[:QROWS]
            scores[2 * pair + 1, span, :] = found[QROWS:]
    lane = lax.broadcasted_iota(jnp.int32, (ROWS, HD), 1)
    table = jnp.zeros((ROWS, HD), F32)
    for peer in range(SIDE):
        found = scores[peer]
        top = jnp.max(found, axis=1, keepdims=True)
        first = top.astype(BF).astype(F32)
        second = (top - first).astype(BF).astype(F32)
        weight = jnp.exp(found - (first + second))
        total = jnp.sum(weight, axis=1, keepdims=True)
        weights[peer] = weight.astype(BF)
        total_first = total.astype(BF).astype(F32)
        for place, value in enumerate((first, total_first, second, total - total_first)):
            table = jnp.where(lane == peer * 8 + place, value, table)
    stats[:ROWS, :] = table
    stats[ROWS:, :] = jnp.zeros((2 * HD - ROWS, HD), F32)
    low = stats[:HD, :].T
    high = stats[HD:, :].T
    for peer in range(SIDE):
        rows = slice(peer * 8, (peer + 1) * 8)
        payload[peer, ROWS:, :] = jnp.concatenate([low[rows], high[rows]], 0).astype(BF)
    for row in range(SLOTS):
        span = slice(row * QROWS, (row + 1) * QROWS)
        for pair in range(PAIRS):
            weight = jnp.concatenate([weights[2 * pair, span, :], weights[2 * pair + 1, span, :]], 0)
            blended = jnp.dot(weight, stored(row, PAIRS + pair), preferred_element_type=F32).astype(BF)
            payload[2 * pair, span, :] = blended[:QROWS]
            payload[2 * pair + 1, span, :] = blended[QROWS:]


def merge_kernel(origin, gathered, everyone, sent, kept):
    y, x = place_of()
    first = jnp.where(y > 1, 2, 0)
    asked = everyone[first + x % 2, :ROWS, :]
    keys = everyone[first, ROWS:, :]
    values = everyone[first + 1, ROWS:, :]
    row = lax.broadcasted_iota(jnp.int32, (ROWS, ENTRIES), 0)
    lane = lax.broadcasted_iota(jnp.int32, (ROWS, ENTRIES), 1)
    causal = (lane // STEPS == row // QROWS) & (lane % STEPS <= row % STEPS)
    fresh = jnp.where(causal, scores_of(asked, keys), FLOOR)
    fresh_top = jnp.max(fresh, axis=1, keepdims=True)

    tops = gathered[:, ROWS:, :].astype(F32)
    blank = jnp.zeros((HD - SIDE * 8, HD), F32)
    low = jnp.concatenate([tops[:, :8, :].reshape(SIDE * 8, HD), blank], 0).T
    high = jnp.concatenate([tops[:, 8:, :].reshape(SIDE * 8, HD), blank], 0).T[: ROWS - HD]
    pairs = jnp.concatenate([low, high], 0)
    both = pairs + pltpu.roll(pairs, HD - 2, 1)
    lane = lax.broadcasted_iota(jnp.int32, (ROWS, HD), 1)
    is_top = (lane % 8 == 0) & (lane < SIDE * 8)
    tops = jnp.where(is_top, both, FLOOR)
    sums = pltpu.roll(both, HD - 1, 1)
    highest = jnp.maximum(jnp.max(tops, axis=1, keepdims=True), fresh_top)
    factors = jnp.where(is_top, jnp.exp(tops - highest), 0.0)
    fresh_weights = jnp.where(causal, jnp.exp(fresh - highest), 0.0)
    totals = jnp.sum(jnp.where(is_top, factors * sums, 0.0), axis=1, keepdims=True)
    totals += jnp.sum(fresh_weights, axis=1, keepdims=True)
    blended = jnp.dot(fresh_weights.astype(BF), values, preferred_element_type=F32)
    for peer in range(SIDE):
        blended += factors[:, peer * 8 : peer * 8 + 1] * gathered[peer, :ROWS, :].astype(F32)
    result = (blended / totals).astype(BF)

    sent[...] = jnp.zeros_like(sent)
    for slot in range(MIG):
        sent[origin[slot]] = result[slot * QROWS : (slot + 1) * QROWS]
    for slot in range(RES):
        kept[slot] = result[(MIG + slot) * QROWS : (MIG + slot + 1) * QROWS]


def select_kernel(target, returned, kept, out):
    for slot in range(RES):
        out[slot] = kept[slot]
    for slot in range(MIG):
        out[RES + slot] = returned[target[slot]]


def body(
    queries,
    new_entries,
    resident_cache,
    prefill_cache,
    resident_kept,
    kept_tokens,
    prefill_slot,
    decode_slot,
):
    shape = jax.ShapeDtypeStruct
    whole = [(y, x) for y in range(SIDE) for x in range(SIDE)]
    peers = [[y * SIDE + x for y in (low, 3 - low) for x in (2 * half, 2 * half + 1)] for low in range(2) for half in range(2)]

    def across(array):
        return lax.all_to_all(array, "tensor", 0, 0, axis_index_groups=peers, tiled=True)

    asked = queries.reshape(SLOTS, STEPS, HEADS, HD).transpose(0, 2, 1, 3)
    sent, kept = call(
        pack_kernel,
        (shape((GROUPS, TILES, STEPS, HD), BF), shape((RES, TILES, STEPS, HD), BF)),
        [HB] * 4,
        scratch=[
            pltpu.VMEM((SLOTS, HEADS, STEPS, HD), BF),
            pltpu.VMEM((SLOTS, STEPS, HD), BF),
            pltpu.VMEM((2, HD), jnp.int32),
            pltpu.VMEM((2, HD), jnp.int32),
            pltpu.SemaphoreType.DMA((4,)),
        ],
        limit=FULL,
    )(decode_slot.reshape(2, HD), prefill_slot.reshape(2, HD), asked, new_entries)
    arrived = lax.all_to_all(sent, "group", 0, 0, tiled=True)

    (resident_kept, kept_tokens, prefill_slot, decode_slot), kept = lax.optimization_barrier(
        ((resident_kept, kept_tokens, prefill_slot, decode_slot), kept)
    )
    group = lax.axis_index("group")

    def looked_up(names, first, values):
        wanted = first + jnp.arange(MIG, dtype=jnp.int32)
        return jnp.sum(jnp.where(names[None, :] == wanted[:, None], values[None, :], 0), axis=1)

    target = looked_up(decode_slot, group * SLOTS + RES, prefill_slot) // MIG
    origin = looked_up(prefill_slot, group * MIG, decode_slot) // SLOTS
    moved_len = looked_up(prefill_slot, group * MIG, kept_tokens)
    resident_len = lax.dynamic_slice_in_dim(resident_kept, group * RES, RES)
    lengths = jnp.concatenate([moved_len, resident_len])

    split = call(
        split_kernel,
        (shape((SLOTS, STRIDE, 2 * PAIRS * HD), BF),) * SIDE,
        [HB, HB],
        moved=3 * 2**20,
        scratch=[pltpu.SemaphoreType.DMA((8 * SIDE,))],
        limit=FULL,
        place=HB,
    )(prefill_cache, resident_cache)
    blocks = [split[0]]
    for step in range(1, SIDE):
        steps = []
        for y, x in whole:
            other, side = swapped(step, y, x)
            steps.append((y * SIDE + x, other * SIDE + side))
        blocks.append(lax.ppermute(split[step], "tensor", steps))

    asking = call(
        spread_kernel, shape((SIDE, SLOTS * TILES, STEPS, HD), BF), [SM, VM, VM]
    )(origin, arrived, kept)
    everyone = across(asking).reshape(SIDE, ROWS + ENTRIES, HD)

    payload = call(
        partial_kernel,
        shape((SIDE, PAYLOAD, HD), BF),
        [SM] + [VM] * (1 + SIDE),
        flops=10**8,
        moved=3 * 2**20,
        scratch=[
            pltpu.VMEM((SIDE, ROWS, HD), F32),
            pltpu.VMEM((SIDE, ROWS, HD), BF),
            pltpu.VMEM((2 * HD, HD), F32),
        ],
    )(lengths, everyone, *blocks)
    gathered = across(payload)

    finished, here = call(
        merge_kernel,
        (shape((GROUPS, QROWS, HD), BF), shape((RES, QROWS, HD), BF)),
        [SM, VM, VM],
    )(origin, gathered, everyone)
    returned = lax.all_to_all(finished, "group", 0, 0, tiled=True)

    result = call(select_kernel, shape((SLOTS, QROWS, HD), BF), [SM, VM, VM])(target, returned, here)
    result = result.reshape(SLOTS, HEADS, STEPS, HD).transpose(0, 2, 1, 3)
    return result.reshape(SLOTS, STEPS, HEADS * HD)


def solution(mesh):
    in_specs = (
        P("group", None, "tensor"),
        P("group", None, None),
        P("group", "tensor", None),
        P("group", "tensor", None),
        P(),
        P(),
        P(),
        P(),
    )
    out_specs = P("group", None, "tensor")
    return jax.shard_map(body, mesh=mesh, in_specs=in_specs, out_specs=out_specs, check_vma=False)
```

time: 91.3 us -> 138 us (1.51)
  Pallas kernels: 6.59 us -> 56.6 us
  blocking collectives: 36 us -> 9.47 us
  starting transfers between devices: 31.5 us -> 45 us
  waiting for transfers between devices: 10.8 us -> 24.2 us
  local copies, waits for them, and re-layouts: 3.68 us -> 1.41 us
    pallas_call x4, Pallas kernels: 4.01 us -> 53.4 us  [the longest x1 49.1 us: body(): call(split_kernel, (shape((SLOTS, STRIDE, 2 * PAIRS * HD), BF),) * SIDE,...]
    all_to_all x2 -> x1, blocking collectives: 36 us -> 9.47 us  [across(): lax.all_to_all(array, 'tensor', 0, 0, axis_index_groups=peers, tiled=True)]
    all_to_all x1 -> x2, starting transfers between devices: 4.01 us -> 18.6 us  [the longest x1 14.6 us: body(): returned = lax.all_to_all(finished, 'group', 0, 0, tiled=True)]
    all_to_all x1 -> x2, waiting for transfers between devices: 3.23 us -> 15.8 us  [the longest x1 15.8 us: body(): returned = lax.all_to_all(finished, 'group', 0, 0, tiled=True)]
    ppermute x3, waiting for transfers between devices: 1.14 us -> 8.31 us  [body(): blocks.append(lax.ppermute(split[step], 'tensor', steps))]
    all_to_all x1, waiting for transfers between devices: 6.42 us -> 0.01 us  [body(): arrived = lax.all_to_all(sent, 'group', 0, 0, tiled=True)]
    unnamed x10 -> x12, local copies, waits for them, and re-layouts: 3.6 us -> 1.33 us
  transfers between devices with their start and end apart: 5 -> 6, of which waited for: 3 -> 2; matrix products, arithmetic and copies ran while one was open for 0% -> 0% of each run, Pallas kernels for 2% -> 37%
where the time goes in v3:
time: 138 us; the launch traced here: 137 us
  Pallas kernels  56.6 us (41%)
  starting transfers between devices  45 us (33%)
  waiting for transfers between devices  24.2 us (18%)
  blocking collectives  9.47 us (7%)
  local copies, waits for them, and re-layouts  1.41 us (1%)
    pallas_call x1, Pallas kernels, body(): call(split_kernel, (shape((SLOTS, STRIDE, 2 * PAIRS * HD), BF),) * SIDE,...  49.1 us
    all_to_all x1, starting transfers between devices, body(): arrived = lax.all_to_all(sent, 'group', 0, 0, tiled=True)  16.8 us
    all_to_all x1, waiting for transfers between devices, body(): returned = lax.all_to_all(finished, 'group', 0, 0, tiled=True)  15.8 us
    all_to_all x1, starting transfers between devices, body(): returned = lax.all_to_all(finished, 'group', 0, 0, tiled=True)  14.6 us
    ppermute x3, starting transfers between devices, body(): blocks.append(lax.ppermute(split[step], 'tensor', steps))  9.58 us
    all_to_all x1, blocking collectives, across(): lax.all_to_all(array, 'tensor', 0, 0, axis_index_groups=peers, tiled=True)  9.47 us
    ppermute x3, waiting for transfers between devices, body(): blocks.append(lax.ppermute(split[step], 'tensor', steps))  8.31 us
    all_to_all x1, starting transfers between devices, across(): lax.all_to_all(array, 'tensor', 0, 0, axis_index_groups=peers, tiled=True)  4 us
  transfers between devices with their start and end apart: 6, of which 2 were waited for; matrix products, arithmetic and copies ran while one was open for 0% of the time, Pallas kernels for 37%

profile of v3, /device:TPU:1, one launch (start us, length us, event | category | flops | bytes accessed | tf_op | source)
XLA Modules:
  0.0 137.1 jit_solution(4473878792026504224)
XLA Ops:
  0.0 1.7 %shard_map.82 = (bf16[32,5,4,128]{3,2,1,0:T(4,128)(2,1)}, bf16[4,5,4,128]{3,2,1,0:T(4,128)(2,1)}) custom-call(s32[2,128]{1,0:T(2,128)} %bitcast.15, s32[2,128]{1,0:T(2,128)} %bitcast.14, bf16[12,4,4,128]{3,2,1,0:T(4,128)(2,1)} %bitcast.13, bf16[12,4,2048]{2,1,0:T(4,128)(2,1)} %fresh.1), custom_call_target="tpu_custom_call" | custom-call | tf_op jit(solution)/shard_map/pallas_call | solution.py:242
  1.7 16.8 %all-to-all-start = ((bf16[32,5,4,128]{3,2,1,0:T(4,128)(2,1)}), bf16[32,5,4,128]{3,2,1,0:T(4,128)(2,1)S(1)}, u32[]{:S(2)}, u32[]{:S(2)}) async-start(bf16[32,5,4,128]{3,2,1,0:T(4,128)(2,1)} %get-tuple-element.23), calls=%async_computation | async-start | bytes 327680 | tf_op jit(solution)/shard_map/all_to_all | solution.py:255
  18.5 49.1 %shard_map.84 = (bf16[12,32,512]{2,1,0:T(8,128)(2,1)}, bf16[12,32,512]{2,1,0:T(8,128)(2,1)}, bf16[12,32,512]{2,1,0:T(8,128)(2,1)}, bf16[12,32,512]{2,1,0:T(8,128)(2,1)}) custom-call(bf16[8,32,2048]{2,1,0:T(8,128)(2,1)} %moved.1, bf16[4,32,2048]{2,1,0:T(8,128)(2,1)} %resident.1), custom_call_target="tpu_custom_call" | custom-call | bytes 3145728 | tf_op jit(solution)/shard_map/pallas_call | solution.py:272
  67.5 0.0 copy-start.1
  67.6 3.2 %collective-permute-start = (bf16[12,32,512]{2,1,0:T(8,128)(2,1)}, bf16[12,32,512]{2,1,0:T(8,128)(2,1)S(1)}, u32[]{:S(2)}, u32[]{:S(2)}) collective-permute-start(bf16[12,32,512]{2,1,0:T(8,128)(2,1)} %get-tuple-element.26), channel_id=1, source_target_pairs={{0,4},{1,5},{2,6},{3,7},{4,0},{5,1},{6,2},{7,3},{8,12},{9,13},{10,... | collective-permute-start | bytes 1179656 | tf_op jit(solution)/shard_map/ppermute | solution.py:287
  70.8 0.0 copy-start.3
  70.8 0.0 copy-start.4
  70.8 4.4 %collective-permute-start.1 = (bf16[12,32,512]{2,1,0:T(8,128)(2,1)}, bf16[12,32,512]{2,1,0:T(8,128)(2,1)S(1)}, u32[]{:S(2)}, u32[]{:S(2)}) collective-permute-start(bf16[12,32,512]{2,1,0:T(8,128)(2,1)} %get-tuple-element.27), channel_id=1, source_target_pairs={{0,3},{1,2},{2,1},{3,0},{4,7},{5,6},{6,5},{7,4},{8,11},{9,10},{10,... | collective-permute-start | bytes 1179656 | tf_op jit(solution)/shard_map/ppermute | solution.py:287
  75.2 2.0 %collective-permute-start.2 = (bf16[12,32,512]{2,1,0:T(8,128)(2,1)}, bf16[12,32,512]{2,1,0:T(8,128)(2,1)S(1)}, u32[]{:S(2)}, u32[]{:S(2)}) collective-permute-start(bf16[12,32,512]{2,1,0:T(8,128)(2,1)} %get-tuple-element.28), channel_id=1, source_target_pairs={{0,7},{1,6},{2,5},{3,4},{4,3},{5,2},{6,1},{7,0},{8,15},{9,14},{10,... | collective-permute-start | bytes 1179656 | tf_op jit(solution)/shard_map/ppermute | solution.py:287
  77.2 0.0 copy-start.2
  77.2 0.0 copy-done.3
  77.2 0.0 copy-done.4
  77.2 0.7 copy-done.2
  77.9 0.2 fusion
  78.1 0.0 copy-start
  78.1 0.0 all-to-all-done.arrived
  78.1 0.0 copy-done.1
  78.1 1.3 shard_map.83
  79.5 4.0 %all-to-all-start.1 = ((bf16[4,60,4,128]{3,2,1,0:T(4,128)(2,1)}), bf16[4,60,4,128]{3,2,1,0:T(4,128)(2,1)S(1)}, u32[]{:S(2)}, u32[]{:S(2)}) async-start(bf16[4,60,4,128]{3,2,1,0:T(4,128)(2,1)} %shard_map.83), calls=%async_computation.1 | async-start | bytes 491520 | tf_op jit(solution)/shard_map/all_to_all | solution.py:239
  83.5 0.0 copy-start.5
  83.5 0.7 copy-done.5
  84.1 0.1 dynamic_slice.3
  84.2 0.1 pad_add_fusion.lengths
  84.3 0.0 collective-permute-done.rest_1_
  84.3 0.0 collective-permute-done.1.rest_2_
  84.3 8.3 %collective-permute-done.2.rest_3_ = bf16[12,32,512]{2,1,0:T(8,128)(2,1)S(1)} collective-permute-done((bf16[12,32,512]{2,1,0:T(8,128)(2,1)}, bf16[12,32,512]{2,1,0:T(8,128)(2,1)S(1)}, u32[]{:S(2)}, u32[]{:S(2)}) %collective-permute-start.2) | collective-permute-done | bytes 393248 | tf_op jit(solution)/shard_map/ppermute | solution.py:287
  92.6 0.0 all-to-all-done.1
  92.6 0.0 copy-done
  92.6 1.3 shard_map.85
  93.9 9.5 %all_to_all.20.gathered = bf16[4,208,128]{2,1,0:T(8,128)(2,1)S(1)} all-to-all(bf16[4,208,128]{2,1,0:T(8,128)(2,1)S(1)} %shard_map.85), channel_id=1, replica_groups={{0,1,12,13},{2,3,14,15},{4,5,8,9},{6,7,10,11},{16,17,28,29},{18,19,30,3..., dimensions={0} | all-to-all | bytes 425984 | tf_op jit(solution)/shard_map/all_to_all | solution.py:239
  103.4 2.1 %shard_map.86 = (bf16[32,16,128]{2,1,0:T(8,128)(2,1)}, bf16[4,16,128]{2,1,0:T(8,128)(2,1)S(1)}) custom-call(s32[8]{0:T(128)S(1)} %and_select_fusion.origin, bf16[4,208,128]{2,1,0:T(8,128)(2,1)S(1)} %all_to_all.20.gathered, bf16[4,240,128]{2,1,0:T(8,128)(2,1)S(1)} %bitcast.12), custom_call_target="tpu_custom_call" | custom-call | tf_op jit(solution)/shard_map/pallas_call | solution.py:308
  105.5 14.6 %all-to-all-start.3 = ((bf16[32,16,128]{2,1,0:T(8,128)(2,1)}), bf16[32,16,128]{2,1,0:T(8,128)(2,1)S(1)}, u32[]{:S(2)}, u32[]{:S(2)}) async-start(bf16[32,16,128]{2,1,0:T(8,128)(2,1)} %get-tuple-element.29), calls=%async_computation.3 | async-start | bytes 262144 | tf_op jit(solution)/shard_map/all_to_all | solution.py:313
  120.1 15.8 %all-to-all-done.3.returned = bf16[32,16,128]{2,1,0:T(8,128)(2,1)S(1)} async-done(((bf16[32,16,128]{2,1,0:T(8,128)(2,1)}), bf16[32,16,128]{2,1,0:T(8,128)(2,1)S(1)}, u32[]{:S(2)}, u32[]{:S(2)}) %all-to-all-start.3) | async-done | bytes 131104 | tf_op jit(solution)/shard_map/all_to_all | solution.py:313
  135.9 1.2 shard_map.87
  (3 shorter events, 0.0 us)
Async XLA Ops:
  1.7 76.4 %all-to-all-start = ((bf16[32,5,4,128]{3,2,1,0:T(4,128)(2,1)}), bf16[32,5,4,128]{3,2,1,0:T(4,128)(2,1)S(1)}, u32[]{:S(2)}, u32[]{:S(2)}) async-start(bf16[32,5,4,128]{3,2,1,0:T(4,128)(2,1)} %get-tuple-element.23), calls=%async_computation | async-start | bytes 327680 | tf_op jit(solution)/shard_map/all_to_all | solution.py:255
  67.5 10.6 %copy-start.1 = (bf16[4,5,4,128]{3,2,1,0:T(4,128)(2,1)S(1)}, bf16[4,5,4,128]{3,2,1,0:T(4,128)(2,1)}, u32[]{:S(2)}) copy-start(bf16[4,5,4,128]{3,2,1,0:T(4,128)(2,1)} %get-tuple-element.24.kept) | copy-start | bytes 61444
  67.6 16.7 %collective-permute-start = (bf16[12,32,512]{2,1,0:T(8,128)(2,1)}, bf16[12,32,512]{2,1,0:T(8,128)(2,1)S(1)}, u32[]{:S(2)}, u32[]{:S(2)}) collective-permute-start(bf16[12,32,512]{2,1,0:T(8,128)(2,1)} %get-tuple-element.26), channel_id=1, source_target_pairs={{0,4},{1,5},{2,6},{3,7},{4,0},{5,1},{6,2},{7,3},{8,12},{9,13},{10,... | collective-permute-start | bytes 1179656 | tf_op jit(solution)/shard_map/ppermute | solution.py:287
  70.8 6.5 %copy-start.3 = (s32[256]{0:T(256)S(1)}, s32[256]{0:T(256)}, u32[]{:S(2)}) copy-start(s32[256]{0:T(256)} %param.15) | copy-start | bytes 3076
  70.8 6.4 %copy-start.4 = (s32[256]{0:T(256)S(1)}, s32[256]{0:T(256)}, u32[]{:S(2)}) copy-start(s32[256]{0:T(256)} %param.13) | copy-start | bytes 3076
  70.8 13.5 %collective-permute-start.1 = (bf16[12,32,512]{2,1,0:T(8,128)(2,1)}, bf16[12,32,512]{2,1,0:T(8,128)(2,1)S(1)}, u32[]{:S(2)}, u32[]{:S(2)}) collective-permute-start(bf16[12,32,512]{2,1,0:T(8,128)(2,1)} %get-tuple-element.27), channel_id=1, source_target_pairs={{0,3},{1,2},{2,1},{3,0},{4,7},{5,6},{6,5},{7,4},{8,11},{9,10},{10,... | collective-permute-start | bytes 1179656 | tf_op jit(solution)/shard_map/ppermute | solution.py:287
  75.2 17.4 %collective-permute-start.2 = (bf16[12,32,512]{2,1,0:T(8,128)(2,1)}, bf16[12,32,512]{2,1,0:T(8,128)(2,1)S(1)}, u32[]{:S(2)}, u32[]{:S(2)}) collective-permute-start(bf16[12,32,512]{2,1,0:T(8,128)(2,1)} %get-tuple-element.28), channel_id=1, source_target_pairs={{0,7},{1,6},{2,5},{3,4},{4,3},{5,2},{6,1},{7,0},{8,15},{9,14},{10,... | collective-permute-start | bytes 1179656 | tf_op jit(solution)/shard_map/ppermute | solution.py:287
  77.2 0.7 copy-start.2
  78.1 14.5 %copy-start = (bf16[12,32,512]{2,1,0:T(8,128)(2,1)S(1)}, bf16[12,32,512]{2,1,0:T(8,128)(2,1)}, u32[]{:S(2)}) copy-start(bf16[12,32,512]{2,1,0:T(8,128)(2,1)} %get-tuple-element.25.rest_0_) | copy-start | bytes 1179652
  79.5 13.1 %all-to-all-start.1 = ((bf16[4,60,4,128]{3,2,1,0:T(4,128)(2,1)}), bf16[4,60,4,128]{3,2,1,0:T(4,128)(2,1)S(1)}, u32[]{:S(2)}, u32[]{:S(2)}) async-start(bf16[4,60,4,128]{3,2,1,0:T(4,128)(2,1)} %shard_map.83), calls=%async_computation.1 | async-start | bytes 491520 | tf_op jit(solution)/shard_map/all_to_all | solution.py:239
  83.5 0.7 copy-start.5
  105.5 30.5 %all-to-all-start.3 = ((bf16[32,16,128]{2,1,0:T(8,128)(2,1)}), bf16[32,16,128]{2,1,0:T(8,128)(2,1)S(1)}, u32[]{:S(2)}, u32[]{:S(2)}) async-start(bf16[32,16,128]{2,1,0:T(8,128)(2,1)} %get-tuple-element.29), calls=%async_computation.3 | async-start | bytes 262144 | tf_op jit(solution)/shard_map/all_to_all | solution.py:313

commit v4 on v3

--- a/solution.py
+++ b/solution.py
@@ -38,12 +38,12 @@
 HB = pl.BlockSpec(memory_space=pltpu.HBM)
 
 
-def call(kernel, outs, specs, flops=0, moved=0, scratch=(), limit=LIMIT, place=VM):
+def call(kernel, outs, specs, flops=0, moved=0, scratch=(), limit=LIMIT):
     return pl.pallas_call(
         kernel,
         out_shape=outs,
         in_specs=specs,
-        out_specs=jax.tree.map(lambda _: place, outs),
+        out_specs=jax.tree.map(lambda _: VM, outs),
         scratch_shapes=scratch,
         compiler_params=pltpu.CompilerParams(vmem_limit_bytes=limit),
         cost_estimate=pl.CostEstimate(flops=flops, bytes_accessed=moved, transcendentals=0),
@@ -96,24 +96,16 @@
         sent[group, HEADS] = fresh_here[slot]
 
 
-def split_kernel(moved, resident, *rest):
-    *outs, sems = rest
+def split_kernel(moved, resident, *outs):
     here = place_of()
-    copies = []
-    for step in (*range(1, SIDE), 0):
+    for step, out in enumerate(outs):
         low, half = class_of(*swapped(step, *here))
         for place, pair in enumerate((2 * low + half, 6 - 2 * low + half)):
             for part in range(2):
                 lanes = pl.ds(pl.multiple_of(pair * HD + part * FEATURES, HD), HD)
-                columns = pl.ds((part * PAIRS + place) * HD, HD)
-                for source, rows in ((moved, pl.ds(0, MIG)), (resident, pl.ds(MIG, RES))):
-                    target = outs[step].at[rows, :, columns]
-                    sem = sems.at[len(copies)]
-                    copies.append(pltpu.make_async_copy(source.at[:, :, lanes], target, sem))
-    for copy in copies:
-        copy.start()
-    for copy in copies:
-        copy.wait()
+                columns = slice((part * PAIRS + place) * HD, (part * PAIRS + place + 1) * HD)
+                out[:MIG, :, columns] = moved[:, :, lanes]
+                out[MIG:, :, columns] = resident[:, :, lanes]
 
 
 def spread_kernel(origin, arrived, kept, asking):
@@ -254,9 +246,9 @@
     )(decode_slot.reshape(2, HD), prefill_slot.reshape(2, HD), asked, new_entries)
     arrived = lax.all_to_all(sent, "group", 0, 0, tiled=True)
 
-    (resident_kept, kept_tokens, prefill_slot, decode_slot), kept = lax.optimization_barrier(
-        ((resident_kept, kept_tokens, prefill_slot, decode_slot), kept)
-    )
+    later = (resident_kept, kept_tokens, prefill_slot, decode_slot, prefill_cache, resident_cache)
+    later, kept = lax.optimization_barrier((later, kept))
+    resident_kept, kept_tokens, prefill_slot, decode_slot, prefill_cache, resident_cache = later
     group = lax.axis_index("group")
 
     def looked_up(names, first, values):
@@ -272,11 +264,8 @@
     split = call(
         split_kernel,
         (shape((SLOTS, STRIDE, 2 * PAIRS * HD), BF),) * SIDE,
-        [HB, HB],
+        [VM, VM],
         moved=3 * 2**20,
-        scratch=[pltpu.SemaphoreType.DMA((8 * SIDE,))],
-        limit=FULL,
-        place=HB,
     )(prefill_cache, resident_cache)
     blocks = [split[0]]
     for step in range(1, SIDE):

time: 138 us -> 91.7 us (0.66)
  Pallas kernels: 56.6 us -> 8.83 us
  blocking collectives: 9.47 us -> 8.04 us
    pallas_call x1, Pallas kernels: 49.1 us -> 1.16 us  [body(): call(split_kernel, (shape((SLOTS, STRIDE, 2 * PAIRS * HD), BF),) * SIDE,...]
    ppermute x3, waiting for transfers between devices: 8.31 us -> 3.14 us  [body(): blocks.append(lax.ppermute(split[step], 'tensor', steps))]
    all_to_all x1, waiting for transfers between devices: 0.01 us -> 4.07 us  [body(): arrived = lax.all_to_all(sent, 'group', 0, 0, tiled=True)]
    all_to_all x1, waiting for transfers between devices: 0.01 us -> 1.44 us  [across(): lax.all_to_all(array, 'tensor', 0, 0, axis_index_groups=peers, tiled=True)]
    all_to_all x1, blocking collectives: 9.47 us -> 8.04 us  [across(): lax.all_to_all(array, 'tensor', 0, 0, axis_index_groups=peers, tiled=True)]
  transfers between devices with their start and end apart: 6 -> 6, of which waited for: 2 -> 4; matrix products, arithmetic and copies ran while one was open for 0% -> 0% of each run, Pallas kernels for 37% -> 3%
where the time goes in v4:
time: 91.7 us; the launch traced here: 90.4 us
  starting transfers between devices  46 us (50%)
  waiting for transfers between devices  24.5 us (27%)
  Pallas kernels  8.83 us (10%)
  blocking collectives  8.04 us (9%)
  local copies, waits for them, and re-layouts  2.62 us (3%)
    all_to_all x1, starting transfers between devices, body(): arrived = lax.all_to_all(sent, 'group', 0, 0, tiled=True)  16.8 us
    all_to_all x1, waiting for transfers between devices, body(): returned = lax.all_to_all(finished, 'group', 0, 0, tiled=True)  15.8 us
    all_to_all x1, starting transfers between devices, body(): returned = lax.all_to_all(finished, 'group', 0, 0, tiled=True)  14.6 us
    ppermute x3, starting transfers between devices, body(): blocks.append(lax.ppermute(split[step], 'tensor', steps))  9.7 us
    all_to_all x1, blocking collectives, across(): lax.all_to_all(array, 'tensor', 0, 0, axis_index_groups=peers, tiled=True)  8.04 us
    all_to_all x1, starting transfers between devices, across(): lax.all_to_all(array, 'tensor', 0, 0, axis_index_groups=peers, tiled=True)  4.93 us
    all_to_all x1, waiting for transfers between devices, body(): arrived = lax.all_to_all(sent, 'group', 0, 0, tiled=True)  4.07 us
    ppermute x3, waiting for transfers between devices, body(): blocks.append(lax.ppermute(split[step], 'tensor', steps))  3.14 us
  transfers between devices with their start and end apart: 6, of which 4 were waited for; matrix products, arithmetic and copies ran while one was open for 0% of the time, Pallas kernels for 3%

profile of v4, /device:TPU:1, one launch (start us, length us, event | category | flops | bytes accessed | tf_op | source)
XLA Modules:
  0.0 90.4 jit_solution(4111182253161548591)
XLA Ops:
  0.0 0.0 copy-start.1
  0.0 1.8 %shard_map.82 = (bf16[32,5,4,128]{3,2,1,0:T(4,128)(2,1)}, bf16[4,5,4,128]{3,2,1,0:T(4,128)(2,1)}) custom-call(s32[2,128]{1,0:T(2,128)} %bitcast.15, s32[2,128]{1,0:T(2,128)} %bitcast.14, bf16[12,4,4,128]{3,2,1,0:T(4,128)(2,1)} %bitcast.13, bf16[12,4,2048]{2,1,0:T(4,128)(2,1)} %fresh.1), custom_call_target="tpu_custom_call" | custom-call | tf_op jit(solution)/shard_map/pallas_call | solution.py:234
  1.8 16.8 %all-to-all-start = ((bf16[32,5,4,128]{3,2,1,0:T(4,128)(2,1)}), bf16[32,5,4,128]{3,2,1,0:T(4,128)(2,1)S(1)}, u32[]{:S(2)}, u32[]{:S(2)}) async-start(bf16[32,5,4,128]{3,2,1,0:T(4,128)(2,1)} %get-tuple-element.25), calls=%async_computation | async-start | bytes 327680 | tf_op jit(solution)/shard_map/all_to_all | solution.py:247
  18.6 0.0 copy-done.1
  18.6 0.0 copy-start
  18.6 1.2 %copy-done = bf16[8,32,2048]{2,1,0:T(8,128)(2,1)S(1)} copy-done((bf16[8,32,2048]{2,1,0:T(8,128)(2,1)S(1)}, bf16[8,32,2048]{2,1,0:T(8,128)(2,1)}, u32[]{:S(2)}) %copy-start) | copy-done | bytes 1048600
  19.8 1.2 %shard_map.84 = (bf16[12,32,512]{2,1,0:T(8,128)(2,1)S(1)}, bf16[12,32,512]{2,1,0:T(8,128)(2,1)}, bf16[12,32,512]{2,1,0:T(8,128)(2,1)S(1)}, bf16[12,32,512]{2,1,0:T(8,128)(2,1)S(1)}) custom-call(bf16[8,32,2048]{2,1,0:T(8,128)(2,1)S(1)} %copy-done, bf16[4,32,2048]{2,1,0:T(8,128)(2,1)S(1)} %copy-done.1), custom_call_target="tpu_custom_call" | custom-call | bytes 3145728 | tf_op jit(solution)/shard_map/pallas_call | solution.py:264
  21.0 0.0 copy-start.4
  21.0 0.0 copy-start.5
  21.0 0.0 copy-start.2
  21.0 3.3 %collective-permute-start = (bf16[12,32,512]{2,1,0:T(8,128)(2,1)}, bf16[12,32,512]{2,1,0:T(8,128)(2,1)S(1)}, u32[]{:S(2)}, u32[]{:S(2)}) collective-permute-start(bf16[12,32,512]{2,1,0:T(8,128)(2,1)} %get-tuple-element.30), channel_id=1, source_target_pairs={{0,4},{1,5},{2,6},{3,7},{4,0},{5,1},{6,2},{7,3},{8,12},{9,13},{10,... | collective-permute-start | bytes 1179656 | tf_op jit(solution)/shard_map/ppermute | solution.py:276
  24.3 4.4 %collective-permute-start.1 = (bf16[12,32,512]{2,1,0:T(8,128)(2,1)S(1)}, bf16[12,32,512]{2,1,0:T(8,128)(2,1)S(1)}, u32[]{:S(2)}, u32[]{:S(2)}) collective-permute-start(bf16[12,32,512]{2,1,0:T(8,128)(2,1)S(1)} %get-tuple-element.31), channel_id=1, source_target_pairs={{0,3},{1,2},{2,1},{3,0},{4,7},{5,6},{6,5},{7,4},{8,11},{9,10},{10,... | collective-permute-start | bytes 1179656 | tf_op jit(solution)/shard_map/ppermute | solution.py:276
  28.7 2.0 %collective-permute-start.2 = (bf16[12,32,512]{2,1,0:T(8,128)(2,1)S(1)}, bf16[12,32,512]{2,1,0:T(8,128)(2,1)S(1)}, u32[]{:S(2)}, u32[]{:S(2)}) collective-permute-start(bf16[12,32,512]{2,1,0:T(8,128)(2,1)S(1)} %get-tuple-element.32), channel_id=1, source_target_pairs={{0,7},{1,6},{2,5},{3,4},{4,3},{5,2},{6,1},{7,0},{8,15},{9,14},{10,... | collective-permute-start | bytes 1179656 | tf_op jit(solution)/shard_map/ppermute | solution.py:276
  30.7 0.0 copy-start.3
  30.7 0.0 copy-done.4
  30.7 0.0 copy-done.5
  30.7 0.7 copy-done.3
  31.4 0.2 fusion
  31.6 4.1 %all-to-all-done.arrived = bf16[32,5,4,128]{3,2,1,0:T(4,128)(2,1)S(1)} async-done(((bf16[32,5,4,128]{3,2,1,0:T(4,128)(2,1)}), bf16[32,5,4,128]{3,2,1,0:T(4,128)(2,1)S(1)}, u32[]{:S(2)}, u32[]{:S(2)}) %all-to-all-start) | async-done | bytes 163872 | tf_op jit(solution)/shard_map/all_to_all | solution.py:247
  35.7 0.0 copy-done.2
  35.7 1.3 %shard_map.83 = bf16[4,60,4,128]{3,2,1,0:T(4,128)(2,1)} custom-call(s32[8]{0:T(128)S(1)} %and_select_fusion.origin, bf16[32,5,4,128]{3,2,1,0:T(4,128)(2,1)S(1)} %all-to-all-done.arrived, bf16[4,5,4,128]{3,2,1,0:T(4,128)(2,1)S(1)} %copy-done.2), custom_call_target="tpu_custom_call" | custom-call | tf_op jit(solution)/shard_map/pallas_call | solution.py:278
  37.0 4.9 %all-to-all-start.1 = ((bf16[4,60,4,128]{3,2,1,0:T(4,128)(2,1)}), bf16[4,60,4,128]{3,2,1,0:T(4,128)(2,1)S(1)}, u32[]{:S(2)}, u32[]{:S(2)}) async-start(bf16[4,60,4,128]{3,2,1,0:T(4,128)(2,1)} %shard_map.83), calls=%async_computation.1 | async-start | bytes 491520 | tf_op jit(solution)/shard_map/all_to_all | solution.py:231
  41.9 0.0 copy-start.6
  41.9 0.7 copy-done.6
  42.6 0.1 dynamic_slice.3
  42.6 0.1 pad_add_fusion.lengths
  42.7 0.0 collective-permute-done.rest_1_
  42.7 0.0 collective-permute-done.1.rest_2_
  42.7 3.1 %collective-permute-done.2.rest_3_ = bf16[12,32,512]{2,1,0:T(8,128)(2,1)S(1)} collective-permute-done((bf16[12,32,512]{2,1,0:T(8,128)(2,1)S(1)}, bf16[12,32,512]{2,1,0:T(8,128)(2,1)S(1)}, u32[]{:S(2)}, u32[]{:S(2)}) %collective-permute-start.2) | collective-permute-done | bytes 393248 | tf_op jit(solution)/shard_map/ppermute | solution.py:276
  45.9 1.4 %all-to-all-done.1 = bf16[4,60,4,128]{3,2,1,0:T(4,128)(2,1)S(1)} async-done(((bf16[4,60,4,128]{3,2,1,0:T(4,128)(2,1)}), bf16[4,60,4,128]{3,2,1,0:T(4,128)(2,1)S(1)}, u32[]{:S(2)}, u32[]{:S(2)}) %all-to-all-start.1) | async-done | bytes 245792 | tf_op jit(solution)/shard_map/all_to_all | solution.py:231
  47.3 1.3 %shard_map.85 = bf16[4,208,128]{2,1,0:T(8,128)(2,1)S(1)} custom-call(s32[12]{0:T(128)S(1)} %pad_add_fusion.lengths, bf16[4,240,128]{2,1,0:T(8,128)(2,1)S(1)} %bitcast.11, bf16[12,32,512]{2,1,0:T(8,128)(2,1)S(1)} %get-tuple-element.29.rest_0_, bf16[12,32,512]{2,1,0:T(8,128)(2,1)S(1)} %collective-permute-done.rest_1_, ...), custom_call_target="tpu_custom_call" | custom-call | flops 100000000 | bytes 3145728 | tf_op jit(solution)/shard_map/pallas_call | solution.py:283
  48.6 8.0 %all_to_all.20.gathered = bf16[4,208,128]{2,1,0:T(8,128)(2,1)S(1)} all-to-all(bf16[4,208,128]{2,1,0:T(8,128)(2,1)S(1)} %shard_map.85), channel_id=1, replica_groups={{0,1,12,13},{2,3,14,15},{4,5,8,9},{6,7,10,11},{16,17,28,29},{18,19,30,3..., dimensions={0} | all-to-all | bytes 425984 | tf_op jit(solution)/shard_map/all_to_all | solution.py:231
  56.7 2.1 %shard_map.86 = (bf16[32,16,128]{2,1,0:T(8,128)(2,1)}, bf16[4,16,128]{2,1,0:T(8,128)(2,1)S(1)}) custom-call(s32[8]{0:T(128)S(1)} %and_select_fusion.origin, bf16[4,208,128]{2,1,0:T(8,128)(2,1)S(1)} %all_to_all.20.gathered, bf16[4,240,128]{2,1,0:T(8,128)(2,1)S(1)} %bitcast.12), custom_call_target="tpu_custom_call" | custom-call | tf_op jit(solution)/shard_map/pallas_call | solution.py:297
  58.8 14.6 %all-to-all-start.3 = ((bf16[32,16,128]{2,1,0:T(8,128)(2,1)}), bf16[32,16,128]{2,1,0:T(8,128)(2,1)S(1)}, u32[]{:S(2)}, u32[]{:S(2)}) async-start(bf16[32,16,128]{2,1,0:T(8,128)(2,1)} %get-tuple-element.33), calls=%async_computation.3 | async-start | bytes 262144 | tf_op jit(solution)/shard_map/all_to_all | solution.py:302
  73.4 15.8 %all-to-all-done.3.returned = bf16[32,16,128]{2,1,0:T(8,128)(2,1)S(1)} async-done(((bf16[32,16,128]{2,1,0:T(8,128)(2,1)}), bf16[32,16,128]{2,1,0:T(8,128)(2,1)S(1)}, u32[]{:S(2)}, u32[]{:S(2)}) %all-to-all-start.3) | async-done | bytes 131104 | tf_op jit(solution)/shard_map/all_to_all | solution.py:302
  89.2 1.2 %shard_map.87 = bf16[12,16,128]{2,1,0:T(8,128)(2,1)} custom-call(s32[8]{0:T(128)S(1)} %and_select_fusion.1.target, bf16[32,16,128]{2,1,0:T(8,128)(2,1)S(1)} %all-to-all-done.3.returned, bf16[4,16,128]{2,1,0:T(8,128)(2,1)S(1)} %get-tuple-element.34.kept), custom_call_target="tpu_custom_call" | custom-call | tf_op jit(solution)/shard_map/pallas_call | solution.py:304
  (3 shorter events, 0.0 us)
Async XLA Ops:
  0.0 18.6 %copy-start.1 = (bf16[4,32,2048]{2,1,0:T(8,128)(2,1)S(1)}, bf16[4,32,2048]{2,1,0:T(8,128)(2,1)}, u32[]{:S(2)}) copy-start(bf16[4,32,2048]{2,1,0:T(8,128)(2,1)} %resident) | copy-start | bytes 1572868
  1.8 33.9 %all-to-all-start = ((bf16[32,5,4,128]{3,2,1,0:T(4,128)(2,1)}), bf16[32,5,4,128]{3,2,1,0:T(4,128)(2,1)S(1)}, u32[]{:S(2)}, u32[]{:S(2)}) async-start(bf16[32,5,4,128]{3,2,1,0:T(4,128)(2,1)} %get-tuple-element.25), calls=%async_computation | async-start | bytes 327680 | tf_op jit(solution)/shard_map/all_to_all | solution.py:247
  18.6 1.2 %copy-start = (bf16[8,32,2048]{2,1,0:T(8,128)(2,1)S(1)}, bf16[8,32,2048]{2,1,0:T(8,128)(2,1)}, u32[]{:S(2)}) copy-start(bf16[8,32,2048]{2,1,0:T(8,128)(2,1)} %moved) | copy-start | bytes 3145732
  21.0 9.8 %copy-start.4 = (s32[256]{0:T(256)S(1)}, s32[256]{0:T(256)}, u32[]{:S(2)}) copy-start(s32[256]{0:T(256)} %param.15) | copy-start | bytes 3076
  21.0 9.8 %copy-start.5 = (s32[256]{0:T(256)S(1)}, s32[256]{0:T(256)}, u32[]{:S(2)}) copy-start(s32[256]{0:T(256)} %param.13) | copy-start | bytes 3076
  21.0 14.7 %copy-start.2 = (bf16[4,5,4,128]{3,2,1,0:T(4,128)(2,1)S(1)}, bf16[4,5,4,128]{3,2,1,0:T(4,128)(2,1)}, u32[]{:S(2)}) copy-start(bf16[4,5,4,128]{3,2,1,0:T(4,128)(2,1)} %get-tuple-element.26.kept) | copy-start | bytes 61444
  21.0 21.8 %collective-permute-start = (bf16[12,32,512]{2,1,0:T(8,128)(2,1)}, bf16[12,32,512]{2,1,0:T(8,128)(2,1)S(1)}, u32[]{:S(2)}, u32[]{:S(2)}) collective-permute-start(bf16[12,32,512]{2,1,0:T(8,128)(2,1)} %get-tuple-element.30), channel_id=1, source_target_pairs={{0,4},{1,5},{2,6},{3,7},{4,0},{5,1},{6,2},{7,3},{8,12},{9,13},{10,... | collective-permute-start | bytes 1179656 | tf_op jit(solution)/shard_map/ppermute | solution.py:276
  24.3 18.4 %collective-permute-start.1 = (bf16[12,32,512]{2,1,0:T(8,128)(2,1)S(1)}, bf16[12,32,512]{2,1,0:T(8,128)(2,1)S(1)}, u32[]{:S(2)}, u32[]{:S(2)}) collective-permute-start(bf16[12,32,512]{2,1,0:T(8,128)(2,1)S(1)} %get-tuple-element.31), channel_id=1, source_target_pairs={{0,3},{1,2},{2,1},{3,0},{4,7},{5,6},{6,5},{7,4},{8,11},{9,10},{10,... | collective-permute-start | bytes 1179656 | tf_op jit(solution)/shard_map/ppermute | solution.py:276
  28.7 17.2 %collective-permute-start.2 = (bf16[12,32,512]{2,1,0:T(8,128)(2,1)S(1)}, bf16[12,32,512]{2,1,0:T(8,128)(2,1)S(1)}, u32[]{:S(2)}, u32[]{:S(2)}) collective-permute-start(bf16[12,32,512]{2,1,0:T(8,128)(2,1)S(1)} %get-tuple-element.32), channel_id=1, source_target_pairs={{0,7},{1,6},{2,5},{3,4},{4,3},{5,2},{6,1},{7,0},{8,15},{9,14},{10,... | collective-permute-start | bytes 1179656 | tf_op jit(solution)/shard_map/ppermute | solution.py:276
  30.7 0.7 copy-start.3
  37.0 10.3 %all-to-all-start.1 = ((bf16[4,60,4,128]{3,2,1,0:T(4,128)(2,1)}), bf16[4,60,4,128]{3,2,1,0:T(4,128)(2,1)S(1)}, u32[]{:S(2)}, u32[]{:S(2)}) async-start(bf16[4,60,4,128]{3,2,1,0:T(4,128)(2,1)} %shard_map.83), calls=%async_computation.1 | async-start | bytes 491520 | tf_op jit(solution)/shard_map/all_to_all | solution.py:231
  41.9 0.7 copy-start.6
  58.8 30.5 %all-to-all-start.3 = ((bf16[32,16,128]{2,1,0:T(8,128)(2,1)}), bf16[32,16,128]{2,1,0:T(8,128)(2,1)S(1)}, u32[]{:S(2)}, u32[]{:S(2)}) async-start(bf16[32,16,128]{2,1,0:T(8,128)(2,1)} %get-tuple-element.33), calls=%async_computation.3 | async-start | bytes 262144 | tf_op jit(solution)/shard_map/all_to_all | solution.py:302

commit v5 on v4

--- a/solution.py
+++ b/solution.py
@@ -19,7 +19,10 @@
 SIDE = 4
 STRIDE = 32
 HEADS = H // SHARDS
-PAIRS = KVH // SIDE
+BLOCKS = 2
+PEERS = SHARDS // BLOCKS
+PAIRS = PEERS // 2
+WIDE = BLOCKS * STRIDE
 QROWS = HEADS * STEPS
 ROWS = SLOTS * QROWS
 FEATURES = KVH * HD
@@ -50,12 +53,8 @@
     )
 
 
-def swapped(step, y, x):
-    return y ^ (step % 2), x ^ (step // 2 * 3)
-
-
-def class_of(y, x):
-    return jnp.minimum(y, 3 - y), x // 2
+def swapped(step, x):
+    return x ^ (step * 3)
 
 
 def place_of():
@@ -97,12 +96,12 @@
 
 
 def split_kernel(moved, resident, *outs):
-    here = place_of()
+    _, here = place_of()
     for step, out in enumerate(outs):
-        low, half = class_of(*swapped(step, *here))
-        for place, pair in enumerate((2 * low + half, 6 - 2 * low + half)):
+        half = swapped(step, here) // 2
+        for place in range(PAIRS):
             for part in range(2):
-                lanes = pl.ds(pl.multiple_of(pair * HD + part * FEATURES, HD), HD)
+                lanes = pl.ds(pl.multiple_of((2 * place + half) * HD + part * FEATURES, HD), HD)
                 columns = slice((part * PAIRS + place) * HD, (part * PAIRS + place + 1) * HD)
                 out[:MIG, :, columns] = moved[:, :, lanes]
                 out[MIG:, :, columns] = resident[:, :, lanes]
@@ -111,7 +110,7 @@
 def spread_kernel(origin, arrived, kept, asking):
     for row in range(SLOTS):
         chunk = arrived.at[origin[row]] if row < MIG else kept.at[row - MIG]
-        for peer in range(SIDE):
+        for peer in range(PEERS):
             asking[peer, row * HEADS : (row + 1) * HEADS] = chunk[:HEADS]
             asking[peer, SLOTS * HEADS + row] = chunk[HEADS]
 
@@ -122,9 +121,9 @@
 
 def partial_kernel(lengths, asking, *rest):
     *blocks, payload, scores, weights, stats = rest
-    column = lax.broadcasted_iota(jnp.int32, (1, HD), 1)
-    y, x = swapped(column // STRIDE, *place_of())
-    position = (y * SIDE + x) * STRIDE + column % STRIDE
+    y, x = place_of()
+    column = lax.broadcasted_iota(jnp.int32, (1, WIDE), 1)
+    position = (y * SIDE + swapped(column // STRIDE, x)) * STRIDE + column % STRIDE
 
     def stored(row, place):
         lanes = slice(place * HD, (place + 1) * HD)
@@ -140,7 +139,7 @@
             scores[2 * pair + 1, span, :] = found[QROWS:]
     lane = lax.broadcasted_iota(jnp.int32, (ROWS, HD), 1)
     table = jnp.zeros((ROWS, HD), F32)
-    for peer in range(SIDE):
+    for peer in range(PEERS):
         found = scores[peer]
         top = jnp.max(found, axis=1, keepdims=True)
         first = top.astype(BF).astype(F32)
@@ -155,7 +154,7 @@
     stats[ROWS:, :] = jnp.zeros((2 * HD - ROWS, HD), F32)
     low = stats[:HD, :].T
     high = stats[HD:, :].T
-    for peer in range(SIDE):
+    for peer in range(PEERS):
         rows = slice(peer * 8, (peer + 1) * 8)
         payload[peer, ROWS:, :] = jnp.concatenate([low[rows], high[rows]], 0).astype(BF)
     for row in range(SLOTS):
@@ -169,7 +168,7 @@
 
 def merge_kernel(origin, gathered, everyone, sent, kept):
     y, x = place_of()
-    first = jnp.where(y > 1, 2, 0)
+    first = 2 * y
     asked = everyone[first + x % 2, :ROWS, :]
     keys = everyone[first, ROWS:, :]
     values = everyone[first + 1, ROWS:, :]
@@ -180,13 +179,13 @@
     fresh_top = jnp.max(fresh, axis=1, keepdims=True)
 
     tops = gathered[:, ROWS:, :].astype(F32)
-    blank = jnp.zeros((HD - SIDE * 8, HD), F32)
-    low = jnp.concatenate([tops[:, :8, :].reshape(SIDE * 8, HD), blank], 0).T
-    high = jnp.concatenate([tops[:, 8:, :].reshape(SIDE * 8, HD), blank], 0).T[: ROWS - HD]
+    blank = jnp.zeros((HD - PEERS * 8, HD), F32)
+    low = jnp.concatenate([tops[:, :8, :].reshape(PEERS * 8, HD), blank], 0).T
+    high = jnp.concatenate([tops[:, 8:, :].reshape(PEERS * 8, HD), blank], 0).T[: ROWS - HD]
     pairs = jnp.concatenate([low, high], 0)
     both = pairs + pltpu.roll(pairs, HD - 2, 1)
     lane = lax.broadcasted_iota(jnp.int32, (ROWS, HD), 1)
-    is_top = (lane % 8 == 0) & (lane < SIDE * 8)
+    is_top = (lane % 8 == 0) & (lane < PEERS * 8)
     tops = jnp.where(is_top, both, FLOOR)
     sums = pltpu.roll(both, HD - 1, 1)
     highest = jnp.maximum(jnp.max(tops, axis=1, keepdims=True), fresh_top)
@@ -195,7 +194,7 @@
     totals = jnp.sum(jnp.where(is_top, factors * sums, 0.0), axis=1, keepdims=True)
     totals += jnp.sum(fresh_weights, axis=1, keepdims=True)
     blended = jnp.dot(fresh_weights.astype(BF), values, preferred_element_type=F32)
-    for peer in range(SIDE):
+    for peer in range(PEERS):
         blended += factors[:, peer * 8 : peer * 8 + 1] * gathered[peer, :ROWS, :].astype(F32)
     result = (blended / totals).astype(BF)
 
@@ -224,8 +223,7 @@
     decode_slot,
 ):
     shape = jax.ShapeDtypeStruct
-    whole = [(y, x) for y in range(SIDE) for x in range(SIDE)]
-    peers = [[y * SIDE + x for y in (low, 3 - low) for x in (2 * half, 2 * half + 1)] for low in range(2) for half in range(2)]
+    peers = [[y * SIDE + 2 * half + x for y in range(SIDE) for x in range(2)] for half in range(2)]
 
     def across(array):
         return lax.all_to_all(array, "tensor", 0, 0, axis_index_groups=peers, tiled=True)
@@ -263,32 +261,29 @@
 
     split = call(
         split_kernel,
-        (shape((SLOTS, STRIDE, 2 * PAIRS * HD), BF),) * SIDE,
+        (shape((SLOTS, STRIDE, 2 * PAIRS * HD), BF),) * BLOCKS,
         [VM, VM],
         moved=3 * 2**20,
     )(prefill_cache, resident_cache)
     blocks = [split[0]]
-    for step in range(1, SIDE):
-        steps = []
-        for y, x in whole:
-            other, side = swapped(step, y, x)
-            steps.append((y * SIDE + x, other * SIDE + side))
+    for step in range(1, BLOCKS):
+        steps = [(t, t // SIDE * SIDE + swapped(step, t % SIDE)) for t in range(SHARDS)]
         blocks.append(lax.ppermute(split[step], "tensor", steps))
 
     asking = call(
-        spread_kernel, shape((SIDE, SLOTS * TILES, STEPS, HD), BF), [SM, VM, VM]
+        spread_kernel, shape((PEERS, SLOTS * TILES, STEPS, HD), BF), [SM, VM, VM]
     )(origin, arrived, kept)
-    everyone = across(asking).reshape(SIDE, ROWS + ENTRIES, HD)
+    everyone = across(asking).reshape(PEERS, ROWS + ENTRIES, HD)
 
     payload = call(
         partial_kernel,
-        shape((SIDE, PAYLOAD, HD), BF),
-        [SM] + [VM] * (1 + SIDE),
+        shape((PEERS, PAYLOAD, HD), BF),
+        [SM] + [VM] * (1 + BLOCKS),
         flops=10**8,
         moved=3 * 2**20,
         scratch=[
-            pltpu.VMEM((SIDE, ROWS, HD), F32),
-            pltpu.VMEM((SIDE, ROWS, HD), BF),
+            pltpu.VMEM((PEERS, ROWS, WIDE), F32),
+            pltpu.VMEM((PEERS, ROWS, WIDE), BF),
             pltpu.VMEM((2 * HD, HD), F32),
         ],
     )(lengths, everyone, *blocks)

time: 91.7 us -> 91 us (level)
  starting transfers between devices: 46 us -> 35.8 us
  waiting for transfers between devices: 24.5 us -> 32.3 us
  blocking collectives: 8.04 us -> 10 us
    all_to_all x1, waiting for transfers between devices: 4.07 us -> 9.79 us  [body(): arrived = lax.all_to_all(sent, 'group', 0, 0, tiled=True)]
    all_to_all x1, starting transfers between devices: 14.6 us -> 9.38 us  [body(): returned = lax.all_to_all(finished, 'group', 0, 0, tiled=True)]
    ppermute x3 -> x1, starting transfers between devices: 9.7 us -> 4.5 us  [body(): blocks.append(lax.ppermute(split[step], 'tensor', steps))]
    all_to_all x1, waiting for transfers between devices: 1.44 us -> 6.3 us  [across(): lax.all_to_all(array, 'tensor', 0, 0, axis_index_groups=peers, tiled=True)]
    ppermute x3 -> x1, waiting for transfers between devices: 3.14 us -> 0.36 us  [body(): blocks.append(lax.ppermute(split[step], 'tensor', steps))]
    all_to_all x1, blocking collectives: 8.04 us -> 10 us  [across(): lax.all_to_all(array, 'tensor', 0, 0, axis_index_groups=peers, tiled=True)]
  transfers between devices with their start and end apart: 6 -> 4, of which waited for: 4 -> 4; matrix products, arithmetic and copies ran while one was open for 0% -> 0% of each run, Pallas kernels for 3% -> 3%
where the time goes in v5:
time: 91 us; the launch traced here: 89.8 us
  starting transfers between devices  35.8 us (39%)
  waiting for transfers between devices  32.3 us (35%)
  blocking collectives  10 us (11%)
  Pallas kernels  9.34 us (10%)
  local copies, waits for them, and re-layouts  1.96 us (2%)
    all_to_all x1, starting transfers between devices, body(): arrived = lax.all_to_all(sent, 'group', 0, 0, tiled=True)  16.8 us
    all_to_all x1, waiting for transfers between devices, body(): returned = lax.all_to_all(finished, 'group', 0, 0, tiled=True)  15.8 us
    all_to_all x1, blocking collectives, across(): lax.all_to_all(array, 'tensor', 0, 0, axis_index_groups=peers, tiled=True)  10 us
    all_to_all x1, waiting for transfers between devices, body(): arrived = lax.all_to_all(sent, 'group', 0, 0, tiled=True)  9.79 us
    all_to_all x1, starting transfers between devices, body(): returned = lax.all_to_all(finished, 'group', 0, 0, tiled=True)  9.38 us
    all_to_all x1, waiting for transfers between devices, across(): lax.all_to_all(array, 'tensor', 0, 0, axis_index_groups=peers, tiled=True)  6.3 us
    all_to_all x1, starting transfers between devices, across(): lax.all_to_all(array, 'tensor', 0, 0, axis_index_groups=peers, tiled=True)  5.12 us
    ppermute x1, starting transfers between devices, body(): blocks.append(lax.ppermute(split[step], 'tensor', steps))  4.5 us
  transfers between devices with their start and end apart: 4, of which 4 were waited for; matrix products, arithmetic and copies ran while one was open for 0% of the time, Pallas kernels for 3%

profile of v5, /device:TPU:1, one launch (start us, length us, event | category | flops | bytes accessed | tf_op | source)
XLA Modules:
  0.0 89.8 jit_solution(4216293039546279270)
XLA Ops:
  0.0 0.0 copy-start.1
  0.0 1.8 %shard_map.82 = (bf16[32,5,4,128]{3,2,1,0:T(4,128)(2,1)}, bf16[4,5,4,128]{3,2,1,0:T(4,128)(2,1)}) custom-call(s32[2,128]{1,0:T(2,128)} %bitcast.15, s32[2,128]{1,0:T(2,128)} %bitcast.14, bf16[12,4,4,128]{3,2,1,0:T(4,128)(2,1)} %bitcast.13, bf16[12,4,2048]{2,1,0:T(4,128)(2,1)} %fresh.1), custom_call_target="tpu_custom_call" | custom-call | tf_op jit(solution)/shard_map/pallas_call | solution.py:232
  1.8 16.8 %all-to-all-start = ((bf16[32,5,4,128]{3,2,1,0:T(4,128)(2,1)}), bf16[32,5,4,128]{3,2,1,0:T(4,128)(2,1)S(1)}, u32[]{:S(2)}, u32[]{:S(2)}) async-start(bf16[32,5,4,128]{3,2,1,0:T(4,128)(2,1)} %get-tuple-element.23), calls=%async_computation | async-start | bytes 327680 | tf_op jit(solution)/shard_map/all_to_all | solution.py:245
  18.5 0.0 copy-done.1
  18.6 0.0 copy-start
  18.6 1.2 %copy-done = bf16[8,32,2048]{2,1,0:T(8,128)(2,1)S(1)} copy-done((bf16[8,32,2048]{2,1,0:T(8,128)(2,1)S(1)}, bf16[8,32,2048]{2,1,0:T(8,128)(2,1)}, u32[]{:S(2)}) %copy-start) | copy-done | bytes 1048600
  19.8 0.0 copy-start.3
  19.8 0.0 copy-start.4
  19.8 0.0 copy-start.5
  19.8 1.3 %shard_map.84 = (bf16[12,32,1024]{2,1,0:T(8,128)(2,1)S(1)}, bf16[12,32,1024]{2,1,0:T(8,128)(2,1)}) custom-call(bf16[8,32,2048]{2,1,0:T(8,128)(2,1)S(1)} %copy-done, bf16[4,32,2048]{2,1,0:T(8,128)(2,1)S(1)} %copy-done.1), custom_call_target="tpu_custom_call" | custom-call | bytes 3145728 | tf_op jit(solution)/shard_map/pallas_call | solution.py:262
  21.1 0.0 copy-start.2
  21.1 4.5 %collective-permute-start = (bf16[12,32,1024]{2,1,0:T(8,128)(2,1)}, bf16[12,32,1024]{2,1,0:T(8,128)(2,1)S(1)}, u32[]{:S(2)}, u32[]{:S(2)}) collective-permute-start(bf16[12,32,1024]{2,1,0:T(8,128)(2,1)} %get-tuple-element.28), channel_id=1, source_target_pairs={{0,3},{1,2},{2,1},{3,0},{4,7},{5,6},{6,5},{7,4},{8,11},{9,10},{10,... | collective-permute-start | bytes 2359304 | tf_op jit(solution)/shard_map/ppermute | solution.py:271
  25.6 0.0 copy-done.3
  25.6 0.0 copy-done.4
  25.7 0.0 copy-done.5
  25.7 0.2 fusion
  25.9 9.8 %all-to-all-done.arrived = bf16[32,5,4,128]{3,2,1,0:T(4,128)(2,1)S(1)} async-done(((bf16[32,5,4,128]{3,2,1,0:T(4,128)(2,1)}), bf16[32,5,4,128]{3,2,1,0:T(4,128)(2,1)S(1)}, u32[]{:S(2)}, u32[]{:S(2)}) %all-to-all-start) | async-done | bytes 163872 | tf_op jit(solution)/shard_map/all_to_all | solution.py:245
  35.7 0.0 copy-done.2
  35.7 1.5 %shard_map.83 = bf16[8,60,4,128]{3,2,1,0:T(4,128)(2,1)} custom-call(s32[8]{0:T(128)S(1)} %and_select_fusion.origin, bf16[32,5,4,128]{3,2,1,0:T(4,128)(2,1)S(1)} %all-to-all-done.arrived, bf16[4,5,4,128]{3,2,1,0:T(4,128)(2,1)S(1)} %copy-done.2), custom_call_target="tpu_custom_call" | custom-call | tf_op jit(solution)/shard_map/pallas_call | solution.py:273
  37.2 5.1 %all-to-all-start.1 = ((bf16[8,60,4,128]{3,2,1,0:T(4,128)(2,1)}), bf16[8,60,4,128]{3,2,1,0:T(4,128)(2,1)S(1)}, u32[]{:S(2)}, u32[]{:S(2)}) async-start(bf16[8,60,4,128]{3,2,1,0:T(4,128)(2,1)} %shard_map.83), calls=%async_computation.1 | async-start | bytes 983040 | tf_op jit(solution)/shard_map/all_to_all | solution.py:229
  42.3 0.0 copy-start.6
  42.3 0.7 copy-done.6
  42.9 0.1 dynamic_slice.3
  43.0 0.1 pad_add_fusion.lengths
  43.1 0.4 collective-permute-done.rest_1_
  43.4 6.3 %all-to-all-done.1 = bf16[8,60,4,128]{3,2,1,0:T(4,128)(2,1)S(1)} async-done(((bf16[8,60,4,128]{3,2,1,0:T(4,128)(2,1)}), bf16[8,60,4,128]{3,2,1,0:T(4,128)(2,1)S(1)}, u32[]{:S(2)}, u32[]{:S(2)}) %all-to-all-start.1) | async-done | bytes 491552 | tf_op jit(solution)/shard_map/all_to_all | solution.py:229
  49.7 1.5 %shard_map.85 = bf16[8,208,128]{2,1,0:T(8,128)(2,1)S(1)} custom-call(s32[12]{0:T(128)S(1)} %pad_add_fusion.lengths, bf16[8,240,128]{2,1,0:T(8,128)(2,1)S(1)} %bitcast.11, bf16[12,32,1024]{2,1,0:T(8,128)(2,1)S(1)} %get-tuple-element.27.rest_0_, bf16[12,32,1024]{2,1,0:T(8,128)(2,1)S(1)} %collective-permute-done.rest_1_), custom_call_target="tpu_custom_call" | custom-call | flops 100000000 | bytes 3145728 | tf_op jit(solution)/shard_map/pallas_call | solution.py:278
  51.2 10.0 %all_to_all.20.gathered = bf16[8,208,128]{2,1,0:T(8,128)(2,1)S(1)} all-to-all(bf16[8,208,128]{2,1,0:T(8,128)(2,1)S(1)} %shard_map.85), channel_id=1, replica_groups={{0,1,4,5,8,9,12,13},{2,3,6,7,10,11,14,15},{16,17,20,21,24,25,28,29},{18..., dimensions={0} | all-to-all | bytes 851968 | tf_op jit(solution)/shard_map/all_to_all | solution.py:229
  61.3 2.1 %shard_map.86 = (bf16[32,16,128]{2,1,0:T(8,128)(2,1)}, bf16[4,16,128]{2,1,0:T(8,128)(2,1)S(1)}) custom-call(s32[8]{0:T(128)S(1)} %and_select_fusion.origin, bf16[8,208,128]{2,1,0:T(8,128)(2,1)S(1)} %all_to_all.20.gathered, bf16[8,240,128]{2,1,0:T(8,128)(2,1)S(1)} %bitcast.12), custom_call_target="tpu_custom_call" | custom-call | tf_op jit(solution)/shard_map/pallas_call | solution.py:292
  63.4 9.4 %all-to-all-start.3 = ((bf16[32,16,128]{2,1,0:T(8,128)(2,1)}), bf16[32,16,128]{2,1,0:T(8,128)(2,1)S(1)}, u32[]{:S(2)}, u32[]{:S(2)}) async-start(bf16[32,16,128]{2,1,0:T(8,128)(2,1)} %get-tuple-element.29), calls=%async_computation.3 | async-start | bytes 262144 | tf_op jit(solution)/shard_map/all_to_all | solution.py:297
  72.8 15.8 %all-to-all-done.3.returned = bf16[32,16,128]{2,1,0:T(8,128)(2,1)S(1)} async-done(((bf16[32,16,128]{2,1,0:T(8,128)(2,1)}), bf16[32,16,128]{2,1,0:T(8,128)(2,1)S(1)}, u32[]{:S(2)}, u32[]{:S(2)}) %all-to-all-start.3) | async-done | bytes 131104 | tf_op jit(solution)/shard_map/all_to_all | solution.py:297
  88.7 1.2 %shard_map.87 = bf16[12,16,128]{2,1,0:T(8,128)(2,1)} custom-call(s32[8]{0:T(128)S(1)} %and_select_fusion.1.target, bf16[32,16,128]{2,1,0:T(8,128)(2,1)S(1)} %all-to-all-done.3.returned, bf16[4,16,128]{2,1,0:T(8,128)(2,1)S(1)} %get-tuple-element.30.kept), custom_call_target="tpu_custom_call" | custom-call | tf_op jit(solution)/shard_map/pallas_call | solution.py:299
  (3 shorter events, 0.0 us)
Async XLA Ops:
  0.0 18.5 %copy-start.1 = (bf16[4,32,2048]{2,1,0:T(8,128)(2,1)S(1)}, bf16[4,32,2048]{2,1,0:T(8,128)(2,1)}, u32[]{:S(2)}) copy-start(bf16[4,32,2048]{2,1,0:T(8,128)(2,1)} %resident) | copy-start | bytes 1572868
  1.8 33.9 %all-to-all-start = ((bf16[32,5,4,128]{3,2,1,0:T(4,128)(2,1)}), bf16[32,5,4,128]{3,2,1,0:T(4,128)(2,1)S(1)}, u32[]{:S(2)}, u32[]{:S(2)}) async-start(bf16[32,5,4,128]{3,2,1,0:T(4,128)(2,1)} %get-tuple-element.23), calls=%async_computation | async-start | bytes 327680 | tf_op jit(solution)/shard_map/all_to_all | solution.py:245
  18.6 1.2 %copy-start = (bf16[8,32,2048]{2,1,0:T(8,128)(2,1)S(1)}, bf16[8,32,2048]{2,1,0:T(8,128)(2,1)}, u32[]{:S(2)}) copy-start(bf16[8,32,2048]{2,1,0:T(8,128)(2,1)} %moved) | copy-start | bytes 3145732
  19.8 5.8 %copy-start.3 = (s32[256]{0:T(256)S(1)}, s32[256]{0:T(256)}, u32[]{:S(2)}) copy-start(s32[256]{0:T(256)} %param.14) | copy-start | bytes 3076
  19.8 5.9 %copy-start.4 = (s32[256]{0:T(256)S(1)}, s32[256]{0:T(256)}, u32[]{:S(2)}) copy-start(s32[256]{0:T(256)} %param.15) | copy-start | bytes 3076
  19.8 5.9 %copy-start.5 = (s32[256]{0:T(256)S(1)}, s32[256]{0:T(256)}, u32[]{:S(2)}) copy-start(s32[256]{0:T(256)} %param.13) | copy-start | bytes 3076
  21.1 14.6 %copy-start.2 = (bf16[4,5,4,128]{3,2,1,0:T(4,128)(2,1)S(1)}, bf16[4,5,4,128]{3,2,1,0:T(4,128)(2,1)}, u32[]{:S(2)}) copy-start(bf16[4,5,4,128]{3,2,1,0:T(4,128)(2,1)} %get-tuple-element.24.kept) | copy-start | bytes 61444
  21.1 22.3 %collective-permute-start = (bf16[12,32,1024]{2,1,0:T(8,128)(2,1)}, bf16[12,32,1024]{2,1,0:T(8,128)(2,1)S(1)}, u32[]{:S(2)}, u32[]{:S(2)}) collective-permute-start(bf16[12,32,1024]{2,1,0:T(8,128)(2,1)} %get-tuple-element.28), channel_id=1, source_target_pairs={{0,3},{1,2},{2,1},{3,0},{4,7},{5,6},{6,5},{7,4},{8,11},{9,10},{10,... | collective-permute-start | bytes 2359304 | tf_op jit(solution)/shard_map/ppermute | solution.py:271
  37.2 12.6 %all-to-all-start.1 = ((bf16[8,60,4,128]{3,2,1,0:T(4,128)(2,1)}), bf16[8,60,4,128]{3,2,1,0:T(4,128)(2,1)S(1)}, u32[]{:S(2)}, u32[]{:S(2)}) async-start(bf16[8,60,4,128]{3,2,1,0:T(4,128)(2,1)} %shard_map.83), calls=%async_computation.1 | async-start | bytes 983040 | tf_op jit(solution)/shard_map/all_to_all | solution.py:229
  42.3 0.7 copy-start.6
  63.4 25.2 %all-to-all-start.3 = ((bf16[32,16,128]{2,1,0:T(8,128)(2,1)}), bf16[32,16,128]{2,1,0:T(8,128)(2,1)S(1)}, u32[]{:S(2)}, u32[]{:S(2)}) async-start(bf16[32,16,128]{2,1,0:T(8,128)(2,1)} %get-tuple-element.29), calls=%async_computation.3 | async-start | bytes 262144 | tf_op jit(solution)/shard_map/all_to_all | solution.py:297

commit v6 on v4

--- a/solution.py
+++ b/solution.py
@@ -63,24 +63,24 @@
     return shard // SIDE, shard % SIDE
 
 
-def pack_kernel(named, holders, asked, fresh, sent, kept, asked_here, fresh_here, named_here, holders_here, sems):
+def pack_kernel(named, holders, asked, fresh, moved, resident, *rest):
+    sent, kept, *blocks = rest[: 2 + SIDE]
+    asked_here, fresh_here, named_here, holders_here, moved_here, resident_here, sems = rest[2 + SIDE :]
     shard = lax.axis_index("tensor")
     first = pl.multiple_of(shard % 2 * FEATURES + shard // 2 * HD, HD)
-    copies = [
-        pltpu.make_async_copy(source, target, sems.at[n])
-        for n, (source, target) in enumerate(
-            (
-                (named, named_here),
-                (holders, holders_here),
-                (asked, asked_here),
-                (fresh.at[:, :, pl.ds(first, HD)], fresh_here),
-            )
-        )
-    ]
+    pairs = (
+        (named, named_here),
+        (holders, holders_here),
+        (asked, asked_here),
+        (fresh.at[:, :, pl.ds(first, HD)], fresh_here),
+        (moved, moved_here),
+        (resident, resident_here),
+    )
+    copies = [pltpu.make_async_copy(*pair, sems.at[n]) for n, pair in enumerate(pairs)]
     for copy in copies:
         copy.start()
     sent[...] = jnp.zeros_like(sent)
-    for copy in copies:
+    for copy in copies[:4]:
         copy.wait()
     names = named_here[...]
     slots = holders_here[...].astype(F32)
@@ -94,23 +94,26 @@
     for slot, group in zip(range(RES, SLOTS), groups):
         sent[group, :HEADS] = asked_here[slot]
         sent[group, HEADS] = fresh_here[slot]
-
-
-def split_kernel(moved, resident, *outs):
+    for copy in copies[4:]:
+        copy.wait()
     here = place_of()
-    for step, out in enumerate(outs):
+    for step, block in enumerate(blocks):
         low, half = class_of(*swapped(step, *here))
         for place, pair in enumerate((2 * low + half, 6 - 2 * low + half)):
             for part in range(2):
                 lanes = pl.ds(pl.multiple_of(pair * HD + part * FEATURES, HD), HD)
                 columns = slice((part * PAIRS + place) * HD, (part * PAIRS + place + 1) * HD)
-                out[:MIG, :, columns] = moved[:, :, lanes]
-                out[MIG:, :, columns] = resident[:, :, lanes]
+                block[:MIG, :, columns] = moved_here[:, :, lanes]
+                block[MIG:, :, columns] = resident_here[:, :, lanes]
 
 
 def spread_kernel(origin, arrived, kept, asking):
+    core = lax.axis_index("group") % 2
     for row in range(SLOTS):
-        chunk = arrived.at[origin[row]] if row < MIG else kept.at[row - MIG]
+        if row < MIG:
+            chunk = arrived.at[origin[row] % 2, origin[row] // 2, core]
+        else:
+            chunk = kept.at[row - MIG]
         for peer in range(SIDE):
             asking[peer, row * HEADS : (row + 1) * HEADS] = chunk[:HEADS]
             asking[peer, SLOTS * HEADS + row] = chunk[HEADS]
@@ -123,7 +126,8 @@
 def partial_kernel(lengths, asking, *rest):
     *blocks, payload, scores, weights, stats = rest
     column = lax.broadcasted_iota(jnp.int32, (1, HD), 1)
-    y, x = swapped(column // STRIDE, *place_of())
+    block = column // STRIDE
+    y, x = swapped(jnp.where(block == 0, 0, (block + 1) % 3 + 1), *place_of())
     position = (y * SIDE + x) * STRIDE + column % STRIDE
 
     def stored(row, place):
@@ -167,7 +171,7 @@
             payload[2 * pair + 1, span, :] = blended[QROWS:]
 
 
-def merge_kernel(origin, gathered, everyone, sent, kept):
+def merge_kernel(origin, target, gathered, everyone, sent, kept):
     y, x = place_of()
     first = jnp.where(y > 1, 2, 0)
     asked = everyone[first + x % 2, :ROWS, :]
@@ -231,24 +235,32 @@
         return lax.all_to_all(array, "tensor", 0, 0, axis_index_groups=peers, tiled=True)
 
     asked = queries.reshape(SLOTS, STEPS, HEADS, HD).transpose(0, 2, 1, 3)
-    sent, kept = call(
+    sent, kept, *split = call(
         pack_kernel,
-        (shape((GROUPS, TILES, STEPS, HD), BF), shape((RES, TILES, STEPS, HD), BF)),
-        [HB] * 4,
+        (shape((GROUPS, TILES, STEPS, HD), BF), shape((RES, TILES, STEPS, HD), BF))
+        + (shape((SLOTS, STRIDE, 2 * PAIRS * HD), BF),) * SIDE,
+        [HB] * 6,
+        moved=3 * 2**20,
         scratch=[
             pltpu.VMEM((SLOTS, HEADS, STEPS, HD), BF),
             pltpu.VMEM((SLOTS, STEPS, HD), BF),
             pltpu.VMEM((2, HD), jnp.int32),
             pltpu.VMEM((2, HD), jnp.int32),
-            pltpu.SemaphoreType.DMA((4,)),
+            pltpu.VMEM((MIG, STRIDE, 2 * FEATURES), BF),
+            pltpu.VMEM((RES, STRIDE, 2 * FEATURES), BF),
+            pltpu.SemaphoreType.DMA((6,)),
         ],
         limit=FULL,
-    )(decode_slot.reshape(2, HD), prefill_slot.reshape(2, HD), asked, new_entries)
-    arrived = lax.all_to_all(sent, "group", 0, 0, tiled=True)
-
-    later = (resident_kept, kept_tokens, prefill_slot, decode_slot, prefill_cache, resident_cache)
+    )(decode_slot.reshape(2, HD), prefill_slot.reshape(2, HD), asked, new_entries, prefill_cache, resident_cache)
+    layers = [[2 * z + core for z in range(GROUPS // 2)] for core in range(2)]
+    chips = [[2 * z, 2 * z + 1] for z in range(GROUPS // 2)]
+    sent = sent.reshape(GROUPS // 2, 2, TILES, STEPS, HD)
+    arrived = lax.all_to_all(sent, "group", 0, 0, axis_index_groups=layers, tiled=True)
+    arrived = lax.all_gather(arrived, "group", axis_index_groups=chips)
+
+    later = (resident_kept, kept_tokens, prefill_slot, decode_slot)
     later, kept = lax.optimization_barrier((later, kept))
-    resident_kept, kept_tokens, prefill_slot, decode_slot, prefill_cache, resident_cache = later
+    resident_kept, kept_tokens, prefill_slot, decode_slot = later
     group = lax.axis_index("group")
 
     def looked_up(names, first, values):
@@ -261,14 +273,8 @@
     resident_len = lax.dynamic_slice_in_dim(resident_kept, group * RES, RES)
     lengths = jnp.concatenate([moved_len, resident_len])
 
-    split = call(
-        split_kernel,
-        (shape((SLOTS, STRIDE, 2 * PAIRS * HD), BF),) * SIDE,
-        [VM, VM],
-        moved=3 * 2**20,
-    )(prefill_cache, resident_cache)
     blocks = [split[0]]
-    for step in range(1, SIDE):
+    for step in (3, 1, 2):
         steps = []
         for y, x in whole:
             other, side = swapped(step, y, x)
@@ -297,8 +303,8 @@
     finished, here = call(
         merge_kernel,
         (shape((GROUPS, QROWS, HD), BF), shape((RES, QROWS, HD), BF)),
-        [SM, VM, VM],
-    )(origin, gathered, everyone)
+        [SM, SM, VM, VM],
+    )(origin, target, gathered, everyone)
     returned = lax.all_to_all(finished, "group", 0, 0, tiled=True)
 
     result = call(select_kernel, shape((SLOTS, QROWS, HD), BF), [SM, VM, VM])(target, returned, here)

time: 91.7 us -> 89.3 us (0.974)
  blocking collectives: 8.04 us -> 31.7 us
  waiting for transfers between devices: 24.5 us -> 11.5 us
  starting transfers between devices: 46 us -> 33.8 us
  local copies, waits for them, and re-layouts: 2.62 us -> 1.41 us
    all_to_all x2 -> x1, waiting for transfers between devices: 19.9 us -> 1.64 us  [body(): lax.all_to_all(sent, 'group', 0, 0, axis_index_groups=layers, tiled=True)]
    all_to_all x1, blocking collectives: 8.04 us -> 25.7 us  [body(): returned = lax.all_to_all(finished, 'group', 0, 0, tiled=True)]
    all_to_all x2 -> x1, starting transfers between devices: 31.4 us -> 15.8 us  [body(): lax.all_to_all(sent, 'group', 0, 0, axis_index_groups=layers, tiled=True)]
    all_to_all x1 -> x2, waiting for transfers between devices: 1.44 us -> 9.87 us  [across(): lax.all_to_all(array, 'tensor', 0, 0, axis_index_groups=peers, tiled=True)]
    all_gather x0 -> x1, blocking collectives: none -> 6.04 us  [body(): arrived = lax.all_gather(arrived, 'group', axis_index_groups=chips)]
    all_to_all x1 -> x2, starting transfers between devices: 4.93 us -> 8.44 us  [across(): lax.all_to_all(array, 'tensor', 0, 0, axis_index_groups=peers, tiled=True)]
    ppermute x3, waiting for transfers between devices: 3.14 us -> 0.01 us  [body(): blocks.append(lax.ppermute(split[step], 'tensor', steps))]
    pallas_call x1, Pallas kernels: 1.77 us -> 3.13 us  [body(): call(pack_kernel, (shape((GROUPS, TILES, STEPS, HD), BF), shape((RES, TIL...]
  transfers between devices with their start and end apart: 6 -> 6, of which waited for: 4 -> 3; matrix products, arithmetic and copies ran while one was open for 0% -> 0% of each run, Pallas kernels for 3% -> 1%
where the time goes in v6:
time: 89.3 us; the launch traced here: 88 us
  starting transfers between devices  33.8 us (38%)
  blocking collectives  31.7 us (35%)
  waiting for transfers between devices  11.5 us (13%)
  Pallas kernels  9.11 us (10%)
  local copies, waits for them, and re-layouts  1.41 us (2%)
    all_to_all x1, blocking collectives, body(): returned = lax.all_to_all(finished, 'group', 0, 0, tiled=True)  25.7 us
    all_to_all x1, starting transfers between devices, body(): lax.all_to_all(sent, 'group', 0, 0, axis_index_groups=layers, tiled=True)  15.8 us
    all_to_all x2, waiting for transfers between devices, across(): lax.all_to_all(array, 'tensor', 0, 0, axis_index_groups=peers, tiled=True)  9.87 us
    ppermute x3, starting transfers between devices, body(): blocks.append(lax.ppermute(split[step], 'tensor', steps))  9.58 us
    all_to_all x2, starting transfers between devices, across(): lax.all_to_all(array, 'tensor', 0, 0, axis_index_groups=peers, tiled=True)  8.44 us
    all_gather x1, blocking collectives, body(): arrived = lax.all_gather(arrived, 'group', axis_index_groups=chips)  6.04 us
    pallas_call x1, Pallas kernels, body(): call(pack_kernel, (shape((GROUPS, TILES, STEPS, HD), BF), shape((RES, TIL...  3.13 us
    pallas_call x1, Pallas kernels, body(): call(partial_kernel, shape((SIDE, PAYLOAD, HD), BF), [SM] + [VM] * (1 + S...  2.02 us
  transfers between devices with their start and end apart: 6, of which 3 were waited for; matrix products, arithmetic and copies ran while one was open for 0% of the time, Pallas kernels for 1%

profile of v6, /device:TPU:1, one launch (start us, length us, event | category | flops | bytes accessed | tf_op | source)
XLA Modules:
  0.0 88.0 jit_solution(788310396374492393)
XLA Ops:
  0.0 3.1 %shard_map.82 = (bf16[32,5,4,128]{3,2,1,0:T(4,128)(2,1)}, bf16[4,5,4,128]{3,2,1,0:T(4,128)(2,1)}, bf16[12,32,512]{2,1,0:T(8,128)(2,1)}, bf16[12,32,512]{2,1,0:T(...) custom-call(s32[2,128]{1,0:T(2,128)} %bitcast.19, s32[2,128]{1,0:T(2,128)} %bitcast.18, ...), custom_call_target="tpu_custom_call" | custom-call | bytes 3145728 | tf_op jit(solution)/shard_map/pallas_call | solution.py:238
  3.1 15.8 %all-to-all-start = ((bf16[16,2,5,4,128]{4,3,2,1,0:T(4,128)(2,1)}), bf16[16,2,5,4,128]{4,3,2,1,0:T(4,128)(2,1)S(1)}, u32[]{:S(2)}, u32[]{:S(2)}) async-start(bf16[16,2,5,4,128]{4,3,2,1,0:T(4,128)(2,1)} %bitcast.16), calls=%async_computation | async-start | bytes 327680 | tf_op jit(solution)/shard_map/all_to_all | solution.py:258
  18.9 5.4 %collective-permute-start = (bf16[12,32,512]{2,1,0:T(8,128)(2,1)}, bf16[12,32,512]{2,1,0:T(8,128)(2,1)S(1)}, u32[]{:S(2)}, u32[]{:S(2)}) collective-permute-start(bf16[12,32,512]{2,1,0:T(8,128)(2,1)} %get-tuple-element.26), channel_id=1, source_target_pairs={{0,7},{1,6},{2,5},{3,4},{4,3},{5,2},{6,1},{7,0},{8,15},{9,14},{10,... | collective-permute-start | bytes 1179656 | tf_op jit(solution)/shard_map/ppermute | solution.py:282
  24.3 0.0 copy-start.3
  24.3 0.0 copy-start.4
  24.3 2.1 %collective-permute-start.1 = (bf16[12,32,512]{2,1,0:T(8,128)(2,1)}, bf16[12,32,512]{2,1,0:T(8,128)(2,1)S(1)}, u32[]{:S(2)}, u32[]{:S(2)}) collective-permute-start(bf16[12,32,512]{2,1,0:T(8,128)(2,1)} %get-tuple-element.27), channel_id=1, source_target_pairs={{0,4},{1,5},{2,6},{3,7},{4,0},{5,1},{6,2},{7,3},{8,12},{9,13},{10,... | collective-permute-start | bytes 1179656 | tf_op jit(solution)/shard_map/ppermute | solution.py:282
  26.4 2.1 %collective-permute-start.2 = (bf16[12,32,512]{2,1,0:T(8,128)(2,1)}, bf16[12,32,512]{2,1,0:T(8,128)(2,1)S(1)}, u32[]{:S(2)}, u32[]{:S(2)}) collective-permute-start(bf16[12,32,512]{2,1,0:T(8,128)(2,1)} %get-tuple-element.28), channel_id=1, source_target_pairs={{0,3},{1,2},{2,1},{3,0},{4,7},{5,6},{6,5},{7,4},{8,11},{9,10},{10,... | collective-permute-start | bytes 1179656 | tf_op jit(solution)/shard_map/ppermute | solution.py:282
  28.6 0.0 copy-start.2
  28.6 0.0 copy-done.3
  28.6 0.0 copy-done.4
  28.6 0.7 copy-done.2
  29.2 0.2 fusion
  29.5 0.0 copy-start.1
  29.5 1.6 %all-to-all-done = bf16[16,2,5,4,128]{4,3,2,1,0:T(4,128)(2,1)S(1)} async-done(((bf16[16,2,5,4,128]{4,3,2,1,0:T(4,128)(2,1)}), bf16[16,2,5,4,128]{4,3,2,1,0:T(4,128)(2,1)S(1)}, u32[]{:S(2)}, u32[]{:S(2)}) %all-to-all-start) | async-done | bytes 163872 | tf_op jit(solution)/shard_map/all_to_all | solution.py:258
  31.1 6.0 %all-gather = bf16[32,2,5,4,128]{4,3,2,1,0:T(4,128)(2,1)S(1)} all-gather(bf16[16,2,5,4,128]{4,3,2,1,0:T(4,128)(2,1)S(1)} %all-to-all-done), channel_id=2, replica_groups={{0,16},{32,48},{64,80},{96,112},{128,144},{160,176},{192,208},{224,240}..., dimensions={0}, use_global_device_ids=true | all-gather | bytes 491520 | tf_op jit(solution)/shard_map/all_gather | solution.py:259
  37.2 0.0 copy-done.1
  37.2 1.3 %shard_map.83 = bf16[4,60,4,128]{3,2,1,0:T(4,128)(2,1)} custom-call(s32[8]{0:T(128)S(1)} %and_select_fusion.origin, bf16[2,16,2,5,4,128]{5,4,3,2,1,0:T(4,128)(2,1)S(1)} %bitcast.15, bf16[4,5,4,128]{3,2,1,0:T(4,128)(2,1)S(1)} %copy-done.1), custom_call_target="tpu_custom_call" | custom-call | tf_op jit(solution)/shard_map/pallas_call | solution.py:284
  38.5 0.0 copy-start
  38.5 5.1 %all-to-all-start.1 = ((bf16[4,60,4,128]{3,2,1,0:T(4,128)(2,1)}), bf16[4,60,4,128]{3,2,1,0:T(4,128)(2,1)S(1)}, u32[]{:S(2)}, u32[]{:S(2)}) async-start(bf16[4,60,4,128]{3,2,1,0:T(4,128)(2,1)} %shard_map.83), calls=%async_computation.1 | async-start | bytes 491520 | tf_op jit(solution)/shard_map/all_to_all | solution.py:235
  43.5 0.0 copy-start.5
  43.5 0.7 copy-done.5
  44.2 0.1 dynamic_slice.3
  44.3 0.1 pad_add_fusion.lengths
  44.3 0.0 collective-permute-done.rest_1_
  44.4 0.0 collective-permute-done.1.rest_2_
  44.4 0.0 collective-permute-done.2.rest_3_
  44.4 4.6 %all-to-all-done.1 = bf16[4,60,4,128]{3,2,1,0:T(4,128)(2,1)S(1)} async-done(((bf16[4,60,4,128]{3,2,1,0:T(4,128)(2,1)}), bf16[4,60,4,128]{3,2,1,0:T(4,128)(2,1)S(1)}, u32[]{:S(2)}, u32[]{:S(2)}) %all-to-all-start.1) | async-done | bytes 245792 | tf_op jit(solution)/shard_map/all_to_all | solution.py:235
  49.0 0.0 copy-done
  49.0 2.0 %shard_map.84 = bf16[4,208,128]{2,1,0:T(8,128)(2,1)} custom-call(s32[12]{0:T(128)S(1)} %pad_add_fusion.lengths, bf16[4,240,128]{2,1,0:T(8,128)(2,1)S(1)} %bitcast.13, bf16[12,32,512]{2,1,0:T(8,128)(2,1)S(1)} %copy-done, bf16[12,32,512]{2,1,0:T(8,128)(2,1)S(1)} %collective-permute-done.rest_1_, bf16[12,32,512]{2,1,0:T(8,128)(2,1)S(1)} %collective-permute-done.1.rest_2_, ...), custom_call_target="tpu_custom_call" | custom-call | flops 100000000 | bytes 3145728 | tf_op jit(solution)/shard_map/pallas_call | solution.py:289
  51.0 3.4 %all-to-all-start.2 = ((bf16[4,208,128]{2,1,0:T(8,128)(2,1)}), bf16[4,208,128]{2,1,0:T(8,128)(2,1)S(1)}, u32[]{:S(2)}, u32[]{:S(2)}) async-start(bf16[4,208,128]{2,1,0:T(8,128)(2,1)} %shard_map.84), calls=%async_computation.2 | async-start | bytes 425984 | tf_op jit(solution)/shard_map/all_to_all | solution.py:235
  54.4 5.3 %all-to-all-done.2.gathered = bf16[4,208,128]{2,1,0:T(8,128)(2,1)S(1)} async-done(((bf16[4,208,128]{2,1,0:T(8,128)(2,1)}), bf16[4,208,128]{2,1,0:T(8,128)(2,1)S(1)}, u32[]{:S(2)}, u32[]{:S(2)}) %all-to-all-start.2) | async-done | bytes 213024 | tf_op jit(solution)/shard_map/all_to_all | solution.py:235
  59.6 1.5 %shard_map.85 = (bf16[32,16,128]{2,1,0:T(8,128)(2,1)S(1)}, bf16[4,16,128]{2,1,0:T(8,128)(2,1)S(1)}) custom-call(s32[8]{0:T(128)S(1)} %and_select_fusion.origin, s32[8]{0:T(128)S(1)} %and_select_fusion.1.target, bf16[4,208,128]{2,1,0:T(8,128)(2,1)S(1)} %all-to-all-done.2.gathered, bf16[4,240,128]{2,1,0:T(8,128)(2,1)S(1)} %bitcast.14), custom_call_target="tpu_custom_call" | custom-call | tf_op jit(solution)/shard_map/pallas_call | solution.py:303
  61.1 25.7 %all_to_all.20.returned = bf16[32,16,128]{2,1,0:T(8,128)(2,1)S(1)} all-to-all(bf16[32,16,128]{2,1,0:T(8,128)(2,1)S(1)} %get-tuple-element.29), channel_id=1, replica_groups=mesh['group'=32,'tensor'=16] {'group'}, dimensions={0} | all-to-all | bytes 262144 | tf_op jit(solution)/shard_map/all_to_all | solution.py:308
  86.8 1.2 %shard_map.86 = bf16[12,16,128]{2,1,0:T(8,128)(2,1)} custom-call(s32[8]{0:T(128)S(1)} %and_select_fusion.1.target, bf16[32,16,128]{2,1,0:T(8,128)(2,1)S(1)} %all_to_all.20.returned, bf16[4,16,128]{2,1,0:T(8,128)(2,1)S(1)} %get-tuple-element.30.kept), custom_call_target="tpu_custom_call" | custom-call | tf_op jit(solution)/shard_map/pallas_call | solution.py:310
  (3 shorter events, 0.0 us)
Async XLA Ops:
  3.1 28.0 %all-to-all-start = ((bf16[16,2,5,4,128]{4,3,2,1,0:T(4,128)(2,1)}), bf16[16,2,5,4,128]{4,3,2,1,0:T(4,128)(2,1)S(1)}, u32[]{:S(2)}, u32[]{:S(2)}) async-start(bf16[16,2,5,4,128]{4,3,2,1,0:T(4,128)(2,1)} %bitcast.16), calls=%async_computation | async-start | bytes 327680 | tf_op jit(solution)/shard_map/all_to_all | solution.py:258
  18.9 25.4 %collective-permute-start = (bf16[12,32,512]{2,1,0:T(8,128)(2,1)}, bf16[12,32,512]{2,1,0:T(8,128)(2,1)S(1)}, u32[]{:S(2)}, u32[]{:S(2)}) collective-permute-start(bf16[12,32,512]{2,1,0:T(8,128)(2,1)} %get-tuple-element.26), channel_id=1, source_target_pairs={{0,7},{1,6},{2,5},{3,4},{4,3},{5,2},{6,1},{7,0},{8,15},{9,14},{10,... | collective-permute-start | bytes 1179656 | tf_op jit(solution)/shard_map/ppermute | solution.py:282
  24.3 4.3 %copy-start.3 = (s32[256]{0:T(256)S(1)}, s32[256]{0:T(256)}, u32[]{:S(2)}) copy-start(s32[256]{0:T(256)} %param.15) | copy-start | bytes 3076
  24.3 4.3 %copy-start.4 = (s32[256]{0:T(256)S(1)}, s32[256]{0:T(256)}, u32[]{:S(2)}) copy-start(s32[256]{0:T(256)} %param.13) | copy-start | bytes 3076
  24.3 20.0 %collective-permute-start.1 = (bf16[12,32,512]{2,1,0:T(8,128)(2,1)}, bf16[12,32,512]{2,1,0:T(8,128)(2,1)S(1)}, u32[]{:S(2)}, u32[]{:S(2)}) collective-permute-start(bf16[12,32,512]{2,1,0:T(8,128)(2,1)} %get-tuple-element.27), channel_id=1, source_target_pairs={{0,4},{1,5},{2,6},{3,7},{4,0},{5,1},{6,2},{7,3},{8,12},{9,13},{10,... | collective-permute-start | bytes 1179656 | tf_op jit(solution)/shard_map/ppermute | solution.py:282
  26.4 17.9 %collective-permute-start.2 = (bf16[12,32,512]{2,1,0:T(8,128)(2,1)}, bf16[12,32,512]{2,1,0:T(8,128)(2,1)S(1)}, u32[]{:S(2)}, u32[]{:S(2)}) collective-permute-start(bf16[12,32,512]{2,1,0:T(8,128)(2,1)} %get-tuple-element.28), channel_id=1, source_target_pairs={{0,3},{1,2},{2,1},{3,0},{4,7},{5,6},{6,5},{7,4},{8,11},{9,10},{10,... | collective-permute-start | bytes 1179656 | tf_op jit(solution)/shard_map/ppermute | solution.py:282
  28.6 0.7 copy-start.2
  29.5 7.7 %copy-start.1 = (bf16[4,5,4,128]{3,2,1,0:T(4,128)(2,1)S(1)}, bf16[4,5,4,128]{3,2,1,0:T(4,128)(2,1)}, u32[]{:S(2)}) copy-start(bf16[4,5,4,128]{3,2,1,0:T(4,128)(2,1)} %get-tuple-element.24.kept) | copy-start | bytes 61444
  38.5 10.5 %copy-start = (bf16[12,32,512]{2,1,0:T(8,128)(2,1)S(1)}, bf16[12,32,512]{2,1,0:T(8,128)(2,1)}, u32[]{:S(2)}) copy-start(bf16[12,32,512]{2,1,0:T(8,128)(2,1)} %get-tuple-element.25.rest_0_) | copy-start | bytes 1179652
  38.5 10.5 %all-to-all-start.1 = ((bf16[4,60,4,128]{3,2,1,0:T(4,128)(2,1)}), bf16[4,60,4,128]{3,2,1,0:T(4,128)(2,1)S(1)}, u32[]{:S(2)}, u32[]{:S(2)}) async-start(bf16[4,60,4,128]{3,2,1,0:T(4,128)(2,1)} %shard_map.83), calls=%async_computation.1 | async-start | bytes 491520 | tf_op jit(solution)/shard_map/all_to_all | solution.py:235
  43.5 0.7 copy-start.5
  51.0 8.7 %all-to-all-start.2 = ((bf16[4,208,128]{2,1,0:T(8,128)(2,1)}), bf16[4,208,128]{2,1,0:T(8,128)(2,1)S(1)}, u32[]{:S(2)}, u32[]{:S(2)}) async-start(bf16[4,208,128]{2,1,0:T(8,128)(2,1)} %shard_map.84), calls=%async_computation.2 | async-start | bytes 425984 | tf_op jit(solution)/shard_map/all_to_all | solution.py:235

commit v7 on v5

--- a/solution.py
+++ b/solution.py
@@ -41,12 +41,16 @@
 HB = pl.BlockSpec(memory_space=pltpu.HBM)
 
 
-def call(kernel, outs, specs, flops=0, moved=0, scratch=(), limit=LIMIT):
+ANY = pl.BlockSpec(memory_space=pl.ANY)
+TARGET, ORIGIN, LENGTH = 0, MIG, 2 * MIG
+
+
+def call(kernel, outs, specs, flops=0, moved=0, scratch=(), limit=LIMIT, places=None):
     return pl.pallas_call(
         kernel,
         out_shape=outs,
         in_specs=specs,
-        out_specs=jax.tree.map(lambda _: VM, outs),
+        out_specs=jax.tree.map(lambda _: VM, outs) if places is None else places,
         scratch_shapes=scratch,
         compiler_params=pltpu.CompilerParams(vmem_limit_bytes=limit),
         cost_estimate=pl.CostEstimate(flops=flops, bytes_accessed=moved, transcendentals=0),
@@ -62,54 +66,67 @@
     return shard // SIDE, shard % SIDE
 
 
-def pack_kernel(named, holders, asked, fresh, sent, kept, asked_here, fresh_here, named_here, holders_here, sems):
-    shard = lax.axis_index("tensor")
+def pack_kernel(*refs):
+    n = BLOCKS
+    given, refs = refs[:8], refs[8:]
+    plan, outs, refs = refs[0], refs[1 : 3 + n], refs[3 + n :]
+    inside, (sent, kept, *blocks), (come, go) = refs[:8], refs[8 : 10 + n], refs[10 + n :]
+    shard, group = lax.axis_index("tensor"), lax.axis_index("group")
     first = pl.multiple_of(shard % 2 * FEATURES + shard // 2 * HD, HD)
-    copies = [
-        pltpu.make_async_copy(source, target, sems.at[n])
-        for n, (source, target) in enumerate(
-            (
-                (named, named_here),
-                (holders, holders_here),
-                (asked, asked_here),
-                (fresh.at[:, :, pl.ds(first, HD)], fresh_here),
-            )
-        )
-    ]
+    given = list(given)
+    given[5] = given[5].at[:, :, pl.ds(first, HD)]
+    copies = [pltpu.make_async_copy(p, q, come.at[k]) for k, (p, q) in enumerate(zip(given, inside))]
     for copy in copies:
         copy.start()
     sent[...] = jnp.zeros_like(sent)
-    for copy in copies:
+    for copy in copies[:6]:
         copy.wait()
-    names = named_here[...]
-    slots = holders_here[...].astype(F32)
+    names, holders, tokens, residents = (ref[...].astype(F32) for ref in inside[:4])
+    asked, fresh, moved, resident = inside[4:]
+
+    def found(where, name, values):
+        return jnp.sum(jnp.where(where == name, values, 0.0)).astype(jnp.int32)
+
     for slot in range(RES):
-        kept[slot, :HEADS] = asked_here[slot]
-        kept[slot, HEADS] = fresh_here[slot]
-    groups = []
-    for slot in range(RES, SLOTS):
-        mine = names == lax.axis_index("group") * SLOTS + slot
-        groups.append(jnp.sum(jnp.where(mine, slots, 0.0)).astype(jnp.int32) // MIG)
-    for slot, group in zip(range(RES, SLOTS), groups):
-        sent[group, :HEADS] = asked_here[slot]
-        sent[group, HEADS] = fresh_here[slot]
-
-
-def split_kernel(moved, resident, *outs):
-    _, here = place_of()
-    for step, out in enumerate(outs):
-        half = swapped(step, here) // 2
-        for place in range(PAIRS):
+        kept[slot, :HEADS] = asked[slot]
+        kept[slot, HEADS] = fresh[slot]
+    for slot in range(MIG):
+        name = (group * SLOTS + RES + slot).astype(F32)
+        to = lax.div(found(names, name, holders), MIG)
+        plan[TARGET + slot] = to
+        sent[to, :HEADS] = asked[RES + slot]
+        sent[to, HEADS] = fresh[RES + slot]
+    writes = [pltpu.make_async_copy(p, q, go.at[k]) for k, (p, q) in enumerate(zip((sent, kept, *blocks), outs))]
+    writes[0].start()
+    writes[1].start()
+    for slot in range(MIG):
+        name = (group * MIG + slot).astype(F32)
+        plan[ORIGIN + slot] = lax.div(found(holders, name, names), SLOTS)
+        plan[LENGTH + slot] = found(holders, name, tokens)
+    lane = lax.broadcasted_iota(jnp.int32, (1, HD), 1)
+    for slot in range(RES):
+        plan[LENGTH + MIG + slot] = found(lane, group * RES + slot, residents)
+    for copy in copies[6:]:
+        copy.wait()
+    y, x = place_of()
+    for step in (*range(1, n), 0):
+        block = blocks[step]
+        half = swapped(step, x) // 2
+        heads = [2 * place + half for place in range(PAIRS)]
+        for place, pair in enumerate(heads):
             for part in range(2):
-                lanes = pl.ds(pl.multiple_of((2 * place + half) * HD + part * FEATURES, HD), HD)
+                lanes = pl.ds(pl.multiple_of(pair * HD + part * FEATURES, HD), HD)
                 columns = slice((part * PAIRS + place) * HD, (part * PAIRS + place + 1) * HD)
-                out[:MIG, :, columns] = moved[:, :, lanes]
-                out[MIG:, :, columns] = resident[:, :, lanes]
-
-
-def spread_kernel(origin, arrived, kept, asking):
+                block[:MIG, :, columns] = moved[:, :, lanes]
+                block[MIG:, :, columns] = resident[:, :, lanes]
+        writes[2 + step].start()
+    for write in writes:
+        write.wait()
+
+
+def spread_kernel(plan, arrived, kept, asking):
     for row in range(SLOTS):
-        chunk = arrived.at[origin[row]] if row < MIG else kept.at[row - MIG]
+        chunk = arrived.at[plan[ORIGIN + row]] if row < MIG else kept.at[row - MIG]
         for peer in range(PEERS):
             asking[peer, row * HEADS : (row + 1) * HEADS] = chunk[:HEADS]
             asking[peer, SLOTS * HEADS + row] = chunk[HEADS]
@@ -119,7 +136,7 @@
     return lax.dot_general(left, right, (((1,), (1,)), ((), ())), preferred_element_type=F32) * SCALE
 
 
-def partial_kernel(lengths, asking, *rest):
+def partial_kernel(plan, asking, *rest):
     *blocks, payload, scores, weights, stats = rest
     y, x = place_of()
     column = lax.broadcasted_iota(jnp.int32, (1, WIDE), 1)
@@ -130,7 +147,7 @@
         return jnp.concatenate([block[row, :, lanes] for block in blocks], 0)
 
     for row in range(SLOTS):
-        usable = position < lengths[row]
+        usable = position < plan[LENGTH + row]
         span = slice(row * QROWS, (row + 1) * QROWS)
         for pair in range(PAIRS):
             asked = jnp.concatenate([asking[2 * pair, span, :], asking[2 * pair + 1, span, :]], 0)
@@ -166,7 +183,7 @@
             payload[2 * pair + 1, span, :] = blended[QROWS:]
 
 
-def merge_kernel(origin, gathered, everyone, sent, kept):
+def merge_kernel(plan, gathered, everyone, sent, kept):
     y, x = place_of()
     first = 2 * y
     asked = everyone[first + x % 2, :ROWS, :]
@@ -200,16 +217,16 @@
 
     sent[...] = jnp.zeros_like(sent)
     for slot in range(MIG):
-        sent[origin[slot]] = result[slot * QROWS : (slot + 1) * QROWS]
+        sent[plan[ORIGIN + slot]] = result[slot * QROWS : (slot + 1) * QROWS]
     for slot in range(RES):
         kept[slot] = result[(MIG + slot) * QROWS : (MIG + slot + 1) * QROWS]
 
 
-def select_kernel(target, returned, kept, out):
+def select_kernel(plan, returned, kept, out):
     for slot in range(RES):
         out[slot] = kept[slot]
     for slot in range(MIG):
-        out[RES + slot] = returned[target[slot]]
+        out[RES + slot] = returned[plan[TARGET + slot]]
 
 
 def body(
@@ -229,42 +246,41 @@
         return lax.all_to_all(array, "tensor", 0, 0, axis_index_groups=peers, tiled=True)
 
     asked = queries.reshape(SLOTS, STEPS, HEADS, HD).transpose(0, 2, 1, 3)
-    sent, kept = call(
+    tile = (SLOTS, STRIDE, 2 * PAIRS * HD)
+    held = [
+        ((GROUPS, TILES, STEPS, HD), BF),
+        ((RES, TILES, STEPS, HD), BF),
+        *([(tile, BF)] * BLOCKS),
+    ]
+    taken = [
+        *([((2, HD), jnp.int32)] * 3),
+        ((1, HD), jnp.int32),
+        ((SLOTS, HEADS, STEPS, HD), BF),
+        ((SLOTS, STEPS, HD), BF),
+        (prefill_cache.shape, BF),
+        (resident_cache.shape, BF),
+    ]
+    plan, sent, kept, *split = call(
         pack_kernel,
-        (shape((GROUPS, TILES, STEPS, HD), BF), shape((RES, TILES, STEPS, HD), BF)),
-        [HB] * 4,
-        scratch=[
-            pltpu.VMEM((SLOTS, HEADS, STEPS, HD), BF),
-            pltpu.VMEM((SLOTS, STEPS, HD), BF),
-            pltpu.VMEM((2, HD), jnp.int32),
-            pltpu.VMEM((2, HD), jnp.int32),
-            pltpu.SemaphoreType.DMA((4,)),
-        ],
+        (shape((2 * MIG + SLOTS,), jnp.int32), *(shape(*one) for one in held)),
+        [HB] * 8,
+        moved=3 * 2**20,
+        scratch=[pltpu.VMEM(*one) for one in taken + held]
+        + [pltpu.SemaphoreType.DMA((8,)), pltpu.SemaphoreType.DMA((len(held),))],
         limit=FULL,
-    )(decode_slot.reshape(2, HD), prefill_slot.reshape(2, HD), asked, new_entries)
+        places=(SM, *([ANY] * len(held))),
+    )(
+        decode_slot.reshape(2, HD),
+        prefill_slot.reshape(2, HD),
+        kept_tokens.reshape(2, HD),
+        resident_kept.reshape(1, HD),
+        asked,
+        new_entries,
+        prefill_cache,
+        resident_cache,
+    )
     arrived = lax.all_to_all(sent, "group", 0, 0, tiled=True)
 
-    later = (resident_kept, kept_tokens, prefill_slot, decode_slot, prefill_cache, resident_cache)
-    later, kept = lax.optimization_barrier((later, kept))
-    resident_kept, kept_tokens, prefill_slot, decode_slot, prefill_cache, resident_cache = later
-    group = lax.axis_index("group")
-
-    def looked_up(names, first, values):
-        wanted = first + jnp.arange(MIG, dtype=jnp.int32)
-        return jnp.sum(jnp.where(names[None, :] == wanted[:, None], values[None, :], 0), axis=1)
-
-    target = looked_up(decode_slot, group * SLOTS + RES, prefill_slot) // MIG
-    origin = looked_up(prefill_slot, group * MIG, decode_slot) // SLOTS
-    moved_len = looked_up(prefill_slot, group * MIG, kept_tokens)
-    resident_len = lax.dynamic_slice_in_dim(resident_kept, group * RES, RES)
-    lengths = jnp.concatenate([moved_len, resident_len])
-
-    split = call(
-        split_kernel,
-        (shape((SLOTS, STRIDE, 2 * PAIRS * HD), BF),) * BLOCKS,
-        [VM, VM],
-        moved=3 * 2**20,
-    )(prefill_cache, resident_cache)
     blocks = [split[0]]
     for step in range(1, BLOCKS):
         steps = [(t, t // SIDE * SIDE + swapped(step, t % SIDE)) for t in range(SHARDS)]
@@ -272,7 +288,7 @@
 
     asking = call(
         spread_kernel, shape((PEERS, SLOTS * TILES, STEPS, HD), BF), [SM, VM, VM]
-    )(origin, arrived, kept)
+    )(plan, arrived, kept)
     everyone = across(asking).reshape(PEERS, ROWS + ENTRIES, HD)
 
     payload = call(
@@ -286,17 +302,17 @@
             pltpu.VMEM((PEERS, ROWS, WIDE), BF),
             pltpu.VMEM((2 * HD, HD), F32),
         ],
-    )(lengths, everyone, *blocks)
+    )(plan, everyone, *blocks)
     gathered = across(payload)
 
     finished, here = call(
         merge_kernel,
         (shape((GROUPS, QROWS, HD), BF), shape((RES, QROWS, HD), BF)),
         [SM, VM, VM],
-    )(origin, gathered, everyone)
+    )(plan, gathered, everyone)
     returned = lax.all_to_all(finished, "group", 0, 0, tiled=True)
 
-    result = call(select_kernel, shape((SLOTS, QROWS, HD), BF), [SM, VM, VM])(target, returned, here)
+    result = call(select_kernel, shape((SLOTS, QROWS, HD), BF), [SM, VM, VM])(plan, returned, here)
     result = result.reshape(SLOTS, HEADS, STEPS, HD).transpose(0, 2, 1, 3)
     return result.reshape(SLOTS, STEPS, HEADS * HD)
 

time: 91 us -> 90.6 us (level)
  blocking collectives: 10 us -> 33.6 us
  waiting for transfers between devices: 32.3 us -> 20.2 us
  starting transfers between devices: 35.8 us -> 26.3 us
  local copies, waits for them, and re-layouts: 1.96 us -> 0.67 us
    all_to_all x0 -> x1, blocking collectives: none -> 23.6 us  [body(): returned = lax.all_to_all(finished, 'group', 0, 0, tiled=True)]
    all_to_all x1 -> x0, waiting for transfers between devices: 15.8 us -> none  [body(): returned = lax.all_to_all(finished, 'group', 0, 0, tiled=True)]
    all_to_all x1 -> x0, starting transfers between devices: 9.38 us -> none  [body(): returned = lax.all_to_all(finished, 'group', 0, 0, tiled=True)]
    all_to_all x1, waiting for transfers between devices: 9.79 us -> 12.7 us  [body(): arrived = lax.all_to_all(sent, 'group', 0, 0, tiled=True)]
    unnamed x14 -> x6, local copies, waits for them, and re-layouts: 1.89 us -> 0.67 us
    all_to_all x1, waiting for transfers between devices: 6.3 us -> 7.46 us  [across(): lax.all_to_all(array, 'tensor', 0, 0, axis_index_groups=peers, tiled=True)]
    pallas_call x2 -> x1, Pallas kernels: 3.08 us -> 3.44 us  [body(): call(pack_kernel, (shape((2 * MIG + SLOTS,), jnp.int32), *(shape(*one) fo...]
  transfers between devices with their start and end apart: 4 -> 3, of which waited for: 4 -> 2; matrix products, arithmetic and copies ran while one was open for 0% -> 0% of each run, Pallas kernels for 3% -> 2%
where the time goes in v7:
time: 90.6 us; the launch traced here: 89.9 us
  blocking collectives  33.6 us (37%)
  starting transfers between devices  26.3 us (29%)
  waiting for transfers between devices  20.2 us (22%)
  Pallas kernels  9.09 us (10%)
    all_to_all x1, blocking collectives, body(): returned = lax.all_to_all(finished, 'group', 0, 0, tiled=True)  23.6 us
    all_to_all x1, starting transfers between devices, body(): arrived = lax.all_to_all(sent, 'group', 0, 0, tiled=True)  16.8 us
    all_to_all x1, waiting for transfers between devices, body(): arrived = lax.all_to_all(sent, 'group', 0, 0, tiled=True)  12.7 us
    all_to_all x1, blocking collectives, across(): lax.all_to_all(array, 'tensor', 0, 0, axis_index_groups=peers, tiled=True)  10 us
    all_to_all x1, waiting for transfers between devices, across(): lax.all_to_all(array, 'tensor', 0, 0, axis_index_groups=peers, tiled=True)  7.46 us
    all_to_all x1, starting transfers between devices, across(): lax.all_to_all(array, 'tensor', 0, 0, axis_index_groups=peers, tiled=True)  5.12 us
    ppermute x1, starting transfers between devices, body(): blocks.append(lax.ppermute(split[step], 'tensor', steps))  4.39 us
    pallas_call x1, Pallas kernels, body(): call(pack_kernel, (shape((2 * MIG + SLOTS,), jnp.int32), *(shape(*one) fo...  3.44 us
  transfers between devices with their start and end apart: 3, of which 2 were waited for; matrix products, arithmetic and copies ran while one was open for 0% of the time, Pallas kernels for 2%

profile of v7, /device:TPU:1, one launch (start us, length us, event | category | flops | bytes accessed | tf_op | source)
XLA Modules:
  0.0 89.9 jit_solution(13271337809860552852)
XLA Ops:
  0.0 3.4 %shard_map.82 = (s32[28]{0:T(128)}, bf16[32,5,4,128]{3,2,1,0:T(4,128)(2,1)}, bf16[4,5,4,128]{3,2,1,0:T(4,128)(2,1)}, bf16[12,32,1024]{2,1,0:T(8,128)(2,1)}, bf16[12,32,1024]{2,1,0:T(8,128)(2,1)}) custom-call(s32[2,128]{1,0:T(2,128)} %bitcast.16, s32[2,128]{1,0:T(2,128)} %bitcast.17, s32[2,128]{1,0:T(2,128)} %bitcast.18, s32[1,128]{1,0:T(1,128)} %bitcast.19, ...), custom_call_target="tpu_custom_call" | custom-call | bytes 3145728 | tf_op jit(solution)/shard_map/pallas_call | solution.py:263
  3.4 0.0 copy-start.1
  3.5 16.8 %all-to-all-start = ((bf16[32,5,4,128]{3,2,1,0:T(4,128)(2,1)}), bf16[32,5,4,128]{3,2,1,0:T(4,128)(2,1)S(1)}, u32[]{:S(2)}, u32[]{:S(2)}) async-start(bf16[32,5,4,128]{3,2,1,0:T(4,128)(2,1)} %get-tuple-element.13), calls=%async_computation | async-start | bytes 327680 | tf_op jit(solution)/shard_map/all_to_all | solution.py:282
  20.2 4.4 %collective-permute-start = (bf16[12,32,1024]{2,1,0:T(8,128)(2,1)}, bf16[12,32,1024]{2,1,0:T(8,128)(2,1)S(1)}, u32[]{:S(2)}, u32[]{:S(2)}) collective-permute-start(bf16[12,32,1024]{2,1,0:T(8,128)(2,1)} %get-tuple-element.16), channel_id=1, source_target_pairs={{0,3},{1,2},{2,1},{3,0},{4,7},{5,6},{6,5},{7,4},{8,11},{9,10},{10,... | collective-permute-start | bytes 2359304 | tf_op jit(solution)/shard_map/ppermute | solution.py:287
  24.6 12.7 %all-to-all-done.arrived = bf16[32,5,4,128]{3,2,1,0:T(4,128)(2,1)S(1)} async-done(((bf16[32,5,4,128]{3,2,1,0:T(4,128)(2,1)}), bf16[32,5,4,128]{3,2,1,0:T(4,128)(2,1)S(1)}, u32[]{:S(2)}, u32[]{:S(2)}) %all-to-all-start) | async-done | bytes 163872 | tf_op jit(solution)/shard_map/all_to_all | solution.py:282
  37.4 0.0 copy-start.2
  37.4 0.0 copy-done.1
  37.4 0.7 copy-done.2
  38.0 0.0 copy-start
  38.0 1.4 %shard_map.83 = bf16[8,60,4,128]{3,2,1,0:T(4,128)(2,1)} custom-call(s32[28]{0:T(128)S(1)} %copy-done.2, bf16[32,5,4,128]{3,2,1,0:T(4,128)(2,1)S(1)} %all-to-all-done.arrived, bf16[4,5,4,128]{3,2,1,0:T(4,128)(2,1)S(1)} %copy-done.1), custom_call_target="tpu_custom_call" | custom-call | tf_op jit(solution)/shard_map/pallas_call | solution.py:289
  39.5 5.1 %all-to-all-start.1 = ((bf16[8,60,4,128]{3,2,1,0:T(4,128)(2,1)}), bf16[8,60,4,128]{3,2,1,0:T(4,128)(2,1)S(1)}, u32[]{:S(2)}, u32[]{:S(2)}) async-start(bf16[8,60,4,128]{3,2,1,0:T(4,128)(2,1)} %shard_map.83), calls=%async_computation.1 | async-start | bytes 983040 | tf_op jit(solution)/shard_map/all_to_all | solution.py:246
  44.6 0.0 collective-permute-done.rest_1_
  44.6 7.5 %all-to-all-done.1 = bf16[8,60,4,128]{3,2,1,0:T(4,128)(2,1)S(1)} async-done(((bf16[8,60,4,128]{3,2,1,0:T(4,128)(2,1)}), bf16[8,60,4,128]{3,2,1,0:T(4,128)(2,1)S(1)}, u32[]{:S(2)}, u32[]{:S(2)}) %all-to-all-start.1) | async-done | bytes 491552 | tf_op jit(solution)/shard_map/all_to_all | solution.py:246
  52.1 0.0 copy-done
  52.1 1.5 %shard_map.84 = bf16[8,208,128]{2,1,0:T(8,128)(2,1)S(1)} custom-call(s32[28]{0:T(128)S(1)} %copy-done.2, bf16[8,240,128]{2,1,0:T(8,128)(2,1)S(1)} %bitcast.13, bf16[12,32,1024]{2,1,0:T(8,128)(2,1)S(1)} %copy-done, bf16[12,32,1024]{2,1,0:T(8,128)(2,1)S(1)} %collective-permute-done.rest_1_), custom_call_target="tpu_custom_call" | custom-call | flops 100000000 | bytes 3145728 | tf_op jit(solution)/shard_map/pallas_call | solution.py:294
  53.6 10.0 %all_to_all.20.gathered = bf16[8,208,128]{2,1,0:T(8,128)(2,1)S(1)} all-to-all(bf16[8,208,128]{2,1,0:T(8,128)(2,1)S(1)} %shard_map.84), channel_id=1, replica_groups={{0,1,4,5,8,9,12,13},{2,3,6,7,10,11,14,15},{16,17,20,21,24,25,28,29},{18..., dimensions={0} | all-to-all | bytes 851968 | tf_op jit(solution)/shard_map/all_to_all | solution.py:246
  63.6 1.5 %shard_map.85 = (bf16[32,16,128]{2,1,0:T(8,128)(2,1)S(1)}, bf16[4,16,128]{2,1,0:T(8,128)(2,1)S(1)}) custom-call(s32[28]{0:T(128)S(1)} %copy-done.2, bf16[8,208,128]{2,1,0:T(8,128)(2,1)S(1)} %all_to_all.20.gathered, bf16[8,240,128]{2,1,0:T(8,128)(2,1)S(1)} %bitcast.14), custom_call_target="tpu_custom_call" | custom-call | tf_op jit(solution)/shard_map/pallas_call | solution.py:308
  65.2 23.6 %all_to_all.21.returned = bf16[32,16,128]{2,1,0:T(8,128)(2,1)S(1)} all-to-all(bf16[32,16,128]{2,1,0:T(8,128)(2,1)S(1)} %get-tuple-element.17), channel_id=1, replica_groups=mesh['group'=32,'tensor'=16] {'group'}, dimensions={0} | all-to-all | bytes 262144 | tf_op jit(solution)/shard_map/all_to_all | solution.py:313
  88.8 1.2 %shard_map.86 = bf16[12,16,128]{2,1,0:T(8,128)(2,1)} custom-call(s32[28]{0:T(128)S(1)} %copy-done.2, bf16[32,16,128]{2,1,0:T(8,128)(2,1)S(1)} %all_to_all.21.returned, bf16[4,16,128]{2,1,0:T(8,128)(2,1)S(1)} %get-tuple-element.18.kept), custom_call_target="tpu_custom_call" | custom-call | tf_op jit(solution)/shard_map/pallas_call | solution.py:315
Async XLA Ops:
  3.4 33.9 %copy-start.1 = (bf16[4,5,4,128]{3,2,1,0:T(4,128)(2,1)S(1)}, bf16[4,5,4,128]{3,2,1,0:T(4,128)(2,1)}, u32[]{:S(2)}) copy-start(bf16[4,5,4,128]{3,2,1,0:T(4,128)(2,1)} %get-tuple-element.14.kept) | copy-start | bytes 61444
  3.5 33.9 %all-to-all-start = ((bf16[32,5,4,128]{3,2,1,0:T(4,128)(2,1)}), bf16[32,5,4,128]{3,2,1,0:T(4,128)(2,1)S(1)}, u32[]{:S(2)}, u32[]{:S(2)}) async-start(bf16[32,5,4,128]{3,2,1,0:T(4,128)(2,1)} %get-tuple-element.13), calls=%async_computation | async-start | bytes 327680 | tf_op jit(solution)/shard_map/all_to_all | solution.py:282
  20.2 24.4 %collective-permute-start = (bf16[12,32,1024]{2,1,0:T(8,128)(2,1)}, bf16[12,32,1024]{2,1,0:T(8,128)(2,1)S(1)}, u32[]{:S(2)}, u32[]{:S(2)}) collective-permute-start(bf16[12,32,1024]{2,1,0:T(8,128)(2,1)} %get-tuple-element.16), channel_id=1, source_target_pairs={{0,3},{1,2},{2,1},{3,0},{4,7},{5,6},{6,5},{7,4},{8,11},{9,10},{10,... | collective-permute-start | bytes 2359304 | tf_op jit(solution)/shard_map/ppermute | solution.py:287
  37.4 0.7 copy-start.2
  38.0 14.0 %copy-start = (bf16[12,32,1024]{2,1,0:T(8,128)(2,1)S(1)}, bf16[12,32,1024]{2,1,0:T(8,128)(2,1)}, u32[]{:S(2)}) copy-start(bf16[12,32,1024]{2,1,0:T(8,128)(2,1)} %get-tuple-element.15.rest_0_) | copy-start | bytes 2359300
  39.5 12.6 %all-to-all-start.1 = ((bf16[8,60,4,128]{3,2,1,0:T(4,128)(2,1)}), bf16[8,60,4,128]{3,2,1,0:T(4,128)(2,1)S(1)}, u32[]{:S(2)}, u32[]{:S(2)}) async-start(bf16[8,60,4,128]{3,2,1,0:T(4,128)(2,1)} %shard_map.83), calls=%async_computation.1 | async-start | bytes 983040 | tf_op jit(solution)/shard_map/all_to_all | solution.py:246

commit v8 on v7

--- a/solution.py
+++ b/solution.py
@@ -19,10 +19,7 @@
 SIDE = 4
 STRIDE = 32
 HEADS = H // SHARDS
-BLOCKS = 2
-PEERS = SHARDS // BLOCKS
-PAIRS = PEERS // 2
-WIDE = BLOCKS * STRIDE
+PAIRS = KVH // SIDE
 QROWS = HEADS * STEPS
 ROWS = SLOTS * QROWS
 FEATURES = KVH * HD
@@ -32,7 +29,7 @@
 FLOOR = -(2.0**100)
 SCALE = 1.0 / math.sqrt(HD)
 LIMIT = 48 * 1024 * 1024
-FULL = 63 * 1024 * 1024
+FULL = 62 * 1024 * 1024
 BF = jnp.bfloat16
 F32 = jnp.float32
 
@@ -57,8 +54,12 @@
     )
 
 
-def swapped(step, x):
-    return x ^ (step * 3)
+def swapped(step, y, x):
+    return y ^ (step % 2), x ^ (step // 2 * 3)
+
+
+def class_of(y, x):
+    return jnp.minimum(y, 3 - y), x // 2
 
 
 def place_of():
@@ -67,10 +68,8 @@
 
 
 def pack_kernel(*refs):
-    n = BLOCKS
-    given, refs = refs[:8], refs[8:]
-    plan, outs, refs = refs[0], refs[1 : 3 + n], refs[3 + n :]
-    inside, (sent, kept, *blocks), (come, go) = refs[:8], refs[8 : 10 + n], refs[10 + n :]
+    given, plan, outs, refs = refs[:6], refs[6], refs[7:9], refs[9:]
+    inside, (sent, kept), (come, go) = refs[:6], refs[6:8], refs[8:]
     shard, group = lax.axis_index("tensor"), lax.axis_index("group")
     first = pl.multiple_of(shard % 2 * FEATURES + shard // 2 * HD, HD)
     given = list(given)
@@ -79,10 +78,10 @@
     for copy in copies:
         copy.start()
     sent[...] = jnp.zeros_like(sent)
-    for copy in copies[:6]:
+    for copy in copies:
         copy.wait()
     names, holders, tokens, residents = (ref[...].astype(F32) for ref in inside[:4])
-    asked, fresh, moved, resident = inside[4:]
+    asked, fresh = inside[4:]
 
     def found(where, name, values):
         return jnp.sum(jnp.where(where == name, values, 0.0)).astype(jnp.int32)
@@ -96,7 +95,7 @@
         plan[TARGET + slot] = to
         sent[to, :HEADS] = asked[RES + slot]
         sent[to, HEADS] = fresh[RES + slot]
-    writes = [pltpu.make_async_copy(p, q, go.at[k]) for k, (p, q) in enumerate(zip((sent, kept, *blocks), outs))]
+    writes = [pltpu.make_async_copy(p, q, go.at[k]) for k, (p, q) in enumerate(zip((sent, kept), outs))]
     writes[0].start()
     writes[1].start()
     for slot in range(MIG):
@@ -106,28 +105,26 @@
     lane = lax.broadcasted_iota(jnp.int32, (1, HD), 1)
     for slot in range(RES):
         plan[LENGTH + MIG + slot] = found(lane, group * RES + slot, residents)
-    for copy in copies[6:]:
-        copy.wait()
+    for write in writes:
+        write.wait()
+
+
+def split_kernel(moved, resident, *outs):
     y, x = place_of()
-    for step in (*range(1, n), 0):
-        block = blocks[step]
-        half = swapped(step, x) // 2
-        heads = [2 * place + half for place in range(PAIRS)]
-        for place, pair in enumerate(heads):
+    for step, out in enumerate(outs):
+        low, half = class_of(*swapped(step, y, x))
+        for place, pair in enumerate((2 * low + half, 6 - 2 * low + half)):
             for part in range(2):
                 lanes = pl.ds(pl.multiple_of(pair * HD + part * FEATURES, HD), HD)
                 columns = slice((part * PAIRS + place) * HD, (part * PAIRS + place + 1) * HD)
-                block[:MIG, :, columns] = moved[:, :, lanes]
-                block[MIG:, :, columns] = resident[:, :, lanes]
-        writes[2 + step].start()
-    for write in writes:
-        write.wait()
+                out[:MIG, :, columns] = moved[:, :, lanes]
+                out[MIG:, :, columns] = resident[:, :, lanes]
 
 
 def spread_kernel(plan, arrived, kept, asking):
     for row in range(SLOTS):
         chunk = arrived.at[plan[ORIGIN + row]] if row < MIG else kept.at[row - MIG]
-        for peer in range(PEERS):
+        for peer in range(SIDE):
             asking[peer, row * HEADS : (row + 1) * HEADS] = chunk[:HEADS]
             asking[peer, SLOTS * HEADS + row] = chunk[HEADS]
 
@@ -138,9 +135,10 @@
 
 def partial_kernel(plan, asking, *rest):
     *blocks, payload, scores, weights, stats = rest
-    y, x = place_of()
-    column = lax.broadcasted_iota(jnp.int32, (1, WIDE), 1)
-    position = (y * SIDE + swapped(column // STRIDE, x)) * STRIDE + column % STRIDE
+    column = lax.broadcasted_iota(jnp.int32, (1, HD), 1)
+    block = column // STRIDE
+    y, x = swapped(jnp.where(block == 0, 0, (block + 1) % 3 + 1), *place_of())
+    position = (y * SIDE + x) * STRIDE + column % STRIDE
 
     def stored(row, place):
         lanes = slice(place * HD, (place + 1) * HD)
@@ -156,7 +154,7 @@
             scores[2 * pair + 1, span, :] = found[QROWS:]
     lane = lax.broadcasted_iota(jnp.int32, (ROWS, HD), 1)
     table = jnp.zeros((ROWS, HD), F32)
-    for peer in range(PEERS):
+    for peer in range(SIDE):
         found = scores[peer]
         top = jnp.max(found, axis=1, keepdims=True)
         first = top.astype(BF).astype(F32)
@@ -171,7 +169,7 @@
     stats[ROWS:, :] = jnp.zeros((2 * HD - ROWS, HD), F32)
     low = stats[:HD, :].T
     high = stats[HD:, :].T
-    for peer in range(PEERS):
+    for peer in range(SIDE):
         rows = slice(peer * 8, (peer + 1) * 8)
         payload[peer, ROWS:, :] = jnp.concatenate([low[rows], high[rows]], 0).astype(BF)
     for row in range(SLOTS):
@@ -185,7 +183,7 @@
 
 def merge_kernel(plan, gathered, everyone, sent, kept):
     y, x = place_of()
-    first = 2 * y
+    first = jnp.where(y > 1, 2, 0)
     asked = everyone[first + x % 2, :ROWS, :]
     keys = everyone[first, ROWS:, :]
     values = everyone[first + 1, ROWS:, :]
@@ -196,13 +194,13 @@
     fresh_top = jnp.max(fresh, axis=1, keepdims=True)
 
     tops = gathered[:, ROWS:, :].astype(F32)
-    blank = jnp.zeros((HD - PEERS * 8, HD), F32)
-    low = jnp.concatenate([tops[:, :8, :].reshape(PEERS * 8, HD), blank], 0).T
-    high = jnp.concatenate([tops[:, 8:, :].reshape(PEERS * 8, HD), blank], 0).T[: ROWS - HD]
+    blank = jnp.zeros((HD - SIDE * 8, HD), F32)
+    low = jnp.concatenate([tops[:, :8, :].reshape(SIDE * 8, HD), blank], 0).T
+    high = jnp.concatenate([tops[:, 8:, :].reshape(SIDE * 8, HD), blank], 0).T[: ROWS - HD]
     pairs = jnp.concatenate([low, high], 0)
     both = pairs + pltpu.roll(pairs, HD - 2, 1)
     lane = lax.broadcasted_iota(jnp.int32, (ROWS, HD), 1)
-    is_top = (lane % 8 == 0) & (lane < PEERS * 8)
+    is_top = (lane % 8 == 0) & (lane < SIDE * 8)
     tops = jnp.where(is_top, both, FLOOR)
     sums = pltpu.roll(both, HD - 1, 1)
     highest = jnp.maximum(jnp.max(tops, axis=1, keepdims=True), fresh_top)
@@ -211,7 +209,7 @@
     totals = jnp.sum(jnp.where(is_top, factors * sums, 0.0), axis=1, keepdims=True)
     totals += jnp.sum(fresh_weights, axis=1, keepdims=True)
     blended = jnp.dot(fresh_weights.astype(BF), values, preferred_element_type=F32)
-    for peer in range(PEERS):
+    for peer in range(SIDE):
         blended += factors[:, peer * 8 : peer * 8 + 1] * gathered[peer, :ROWS, :].astype(F32)
     result = (blended / totals).astype(BF)
 
@@ -240,33 +238,29 @@
     decode_slot,
 ):
     shape = jax.ShapeDtypeStruct
-    peers = [[y * SIDE + 2 * half + x for y in range(SIDE) for x in range(2)] for half in range(2)]
+    whole = [(y, x) for y in range(SIDE) for x in range(SIDE)]
+    peers = [[y * SIDE + x for y in (low, 3 - low) for x in (2 * half, 2 * half + 1)] for low in range(2) for half in range(2)]
 
     def across(array):
         return lax.all_to_all(array, "tensor", 0, 0, axis_index_groups=peers, tiled=True)
 
     asked = queries.reshape(SLOTS, STEPS, HEADS, HD).transpose(0, 2, 1, 3)
-    tile = (SLOTS, STRIDE, 2 * PAIRS * HD)
     held = [
         ((GROUPS, TILES, STEPS, HD), BF),
         ((RES, TILES, STEPS, HD), BF),
-        *([(tile, BF)] * BLOCKS),
     ]
     taken = [
         *([((2, HD), jnp.int32)] * 3),
         ((1, HD), jnp.int32),
         ((SLOTS, HEADS, STEPS, HD), BF),
         ((SLOTS, STEPS, HD), BF),
-        (prefill_cache.shape, BF),
-        (resident_cache.shape, BF),
     ]
-    plan, sent, kept, *split = call(
+    plan, sent, kept = call(
         pack_kernel,
         (shape((2 * MIG + SLOTS,), jnp.int32), *(shape(*one) for one in held)),
-        [HB] * 8,
-        moved=3 * 2**20,
+        [HB] * 6,
         scratch=[pltpu.VMEM(*one) for one in taken + held]
-        + [pltpu.SemaphoreType.DMA((8,)), pltpu.SemaphoreType.DMA((len(held),))],
+        + [pltpu.SemaphoreType.DMA((6,)), pltpu.SemaphoreType.DMA((len(held),))],
         limit=FULL,
         places=(SM, *([ANY] * len(held))),
     )(
@@ -276,30 +270,37 @@
         resident_kept.reshape(1, HD),
         asked,
         new_entries,
-        prefill_cache,
-        resident_cache,
     )
     arrived = lax.all_to_all(sent, "group", 0, 0, tiled=True)
 
+    split = call(
+        split_kernel,
+        (shape((SLOTS, STRIDE, 2 * PAIRS * HD), BF),) * SIDE,
+        [VM, VM],
+        moved=3 * 2**20,
+    )(prefill_cache, resident_cache)
     blocks = [split[0]]
-    for step in range(1, BLOCKS):
-        steps = [(t, t // SIDE * SIDE + swapped(step, t % SIDE)) for t in range(SHARDS)]
+    for step in (3, 1, 2):
+        steps = []
+        for y, x in whole:
+            other, side = swapped(step, y, x)
+            steps.append((y * SIDE + x, other * SIDE + side))
         blocks.append(lax.ppermute(split[step], "tensor", steps))
 
     asking = call(
-        spread_kernel, shape((PEERS, SLOTS * TILES, STEPS, HD), BF), [SM, VM, VM]
+        spread_kernel, shape((SIDE, SLOTS * TILES, STEPS, HD), BF), [SM, VM, VM]
     )(plan, arrived, kept)
-    everyone = across(asking).reshape(PEERS, ROWS + ENTRIES, HD)
+    everyone = across(asking).reshape(SIDE, ROWS + ENTRIES, HD)
 
     payload = call(
         partial_kernel,
-        shape((PEERS, PAYLOAD, HD), BF),
-        [SM] + [VM] * (1 + BLOCKS),
+        shape((SIDE, PAYLOAD, HD), BF),
+        [SM] + [VM] * (1 + SIDE),
         flops=10**8,
         moved=3 * 2**20,
         scratch=[
-            pltpu.VMEM((PEERS, ROWS, WIDE), F32),
-            pltpu.VMEM((PEERS, ROWS, WIDE), BF),
+            pltpu.VMEM((SIDE, ROWS, HD), F32),
+            pltpu.VMEM((SIDE, ROWS, HD), BF),
             pltpu.VMEM((2 * HD, HD), F32),
         ],
     )(plan, everyone, *blocks)

time: 90.6 us -> 88.3 us (0.975)
  waiting for transfers between devices: 20.2 us -> 11.3 us
  starting transfers between devices: 26.3 us -> 31.3 us
  local copies, waits for them, and re-layouts: 0.67 us -> 1.89 us
  Pallas kernels: 9.09 us -> 8.05 us
  blocking collectives: 33.6 us -> 34.6 us
    all_to_all x1, waiting for transfers between devices: 12.7 us -> 5.87 us  [body(): arrived = lax.all_to_all(sent, 'group', 0, 0, tiled=True)]
    ppermute x1 -> x3, starting transfers between devices: 4.39 us -> 9.58 us  [body(): blocks.append(lax.ppermute(split[step], 'tensor', steps))]
    all_to_all x1, waiting for transfers between devices: 7.46 us -> 4.29 us  [across(): lax.all_to_all(array, 'tensor', 0, 0, axis_index_groups=peers, tiled=True)]
    all_to_all x1, blocking collectives: 23.6 us -> 26.5 us  [body(): returned = lax.all_to_all(finished, 'group', 0, 0, tiled=True)]
    all_to_all x1, blocking collectives: 10 us -> 8.04 us  [across(): lax.all_to_all(array, 'tensor', 0, 0, axis_index_groups=peers, tiled=True)]
    unnamed x6 -> x8, local copies, waits for them, and re-layouts: 0.67 us -> 1.89 us
    ppermute x1 -> x3, waiting for transfers between devices: 0.01 us -> 1.1 us  [body(): blocks.append(lax.ppermute(split[step], 'tensor', steps))]
    pallas_call x1, Pallas kernels: 3.44 us -> 2.38 us  [body(): call(pack_kernel, (shape((2 * MIG + SLOTS,), jnp.int32), *(shape(*one) fo...]
  transfers between devices with their start and end apart: 3 -> 5, of which waited for: 2 -> 3; matrix products, arithmetic and copies ran while one was open for 0% -> 0% of each run, Pallas kernels for 2% -> 2%
where the time goes in v8:
time: 88.3 us; the launch traced here: 87.1 us
  blocking collectives  34.6 us (39%)
  starting transfers between devices  31.3 us (35%)
  waiting for transfers between devices  11.3 us (13%)
  Pallas kernels  8.05 us (9%)
  local copies, waits for them, and re-layouts  1.89 us (2%)
    all_to_all x1, blocking collectives, body(): returned = lax.all_to_all(finished, 'group', 0, 0, tiled=True)  26.5 us
    all_to_all x1, starting transfers between devices, body(): arrived = lax.all_to_all(sent, 'group', 0, 0, tiled=True)  16.8 us
    ppermute x3, starting transfers between devices, body(): blocks.append(lax.ppermute(split[step], 'tensor', steps))  9.58 us
    all_to_all x1, blocking collectives, across(): lax.all_to_all(array, 'tensor', 0, 0, axis_index_groups=peers, tiled=True)  8.04 us
    all_to_all x1, waiting for transfers between devices, body(): arrived = lax.all_to_all(sent, 'group', 0, 0, tiled=True)  5.87 us
    all_to_all x1, starting transfers between devices, across(): lax.all_to_all(array, 'tensor', 0, 0, axis_index_groups=peers, tiled=True)  4.93 us
    all_to_all x1, waiting for transfers between devices, across(): lax.all_to_all(array, 'tensor', 0, 0, axis_index_groups=peers, tiled=True)  4.29 us
    pallas_call x1, Pallas kernels, body(): call(pack_kernel, (shape((2 * MIG + SLOTS,), jnp.int32), *(shape(*one) fo...  2.38 us
  transfers between devices with their start and end apart: 5, of which 3 were waited for; matrix products, arithmetic and copies ran while one was open for 0% of the time, Pallas kernels for 2%

profile of v8, /device:TPU:1, one launch (start us, length us, event | category | flops | bytes accessed | tf_op | source)
XLA Modules:
  0.0 87.1 jit_solution(10139223910332452386)
XLA Ops:
  0.0 0.0 copy-start.1
  0.0 2.4 %shard_map.82 = (s32[28]{0:T(128)}, bf16[32,5,4,128]{3,2,1,0:T(4,128)(2,1)}, bf16[4,5,4,128]{3,2,1,0:T(4,128)(2,1)}) custom-call(s32[2,128]{1,0:T(2,128)} %bitcast.16, s32[2,128]{1,0:T(2,128)} %bitcast.17, s32[2,128]{1,0:T(2,128)} %bitcast.18, s32[1,128]{1,0:T(1,128)} %bitcast.19, bf16[12,4,4,128]{3,2,1,0:T(4,128)(2,1)} %bitcast.15, bf16[12,4,2048]{2,1,0:T(4,128)(2,1)} %refs_5_.1), custom_call_target="tpu_custom_call" | custom-call | tf_op jit(solution)/shard_map/pallas_call | solution.py:258
  2.4 16.8 %all-to-all-start = ((bf16[32,5,4,128]{3,2,1,0:T(4,128)(2,1)}), bf16[32,5,4,128]{3,2,1,0:T(4,128)(2,1)S(1)}, u32[]{:S(2)}, u32[]{:S(2)}) async-start(bf16[32,5,4,128]{3,2,1,0:T(4,128)(2,1)} %get-tuple-element.15), calls=%async_computation | async-start | bytes 327680 | tf_op jit(solution)/shard_map/all_to_all | solution.py:274
  19.2 0.0 copy-done.1
  19.2 0.0 copy-start
  19.2 1.2 %copy-done = bf16[8,32,2048]{2,1,0:T(8,128)(2,1)S(1)} copy-done((bf16[8,32,2048]{2,1,0:T(8,128)(2,1)S(1)}, bf16[8,32,2048]{2,1,0:T(8,128)(2,1)}, u32[]{:S(2)}) %copy-start) | copy-done | bytes 1048600
  20.4 0.0 copy-start.2
  20.4 0.4 shard_map.84
  20.8 5.4 %collective-permute-start = (bf16[12,32,512]{2,1,0:T(8,128)(2,1)S(1)}, bf16[12,32,512]{2,1,0:T(8,128)(2,1)S(1)}, u32[]{:S(2)}, u32[]{:S(2)}) collective-permute-start(bf16[12,32,512]{2,1,0:T(8,128)(2,1)S(1)} %get-tuple-element.18), channel_id=1, source_target_pairs={{0,7},{1,6},{2,5},{3,4},{4,3},{5,2},{6,1},{7,0},{8,15},{9,14},{10,... | collective-permute-start | bytes 1179656 | tf_op jit(solution)/shard_map/ppermute | solution.py:288
  26.2 2.1 %collective-permute-start.1 = (bf16[12,32,512]{2,1,0:T(8,128)(2,1)S(1)}, bf16[12,32,512]{2,1,0:T(8,128)(2,1)S(1)}, u32[]{:S(2)}, u32[]{:S(2)}) collective-permute-start(bf16[12,32,512]{2,1,0:T(8,128)(2,1)S(1)} %get-tuple-element.19), channel_id=1, source_target_pairs={{0,4},{1,5},{2,6},{3,7},{4,0},{5,1},{6,2},{7,3},{8,12},{9,13},{10,... | collective-permute-start | bytes 1179656 | tf_op jit(solution)/shard_map/ppermute | solution.py:288
  28.3 2.1 %collective-permute-start.2 = (bf16[12,32,512]{2,1,0:T(8,128)(2,1)S(1)}, bf16[12,32,512]{2,1,0:T(8,128)(2,1)S(1)}, u32[]{:S(2)}, u32[]{:S(2)}) collective-permute-start(bf16[12,32,512]{2,1,0:T(8,128)(2,1)S(1)} %get-tuple-element.20), channel_id=1, source_target_pairs={{0,3},{1,2},{2,1},{3,0},{4,7},{5,6},{6,5},{7,4},{8,11},{9,10},{10,... | collective-permute-start | bytes 1179656 | tf_op jit(solution)/shard_map/ppermute | solution.py:288
  30.4 5.9 %all-to-all-done.arrived = bf16[32,5,4,128]{3,2,1,0:T(4,128)(2,1)S(1)} async-done(((bf16[32,5,4,128]{3,2,1,0:T(4,128)(2,1)}), bf16[32,5,4,128]{3,2,1,0:T(4,128)(2,1)S(1)}, u32[]{:S(2)}, u32[]{:S(2)}) %all-to-all-start) | async-done | bytes 163872 | tf_op jit(solution)/shard_map/all_to_all | solution.py:274
  36.3 0.0 copy-start.3
  36.3 0.0 copy-done.2
  36.3 0.7 copy-done.3
  37.0 1.3 %shard_map.83 = bf16[4,60,4,128]{3,2,1,0:T(4,128)(2,1)} custom-call(s32[28]{0:T(128)S(1)} %copy-done.3, bf16[32,5,4,128]{3,2,1,0:T(4,128)(2,1)S(1)} %all-to-all-done.arrived, bf16[4,5,4,128]{3,2,1,0:T(4,128)(2,1)S(1)} %copy-done.2), custom_call_target="tpu_custom_call" | custom-call | tf_op jit(solution)/shard_map/pallas_call | solution.py:290
  38.3 4.9 %all-to-all-start.1 = ((bf16[4,60,4,128]{3,2,1,0:T(4,128)(2,1)}), bf16[4,60,4,128]{3,2,1,0:T(4,128)(2,1)S(1)}, u32[]{:S(2)}, u32[]{:S(2)}) async-start(bf16[4,60,4,128]{3,2,1,0:T(4,128)(2,1)} %shard_map.83), calls=%async_computation.1 | async-start | bytes 491520 | tf_op jit(solution)/shard_map/all_to_all | solution.py:245
  43.2 0.0 collective-permute-done.rest_1_
  43.2 1.1 %collective-permute-done.1.rest_2_ = bf16[12,32,512]{2,1,0:T(8,128)(2,1)S(1)} collective-permute-done((bf16[12,32,512]{2,1,0:T(8,128)(2,1)S(1)}, bf16[12,32,512]{2,1,0:T(8,128)(2,1)S(1)}, u32[]{:S(2)}, u32[]{:S(2)}) %collective-permute-start.1) | collective-permute-done | bytes 393248 | tf_op jit(solution)/shard_map/ppermute | solution.py:288
  44.3 0.0 collective-permute-done.2.rest_3_
  44.3 4.3 %all-to-all-done.1 = bf16[4,60,4,128]{3,2,1,0:T(4,128)(2,1)S(1)} async-done(((bf16[4,60,4,128]{3,2,1,0:T(4,128)(2,1)}), bf16[4,60,4,128]{3,2,1,0:T(4,128)(2,1)S(1)}, u32[]{:S(2)}, u32[]{:S(2)}) %all-to-all-start.1) | async-done | bytes 245792 | tf_op jit(solution)/shard_map/all_to_all | solution.py:245
  48.6 1.3 %shard_map.85 = bf16[4,208,128]{2,1,0:T(8,128)(2,1)S(1)} custom-call(s32[28]{0:T(128)S(1)} %copy-done.3, bf16[4,240,128]{2,1,0:T(8,128)(2,1)S(1)} %bitcast.13, bf16[12,32,512]{2,1,0:T(8,128)(2,1)S(1)} %get-tuple-element.17.rest_0_, bf16[12,32,512]{2,1,0:T(8,128)(2,1)S(1)} %collective-permute-done.rest_1_, ...), custom_call_target="tpu_custom_call" | custom-call | flops 100000000 | bytes 3145728 | tf_op jit(solution)/shard_map/pallas_call | solution.py:295
  49.9 8.0 %all_to_all.20.gathered = bf16[4,208,128]{2,1,0:T(8,128)(2,1)S(1)} all-to-all(bf16[4,208,128]{2,1,0:T(8,128)(2,1)S(1)} %shard_map.85), channel_id=1, replica_groups={{0,1,12,13},{2,3,14,15},{4,5,8,9},{6,7,10,11},{16,17,28,29},{18,19,30,3..., dimensions={0} | all-to-all | bytes 425984 | tf_op jit(solution)/shard_map/all_to_all | solution.py:245
  57.9 1.5 %shard_map.86 = (bf16[32,16,128]{2,1,0:T(8,128)(2,1)S(1)}, bf16[4,16,128]{2,1,0:T(8,128)(2,1)S(1)}) custom-call(s32[28]{0:T(128)S(1)} %copy-done.3, bf16[4,208,128]{2,1,0:T(8,128)(2,1)S(1)} %all_to_all.20.gathered, bf16[4,240,128]{2,1,0:T(8,128)(2,1)S(1)} %bitcast.14), custom_call_target="tpu_custom_call" | custom-call | tf_op jit(solution)/shard_map/pallas_call | solution.py:309
  59.4 26.5 %all_to_all.21.returned = bf16[32,16,128]{2,1,0:T(8,128)(2,1)S(1)} all-to-all(bf16[32,16,128]{2,1,0:T(8,128)(2,1)S(1)} %get-tuple-element.21), channel_id=1, replica_groups=mesh['group'=32,'tensor'=16] {'group'}, dimensions={0} | all-to-all | bytes 262144 | tf_op jit(solution)/shard_map/all_to_all | solution.py:314
  85.9 1.2 %shard_map.87 = bf16[12,16,128]{2,1,0:T(8,128)(2,1)} custom-call(s32[28]{0:T(128)S(1)} %copy-done.3, bf16[32,16,128]{2,1,0:T(8,128)(2,1)S(1)} %all_to_all.21.returned, bf16[4,16,128]{2,1,0:T(8,128)(2,1)S(1)} %get-tuple-element.22.kept), custom_call_target="tpu_custom_call" | custom-call | tf_op jit(solution)/shard_map/pallas_call | solution.py:316
Async XLA Ops:
  0.0 19.2 %copy-start.1 = (bf16[4,32,2048]{2,1,0:T(8,128)(2,1)S(1)}, bf16[4,32,2048]{2,1,0:T(8,128)(2,1)}, u32[]{:S(2)}) copy-start(bf16[4,32,2048]{2,1,0:T(8,128)(2,1)} %resident.1) | copy-start | bytes 1572868
  2.4 33.9 %all-to-all-start = ((bf16[32,5,4,128]{3,2,1,0:T(4,128)(2,1)}), bf16[32,5,4,128]{3,2,1,0:T(4,128)(2,1)S(1)}, u32[]{:S(2)}, u32[]{:S(2)}) async-start(bf16[32,5,4,128]{3,2,1,0:T(4,128)(2,1)} %get-tuple-element.15), calls=%async_computation | async-start | bytes 327680 | tf_op jit(solution)/shard_map/all_to_all | solution.py:274
  19.2 1.2 %copy-start = (bf16[8,32,2048]{2,1,0:T(8,128)(2,1)S(1)}, bf16[8,32,2048]{2,1,0:T(8,128)(2,1)}, u32[]{:S(2)}) copy-start(bf16[8,32,2048]{2,1,0:T(8,128)(2,1)} %moved.1) | copy-start | bytes 3145732
  20.4 15.9 %copy-start.2 = (bf16[4,5,4,128]{3,2,1,0:T(4,128)(2,1)S(1)}, bf16[4,5,4,128]{3,2,1,0:T(4,128)(2,1)}, u32[]{:S(2)}) copy-start(bf16[4,5,4,128]{3,2,1,0:T(4,128)(2,1)} %get-tuple-element.16.kept) | copy-start | bytes 61444
  20.8 22.4 %collective-permute-start = (bf16[12,32,512]{2,1,0:T(8,128)(2,1)S(1)}, bf16[12,32,512]{2,1,0:T(8,128)(2,1)S(1)}, u32[]{:S(2)}, u32[]{:S(2)}) collective-permute-start(bf16[12,32,512]{2,1,0:T(8,128)(2,1)S(1)} %get-tuple-element.18), channel_id=1, source_target_pairs={{0,7},{1,6},{2,5},{3,4},{4,3},{5,2},{6,1},{7,0},{8,15},{9,14},{10,... | collective-permute-start | bytes 1179656 | tf_op jit(solution)/shard_map/ppermute | solution.py:288
  26.2 18.1 %collective-permute-start.1 = (bf16[12,32,512]{2,1,0:T(8,128)(2,1)S(1)}, bf16[12,32,512]{2,1,0:T(8,128)(2,1)S(1)}, u32[]{:S(2)}, u32[]{:S(2)}) collective-permute-start(bf16[12,32,512]{2,1,0:T(8,128)(2,1)S(1)} %get-tuple-element.19), channel_id=1, source_target_pairs={{0,4},{1,5},{2,6},{3,7},{4,0},{5,1},{6,2},{7,3},{8,12},{9,13},{10,... | collective-permute-start | bytes 1179656 | tf_op jit(solution)/shard_map/ppermute | solution.py:288
  28.3 16.0 %collective-permute-start.2 = (bf16[12,32,512]{2,1,0:T(8,128)(2,1)S(1)}, bf16[12,32,512]{2,1,0:T(8,128)(2,1)S(1)}, u32[]{:S(2)}, u32[]{:S(2)}) collective-permute-start(bf16[12,32,512]{2,1,0:T(8,128)(2,1)S(1)} %get-tuple-element.20), channel_id=1, source_target_pairs={{0,3},{1,2},{2,1},{3,0},{4,7},{5,6},{6,5},{7,4},{8,11},{9,10},{10,... | collective-permute-start | bytes 1179656 | tf_op jit(solution)/shard_map/ppermute | solution.py:288
  36.3 0.7 copy-start.3
  38.3 10.3 %all-to-all-start.1 = ((bf16[4,60,4,128]{3,2,1,0:T(4,128)(2,1)}), bf16[4,60,4,128]{3,2,1,0:T(4,128)(2,1)S(1)}, u32[]{:S(2)}, u32[]{:S(2)}) async-start(bf16[4,60,4,128]{3,2,1,0:T(4,128)(2,1)} %shard_map.83), calls=%async_computation.1 | async-start | bytes 491520 | tf_op jit(solution)/shard_map/all_to_all | solution.py:245

commit v9 on v8

--- a/solution.py
+++ b/solution.py
@@ -15,6 +15,7 @@
 RES = 4
 SLOTS = MIG + RES
 GROUPS = 32
+TURN = 16
 SHARDS = 16
 SIDE = 4
 STRIDE = 32
@@ -93,8 +94,8 @@
         name = (group * SLOTS + RES + slot).astype(F32)
         to = lax.div(found(names, name, holders), MIG)
         plan[TARGET + slot] = to
-        sent[to, :HEADS] = asked[RES + slot]
-        sent[to, HEADS] = fresh[RES + slot]
+        sent[to ^ TURN, :HEADS] = asked[RES + slot]
+        sent[to ^ TURN, HEADS] = fresh[RES + slot]
     writes = [pltpu.make_async_copy(p, q, go.at[k]) for k, (p, q) in enumerate(zip((sent, kept), outs))]
     writes[0].start()
     writes[1].start()
@@ -123,7 +124,7 @@
 
 def spread_kernel(plan, arrived, kept, asking):
     for row in range(SLOTS):
-        chunk = arrived.at[plan[ORIGIN + row]] if row < MIG else kept.at[row - MIG]
+        chunk = arrived.at[plan[ORIGIN + row] ^ TURN] if row < MIG else kept.at[row - MIG]
         for peer in range(SIDE):
             asking[peer, row * HEADS : (row + 1) * HEADS] = chunk[:HEADS]
             asking[peer, SLOTS * HEADS + row] = chunk[HEADS]
@@ -215,7 +216,7 @@
 
     sent[...] = jnp.zeros_like(sent)
     for slot in range(MIG):
-        sent[plan[ORIGIN + slot]] = result[slot * QROWS : (slot + 1) * QROWS]
+        sent[plan[ORIGIN + slot] ^ TURN] = result[slot * QROWS : (slot + 1) * QROWS]
     for slot in range(RES):
         kept[slot] = result[(MIG + slot) * QROWS : (MIG + slot + 1) * QROWS]
 
@@ -224,7 +225,7 @@
     for slot in range(RES):
         out[slot] = kept[slot]
     for slot in range(MIG):
-        out[RES + slot] = returned[plan[TARGET + slot]]
+        out[RES + slot] = returned[plan[TARGET + slot] ^ TURN]
 
 
 def body(
@@ -240,6 +241,11 @@
     shape = jax.ShapeDtypeStruct
     whole = [(y, x) for y in range(SIDE) for x in range(SIDE)]
     peers = [[y * SIDE + x for y in (low, 3 - low) for x in (2 * half, 2 * half + 1)] for low in range(2) for half in range(2)]
+
+    turned = [[group ^ TURN for group in range(GROUPS)]]
+
+    def around(array):
+        return lax.all_to_all(array, "group", 0, 0, axis_index_groups=turned, tiled=True)
 
     def across(array):
         return lax.all_to_all(array, "tensor", 0, 0, axis_index_groups=peers, tiled=True)
@@ -271,7 +277,7 @@
         asked,
         new_entries,
     )
-    arrived = lax.all_to_all(sent, "group", 0, 0, tiled=True)
+    arrived = around(sent)
 
     split = call(
         split_kernel,
@@ -311,7 +317,7 @@
         (shape((GROUPS, QROWS, HD), BF), shape((RES, QROWS, HD), BF)),
         [SM, VM, VM],
     )(plan, gathered, everyone)
-    returned = lax.all_to_all(finished, "group", 0, 0, tiled=True)
+    returned = around(finished)
 
     result = call(select_kernel, shape((SLOTS, QROWS, HD), BF), [SM, VM, VM])(plan, returned, here)
     result = result.reshape(SLOTS, HEADS, STEPS, HD).transpose(0, 2, 1, 3)

time: 88.3 us -> 82.1 us (0.930)
  blocking collectives: 34.6 us -> 30 us
  waiting for transfers between devices: 11.3 us -> 7.88 us
  starting transfers between devices: 31.3 us -> 33.7 us
    ppermute x3, waiting for transfers between devices: 1.1 us -> 7.88 us  [body(): blocks.append(lax.ppermute(split[step], 'tensor', steps))]
    all_to_all x1, blocking collectives: 26.5 us -> 20.5 us  [around(): lax.all_to_all(array, 'group', 0, 0, axis_index_groups=turned, tiled=True)]
    all_to_all x1, waiting for transfers between devices: 5.87 us -> 0.01 us  [around(): lax.all_to_all(array, 'group', 0, 0, axis_index_groups=turned, tiled=True)]
    all_to_all x1, waiting for transfers between devices: 4.29 us -> 0.01 us  [across(): lax.all_to_all(array, 'tensor', 0, 0, axis_index_groups=peers, tiled=True)]
    all_to_all x1, starting transfers between devices: 16.8 us -> 20.2 us  [around(): lax.all_to_all(array, 'group', 0, 0, axis_index_groups=turned, tiled=True)]
    all_to_all x1, blocking collectives: 8.04 us -> 9.49 us  [across(): lax.all_to_all(array, 'tensor', 0, 0, axis_index_groups=peers, tiled=True)]
    all_to_all x1, starting transfers between devices: 4.93 us -> 4 us  [across(): lax.all_to_all(array, 'tensor', 0, 0, axis_index_groups=peers, tiled=True)]
  transfers between devices with their start and end apart: 5 -> 5, of which waited for: 3 -> 1; matrix products, arithmetic and copies ran while one was open for 0% -> 0% of each run, Pallas kernels for 2% -> 2%
where the time goes in v9:
time: 82.1 us; the launch traced here: 81.6 us
  starting transfers between devices  33.7 us (41%)
  blocking collectives  30 us (37%)
  Pallas kernels  8.05 us (10%)
  waiting for transfers between devices  7.88 us (10%)
  local copies, waits for them, and re-layouts  1.88 us (2%)
    all_to_all x1, blocking collectives, around(): lax.all_to_all(array, 'group', 0, 0, axis_index_groups=turned, tiled=True)  20.5 us
    all_to_all x1, starting transfers between devices, around(): lax.all_to_all(array, 'group', 0, 0, axis_index_groups=turned, tiled=True)  20.2 us
    ppermute x3, starting transfers between devices, body(): blocks.append(lax.ppermute(split[step], 'tensor', steps))  9.58 us
    all_to_all x1, blocking collectives, across(): lax.all_to_all(array, 'tensor', 0, 0, axis_index_groups=peers, tiled=True)  9.49 us
    ppermute x3, waiting for transfers between devices, body(): blocks.append(lax.ppermute(split[step], 'tensor', steps))  7.88 us
    all_to_all x1, starting transfers between devices, across(): lax.all_to_all(array, 'tensor', 0, 0, axis_index_groups=peers, tiled=True)  4 us
    pallas_call x1, Pallas kernels, body(): call(pack_kernel, (shape((2 * MIG + SLOTS,), jnp.int32), *(shape(*one) fo...  2.38 us
    unnamed x8, local copies, waits for them, and re-layouts  1.88 us
  transfers between devices with their start and end apart: 5, of which 1 were waited for; matrix products, arithmetic and copies ran while one was open for 0% of the time, Pallas kernels for 2%

profile of v9, /device:TPU:1, one launch (start us, length us, event | category | flops | bytes accessed | tf_op | source)
XLA Modules:
  0.0 81.6 jit_solution(10215668989368824376)
XLA Ops:
  0.0 0.0 copy-start.1
  0.0 2.4 %shard_map.82 = (s32[28]{0:T(128)}, bf16[32,5,4,128]{3,2,1,0:T(4,128)(2,1)}, bf16[4,5,4,128]{3,2,1,0:T(4,128)(2,1)}) custom-call(s32[2,128]{1,0:T(2,128)} %bitcast.16, s32[2,128]{1,0:T(2,128)} %bitcast.17, s32[2,128]{1,0:T(2,128)} %bitcast.18, s32[1,128]{1,0:T(1,128)} %bitcast.19, bf16[12,4,4,128]{3,2,1,0:T(4,128)(2,1)} %bitcast.15, bf16[12,4,2048]{2,1,0:T(4,128)(2,1)} %refs_5_.1), custom_call_target="tpu_custom_call" | custom-call | tf_op jit(solution)/shard_map/pallas_call | solution.py:264
  2.4 20.2 %all-to-all-start = ((bf16[32,5,4,128]{3,2,1,0:T(4,128)(2,1)}), bf16[32,5,4,128]{3,2,1,0:T(4,128)(2,1)S(1)}, u32[]{:S(2)}, u32[]{:S(2)}) async-start(bf16[32,5,4,128]{3,2,1,0:T(4,128)(2,1)} %get-tuple-element.15), calls=%async_computation | async-start | bytes 327680 | tf_op jit(solution)/shard_map/all_to_all | solution.py:248
  22.6 0.0 copy-done.1
  22.6 0.0 copy-start
  22.6 1.2 %copy-done = bf16[8,32,2048]{2,1,0:T(8,128)(2,1)S(1)} copy-done((bf16[8,32,2048]{2,1,0:T(8,128)(2,1)S(1)}, bf16[8,32,2048]{2,1,0:T(8,128)(2,1)}, u32[]{:S(2)}) %copy-start) | copy-done | bytes 1048600
  23.8 0.0 copy-start.2
  23.8 0.4 shard_map.84
  24.2 5.4 %collective-permute-start = (bf16[12,32,512]{2,1,0:T(8,128)(2,1)S(1)}, bf16[12,32,512]{2,1,0:T(8,128)(2,1)S(1)}, u32[]{:S(2)}, u32[]{:S(2)}) collective-permute-start(bf16[12,32,512]{2,1,0:T(8,128)(2,1)S(1)} %get-tuple-element.18), channel_id=1, source_target_pairs={{0,7},{1,6},{2,5},{3,4},{4,3},{5,2},{6,1},{7,0},{8,15},{9,14},{10,... | collective-permute-start | bytes 1179656 | tf_op jit(solution)/shard_map/ppermute | solution.py:294
  29.6 2.1 %collective-permute-start.1 = (bf16[12,32,512]{2,1,0:T(8,128)(2,1)S(1)}, bf16[12,32,512]{2,1,0:T(8,128)(2,1)S(1)}, u32[]{:S(2)}, u32[]{:S(2)}) collective-permute-start(bf16[12,32,512]{2,1,0:T(8,128)(2,1)S(1)} %get-tuple-element.19), channel_id=1, source_target_pairs={{0,4},{1,5},{2,6},{3,7},{4,0},{5,1},{6,2},{7,3},{8,12},{9,13},{10,... | collective-permute-start | bytes 1179656 | tf_op jit(solution)/shard_map/ppermute | solution.py:294
  31.7 2.1 %collective-permute-start.2 = (bf16[12,32,512]{2,1,0:T(8,128)(2,1)S(1)}, bf16[12,32,512]{2,1,0:T(8,128)(2,1)S(1)}, u32[]{:S(2)}, u32[]{:S(2)}) collective-permute-start(bf16[12,32,512]{2,1,0:T(8,128)(2,1)S(1)} %get-tuple-element.20), channel_id=1, source_target_pairs={{0,3},{1,2},{2,1},{3,0},{4,7},{5,6},{6,5},{7,4},{8,11},{9,10},{10,... | collective-permute-start | bytes 1179656 | tf_op jit(solution)/shard_map/ppermute | solution.py:294
  33.8 0.0 all-to-all-done.arrived
  33.8 0.0 copy-start.3
  33.8 0.0 copy-done.2
  33.9 0.6 copy-done.3
  34.5 1.3 %shard_map.83 = bf16[4,60,4,128]{3,2,1,0:T(4,128)(2,1)} custom-call(s32[28]{0:T(128)S(1)} %copy-done.3, bf16[32,5,4,128]{3,2,1,0:T(4,128)(2,1)S(1)} %all-to-all-done.arrived, bf16[4,5,4,128]{3,2,1,0:T(4,128)(2,1)S(1)} %copy-done.2), custom_call_target="tpu_custom_call" | custom-call | tf_op jit(solution)/shard_map/pallas_call | solution.py:296
  35.8 4.0 %all-to-all-start.1 = ((bf16[4,60,4,128]{3,2,1,0:T(4,128)(2,1)}), bf16[4,60,4,128]{3,2,1,0:T(4,128)(2,1)S(1)}, u32[]{:S(2)}, u32[]{:S(2)}) async-start(bf16[4,60,4,128]{3,2,1,0:T(4,128)(2,1)} %shard_map.83), calls=%async_computation.1 | async-start | bytes 491520 | tf_op jit(solution)/shard_map/all_to_all | solution.py:251
  39.8 0.0 collective-permute-done.rest_1_
  39.8 7.9 %collective-permute-done.1.rest_2_ = bf16[12,32,512]{2,1,0:T(8,128)(2,1)S(1)} collective-permute-done((bf16[12,32,512]{2,1,0:T(8,128)(2,1)S(1)}, bf16[12,32,512]{2,1,0:T(8,128)(2,1)S(1)}, u32[]{:S(2)}, u32[]{:S(2)}) %collective-permute-start.1) | collective-permute-done | bytes 393248 | tf_op jit(solution)/shard_map/ppermute | solution.py:294
  47.7 0.0 collective-permute-done.2.rest_3_
  47.7 0.0 all-to-all-done.1
  47.7 1.3 %shard_map.85 = bf16[4,208,128]{2,1,0:T(8,128)(2,1)S(1)} custom-call(s32[28]{0:T(128)S(1)} %copy-done.3, bf16[4,240,128]{2,1,0:T(8,128)(2,1)S(1)} %bitcast.13, bf16[12,32,512]{2,1,0:T(8,128)(2,1)S(1)} %get-tuple-element.17.rest_0_, bf16[12,32,512]{2,1,0:T(8,128)(2,1)S(1)} %collective-permute-done.rest_1_, ...), custom_call_target="tpu_custom_call" | custom-call | flops 100000000 | bytes 3145728 | tf_op jit(solution)/shard_map/pallas_call | solution.py:301
  49.0 9.5 %all_to_all.20.gathered = bf16[4,208,128]{2,1,0:T(8,128)(2,1)S(1)} all-to-all(bf16[4,208,128]{2,1,0:T(8,128)(2,1)S(1)} %shard_map.85), channel_id=1, replica_groups={{0,1,12,13},{2,3,14,15},{4,5,8,9},{6,7,10,11},{16,17,28,29},{18,19,30,3..., dimensions={0} | all-to-all | bytes 425984 | tf_op jit(solution)/shard_map/all_to_all | solution.py:251
  58.5 1.5 %shard_map.86 = (bf16[32,16,128]{2,1,0:T(8,128)(2,1)S(1)}, bf16[4,16,128]{2,1,0:T(8,128)(2,1)S(1)}) custom-call(s32[28]{0:T(128)S(1)} %copy-done.3, bf16[4,208,128]{2,1,0:T(8,128)(2,1)S(1)} %all_to_all.20.gathered, bf16[4,240,128]{2,1,0:T(8,128)(2,1)S(1)} %bitcast.14), custom_call_target="tpu_custom_call" | custom-call | tf_op jit(solution)/shard_map/pallas_call | solution.py:315
  60.0 20.5 %all_to_all.21.returned = bf16[32,16,128]{2,1,0:T(8,128)(2,1)S(1)} all-to-all(bf16[32,16,128]{2,1,0:T(8,128)(2,1)S(1)} %get-tuple-element.21), channel_id=1, replica_groups={{256,272,288,304,320,336,352,368,384,400,416,432,448,464,480,496,0,16,3..., dimensions={0} | all-to-all | bytes 262144 | tf_op jit(solution)/shard_map/all_to_all | solution.py:248
  80.4 1.2 %shard_map.87 = bf16[12,16,128]{2,1,0:T(8,128)(2,1)} custom-call(s32[28]{0:T(128)S(1)} %copy-done.3, bf16[32,16,128]{2,1,0:T(8,128)(2,1)S(1)} %all_to_all.21.returned, bf16[4,16,128]{2,1,0:T(8,128)(2,1)S(1)} %get-tuple-element.22.kept), custom_call_target="tpu_custom_call" | custom-call | tf_op jit(solution)/shard_map/pallas_call | solution.py:322
Async XLA Ops:
  0.0 22.6 %copy-start.1 = (bf16[4,32,2048]{2,1,0:T(8,128)(2,1)S(1)}, bf16[4,32,2048]{2,1,0:T(8,128)(2,1)}, u32[]{:S(2)}) copy-start(bf16[4,32,2048]{2,1,0:T(8,128)(2,1)} %resident.1) | copy-start | bytes 1572868
  2.4 31.4 %all-to-all-start = ((bf16[32,5,4,128]{3,2,1,0:T(4,128)(2,1)}), bf16[32,5,4,128]{3,2,1,0:T(4,128)(2,1)S(1)}, u32[]{:S(2)}, u32[]{:S(2)}) async-start(bf16[32,5,4,128]{3,2,1,0:T(4,128)(2,1)} %get-tuple-element.15), calls=%async_computation | async-start | bytes 327680 | tf_op jit(solution)/shard_map/all_to_all | solution.py:248
  22.6 1.2 %copy-start = (bf16[8,32,2048]{2,1,0:T(8,128)(2,1)S(1)}, bf16[8,32,2048]{2,1,0:T(8,128)(2,1)}, u32[]{:S(2)}) copy-start(bf16[8,32,2048]{2,1,0:T(8,128)(2,1)} %moved.1) | copy-start | bytes 3145732
  23.8 10.1 %copy-start.2 = (bf16[4,5,4,128]{3,2,1,0:T(4,128)(2,1)S(1)}, bf16[4,5,4,128]{3,2,1,0:T(4,128)(2,1)}, u32[]{:S(2)}) copy-start(bf16[4,5,4,128]{3,2,1,0:T(4,128)(2,1)} %get-tuple-element.16.kept) | copy-start | bytes 61444
  24.2 15.6 %collective-permute-start = (bf16[12,32,512]{2,1,0:T(8,128)(2,1)S(1)}, bf16[12,32,512]{2,1,0:T(8,128)(2,1)S(1)}, u32[]{:S(2)}, u32[]{:S(2)}) collective-permute-start(bf16[12,32,512]{2,1,0:T(8,128)(2,1)S(1)} %get-tuple-element.18), channel_id=1, source_target_pairs={{0,7},{1,6},{2,5},{3,4},{4,3},{5,2},{6,1},{7,0},{8,15},{9,14},{10,... | collective-permute-start | bytes 1179656 | tf_op jit(solution)/shard_map/ppermute | solution.py:294
  29.6 18.1 %collective-permute-start.1 = (bf16[12,32,512]{2,1,0:T(8,128)(2,1)S(1)}, bf16[12,32,512]{2,1,0:T(8,128)(2,1)S(1)}, u32[]{:S(2)}, u32[]{:S(2)}) collective-permute-start(bf16[12,32,512]{2,1,0:T(8,128)(2,1)S(1)} %get-tuple-element.19), channel_id=1, source_target_pairs={{0,4},{1,5},{2,6},{3,7},{4,0},{5,1},{6,2},{7,3},{8,12},{9,13},{10,... | collective-permute-start | bytes 1179656 | tf_op jit(solution)/shard_map/ppermute | solution.py:294
  31.7 16.0 %collective-permute-start.2 = (bf16[12,32,512]{2,1,0:T(8,128)(2,1)S(1)}, bf16[12,32,512]{2,1,0:T(8,128)(2,1)S(1)}, u32[]{:S(2)}, u32[]{:S(2)}) collective-permute-start(bf16[12,32,512]{2,1,0:T(8,128)(2,1)S(1)} %get-tuple-element.20), channel_id=1, source_target_pairs={{0,3},{1,2},{2,1},{3,0},{4,7},{5,6},{6,5},{7,4},{8,11},{9,10},{10,... | collective-permute-start | bytes 1179656 | tf_op jit(solution)/shard_map/ppermute | solution.py:294
  33.8 0.7 copy-start.3
  35.8 11.9 %all-to-all-start.1 = ((bf16[4,60,4,128]{3,2,1,0:T(4,128)(2,1)}), bf16[4,60,4,128]{3,2,1,0:T(4,128)(2,1)S(1)}, u32[]{:S(2)}, u32[]{:S(2)}) async-start(bf16[4,60,4,128]{3,2,1,0:T(4,128)(2,1)} %shard_map.83), calls=%async_computation.1 | async-start | bytes 491520 | tf_op jit(solution)/shard_map/all_to_all | solution.py:251

commit v10 on v9

--- a/solution.py
+++ b/solution.py
@@ -216,7 +216,7 @@
 
     sent[...] = jnp.zeros_like(sent)
     for slot in range(MIG):
-        sent[plan[ORIGIN + slot] ^ TURN] = result[slot * QROWS : (slot + 1) * QROWS]
+        sent[plan[ORIGIN + slot]] = result[slot * QROWS : (slot + 1) * QROWS]
     for slot in range(RES):
         kept[slot] = result[(MIG + slot) * QROWS : (MIG + slot + 1) * QROWS]
 
@@ -225,7 +225,7 @@
     for slot in range(RES):
         out[slot] = kept[slot]
     for slot in range(MIG):
-        out[RES + slot] = returned[plan[TARGET + slot] ^ TURN]
+        out[RES + slot] = returned[plan[TARGET + slot]]
 
 
 def body(
@@ -243,9 +243,6 @@
     peers = [[y * SIDE + x for y in (low, 3 - low) for x in (2 * half, 2 * half + 1)] for low in range(2) for half in range(2)]
 
     turned = [[group ^ TURN for group in range(GROUPS)]]
-
-    def around(array):
-        return lax.all_to_all(array, "group", 0, 0, axis_index_groups=turned, tiled=True)
 
     def across(array):
         return lax.all_to_all(array, "tensor", 0, 0, axis_index_groups=peers, tiled=True)
@@ -277,7 +274,7 @@
         asked,
         new_entries,
     )
-    arrived = around(sent)
+    arrived = lax.all_to_all(sent, "group", 0, 0, axis_index_groups=turned, tiled=True)
 
     split = call(
         split_kernel,
@@ -317,7 +314,7 @@
         (shape((GROUPS, QROWS, HD), BF), shape((RES, QROWS, HD), BF)),
         [SM, VM, VM],
     )(plan, gathered, everyone)
-    returned = around(finished)
+    returned = lax.all_to_all(finished, "group", 0, 0, tiled=True)
 
     result = call(select_kernel, shape((SLOTS, QROWS, HD), BF), [SM, VM, VM])(plan, returned, here)
     result = result.reshape(SLOTS, HEADS, STEPS, HD).transpose(0, 2, 1, 3)

time: 82.1 us -> 86.2 us (1.050)
  blocking collectives: 30 us -> 34.1 us
    all_to_all x1, blocking collectives: 20.5 us -> 24.6 us  [body(): returned = lax.all_to_all(finished, 'group', 0, 0, tiled=True)]
where the time goes in v10:
time: 86.2 us; the launch traced here: 85.7 us
  blocking collectives  34.1 us (40%)
  starting transfers between devices  33.7 us (39%)
  Pallas kernels  8.05 us (9%)
  waiting for transfers between devices  7.88 us (9%)
  local copies, waits for them, and re-layouts  1.88 us (2%)
    all_to_all x1, blocking collectives, body(): returned = lax.all_to_all(finished, 'group', 0, 0, tiled=True)  24.6 us
    all_to_all x1, starting transfers between devices, body(): lax.all_to_all(sent, 'group', 0, 0, axis_index_groups=turned, tiled=True)  20.2 us
    ppermute x3, starting transfers between devices, body(): blocks.append(lax.ppermute(split[step], 'tensor', steps))  9.58 us
    all_to_all x1, blocking collectives, across(): lax.all_to_all(array, 'tensor', 0, 0, axis_index_groups=peers, tiled=True)  9.49 us
    ppermute x3, waiting for transfers between devices, body(): blocks.append(lax.ppermute(split[step], 'tensor', steps))  7.88 us
    all_to_all x1, starting transfers between devices, across(): lax.all_to_all(array, 'tensor', 0, 0, axis_index_groups=peers, tiled=True)  4 us
    pallas_call x1, Pallas kernels, body(): call(pack_kernel, (shape((2 * MIG + SLOTS,), jnp.int32), *(shape(*one) fo...  2.38 us
    unnamed x8, local copies, waits for them, and re-layouts  1.88 us
  transfers between devices with their start and end apart: 5, of which 1 were waited for; matrix products, arithmetic and copies ran while one was open for 0% of the time, Pallas kernels for 2%

profile of v10, /device:TPU:1, one launch (start us, length us, event | category | flops | bytes accessed | tf_op | source)
XLA Modules:
  0.0 85.7 jit_solution(12423259743631946261)
XLA Ops:
  0.0 0.0 copy-start.1
  0.0 2.4 %shard_map.82 = (s32[28]{0:T(128)}, bf16[32,5,4,128]{3,2,1,0:T(4,128)(2,1)}, bf16[4,5,4,128]{3,2,1,0:T(4,128)(2,1)}) custom-call(s32[2,128]{1,0:T(2,128)} %bitcast.16, s32[2,128]{1,0:T(2,128)} %bitcast.17, s32[2,128]{1,0:T(2,128)} %bitcast.18, s32[1,128]{1,0:T(1,128)} %bitcast.19, bf16[12,4,4,128]{3,2,1,0:T(4,128)(2,1)} %bitcast.15, bf16[12,4,2048]{2,1,0:T(4,128)(2,1)} %refs_5_.1), custom_call_target="tpu_custom_call" | custom-call | tf_op jit(solution)/shard_map/pallas_call | solution.py:261
  2.4 20.2 %all-to-all-start = ((bf16[32,5,4,128]{3,2,1,0:T(4,128)(2,1)}), bf16[32,5,4,128]{3,2,1,0:T(4,128)(2,1)S(1)}, u32[]{:S(2)}, u32[]{:S(2)}) async-start(bf16[32,5,4,128]{3,2,1,0:T(4,128)(2,1)} %get-tuple-element.15), calls=%async_computation | async-start | bytes 327680 | tf_op jit(solution)/shard_map/all_to_all | solution.py:277
  22.6 0.0 copy-done.1
  22.6 0.0 copy-start
  22.6 1.2 %copy-done = bf16[8,32,2048]{2,1,0:T(8,128)(2,1)S(1)} copy-done((bf16[8,32,2048]{2,1,0:T(8,128)(2,1)S(1)}, bf16[8,32,2048]{2,1,0:T(8,128)(2,1)}, u32[]{:S(2)}) %copy-start) | copy-done | bytes 1048600
  23.8 0.0 copy-start.2
  23.8 0.4 shard_map.84
  24.2 5.4 %collective-permute-start = (bf16[12,32,512]{2,1,0:T(8,128)(2,1)S(1)}, bf16[12,32,512]{2,1,0:T(8,128)(2,1)S(1)}, u32[]{:S(2)}, u32[]{:S(2)}) collective-permute-start(bf16[12,32,512]{2,1,0:T(8,128)(2,1)S(1)} %get-tuple-element.18), channel_id=1, source_target_pairs={{0,7},{1,6},{2,5},{3,4},{4,3},{5,2},{6,1},{7,0},{8,15},{9,14},{10,... | collective-permute-start | bytes 1179656 | tf_op jit(solution)/shard_map/ppermute | solution.py:291
  29.6 2.1 %collective-permute-start.1 = (bf16[12,32,512]{2,1,0:T(8,128)(2,1)S(1)}, bf16[12,32,512]{2,1,0:T(8,128)(2,1)S(1)}, u32[]{:S(2)}, u32[]{:S(2)}) collective-permute-start(bf16[12,32,512]{2,1,0:T(8,128)(2,1)S(1)} %get-tuple-element.19), channel_id=1, source_target_pairs={{0,4},{1,5},{2,6},{3,7},{4,0},{5,1},{6,2},{7,3},{8,12},{9,13},{10,... | collective-permute-start | bytes 1179656 | tf_op jit(solution)/shard_map/ppermute | solution.py:291
  31.7 2.1 %collective-permute-start.2 = (bf16[12,32,512]{2,1,0:T(8,128)(2,1)S(1)}, bf16[12,32,512]{2,1,0:T(8,128)(2,1)S(1)}, u32[]{:S(2)}, u32[]{:S(2)}) collective-permute-start(bf16[12,32,512]{2,1,0:T(8,128)(2,1)S(1)} %get-tuple-element.20), channel_id=1, source_target_pairs={{0,3},{1,2},{2,1},{3,0},{4,7},{5,6},{6,5},{7,4},{8,11},{9,10},{10,... | collective-permute-start | bytes 1179656 | tf_op jit(solution)/shard_map/ppermute | solution.py:291
  33.8 0.0 all-to-all-done.arrived
  33.8 0.0 copy-start.3
  33.8 0.0 copy-done.2
  33.9 0.6 copy-done.3
  34.5 1.3 %shard_map.83 = bf16[4,60,4,128]{3,2,1,0:T(4,128)(2,1)} custom-call(s32[28]{0:T(128)S(1)} %copy-done.3, bf16[32,5,4,128]{3,2,1,0:T(4,128)(2,1)S(1)} %all-to-all-done.arrived, bf16[4,5,4,128]{3,2,1,0:T(4,128)(2,1)S(1)} %copy-done.2), custom_call_target="tpu_custom_call" | custom-call | tf_op jit(solution)/shard_map/pallas_call | solution.py:293
  35.8 4.0 %all-to-all-start.1 = ((bf16[4,60,4,128]{3,2,1,0:T(4,128)(2,1)}), bf16[4,60,4,128]{3,2,1,0:T(4,128)(2,1)S(1)}, u32[]{:S(2)}, u32[]{:S(2)}) async-start(bf16[4,60,4,128]{3,2,1,0:T(4,128)(2,1)} %shard_map.83), calls=%async_computation.1 | async-start | bytes 491520 | tf_op jit(solution)/shard_map/all_to_all | solution.py:248
  39.8 0.0 collective-permute-done.rest_1_
  39.8 7.9 %collective-permute-done.1.rest_2_ = bf16[12,32,512]{2,1,0:T(8,128)(2,1)S(1)} collective-permute-done((bf16[12,32,512]{2,1,0:T(8,128)(2,1)S(1)}, bf16[12,32,512]{2,1,0:T(8,128)(2,1)S(1)}, u32[]{:S(2)}, u32[]{:S(2)}) %collective-permute-start.1) | collective-permute-done | bytes 393248 | tf_op jit(solution)/shard_map/ppermute | solution.py:291
  47.7 0.0 collective-permute-done.2.rest_3_
  47.7 0.0 all-to-all-done.1
  47.7 1.3 %shard_map.85 = bf16[4,208,128]{2,1,0:T(8,128)(2,1)S(1)} custom-call(s32[28]{0:T(128)S(1)} %copy-done.3, bf16[4,240,128]{2,1,0:T(8,128)(2,1)S(1)} %bitcast.13, bf16[12,32,512]{2,1,0:T(8,128)(2,1)S(1)} %get-tuple-element.17.rest_0_, bf16[12,32,512]{2,1,0:T(8,128)(2,1)S(1)} %collective-permute-done.rest_1_, ...), custom_call_target="tpu_custom_call" | custom-call | flops 100000000 | bytes 3145728 | tf_op jit(solution)/shard_map/pallas_call | solution.py:298
  49.0 9.5 %all_to_all.20.gathered = bf16[4,208,128]{2,1,0:T(8,128)(2,1)S(1)} all-to-all(bf16[4,208,128]{2,1,0:T(8,128)(2,1)S(1)} %shard_map.85), channel_id=1, replica_groups={{0,1,12,13},{2,3,14,15},{4,5,8,9},{6,7,10,11},{16,17,28,29},{18,19,30,3..., dimensions={0} | all-to-all | bytes 425984 | tf_op jit(solution)/shard_map/all_to_all | solution.py:248
  58.5 1.5 %shard_map.86 = (bf16[32,16,128]{2,1,0:T(8,128)(2,1)S(1)}, bf16[4,16,128]{2,1,0:T(8,128)(2,1)S(1)}) custom-call(s32[28]{0:T(128)S(1)} %copy-done.3, bf16[4,208,128]{2,1,0:T(8,128)(2,1)S(1)} %all_to_all.20.gathered, bf16[4,240,128]{2,1,0:T(8,128)(2,1)S(1)} %bitcast.14), custom_call_target="tpu_custom_call" | custom-call | tf_op jit(solution)/shard_map/pallas_call | solution.py:312
  60.0 24.6 %all_to_all.21.returned = bf16[32,16,128]{2,1,0:T(8,128)(2,1)S(1)} all-to-all(bf16[32,16,128]{2,1,0:T(8,128)(2,1)S(1)} %get-tuple-element.21), channel_id=1, replica_groups=mesh['group'=32,'tensor'=16] {'group'}, dimensions={0} | all-to-all | bytes 262144 | tf_op jit(solution)/shard_map/all_to_all | solution.py:317
  84.5 1.2 %shard_map.87 = bf16[12,16,128]{2,1,0:T(8,128)(2,1)} custom-call(s32[28]{0:T(128)S(1)} %copy-done.3, bf16[32,16,128]{2,1,0:T(8,128)(2,1)S(1)} %all_to_all.21.returned, bf16[4,16,128]{2,1,0:T(8,128)(2,1)S(1)} %get-tuple-element.22.kept), custom_call_target="tpu_custom_call" | custom-call | tf_op jit(solution)/shard_map/pallas_call | solution.py:319
Async XLA Ops:
  0.0 22.6 %copy-start.1 = (bf16[4,32,2048]{2,1,0:T(8,128)(2,1)S(1)}, bf16[4,32,2048]{2,1,0:T(8,128)(2,1)}, u32[]{:S(2)}) copy-start(bf16[4,32,2048]{2,1,0:T(8,128)(2,1)} %resident.1) | copy-start | bytes 1572868
  2.4 31.4 %all-to-all-start = ((bf16[32,5,4,128]{3,2,1,0:T(4,128)(2,1)}), bf16[32,5,4,128]{3,2,1,0:T(4,128)(2,1)S(1)}, u32[]{:S(2)}, u32[]{:S(2)}) async-start(bf16[32,5,4,128]{3,2,1,0:T(4,128)(2,1)} %get-tuple-element.15), calls=%async_computation | async-start | bytes 327680 | tf_op jit(solution)/shard_map/all_to_all | solution.py:277
  22.6 1.2 %copy-start = (bf16[8,32,2048]{2,1,0:T(8,128)(2,1)S(1)}, bf16[8,32,2048]{2,1,0:T(8,128)(2,1)}, u32[]{:S(2)}) copy-start(bf16[8,32,2048]{2,1,0:T(8,128)(2,1)} %moved.1) | copy-start | bytes 3145732
  23.8 10.1 %copy-start.2 = (bf16[4,5,4,128]{3,2,1,0:T(4,128)(2,1)S(1)}, bf16[4,5,4,128]{3,2,1,0:T(4,128)(2,1)}, u32[]{:S(2)}) copy-start(bf16[4,5,4,128]{3,2,1,0:T(4,128)(2,1)} %get-tuple-element.16.kept) | copy-start | bytes 61444
  24.2 15.6 %collective-permute-start = (bf16[12,32,512]{2,1,0:T(8,128)(2,1)S(1)}, bf16[12,32,512]{2,1,0:T(8,128)(2,1)S(1)}, u32[]{:S(2)}, u32[]{:S(2)}) collective-permute-start(bf16[12,32,512]{2,1,0:T(8,128)(2,1)S(1)} %get-tuple-element.18), channel_id=1, source_target_pairs={{0,7},{1,6},{2,5},{3,4},{4,3},{5,2},{6,1},{7,0},{8,15},{9,14},{10,... | collective-permute-start | bytes 1179656 | tf_op jit(solution)/shard_map/ppermute | solution.py:291
  29.6 18.1 %collective-permute-start.1 = (bf16[12,32,512]{2,1,0:T(8,128)(2,1)S(1)}, bf16[12,32,512]{2,1,0:T(8,128)(2,1)S(1)}, u32[]{:S(2)}, u32[]{:S(2)}) collective-permute-start(bf16[12,32,512]{2,1,0:T(8,128)(2,1)S(1)} %get-tuple-element.19), channel_id=1, source_target_pairs={{0,4},{1,5},{2,6},{3,7},{4,0},{5,1},{6,2},{7,3},{8,12},{9,13},{10,... | collective-permute-start | bytes 1179656 | tf_op jit(solution)/shard_map/ppermute | solution.py:291
  31.7 16.0 %collective-permute-start.2 = (bf16[12,32,512]{2,1,0:T(8,128)(2,1)S(1)}, bf16[12,32,512]{2,1,0:T(8,128)(2,1)S(1)}, u32[]{:S(2)}, u32[]{:S(2)}) collective-permute-start(bf16[12,32,512]{2,1,0:T(8,128)(2,1)S(1)} %get-tuple-element.20), channel_id=1, source_target_pairs={{0,3},{1,2},{2,1},{3,0},{4,7},{5,6},{6,5},{7,4},{8,11},{9,10},{10,... | collective-permute-start | bytes 1179656 | tf_op jit(solution)/shard_map/ppermute | solution.py:291
  33.8 0.7 copy-start.3
  35.8 11.9 %all-to-all-start.1 = ((bf16[4,60,4,128]{3,2,1,0:T(4,128)(2,1)}), bf16[4,60,4,128]{3,2,1,0:T(4,128)(2,1)S(1)}, u32[]{:S(2)}, u32[]{:S(2)}) async-start(bf16[4,60,4,128]{3,2,1,0:T(4,128)(2,1)} %shard_map.83), calls=%async_computation.1 | async-start | bytes 491520 | tf_op jit(solution)/shard_map/all_to_all | solution.py:248

commit v11 on v9

--- a/solution.py
+++ b/solution.py
@@ -15,7 +15,7 @@
 RES = 4
 SLOTS = MIG + RES
 GROUPS = 32
-TURN = 16
+FIRST_G, STRIDE_G = 16, 15
 SHARDS = 16
 SIDE = 4
 STRIDE = 32
@@ -68,6 +68,10 @@
     return shard // SIDE, shard % SIDE
 
 
+def listed(group):
+    return (group * STRIDE_G + FIRST_G) % GROUPS
+
+
 def pack_kernel(*refs):
     given, plan, outs, refs = refs[:6], refs[6], refs[7:9], refs[9:]
     inside, (sent, kept), (come, go) = refs[:6], refs[6:8], refs[8:]
@@ -94,8 +98,8 @@
         name = (group * SLOTS + RES + slot).astype(F32)
         to = lax.div(found(names, name, holders), MIG)
         plan[TARGET + slot] = to
-        sent[to ^ TURN, :HEADS] = asked[RES + slot]
-        sent[to ^ TURN, HEADS] = fresh[RES + slot]
+        sent[listed(to), :HEADS] = asked[RES + slot]
+        sent[listed(to), HEADS] = fresh[RES + slot]
     writes = [pltpu.make_async_copy(p, q, go.at[k]) for k, (p, q) in enumerate(zip((sent, kept), outs))]
     writes[0].start()
     writes[1].start()
@@ -124,7 +128,7 @@
 
 def spread_kernel(plan, arrived, kept, asking):
     for row in range(SLOTS):
-        chunk = arrived.at[plan[ORIGIN + row] ^ TURN] if row < MIG else kept.at[row - MIG]
+        chunk = arrived.at[listed(plan[ORIGIN + row])] if row < MIG else kept.at[row - MIG]
         for peer in range(SIDE):
             asking[peer, row * HEADS : (row + 1) * HEADS] = chunk[:HEADS]
             asking[peer, SLOTS * HEADS + row] = chunk[HEADS]
@@ -216,7 +220,7 @@
 
     sent[...] = jnp.zeros_like(sent)
     for slot in range(MIG):
-        sent[plan[ORIGIN + slot] ^ TURN] = result[slot * QROWS : (slot + 1) * QROWS]
+        sent[listed(plan[ORIGIN + slot])] = result[slot * QROWS : (slot + 1) * QROWS]
     for slot in range(RES):
         kept[slot] = result[(MIG + slot) * QROWS : (MIG + slot + 1) * QROWS]
 
@@ -225,7 +229,7 @@
     for slot in range(RES):
         out[slot] = kept[slot]
     for slot in range(MIG):
-        out[RES + slot] = returned[plan[TARGET + slot] ^ TURN]
+        out[RES + slot] = returned[listed(plan[TARGET + slot])]
 
 
 def body(
@@ -242,7 +246,7 @@
     whole = [(y, x) for y in range(SIDE) for x in range(SIDE)]
     peers = [[y * SIDE + x for y in (low, 3 - low) for x in (2 * half, 2 * half + 1)] for low in range(2) for half in range(2)]
 
-    turned = [[group ^ TURN for group in range(GROUPS)]]
+    turned = [[listed(place) for place in range(GROUPS)]]
 
     def around(array):
         return lax.all_to_all(array, "group", 0, 0, axis_index_groups=turned, tiled=True)

time: 82.1 us -> 82.1 us (level)
  no operation moved by 1% of the time
where the time goes in v11:
time: 82.1 us; the launch traced here: 81.6 us
  starting transfers between devices  33.8 us (41%)
  blocking collectives  29.9 us (36%)
  Pallas kernels  8.1 us (10%)
  waiting for transfers between devices  7.88 us (10%)
  local copies, waits for them, and re-layouts  1.88 us (2%)
    all_to_all x1, blocking collectives, around(): lax.all_to_all(array, 'group', 0, 0, axis_index_groups=turned, tiled=True)  20.4 us
    all_to_all x1, starting transfers between devices, around(): lax.all_to_all(array, 'group', 0, 0, axis_index_groups=turned, tiled=True)  20.2 us
    ppermute x3, starting transfers between devices, body(): blocks.append(lax.ppermute(split[step], 'tensor', steps))  9.58 us
    all_to_all x1, blocking collectives, across(): lax.all_to_all(array, 'tensor', 0, 0, axis_index_groups=peers, tiled=True)  9.49 us
    ppermute x3, waiting for transfers between devices, body(): blocks.append(lax.ppermute(split[step], 'tensor', steps))  7.88 us
    all_to_all x1, starting transfers between devices, across(): lax.all_to_all(array, 'tensor', 0, 0, axis_index_groups=peers, tiled=True)  4 us
    pallas_call x1, Pallas kernels, body(): call(pack_kernel, (shape((2 * MIG + SLOTS,), jnp.int32), *(shape(*one) fo...  2.4 us
    unnamed x8, local copies, waits for them, and re-layouts  1.88 us
  transfers between devices with their start and end apart: 5, of which 1 were waited for; matrix products, arithmetic and copies ran while one was open for 0% of the time, Pallas kernels for 2%

profile of v11, /device:TPU:1, one launch (start us, length us, event | category | flops | bytes accessed | tf_op | source)
XLA Modules:
  0.0 81.6 jit_solution(10054938654365416627)
XLA Ops:
  0.0 0.0 copy-start.1
  0.0 2.4 %shard_map.82 = (s32[28]{0:T(128)}, bf16[32,5,4,128]{3,2,1,0:T(4,128)(2,1)}, bf16[4,5,4,128]{3,2,1,0:T(4,128)(2,1)}) custom-call(s32[2,128]{1,0:T(2,128)} %bitcast.16, s32[2,128]{1,0:T(2,128)} %bitcast.17, s32[2,128]{1,0:T(2,128)} %bitcast.18, s32[1,128]{1,0:T(1,128)} %bitcast.19, bf16[12,4,4,128]{3,2,1,0:T(4,128)(2,1)} %bitcast.15, bf16[12,4,2048]{2,1,0:T(4,128)(2,1)} %refs_5_.1), custom_call_target="tpu_custom_call" | custom-call | tf_op jit(solution)/shard_map/pallas_call | solution.py:268
  2.4 20.2 %all-to-all-start = ((bf16[32,5,4,128]{3,2,1,0:T(4,128)(2,1)}), bf16[32,5,4,128]{3,2,1,0:T(4,128)(2,1)S(1)}, u32[]{:S(2)}, u32[]{:S(2)}) async-start(bf16[32,5,4,128]{3,2,1,0:T(4,128)(2,1)} %get-tuple-element.15), calls=%async_computation | async-start | bytes 327680 | tf_op jit(solution)/shard_map/all_to_all | solution.py:252
  22.6 0.0 copy-done.1
  22.6 0.0 copy-start
  22.6 1.2 %copy-done = bf16[8,32,2048]{2,1,0:T(8,128)(2,1)S(1)} copy-done((bf16[8,32,2048]{2,1,0:T(8,128)(2,1)S(1)}, bf16[8,32,2048]{2,1,0:T(8,128)(2,1)}, u32[]{:S(2)}) %copy-start) | copy-done | bytes 1048600
  23.9 0.0 copy-start.2
  23.9 0.4 shard_map.84
  24.3 5.4 %collective-permute-start = (bf16[12,32,512]{2,1,0:T(8,128)(2,1)S(1)}, bf16[12,32,512]{2,1,0:T(8,128)(2,1)S(1)}, u32[]{:S(2)}, u32[]{:S(2)}) collective-permute-start(bf16[12,32,512]{2,1,0:T(8,128)(2,1)S(1)} %get-tuple-element.18), channel_id=1, source_target_pairs={{0,7},{1,6},{2,5},{3,4},{4,3},{5,2},{6,1},{7,0},{8,15},{9,14},{10,... | collective-permute-start | bytes 1179656 | tf_op jit(solution)/shard_map/ppermute | solution.py:298
  29.7 2.1 %collective-permute-start.1 = (bf16[12,32,512]{2,1,0:T(8,128)(2,1)S(1)}, bf16[12,32,512]{2,1,0:T(8,128)(2,1)S(1)}, u32[]{:S(2)}, u32[]{:S(2)}) collective-permute-start(bf16[12,32,512]{2,1,0:T(8,128)(2,1)S(1)} %get-tuple-element.19), channel_id=1, source_target_pairs={{0,4},{1,5},{2,6},{3,7},{4,0},{5,1},{6,2},{7,3},{8,12},{9,13},{10,... | collective-permute-start | bytes 1179656 | tf_op jit(solution)/shard_map/ppermute | solution.py:298
  31.8 2.1 %collective-permute-start.2 = (bf16[12,32,512]{2,1,0:T(8,128)(2,1)S(1)}, bf16[12,32,512]{2,1,0:T(8,128)(2,1)S(1)}, u32[]{:S(2)}, u32[]{:S(2)}) collective-permute-start(bf16[12,32,512]{2,1,0:T(8,128)(2,1)S(1)} %get-tuple-element.20), channel_id=1, source_target_pairs={{0,3},{1,2},{2,1},{3,0},{4,7},{5,6},{6,5},{7,4},{8,11},{9,10},{10,... | collective-permute-start | bytes 1179656 | tf_op jit(solution)/shard_map/ppermute | solution.py:298
  33.9 0.0 all-to-all-done.arrived
  33.9 0.0 copy-start.3
  33.9 0.0 copy-done.2
  33.9 0.6 copy-done.3
  34.6 1.3 %shard_map.83 = bf16[4,60,4,128]{3,2,1,0:T(4,128)(2,1)} custom-call(s32[28]{0:T(128)S(1)} %copy-done.3, bf16[32,5,4,128]{3,2,1,0:T(4,128)(2,1)S(1)} %all-to-all-done.arrived, bf16[4,5,4,128]{3,2,1,0:T(4,128)(2,1)S(1)} %copy-done.2), custom_call_target="tpu_custom_call" | custom-call | tf_op jit(solution)/shard_map/pallas_call | solution.py:300
  35.9 4.0 %all-to-all-start.1 = ((bf16[4,60,4,128]{3,2,1,0:T(4,128)(2,1)}), bf16[4,60,4,128]{3,2,1,0:T(4,128)(2,1)S(1)}, u32[]{:S(2)}, u32[]{:S(2)}) async-start(bf16[4,60,4,128]{3,2,1,0:T(4,128)(2,1)} %shard_map.83), calls=%async_computation.1 | async-start | bytes 491520 | tf_op jit(solution)/shard_map/all_to_all | solution.py:255
  39.9 0.0 collective-permute-done.rest_1_
  39.9 7.9 %collective-permute-done.1.rest_2_ = bf16[12,32,512]{2,1,0:T(8,128)(2,1)S(1)} collective-permute-done((bf16[12,32,512]{2,1,0:T(8,128)(2,1)S(1)}, bf16[12,32,512]{2,1,0:T(8,128)(2,1)S(1)}, u32[]{:S(2)}, u32[]{:S(2)}) %collective-permute-start.1) | collective-permute-done | bytes 393248 | tf_op jit(solution)/shard_map/ppermute | solution.py:298
  47.8 0.0 collective-permute-done.2.rest_3_
  47.8 0.0 all-to-all-done.1
  47.8 1.3 %shard_map.85 = bf16[4,208,128]{2,1,0:T(8,128)(2,1)S(1)} custom-call(s32[28]{0:T(128)S(1)} %copy-done.3, bf16[4,240,128]{2,1,0:T(8,128)(2,1)S(1)} %bitcast.13, bf16[12,32,512]{2,1,0:T(8,128)(2,1)S(1)} %get-tuple-element.17.rest_0_, bf16[12,32,512]{2,1,0:T(8,128)(2,1)S(1)} %collective-permute-done.rest_1_, ...), custom_call_target="tpu_custom_call" | custom-call | flops 100000000 | bytes 3145728 | tf_op jit(solution)/shard_map/pallas_call | solution.py:305
  49.1 9.5 %all_to_all.20.gathered = bf16[4,208,128]{2,1,0:T(8,128)(2,1)S(1)} all-to-all(bf16[4,208,128]{2,1,0:T(8,128)(2,1)S(1)} %shard_map.85), channel_id=1, replica_groups={{0,1,12,13},{2,3,14,15},{4,5,8,9},{6,7,10,11},{16,17,28,29},{18,19,30,3..., dimensions={0} | all-to-all | bytes 425984 | tf_op jit(solution)/shard_map/all_to_all | solution.py:255
  58.6 1.5 %shard_map.86 = (bf16[32,16,128]{2,1,0:T(8,128)(2,1)S(1)}, bf16[4,16,128]{2,1,0:T(8,128)(2,1)S(1)}) custom-call(s32[28]{0:T(128)S(1)} %copy-done.3, bf16[4,208,128]{2,1,0:T(8,128)(2,1)S(1)} %all_to_all.20.gathered, bf16[4,240,128]{2,1,0:T(8,128)(2,1)S(1)} %bitcast.14), custom_call_target="tpu_custom_call" | custom-call | tf_op jit(solution)/shard_map/pallas_call | solution.py:319
  60.0 20.4 %all_to_all.21.returned = bf16[32,16,128]{2,1,0:T(8,128)(2,1)S(1)} all-to-all(bf16[32,16,128]{2,1,0:T(8,128)(2,1)S(1)} %get-tuple-element.21), channel_id=1, replica_groups={{256,496,224,464,192,432,160,400,128,368,96,336,64,304,32,272,0,240,480..., dimensions={0} | all-to-all | bytes 262144 | tf_op jit(solution)/shard_map/all_to_all | solution.py:252
  80.4 1.2 %shard_map.87 = bf16[12,16,128]{2,1,0:T(8,128)(2,1)} custom-call(s32[28]{0:T(128)S(1)} %copy-done.3, bf16[32,16,128]{2,1,0:T(8,128)(2,1)S(1)} %all_to_all.21.returned, bf16[4,16,128]{2,1,0:T(8,128)(2,1)S(1)} %get-tuple-element.22.kept), custom_call_target="tpu_custom_call" | custom-call | tf_op jit(solution)/shard_map/pallas_call | solution.py:326
Async XLA Ops:
  0.0 22.6 %copy-start.1 = (bf16[4,32,2048]{2,1,0:T(8,128)(2,1)S(1)}, bf16[4,32,2048]{2,1,0:T(8,128)(2,1)}, u32[]{:S(2)}) copy-start(bf16[4,32,2048]{2,1,0:T(8,128)(2,1)} %resident.1) | copy-start | bytes 1572868
  2.4 31.5 %all-to-all-start = ((bf16[32,5,4,128]{3,2,1,0:T(4,128)(2,1)}), bf16[32,5,4,128]{3,2,1,0:T(4,128)(2,1)S(1)}, u32[]{:S(2)}, u32[]{:S(2)}) async-start(bf16[32,5,4,128]{3,2,1,0:T(4,128)(2,1)} %get-tuple-element.15), calls=%async_computation | async-start | bytes 327680 | tf_op jit(solution)/shard_map/all_to_all | solution.py:252
  22.6 1.2 %copy-start = (bf16[8,32,2048]{2,1,0:T(8,128)(2,1)S(1)}, bf16[8,32,2048]{2,1,0:T(8,128)(2,1)}, u32[]{:S(2)}) copy-start(bf16[8,32,2048]{2,1,0:T(8,128)(2,1)} %moved.1) | copy-start | bytes 3145732
  23.9 10.1 %copy-start.2 = (bf16[4,5,4,128]{3,2,1,0:T(4,128)(2,1)S(1)}, bf16[4,5,4,128]{3,2,1,0:T(4,128)(2,1)}, u32[]{:S(2)}) copy-start(bf16[4,5,4,128]{3,2,1,0:T(4,128)(2,1)} %get-tuple-element.16.kept) | copy-start | bytes 61444
  24.3 15.6 %collective-permute-start = (bf16[12,32,512]{2,1,0:T(8,128)(2,1)S(1)}, bf16[12,32,512]{2,1,0:T(8,128)(2,1)S(1)}, u32[]{:S(2)}, u32[]{:S(2)}) collective-permute-start(bf16[12,32,512]{2,1,0:T(8,128)(2,1)S(1)} %get-tuple-element.18), channel_id=1, source_target_pairs={{0,7},{1,6},{2,5},{3,4},{4,3},{5,2},{6,1},{7,0},{8,15},{9,14},{10,... | collective-permute-start | bytes 1179656 | tf_op jit(solution)/shard_map/ppermute | solution.py:298
  29.7 18.1 %collective-permute-start.1 = (bf16[12,32,512]{2,1,0:T(8,128)(2,1)S(1)}, bf16[12,32,512]{2,1,0:T(8,128)(2,1)S(1)}, u32[]{:S(2)}, u32[]{:S(2)}) collective-permute-start(bf16[12,32,512]{2,1,0:T(8,128)(2,1)S(1)} %get-tuple-element.19), channel_id=1, source_target_pairs={{0,4},{1,5},{2,6},{3,7},{4,0},{5,1},{6,2},{7,3},{8,12},{9,13},{10,... | collective-permute-start | bytes 1179656 | tf_op jit(solution)/shard_map/ppermute | solution.py:298
  31.8 16.0 %collective-permute-start.2 = (bf16[12,32,512]{2,1,0:T(8,128)(2,1)S(1)}, bf16[12,32,512]{2,1,0:T(8,128)(2,1)S(1)}, u32[]{:S(2)}, u32[]{:S(2)}) collective-permute-start(bf16[12,32,512]{2,1,0:T(8,128)(2,1)S(1)} %get-tuple-element.20), channel_id=1, source_target_pairs={{0,3},{1,2},{2,1},{3,0},{4,7},{5,6},{6,5},{7,4},{8,11},{9,10},{10,... | collective-permute-start | bytes 1179656 | tf_op jit(solution)/shard_map/ppermute | solution.py:298
  33.9 0.7 copy-start.3
  35.9 11.9 %all-to-all-start.1 = ((bf16[4,60,4,128]{3,2,1,0:T(4,128)(2,1)}), bf16[4,60,4,128]{3,2,1,0:T(4,128)(2,1)S(1)}, u32[]{:S(2)}, u32[]{:S(2)}) async-start(bf16[4,60,4,128]{3,2,1,0:T(4,128)(2,1)} %shard_map.83), calls=%async_computation.1 | async-start | bytes 491520 | tf_op jit(solution)/shard_map/all_to_all | solution.py:255

commit v12 on v4

--- a/solution.py
+++ b/solution.py
@@ -15,6 +15,7 @@
 RES = 4
 SLOTS = MIG + RES
 GROUPS = 32
+FIRST_G, STRIDE_G = 16, 15
 SHARDS = 16
 SIDE = 4
 STRIDE = 32
@@ -29,7 +30,7 @@
 FLOOR = -(2.0**100)
 SCALE = 1.0 / math.sqrt(HD)
 LIMIT = 48 * 1024 * 1024
-FULL = 63 * 1024 * 1024
+FULL = 60 * 1024 * 1024
 BF = jnp.bfloat16
 F32 = jnp.float32
 
@@ -38,12 +39,14 @@
 HB = pl.BlockSpec(memory_space=pltpu.HBM)
 
 
-def call(kernel, outs, specs, flops=0, moved=0, scratch=(), limit=LIMIT):
+ANY = pl.BlockSpec(memory_space=pl.ANY)
+
+def call(kernel, outs, specs, flops=0, moved=0, scratch=(), limit=LIMIT, places=None):
     return pl.pallas_call(
         kernel,
         out_shape=outs,
         in_specs=specs,
-        out_specs=jax.tree.map(lambda _: VM, outs),
+        out_specs=jax.tree.map(lambda _: VM, outs) if places is None else places,
         scratch_shapes=scratch,
         compiler_params=pltpu.CompilerParams(vmem_limit_bytes=limit),
         cost_estimate=pl.CostEstimate(flops=flops, bytes_accessed=moved, transcendentals=0),
@@ -61,6 +64,10 @@
 def place_of():
     shard = lax.axis_index("tensor")
     return shard // SIDE, shard % SIDE
+
+
+def listed(group):
+    return (group * STRIDE_G + FIRST_G) % GROUPS
 
 
 def pack_kernel(named, holders, asked, fresh, sent, kept, asked_here, fresh_here, named_here, holders_here, sems):
@@ -90,16 +97,16 @@
     groups = []
     for slot in range(RES, SLOTS):
         mine = names == lax.axis_index("group") * SLOTS + slot
-        groups.append(jnp.sum(jnp.where(mine, slots, 0.0)).astype(jnp.int32) // MIG)
+        groups.append(jnp.sum(jnp.where(mine, slots, 0.0)).astype(jnp.int32) >> 3)
     for slot, group in zip(range(RES, SLOTS), groups):
-        sent[group, :HEADS] = asked_here[slot]
-        sent[group, HEADS] = fresh_here[slot]
+        sent[listed(group), :HEADS] = asked_here[slot]
+        sent[listed(group), HEADS] = fresh_here[slot]
 
 
 def split_kernel(moved, resident, *outs):
-    here = place_of()
+    y, x = place_of()
     for step, out in enumerate(outs):
-        low, half = class_of(*swapped(step, *here))
+        low, half = class_of(*swapped(step, y, x))
         for place, pair in enumerate((2 * low + half, 6 - 2 * low + half)):
             for part in range(2):
                 lanes = pl.ds(pl.multiple_of(pair * HD + part * FEATURES, HD), HD)
@@ -110,7 +117,7 @@
 
 def spread_kernel(origin, arrived, kept, asking):
     for row in range(SLOTS):
-        chunk = arrived.at[origin[row]] if row < MIG else kept.at[row - MIG]
+        chunk = arrived.at[listed(origin[row])] if row < MIG else kept.at[row - MIG]
         for peer in range(SIDE):
             asking[peer, row * HEADS : (row + 1) * HEADS] = chunk[:HEADS]
             asking[peer, SLOTS * HEADS + row] = chunk[HEADS]
@@ -123,7 +130,8 @@
 def partial_kernel(lengths, asking, *rest):
     *blocks, payload, scores, weights, stats = rest
     column = lax.broadcasted_iota(jnp.int32, (1, HD), 1)
-    y, x = swapped(column // STRIDE, *place_of())
+    block = column // STRIDE
+    y, x = swapped(jnp.where(block == 0, 0, (block + 1) % 3 + 1), *place_of())
     position = (y * SIDE + x) * STRIDE + column % STRIDE
 
     def stored(row, place):
@@ -167,7 +175,7 @@
             payload[2 * pair + 1, span, :] = blended[QROWS:]
 
 
-def merge_kernel(origin, gathered, everyone, sent, kept):
+def merge_kernel(origin, target, gathered, everyone, sent, kept):
     y, x = place_of()
     first = jnp.where(y > 1, 2, 0)
     asked = everyone[first + x % 2, :ROWS, :]
@@ -201,7 +209,7 @@
 
     sent[...] = jnp.zeros_like(sent)
     for slot in range(MIG):
-        sent[origin[slot]] = result[slot * QROWS : (slot + 1) * QROWS]
+        sent[listed(origin[slot])] = result[slot * QROWS : (slot + 1) * QROWS]
     for slot in range(RES):
         kept[slot] = result[(MIG + slot) * QROWS : (MIG + slot + 1) * QROWS]
 
@@ -210,7 +218,7 @@
     for slot in range(RES):
         out[slot] = kept[slot]
     for slot in range(MIG):
-        out[RES + slot] = returned[target[slot]]
+        out[RES + slot] = returned[listed(target[slot])]
 
 
 def body(
@@ -226,6 +234,11 @@
     shape = jax.ShapeDtypeStruct
     whole = [(y, x) for y in range(SIDE) for x in range(SIDE)]
     peers = [[y * SIDE + x for y in (low, 3 - low) for x in (2 * half, 2 * half + 1)] for low in range(2) for half in range(2)]
+
+    turned = [[listed(place) for place in range(GROUPS)]]
+
+    def around(array):
+        return lax.all_to_all(array, "group", 0, 0, axis_index_groups=turned, tiled=True)
 
     def across(array):
         return lax.all_to_all(array, "tensor", 0, 0, axis_index_groups=peers, tiled=True)
@@ -244,11 +257,11 @@
         ],
         limit=FULL,
     )(decode_slot.reshape(2, HD), prefill_slot.reshape(2, HD), asked, new_entries)
-    arrived = lax.all_to_all(sent, "group", 0, 0, tiled=True)
-
-    later = (resident_kept, kept_tokens, prefill_slot, decode_slot, prefill_cache, resident_cache)
+    arrived = around(sent)
+
+    later = (resident_kept, kept_tokens, prefill_slot, decode_slot)
     later, kept = lax.optimization_barrier((later, kept))
-    resident_kept, kept_tokens, prefill_slot, decode_slot, prefill_cache, resident_cache = later
+    resident_kept, kept_tokens, prefill_slot, decode_slot = later
     group = lax.axis_index("group")
 
     def looked_up(names, first, values):
@@ -268,7 +281,7 @@
         moved=3 * 2**20,
     )(prefill_cache, resident_cache)
     blocks = [split[0]]
-    for step in range(1, SIDE):
+    for step in (3, 1, 2):
         steps = []
         for y, x in whole:
             other, side = swapped(step, y, x)
@@ -297,9 +310,9 @@
     finished, here = call(
         merge_kernel,
         (shape((GROUPS, QROWS, HD), BF), shape((RES, QROWS, HD), BF)),
-        [SM, VM, VM],
-    )(origin, gathered, everyone)
-    returned = lax.all_to_all(finished, "group", 0, 0, tiled=True)
+        [SM, SM, VM, VM],
+    )(origin, target, gathered, everyone)
+    returned = around(finished)
 
     result = call(select_kernel, shape((SLOTS, QROWS, HD), BF), [SM, VM, VM])(target, returned, here)
     result = result.reshape(SLOTS, HEADS, STEPS, HD).transpose(0, 2, 1, 3)

time: 91.7 us -> 82.1 us (0.90)
  waiting for transfers between devices: 24.5 us -> 12.1 us
  blocking collectives: 8.04 us -> 20.4 us
  starting transfers between devices: 46 us -> 37.8 us
    all_to_all x2 -> x1, waiting for transfers between devices: 19.9 us -> 0.01 us  [around(): lax.all_to_all(array, 'group', 0, 0, axis_index_groups=turned, tiled=True)]
    all_to_all x1, blocking collectives: 8.04 us -> 20.4 us  [around(): lax.all_to_all(array, 'group', 0, 0, axis_index_groups=turned, tiled=True)]
    all_to_all x2 -> x1, starting transfers between devices: 31.4 us -> 20.2 us  [around(): lax.all_to_all(array, 'group', 0, 0, axis_index_groups=turned, tiled=True)]
    all_to_all x1 -> x2, waiting for transfers between devices: 1.44 us -> 5.32 us  [across(): lax.all_to_all(array, 'tensor', 0, 0, axis_index_groups=peers, tiled=True)]
    ppermute x3, waiting for transfers between devices: 3.14 us -> 6.76 us  [body(): blocks.append(lax.ppermute(split[step], 'tensor', steps))]
    all_to_all x1 -> x2, starting transfers between devices: 4.93 us -> 8.01 us  [across(): lax.all_to_all(array, 'tensor', 0, 0, axis_index_groups=peers, tiled=True)]
  transfers between devices with their start and end apart: 6 -> 6, of which waited for: 4 -> 2; matrix products, arithmetic and copies ran while one was open for 0% -> 0% of each run, Pallas kernels for 3% -> 2%
where the time goes in v12:
time: 82.1 us; the launch traced here: 81.5 us
  starting transfers between devices  37.8 us (46%)
  blocking collectives  20.4 us (25%)
  waiting for transfers between devices  12.1 us (15%)
  Pallas kernels  8.17 us (10%)
  local copies, waits for them, and re-layouts  2.63 us (3%)
    all_to_all x1, blocking collectives, around(): lax.all_to_all(array, 'group', 0, 0, axis_index_groups=turned, tiled=True)  20.4 us
    all_to_all x1, starting transfers between devices, around(): lax.all_to_all(array, 'group', 0, 0, axis_index_groups=turned, tiled=True)  20.2 us
    ppermute x3, starting transfers between devices, body(): blocks.append(lax.ppermute(split[step], 'tensor', steps))  9.58 us
    all_to_all x2, starting transfers between devices, across(): lax.all_to_all(array, 'tensor', 0, 0, axis_index_groups=peers, tiled=True)  8.01 us
    ppermute x3, waiting for transfers between devices, body(): blocks.append(lax.ppermute(split[step], 'tensor', steps))  6.76 us
    all_to_all x2, waiting for transfers between devices, across(): lax.all_to_all(array, 'tensor', 0, 0, axis_index_groups=peers, tiled=True)  5.32 us
    unnamed x14, local copies, waits for them, and re-layouts  2.55 us
    pallas_call x1, Pallas kernels, body(): call(partial_kernel, shape((SIDE, PAYLOAD, HD), BF), [SM] + [VM] * (1 + S...  2.02 us
  transfers between devices with their start and end apart: 6, of which 2 were waited for; matrix products, arithmetic and copies ran while one was open for 0% of the time, Pallas kernels for 2%

profile of v12, /device:TPU:1, one launch (start us, length us, event | category | flops | bytes accessed | tf_op | source)
XLA Modules:
  0.0 81.5 jit_solution(13269891012223528522)
XLA Ops:
  0.0 0.0 copy-start.1
  0.0 1.8 %shard_map.82 = (bf16[32,5,4,128]{3,2,1,0:T(4,128)(2,1)}, bf16[4,5,4,128]{3,2,1,0:T(4,128)(2,1)}) custom-call(s32[2,128]{1,0:T(2,128)} %bitcast.15, s32[2,128]{1,0:T(2,128)} %bitcast.14, bf16[12,4,4,128]{3,2,1,0:T(4,128)(2,1)} %bitcast.13, bf16[12,4,2048]{2,1,0:T(4,128)(2,1)} %fresh.1), custom_call_target="tpu_custom_call" | custom-call | tf_op jit(solution)/shard_map/pallas_call | solution.py:247
  1.8 20.2 %all-to-all-start = ((bf16[32,5,4,128]{3,2,1,0:T(4,128)(2,1)}), bf16[32,5,4,128]{3,2,1,0:T(4,128)(2,1)S(1)}, u32[]{:S(2)}, u32[]{:S(2)}) async-start(bf16[32,5,4,128]{3,2,1,0:T(4,128)(2,1)} %get-tuple-element.23), calls=%async_computation | async-start | bytes 327680 | tf_op jit(solution)/shard_map/all_to_all | solution.py:241
  22.0 0.0 copy-done.1
  22.0 0.0 copy-start
  22.0 1.2 %copy-done = bf16[8,32,2048]{2,1,0:T(8,128)(2,1)S(1)} copy-done((bf16[8,32,2048]{2,1,0:T(8,128)(2,1)S(1)}, bf16[8,32,2048]{2,1,0:T(8,128)(2,1)}, u32[]{:S(2)}) %copy-start) | copy-done | bytes 1048600
  23.2 0.4 shard_map.84
  23.6 0.0 copy-start.2
  23.7 5.4 %collective-permute-start = (bf16[12,32,512]{2,1,0:T(8,128)(2,1)S(1)}, bf16[12,32,512]{2,1,0:T(8,128)(2,1)S(1)}, u32[]{:S(2)}, u32[]{:S(2)}) collective-permute-start(bf16[12,32,512]{2,1,0:T(8,128)(2,1)S(1)} %get-tuple-element.26), channel_id=1, source_target_pairs={{0,7},{1,6},{2,5},{3,4},{4,3},{5,2},{6,1},{7,0},{8,15},{9,14},{10,... | collective-permute-start | bytes 1179656 | tf_op jit(solution)/shard_map/ppermute | solution.py:289
  29.1 0.0 copy-start.4
  29.1 0.0 copy-start.5
  29.1 2.1 %collective-permute-start.1 = (bf16[12,32,512]{2,1,0:T(8,128)(2,1)S(1)}, bf16[12,32,512]{2,1,0:T(8,128)(2,1)S(1)}, u32[]{:S(2)}, u32[]{:S(2)}) collective-permute-start(bf16[12,32,512]{2,1,0:T(8,128)(2,1)S(1)} %get-tuple-element.27), channel_id=1, source_target_pairs={{0,4},{1,5},{2,6},{3,7},{4,0},{5,1},{6,2},{7,3},{8,12},{9,13},{10,... | collective-permute-start | bytes 1179656 | tf_op jit(solution)/shard_map/ppermute | solution.py:289
  31.2 2.1 %collective-permute-start.2 = (bf16[12,32,512]{2,1,0:T(8,128)(2,1)S(1)}, bf16[12,32,512]{2,1,0:T(8,128)(2,1)S(1)}, u32[]{:S(2)}, u32[]{:S(2)}) collective-permute-start(bf16[12,32,512]{2,1,0:T(8,128)(2,1)S(1)} %get-tuple-element.28), channel_id=1, source_target_pairs={{0,3},{1,2},{2,1},{3,0},{4,7},{5,6},{6,5},{7,4},{8,11},{9,10},{10,... | collective-permute-start | bytes 1179656 | tf_op jit(solution)/shard_map/ppermute | solution.py:289
  33.3 0.0 copy-start.3
  33.3 0.0 copy-done.4
  33.3 0.0 copy-done.5
  33.3 0.7 copy-done.3
  34.0 0.2 fusion
  34.2 0.0 all-to-all-done.arrived
  34.2 0.0 copy-done.2
  34.2 1.3 %shard_map.83 = bf16[4,60,4,128]{3,2,1,0:T(4,128)(2,1)} custom-call(s32[8]{0:T(128)S(1)} %and_select_fusion.origin, bf16[32,5,4,128]{3,2,1,0:T(4,128)(2,1)S(1)} %all-to-all-done.arrived, bf16[4,5,4,128]{3,2,1,0:T(4,128)(2,1)S(1)} %copy-done.2), custom_call_target="tpu_custom_call" | custom-call | tf_op jit(solution)/shard_map/pallas_call | solution.py:291
  35.5 4.0 %all-to-all-start.1 = ((bf16[4,60,4,128]{3,2,1,0:T(4,128)(2,1)}), bf16[4,60,4,128]{3,2,1,0:T(4,128)(2,1)S(1)}, u32[]{:S(2)}, u32[]{:S(2)}) async-start(bf16[4,60,4,128]{3,2,1,0:T(4,128)(2,1)} %shard_map.83), calls=%async_computation.1 | async-start | bytes 491520 | tf_op jit(solution)/shard_map/all_to_all | solution.py:244
  39.6 0.0 copy-start.6
  39.6 0.7 copy-done.6
  40.2 0.1 dynamic_slice.3
  40.3 0.1 pad_add_fusion.lengths
  40.4 0.0 collective-permute-done.rest_1_
  40.4 6.8 %collective-permute-done.1.rest_2_ = bf16[12,32,512]{2,1,0:T(8,128)(2,1)S(1)} collective-permute-done((bf16[12,32,512]{2,1,0:T(8,128)(2,1)S(1)}, bf16[12,32,512]{2,1,0:T(8,128)(2,1)S(1)}, u32[]{:S(2)}, u32[]{:S(2)}) %collective-permute-start.1) | collective-permute-done | bytes 393248 | tf_op jit(solution)/shard_map/ppermute | solution.py:289
  47.1 0.0 collective-permute-done.2.rest_3_
  47.1 0.0 all-to-all-done.1
  47.1 2.0 %shard_map.85 = bf16[4,208,128]{2,1,0:T(8,128)(2,1)} custom-call(s32[12]{0:T(128)S(1)} %pad_add_fusion.lengths, bf16[4,240,128]{2,1,0:T(8,128)(2,1)S(1)} %bitcast.11, bf16[12,32,512]{2,1,0:T(8,128)(2,1)S(1)} %get-tuple-element.25.rest_0_, bf16[12,32,512]{2,1,0:T(8,128)(2,1)S(1)} %collective-permute-done.rest_1_, ...), custom_call_target="tpu_custom_call" | custom-call | flops 100000000 | bytes 3145728 | tf_op jit(solution)/shard_map/pallas_call | solution.py:296
  49.1 4.0 %all-to-all-start.2 = ((bf16[4,208,128]{2,1,0:T(8,128)(2,1)}), bf16[4,208,128]{2,1,0:T(8,128)(2,1)S(1)}, u32[]{:S(2)}, u32[]{:S(2)}) async-start(bf16[4,208,128]{2,1,0:T(8,128)(2,1)} %shard_map.85), calls=%async_computation.2 | async-start | bytes 425984 | tf_op jit(solution)/shard_map/all_to_all | solution.py:244
  53.2 5.3 %all-to-all-done.2.gathered = bf16[4,208,128]{2,1,0:T(8,128)(2,1)S(1)} async-done(((bf16[4,208,128]{2,1,0:T(8,128)(2,1)}), bf16[4,208,128]{2,1,0:T(8,128)(2,1)S(1)}, u32[]{:S(2)}, u32[]{:S(2)}) %all-to-all-start.2) | async-done | bytes 213024 | tf_op jit(solution)/shard_map/all_to_all | solution.py:244
  58.5 1.5 %shard_map.86 = (bf16[32,16,128]{2,1,0:T(8,128)(2,1)S(1)}, bf16[4,16,128]{2,1,0:T(8,128)(2,1)S(1)}) custom-call(s32[8]{0:T(128)S(1)} %and_select_fusion.origin, s32[8]{0:T(128)S(1)} %and_select_fusion.1.target, bf16[4,208,128]{2,1,0:T(8,128)(2,1)S(1)} %all-to-all-done.2.gathered, bf16[4,240,128]{2,1,0:T(8,128)(2,1)S(1)} %bitcast.12), custom_call_target="tpu_custom_call" | custom-call | tf_op jit(solution)/shard_map/pallas_call | solution.py:310
  60.0 20.4 %all_to_all.20.returned = bf16[32,16,128]{2,1,0:T(8,128)(2,1)S(1)} all-to-all(bf16[32,16,128]{2,1,0:T(8,128)(2,1)S(1)} %get-tuple-element.29), channel_id=1, replica_groups={{256,496,224,464,192,432,160,400,128,368,96,336,64,304,32,272,0,240,480..., dimensions={0} | all-to-all | bytes 262144 | tf_op jit(solution)/shard_map/all_to_all | solution.py:241
  80.3 1.2 %shard_map.87 = bf16[12,16,128]{2,1,0:T(8,128)(2,1)} custom-call(s32[8]{0:T(128)S(1)} %and_select_fusion.1.target, bf16[32,16,128]{2,1,0:T(8,128)(2,1)S(1)} %all_to_all.20.returned, bf16[4,16,128]{2,1,0:T(8,128)(2,1)S(1)} %get-tuple-element.30.kept), custom_call_target="tpu_custom_call" | custom-call | tf_op jit(solution)/shard_map/pallas_call | solution.py:317
  (3 shorter events, 0.0 us)
Async XLA Ops:
  0.0 22.0 %copy-start.1 = (bf16[4,32,2048]{2,1,0:T(8,128)(2,1)S(1)}, bf16[4,32,2048]{2,1,0:T(8,128)(2,1)}, u32[]{:S(2)}) copy-start(bf16[4,32,2048]{2,1,0:T(8,128)(2,1)} %resident.1) | copy-start | bytes 1572868
  1.8 32.5 %all-to-all-start = ((bf16[32,5,4,128]{3,2,1,0:T(4,128)(2,1)}), bf16[32,5,4,128]{3,2,1,0:T(4,128)(2,1)S(1)}, u32[]{:S(2)}, u32[]{:S(2)}) async-start(bf16[32,5,4,128]{3,2,1,0:T(4,128)(2,1)} %get-tuple-element.23), calls=%async_computation | async-start | bytes 327680 | tf_op jit(solution)/shard_map/all_to_all | solution.py:241
  22.0 1.2 %copy-start = (bf16[8,32,2048]{2,1,0:T(8,128)(2,1)S(1)}, bf16[8,32,2048]{2,1,0:T(8,128)(2,1)}, u32[]{:S(2)}) copy-start(bf16[8,32,2048]{2,1,0:T(8,128)(2,1)} %moved.1) | copy-start | bytes 3145732
  23.6 10.6 %copy-start.2 = (bf16[4,5,4,128]{3,2,1,0:T(4,128)(2,1)S(1)}, bf16[4,5,4,128]{3,2,1,0:T(4,128)(2,1)}, u32[]{:S(2)}) copy-start(bf16[4,5,4,128]{3,2,1,0:T(4,128)(2,1)} %get-tuple-element.24.kept) | copy-start | bytes 61444
  23.7 16.7 %collective-permute-start = (bf16[12,32,512]{2,1,0:T(8,128)(2,1)S(1)}, bf16[12,32,512]{2,1,0:T(8,128)(2,1)S(1)}, u32[]{:S(2)}, u32[]{:S(2)}) collective-permute-start(bf16[12,32,512]{2,1,0:T(8,128)(2,1)S(1)} %get-tuple-element.26), channel_id=1, source_target_pairs={{0,7},{1,6},{2,5},{3,4},{4,3},{5,2},{6,1},{7,0},{8,15},{9,14},{10,... | collective-permute-start | bytes 1179656 | tf_op jit(solution)/shard_map/ppermute | solution.py:289
  29.1 4.3 %copy-start.4 = (s32[256]{0:T(256)S(1)}, s32[256]{0:T(256)}, u32[]{:S(2)}) copy-start(s32[256]{0:T(256)} %param.15) | copy-start | bytes 3076
  29.1 4.3 %copy-start.5 = (s32[256]{0:T(256)S(1)}, s32[256]{0:T(256)}, u32[]{:S(2)}) copy-start(s32[256]{0:T(256)} %param.13) | copy-start | bytes 3076
  29.1 18.0 %collective-permute-start.1 = (bf16[12,32,512]{2,1,0:T(8,128)(2,1)S(1)}, bf16[12,32,512]{2,1,0:T(8,128)(2,1)S(1)}, u32[]{:S(2)}, u32[]{:S(2)}) collective-permute-start(bf16[12,32,512]{2,1,0:T(8,128)(2,1)S(1)} %get-tuple-element.27), channel_id=1, source_target_pairs={{0,4},{1,5},{2,6},{3,7},{4,0},{5,1},{6,2},{7,3},{8,12},{9,13},{10,... | collective-permute-start | bytes 1179656 | tf_op jit(solution)/shard_map/ppermute | solution.py:289
  31.2 16.0 %collective-permute-start.2 = (bf16[12,32,512]{2,1,0:T(8,128)(2,1)S(1)}, bf16[12,32,512]{2,1,0:T(8,128)(2,1)S(1)}, u32[]{:S(2)}, u32[]{:S(2)}) collective-permute-start(bf16[12,32,512]{2,1,0:T(8,128)(2,1)S(1)} %get-tuple-element.28), channel_id=1, source_target_pairs={{0,3},{1,2},{2,1},{3,0},{4,7},{5,6},{6,5},{7,4},{8,11},{9,10},{10,... | collective-permute-start | bytes 1179656 | tf_op jit(solution)/shard_map/ppermute | solution.py:289
  33.3 0.7 copy-start.3
  35.5 11.6 %all-to-all-start.1 = ((bf16[4,60,4,128]{3,2,1,0:T(4,128)(2,1)}), bf16[4,60,4,128]{3,2,1,0:T(4,128)(2,1)S(1)}, u32[]{:S(2)}, u32[]{:S(2)}) async-start(bf16[4,60,4,128]{3,2,1,0:T(4,128)(2,1)} %shard_map.83), calls=%async_computation.1 | async-start | bytes 491520 | tf_op jit(solution)/shard_map/all_to_all | solution.py:244
  39.6 0.7 copy-start.6
  49.1 9.3 %all-to-all-start.2 = ((bf16[4,208,128]{2,1,0:T(8,128)(2,1)}), bf16[4,208,128]{2,1,0:T(8,128)(2,1)S(1)}, u32[]{:S(2)}, u32[]{:S(2)}) async-start(bf16[4,208,128]{2,1,0:T(8,128)(2,1)} %shard_map.85), calls=%async_computation.2 | async-start | bytes 425984 | tf_op jit(solution)/shard_map/all_to_all | solution.py:244

commit v13 on v12

--- a/solution.py
+++ b/solution.py
@@ -127,7 +127,7 @@
     return lax.dot_general(left, right, (((1,), (1,)), ((), ())), preferred_element_type=F32) * SCALE
 
 
-def partial_kernel(lengths, asking, *rest):
+def partial_kernel(lengths, target, asking, *rest):
     *blocks, payload, scores, weights, stats = rest
     column = lax.broadcasted_iota(jnp.int32, (1, HD), 1)
     block = column // STRIDE
@@ -296,7 +296,7 @@
     payload = call(
         partial_kernel,
         shape((SIDE, PAYLOAD, HD), BF),
-        [SM] + [VM] * (1 + SIDE),
+        [SM, SM] + [VM] * (1 + SIDE),
         flops=10**8,
         moved=3 * 2**20,
         scratch=[
@@ -304,7 +304,7 @@
             pltpu.VMEM((SIDE, ROWS, HD), BF),
             pltpu.VMEM((2 * HD, HD), F32),
         ],
-    )(lengths, everyone, *blocks)
+    )(lengths, target, everyone, *blocks)
     gathered = across(payload)
 
     finished, here = call(

time: 82.1 us -> 81.5 us (level)
  blocking collectives: 20.4 us -> 29.9 us
  waiting for transfers between devices: 12.1 us -> 7.38 us
  starting transfers between devices: 37.8 us -> 33.8 us
    all_to_all x0 -> x1, blocking collectives: none -> 9.49 us  [across(): lax.all_to_all(array, 'tensor', 0, 0, axis_index_groups=peers, tiled=True)]
    all_to_all x2 -> x1, waiting for transfers between devices: 5.32 us -> 0.01 us  [across(): lax.all_to_all(array, 'tensor', 0, 0, axis_index_groups=peers, tiled=True)]
    all_to_all x2 -> x1, starting transfers between devices: 8.01 us -> 4 us  [across(): lax.all_to_all(array, 'tensor', 0, 0, axis_index_groups=peers, tiled=True)]
  transfers between devices with their start and end apart: 6 -> 5, of which waited for: 2 -> 1; matrix products, arithmetic and copies ran while one was open for 0% -> 0% of each run, Pallas kernels for 2% -> 2%
where the time goes in v13:
time: 81.5 us; the launch traced here: 81 us
  starting transfers between devices  33.8 us (41%)
  blocking collectives  29.9 us (37%)
  Pallas kernels  7.45 us (9%)
  waiting for transfers between devices  7.38 us (9%)
  local copies, waits for them, and re-layouts  2 us (2%)
    all_to_all x1, blocking collectives, around(): lax.all_to_all(array, 'group', 0, 0, axis_index_groups=turned, tiled=True)  20.4 us
    all_to_all x1, starting transfers between devices, around(): lax.all_to_all(array, 'group', 0, 0, axis_index_groups=turned, tiled=True)  20.2 us
    ppermute x3, starting transfers between devices, body(): blocks.append(lax.ppermute(split[step], 'tensor', steps))  9.58 us
    all_to_all x1, blocking collectives, across(): lax.all_to_all(array, 'tensor', 0, 0, axis_index_groups=peers, tiled=True)  9.49 us
    ppermute x3, waiting for transfers between devices, body(): blocks.append(lax.ppermute(split[step], 'tensor', steps))  7.38 us
    all_to_all x1, starting transfers between devices, across(): lax.all_to_all(array, 'tensor', 0, 0, axis_index_groups=peers, tiled=True)  4 us
    unnamed x14, local copies, waits for them, and re-layouts  1.92 us
    pallas_call x1, Pallas kernels, body(): call(pack_kernel, (shape((GROUPS, TILES, STEPS, HD), BF), shape((RES, TIL...  1.75 us
  transfers between devices with their start and end apart: 5, of which 1 were waited for; matrix products, arithmetic and copies ran while one was open for 0% of the time, Pallas kernels for 2%

profile of v13, /device:TPU:1, one launch (start us, length us, event | category | flops | bytes accessed | tf_op | source)
XLA Modules:
  0.0 81.0 jit_solution(1087805244448517565)
XLA Ops:
  0.0 0.0 copy-start.1
  0.0 1.7 %shard_map.82 = (bf16[32,5,4,128]{3,2,1,0:T(4,128)(2,1)}, bf16[4,5,4,128]{3,2,1,0:T(4,128)(2,1)}) custom-call(s32[2,128]{1,0:T(2,128)} %bitcast.15, s32[2,128]{1,0:T(2,128)} %bitcast.14, bf16[12,4,4,128]{3,2,1,0:T(4,128)(2,1)} %bitcast.13, bf16[12,4,2048]{2,1,0:T(4,128)(2,1)} %fresh.1), custom_call_target="tpu_custom_call" | custom-call | tf_op jit(solution)/shard_map/pallas_call | solution.py:247
  1.8 20.2 %all-to-all-start = ((bf16[32,5,4,128]{3,2,1,0:T(4,128)(2,1)}), bf16[32,5,4,128]{3,2,1,0:T(4,128)(2,1)S(1)}, u32[]{:S(2)}, u32[]{:S(2)}) async-start(bf16[32,5,4,128]{3,2,1,0:T(4,128)(2,1)} %get-tuple-element.23), calls=%async_computation | async-start | bytes 327680 | tf_op jit(solution)/shard_map/all_to_all | solution.py:241
  22.0 0.0 copy-done.1
  22.0 0.0 copy-start
  22.0 1.2 %copy-done = bf16[8,32,2048]{2,1,0:T(8,128)(2,1)S(1)} copy-done((bf16[8,32,2048]{2,1,0:T(8,128)(2,1)S(1)}, bf16[8,32,2048]{2,1,0:T(8,128)(2,1)}, u32[]{:S(2)}) %copy-start) | copy-done | bytes 1048600
  23.2 0.4 shard_map.84
  23.6 5.4 %collective-permute-start = (bf16[12,32,512]{2,1,0:T(8,128)(2,1)S(1)}, bf16[12,32,512]{2,1,0:T(8,128)(2,1)S(1)}, u32[]{:S(2)}, u32[]{:S(2)}) collective-permute-start(bf16[12,32,512]{2,1,0:T(8,128)(2,1)S(1)} %get-tuple-element.26), channel_id=1, source_target_pairs={{0,7},{1,6},{2,5},{3,4},{4,3},{5,2},{6,1},{7,0},{8,15},{9,14},{10,... | collective-permute-start | bytes 1179656 | tf_op jit(solution)/shard_map/ppermute | solution.py:289
  29.0 2.1 %collective-permute-start.1 = (bf16[12,32,512]{2,1,0:T(8,128)(2,1)S(1)}, bf16[12,32,512]{2,1,0:T(8,128)(2,1)S(1)}, u32[]{:S(2)}, u32[]{:S(2)}) collective-permute-start(bf16[12,32,512]{2,1,0:T(8,128)(2,1)S(1)} %get-tuple-element.27), channel_id=1, source_target_pairs={{0,4},{1,5},{2,6},{3,7},{4,0},{5,1},{6,2},{7,3},{8,12},{9,13},{10,... | collective-permute-start | bytes 1179656 | tf_op jit(solution)/shard_map/ppermute | solution.py:289
  31.1 0.0 copy-start.6
  31.1 2.1 %collective-permute-start.2 = (bf16[12,32,512]{2,1,0:T(8,128)(2,1)S(1)}, bf16[12,32,512]{2,1,0:T(8,128)(2,1)S(1)}, u32[]{:S(2)}, u32[]{:S(2)}) collective-permute-start(bf16[12,32,512]{2,1,0:T(8,128)(2,1)S(1)} %get-tuple-element.28), channel_id=1, source_target_pairs={{0,3},{1,2},{2,1},{3,0},{4,7},{5,6},{6,5},{7,4},{8,11},{9,10},{10,... | collective-permute-start | bytes 1179656 | tf_op jit(solution)/shard_map/ppermute | solution.py:289
  33.3 0.0 copy-start.2
  33.3 0.0 copy-start.4
  33.3 0.0 copy-start.5
  33.3 0.0 copy-done.6
  33.3 0.1 dynamic_slice.3
  33.4 0.0 copy-start.3
  33.4 0.6 copy-done.4
  34.0 0.0 copy-done.5
  34.0 0.1 copy-done.3
  34.1 0.2 fusion
  34.3 0.1 pad_add_fusion.lengths
  34.4 0.0 all-to-all-done.arrived
  34.4 0.0 copy-done.2
  34.4 1.3 %shard_map.83 = bf16[4,60,4,128]{3,2,1,0:T(4,128)(2,1)} custom-call(s32[8]{0:T(128)S(1)} %and_select_fusion.origin, bf16[32,5,4,128]{3,2,1,0:T(4,128)(2,1)S(1)} %all-to-all-done.arrived, bf16[4,5,4,128]{3,2,1,0:T(4,128)(2,1)S(1)} %copy-done.2), custom_call_target="tpu_custom_call" | custom-call | tf_op jit(solution)/shard_map/pallas_call | solution.py:291
  35.7 4.0 %all-to-all-start.1 = ((bf16[4,60,4,128]{3,2,1,0:T(4,128)(2,1)}), bf16[4,60,4,128]{3,2,1,0:T(4,128)(2,1)S(1)}, u32[]{:S(2)}, u32[]{:S(2)}) async-start(bf16[4,60,4,128]{3,2,1,0:T(4,128)(2,1)} %shard_map.83), calls=%async_computation.1 | async-start | bytes 491520 | tf_op jit(solution)/shard_map/all_to_all | solution.py:244
  39.7 0.0 collective-permute-done.rest_1_
  39.7 7.4 %collective-permute-done.1.rest_2_ = bf16[12,32,512]{2,1,0:T(8,128)(2,1)S(1)} collective-permute-done((bf16[12,32,512]{2,1,0:T(8,128)(2,1)S(1)}, bf16[12,32,512]{2,1,0:T(8,128)(2,1)S(1)}, u32[]{:S(2)}, u32[]{:S(2)}) %collective-permute-start.1) | collective-permute-done | bytes 393248 | tf_op jit(solution)/shard_map/ppermute | solution.py:289
  47.1 0.0 collective-permute-done.2.rest_3_
  47.1 0.0 all-to-all-done.1
  47.1 1.3 %shard_map.85 = bf16[4,208,128]{2,1,0:T(8,128)(2,1)S(1)} custom-call(s32[12]{0:T(128)S(1)} %pad_add_fusion.lengths, s32[8]{0:T(128)S(1)} %and_select_fusion.1.target, bf16[4,240,128]{2,1,0:T(8,128)(2,1)S(1)} %bitcast.11, bf16[12,32,512]{2,1,0:T(8,128)(2,1)S(1)} %get-tuple-element.25.rest_0_, bf16[12,32,512]{2,1,0:T(8,128)(2,1)S(1)} %collective-permute-done.rest_1_, ...), custom_call_target="tpu_custom_call" | custom-call | flops 100000000 | bytes 3145728 | tf_op jit(solution)/shard_map/pallas_call | solution.py:296
  48.4 9.5 %all_to_all.20.gathered = bf16[4,208,128]{2,1,0:T(8,128)(2,1)S(1)} all-to-all(bf16[4,208,128]{2,1,0:T(8,128)(2,1)S(1)} %shard_map.85), channel_id=1, replica_groups={{0,1,12,13},{2,3,14,15},{4,5,8,9},{6,7,10,11},{16,17,28,29},{18,19,30,3..., dimensions={0} | all-to-all | bytes 425984 | tf_op jit(solution)/shard_map/all_to_all | solution.py:244
  57.9 1.5 %shard_map.86 = (bf16[32,16,128]{2,1,0:T(8,128)(2,1)S(1)}, bf16[4,16,128]{2,1,0:T(8,128)(2,1)S(1)}) custom-call(s32[8]{0:T(128)S(1)} %and_select_fusion.origin, s32[8]{0:T(128)S(1)} %and_select_fusion.1.target, bf16[4,208,128]{2,1,0:T(8,128)(2,1)S(1)} %all_to_all.20.gathered, bf16[4,240,128]{2,1,0:T(8,128)(2,1)S(1)} %bitcast.12), custom_call_target="tpu_custom_call" | custom-call | tf_op jit(solution)/shard_map/pallas_call | solution.py:310
  59.4 20.4 %all_to_all.21.returned = bf16[32,16,128]{2,1,0:T(8,128)(2,1)S(1)} all-to-all(bf16[32,16,128]{2,1,0:T(8,128)(2,1)S(1)} %get-tuple-element.29), channel_id=1, replica_groups={{256,496,224,464,192,432,160,400,128,368,96,336,64,304,32,272,0,240,480..., dimensions={0} | all-to-all | bytes 262144 | tf_op jit(solution)/shard_map/all_to_all | solution.py:241
  79.8 1.2 %shard_map.87 = bf16[12,16,128]{2,1,0:T(8,128)(2,1)} custom-call(s32[8]{0:T(128)S(1)} %and_select_fusion.1.target, bf16[32,16,128]{2,1,0:T(8,128)(2,1)S(1)} %all_to_all.21.returned, bf16[4,16,128]{2,1,0:T(8,128)(2,1)S(1)} %get-tuple-element.30.kept), custom_call_target="tpu_custom_call" | custom-call | tf_op jit(solution)/shard_map/pallas_call | solution.py:317
  (3 shorter events, 0.0 us)
Async XLA Ops:
  0.0 22.0 %copy-start.1 = (bf16[4,32,2048]{2,1,0:T(8,128)(2,1)S(1)}, bf16[4,32,2048]{2,1,0:T(8,128)(2,1)}, u32[]{:S(2)}) copy-start(bf16[4,32,2048]{2,1,0:T(8,128)(2,1)} %resident.1) | copy-start | bytes 1572868
  1.8 32.6 %all-to-all-start = ((bf16[32,5,4,128]{3,2,1,0:T(4,128)(2,1)}), bf16[32,5,4,128]{3,2,1,0:T(4,128)(2,1)S(1)}, u32[]{:S(2)}, u32[]{:S(2)}) async-start(bf16[32,5,4,128]{3,2,1,0:T(4,128)(2,1)} %get-tuple-element.23), calls=%async_computation | async-start | bytes 327680 | tf_op jit(solution)/shard_map/all_to_all | solution.py:241
  22.0 1.2 %copy-start = (bf16[8,32,2048]{2,1,0:T(8,128)(2,1)S(1)}, bf16[8,32,2048]{2,1,0:T(8,128)(2,1)}, u32[]{:S(2)}) copy-start(bf16[8,32,2048]{2,1,0:T(8,128)(2,1)} %moved.1) | copy-start | bytes 3145732
  23.6 16.1 %collective-permute-start = (bf16[12,32,512]{2,1,0:T(8,128)(2,1)S(1)}, bf16[12,32,512]{2,1,0:T(8,128)(2,1)S(1)}, u32[]{:S(2)}, u32[]{:S(2)}) collective-permute-start(bf16[12,32,512]{2,1,0:T(8,128)(2,1)S(1)} %get-tuple-element.26), channel_id=1, source_target_pairs={{0,7},{1,6},{2,5},{3,4},{4,3},{5,2},{6,1},{7,0},{8,15},{9,14},{10,... | collective-permute-start | bytes 1179656 | tf_op jit(solution)/shard_map/ppermute | solution.py:289
  29.0 18.1 %collective-permute-start.1 = (bf16[12,32,512]{2,1,0:T(8,128)(2,1)S(1)}, bf16[12,32,512]{2,1,0:T(8,128)(2,1)S(1)}, u32[]{:S(2)}, u32[]{:S(2)}) collective-permute-start(bf16[12,32,512]{2,1,0:T(8,128)(2,1)S(1)} %get-tuple-element.27), channel_id=1, source_target_pairs={{0,4},{1,5},{2,6},{3,7},{4,0},{5,1},{6,2},{7,3},{8,12},{9,13},{10,... | collective-permute-start | bytes 1179656 | tf_op jit(solution)/shard_map/ppermute | solution.py:289
  31.1 2.2 %copy-start.6 = (s32[128]{0:T(128)S(1)}, s32[128]{0:T(128)}, u32[]{:S(2)}) copy-start(s32[128]{0:T(128)} %param.12) | copy-start | bytes 1540
  31.1 16.0 %collective-permute-start.2 = (bf16[12,32,512]{2,1,0:T(8,128)(2,1)S(1)}, bf16[12,32,512]{2,1,0:T(8,128)(2,1)S(1)}, u32[]{:S(2)}, u32[]{:S(2)}) collective-permute-start(bf16[12,32,512]{2,1,0:T(8,128)(2,1)S(1)} %get-tuple-element.28), channel_id=1, source_target_pairs={{0,3},{1,2},{2,1},{3,0},{4,7},{5,6},{6,5},{7,4},{8,11},{9,10},{10,... | collective-permute-start | bytes 1179656 | tf_op jit(solution)/shard_map/ppermute | solution.py:289
  33.3 1.1 %copy-start.2 = (bf16[4,5,4,128]{3,2,1,0:T(4,128)(2,1)S(1)}, bf16[4,5,4,128]{3,2,1,0:T(4,128)(2,1)}, u32[]{:S(2)}) copy-start(bf16[4,5,4,128]{3,2,1,0:T(4,128)(2,1)} %get-tuple-element.24.kept) | copy-start | bytes 61444
  33.3 0.7 copy-start.4
  33.3 0.7 copy-start.5
  33.4 0.7 copy-start.3
  35.7 11.4 %all-to-all-start.1 = ((bf16[4,60,4,128]{3,2,1,0:T(4,128)(2,1)}), bf16[4,60,4,128]{3,2,1,0:T(4,128)(2,1)S(1)}, u32[]{:S(2)}, u32[]{:S(2)}) async-start(bf16[4,60,4,128]{3,2,1,0:T(4,128)(2,1)} %shard_map.83), calls=%async_computation.1 | async-start | bytes 491520 | tf_op jit(solution)/shard_map/all_to_all | solution.py:244

commit v14 on v13

--- a/solution.py
+++ b/solution.py
@@ -99,8 +99,8 @@
         mine = names == lax.axis_index("group") * SLOTS + slot
         groups.append(jnp.sum(jnp.where(mine, slots, 0.0)).astype(jnp.int32) >> 3)
     for slot, group in zip(range(RES, SLOTS), groups):
-        sent[listed(group), :HEADS] = asked_here[slot]
-        sent[listed(group), HEADS] = fresh_here[slot]
+        sent[group, :HEADS] = asked_here[slot]
+        sent[group, HEADS] = fresh_here[slot]
 
 
 def split_kernel(moved, resident, *outs):
@@ -117,7 +117,7 @@
 
 def spread_kernel(origin, arrived, kept, asking):
     for row in range(SLOTS):
-        chunk = arrived.at[listed(origin[row])] if row < MIG else kept.at[row - MIG]
+        chunk = arrived.at[origin[row]] if row < MIG else kept.at[row - MIG]
         for peer in range(SIDE):
             asking[peer, row * HEADS : (row + 1) * HEADS] = chunk[:HEADS]
             asking[peer, SLOTS * HEADS + row] = chunk[HEADS]
@@ -237,9 +237,6 @@
 
     turned = [[listed(place) for place in range(GROUPS)]]
 
-    def around(array):
-        return lax.all_to_all(array, "group", 0, 0, axis_index_groups=turned, tiled=True)
-
     def across(array):
         return lax.all_to_all(array, "tensor", 0, 0, axis_index_groups=peers, tiled=True)
 
@@ -257,7 +254,7 @@
         ],
         limit=FULL,
     )(decode_slot.reshape(2, HD), prefill_slot.reshape(2, HD), asked, new_entries)
-    arrived = around(sent)
+    arrived = lax.all_to_all(sent, "group", 0, 0, tiled=True)
 
     later = (resident_kept, kept_tokens, prefill_slot, decode_slot)
     later, kept = lax.optimization_barrier((later, kept))
@@ -312,7 +309,7 @@
         (shape((GROUPS, QROWS, HD), BF), shape((RES, QROWS, HD), BF)),
         [SM, SM, VM, VM],
     )(origin, target, gathered, everyone)
-    returned = around(finished)
+    returned = lax.all_to_all(finished, "group", 0, 0, axis_index_groups=turned, tiled=True)
 
     result = call(select_kernel, shape((SLOTS, QROWS, HD), BF), [SM, VM, VM])(target, returned, here)
     result = result.reshape(SLOTS, HEADS, STEPS, HD).transpose(0, 2, 1, 3)

time: 81.5 us -> 82.6 us (1.013)
  waiting for transfers between devices: 7.38 us -> 10.1 us
  starting transfers between devices: 33.8 us -> 31.3 us
  blocking collectives: 29.9 us -> 30.8 us
    ppermute x3, waiting for transfers between devices: 7.38 us -> 1.75 us  [body(): blocks.append(lax.ppermute(split[step], 'tensor', steps))]
    all_to_all x1, waiting for transfers between devices: 0.01 us -> 4.73 us  [body(): arrived = lax.all_to_all(sent, 'group', 0, 0, tiled=True)]
    all_to_all x1, waiting for transfers between devices: 0.01 us -> 3.62 us  [across(): lax.all_to_all(array, 'tensor', 0, 0, axis_index_groups=peers, tiled=True)]
    all_to_all x1, starting transfers between devices: 20.2 us -> 16.8 us  [body(): arrived = lax.all_to_all(sent, 'group', 0, 0, tiled=True)]
    all_to_all x1, blocking collectives: 20.4 us -> 22.8 us  [body(): lax.all_to_all(finished, 'group', 0, 0, axis_index_groups=turned, tiled=T...]
    all_to_all x1, blocking collectives: 9.49 us -> 8.04 us  [across(): lax.all_to_all(array, 'tensor', 0, 0, axis_index_groups=peers, tiled=True)]
    all_to_all x1, starting transfers between devices: 4 us -> 4.93 us  [across(): lax.all_to_all(array, 'tensor', 0, 0, axis_index_groups=peers, tiled=True)]
  transfers between devices with their start and end apart: 5 -> 5, of which waited for: 1 -> 3; matrix products, arithmetic and copies ran while one was open for 0% -> 0% of each run, Pallas kernels for 2% -> 2%
where the time goes in v14:
time: 82.6 us; the launch traced here: 82.1 us
  starting transfers between devices  31.3 us (38%)
  blocking collectives  30.8 us (37%)
  waiting for transfers between devices  10.1 us (12%)
  Pallas kernels  7.43 us (9%)
  local copies, waits for them, and re-layouts  2 us (2%)
    all_to_all x1, blocking collectives, body(): lax.all_to_all(finished, 'group', 0, 0, axis_index_groups=turned, tiled=T...  22.8 us
    all_to_all x1, starting transfers between devices, body(): arrived = lax.all_to_all(sent, 'group', 0, 0, tiled=True)  16.8 us
    ppermute x3, starting transfers between devices, body(): blocks.append(lax.ppermute(split[step], 'tensor', steps))  9.58 us
    all_to_all x1, blocking collectives, across(): lax.all_to_all(array, 'tensor', 0, 0, axis_index_groups=peers, tiled=True)  8.04 us
    all_to_all x1, starting transfers between devices, across(): lax.all_to_all(array, 'tensor', 0, 0, axis_index_groups=peers, tiled=True)  4.93 us
    all_to_all x1, waiting for transfers between devices, body(): arrived = lax.all_to_all(sent, 'group', 0, 0, tiled=True)  4.73 us
    all_to_all x1, waiting for transfers between devices, across(): lax.all_to_all(array, 'tensor', 0, 0, axis_index_groups=peers, tiled=True)  3.62 us
    unnamed x14, local copies, waits for them, and re-layouts  1.92 us
  transfers between devices with their start and end apart: 5, of which 3 were waited for; matrix products, arithmetic and copies ran while one was open for 0% of the time, Pallas kernels for 2%

profile of v14, /device:TPU:1, one launch (start us, length us, event | category | flops | bytes accessed | tf_op | source)
XLA Modules:
  0.0 82.1 jit_solution(8523625924861772864)
XLA Ops:
  0.0 0.0 copy-start.1
  0.0 1.7 %shard_map.82 = (bf16[32,5,4,128]{3,2,1,0:T(4,128)(2,1)}, bf16[4,5,4,128]{3,2,1,0:T(4,128)(2,1)}) custom-call(s32[2,128]{1,0:T(2,128)} %bitcast.15, s32[2,128]{1,0:T(2,128)} %bitcast.14, bf16[12,4,4,128]{3,2,1,0:T(4,128)(2,1)} %bitcast.13, bf16[12,4,2048]{2,1,0:T(4,128)(2,1)} %fresh.1), custom_call_target="tpu_custom_call" | custom-call | tf_op jit(solution)/shard_map/pallas_call | solution.py:244
  1.7 16.8 %all-to-all-start = ((bf16[32,5,4,128]{3,2,1,0:T(4,128)(2,1)}), bf16[32,5,4,128]{3,2,1,0:T(4,128)(2,1)S(1)}, u32[]{:S(2)}, u32[]{:S(2)}) async-start(bf16[32,5,4,128]{3,2,1,0:T(4,128)(2,1)} %get-tuple-element.23), calls=%async_computation | async-start | bytes 327680 | tf_op jit(solution)/shard_map/all_to_all | solution.py:257
  18.5 0.0 copy-done.1
  18.5 0.0 copy-start
  18.5 1.2 %copy-done = bf16[8,32,2048]{2,1,0:T(8,128)(2,1)S(1)} copy-done((bf16[8,32,2048]{2,1,0:T(8,128)(2,1)S(1)}, bf16[8,32,2048]{2,1,0:T(8,128)(2,1)}, u32[]{:S(2)}) %copy-start) | copy-done | bytes 1048600
  19.7 0.4 shard_map.84
  20.2 5.4 %collective-permute-start = (bf16[12,32,512]{2,1,0:T(8,128)(2,1)S(1)}, bf16[12,32,512]{2,1,0:T(8,128)(2,1)S(1)}, u32[]{:S(2)}, u32[]{:S(2)}) collective-permute-start(bf16[12,32,512]{2,1,0:T(8,128)(2,1)S(1)} %get-tuple-element.26), channel_id=1, source_target_pairs={{0,7},{1,6},{2,5},{3,4},{4,3},{5,2},{6,1},{7,0},{8,15},{9,14},{10,... | collective-permute-start | bytes 1179656 | tf_op jit(solution)/shard_map/ppermute | solution.py:286
  25.6 2.1 %collective-permute-start.1 = (bf16[12,32,512]{2,1,0:T(8,128)(2,1)S(1)}, bf16[12,32,512]{2,1,0:T(8,128)(2,1)S(1)}, u32[]{:S(2)}, u32[]{:S(2)}) collective-permute-start(bf16[12,32,512]{2,1,0:T(8,128)(2,1)S(1)} %get-tuple-element.27), channel_id=1, source_target_pairs={{0,4},{1,5},{2,6},{3,7},{4,0},{5,1},{6,2},{7,3},{8,12},{9,13},{10,... | collective-permute-start | bytes 1179656 | tf_op jit(solution)/shard_map/ppermute | solution.py:286
  27.7 0.0 copy-start.6
  27.7 2.1 %collective-permute-start.2 = (bf16[12,32,512]{2,1,0:T(8,128)(2,1)S(1)}, bf16[12,32,512]{2,1,0:T(8,128)(2,1)S(1)}, u32[]{:S(2)}, u32[]{:S(2)}) collective-permute-start(bf16[12,32,512]{2,1,0:T(8,128)(2,1)S(1)} %get-tuple-element.28), channel_id=1, source_target_pairs={{0,3},{1,2},{2,1},{3,0},{4,7},{5,6},{6,5},{7,4},{8,11},{9,10},{10,... | collective-permute-start | bytes 1179656 | tf_op jit(solution)/shard_map/ppermute | solution.py:286
  29.8 0.0 copy-start.2
  29.8 0.0 copy-start.4
  29.8 0.0 copy-start.5
  29.8 0.0 copy-done.6
  29.9 0.1 dynamic_slice.3
  29.9 0.0 copy-start.3
  29.9 0.6 copy-done.4
  30.5 0.0 copy-done.5
  30.5 0.1 copy-done.3
  30.6 0.2 fusion
  30.8 0.1 pad_add_fusion.lengths
  30.9 4.7 %all-to-all-done.arrived = bf16[32,5,4,128]{3,2,1,0:T(4,128)(2,1)S(1)} async-done(((bf16[32,5,4,128]{3,2,1,0:T(4,128)(2,1)}), bf16[32,5,4,128]{3,2,1,0:T(4,128)(2,1)S(1)}, u32[]{:S(2)}, u32[]{:S(2)}) %all-to-all-start) | async-done | bytes 163872 | tf_op jit(solution)/shard_map/all_to_all | solution.py:257
  35.6 0.0 copy-done.2
  35.6 1.3 %shard_map.83 = bf16[4,60,4,128]{3,2,1,0:T(4,128)(2,1)} custom-call(s32[8]{0:T(128)S(1)} %and_select_fusion.origin, bf16[32,5,4,128]{3,2,1,0:T(4,128)(2,1)S(1)} %all-to-all-done.arrived, bf16[4,5,4,128]{3,2,1,0:T(4,128)(2,1)S(1)} %copy-done.2), custom_call_target="tpu_custom_call" | custom-call | tf_op jit(solution)/shard_map/pallas_call | solution.py:288
  36.9 4.9 %all-to-all-start.1 = ((bf16[4,60,4,128]{3,2,1,0:T(4,128)(2,1)}), bf16[4,60,4,128]{3,2,1,0:T(4,128)(2,1)S(1)}, u32[]{:S(2)}, u32[]{:S(2)}) async-start(bf16[4,60,4,128]{3,2,1,0:T(4,128)(2,1)} %shard_map.83), calls=%async_computation.1 | async-start | bytes 491520 | tf_op jit(solution)/shard_map/all_to_all | solution.py:241
  41.9 0.0 collective-permute-done.rest_1_
  41.9 1.7 %collective-permute-done.1.rest_2_ = bf16[12,32,512]{2,1,0:T(8,128)(2,1)S(1)} collective-permute-done((bf16[12,32,512]{2,1,0:T(8,128)(2,1)S(1)}, bf16[12,32,512]{2,1,0:T(8,128)(2,1)S(1)}, u32[]{:S(2)}, u32[]{:S(2)}) %collective-permute-start.1) | collective-permute-done | bytes 393248 | tf_op jit(solution)/shard_map/ppermute | solution.py:286
  43.6 0.0 collective-permute-done.2.rest_3_
  43.6 3.6 %all-to-all-done.1 = bf16[4,60,4,128]{3,2,1,0:T(4,128)(2,1)S(1)} async-done(((bf16[4,60,4,128]{3,2,1,0:T(4,128)(2,1)}), bf16[4,60,4,128]{3,2,1,0:T(4,128)(2,1)S(1)}, u32[]{:S(2)}, u32[]{:S(2)}) %all-to-all-start.1) | async-done | bytes 245792 | tf_op jit(solution)/shard_map/all_to_all | solution.py:241
  47.3 1.3 %shard_map.85 = bf16[4,208,128]{2,1,0:T(8,128)(2,1)S(1)} custom-call(s32[12]{0:T(128)S(1)} %pad_add_fusion.lengths, s32[8]{0:T(128)S(1)} %and_select_fusion.1.target, bf16[4,240,128]{2,1,0:T(8,128)(2,1)S(1)} %bitcast.11, bf16[12,32,512]{2,1,0:T(8,128)(2,1)S(1)} %get-tuple-element.25.rest_0_, bf16[12,32,512]{2,1,0:T(8,128)(2,1)S(1)} %collective-permute-done.rest_1_, ...), custom_call_target="tpu_custom_call" | custom-call | flops 100000000 | bytes 3145728 | tf_op jit(solution)/shard_map/pallas_call | solution.py:293
  48.6 8.0 %all_to_all.20.gathered = bf16[4,208,128]{2,1,0:T(8,128)(2,1)S(1)} all-to-all(bf16[4,208,128]{2,1,0:T(8,128)(2,1)S(1)} %shard_map.85), channel_id=1, replica_groups={{0,1,12,13},{2,3,14,15},{4,5,8,9},{6,7,10,11},{16,17,28,29},{18,19,30,3..., dimensions={0} | all-to-all | bytes 425984 | tf_op jit(solution)/shard_map/all_to_all | solution.py:241
  56.6 1.5 %shard_map.86 = (bf16[32,16,128]{2,1,0:T(8,128)(2,1)S(1)}, bf16[4,16,128]{2,1,0:T(8,128)(2,1)S(1)}) custom-call(s32[8]{0:T(128)S(1)} %and_select_fusion.origin, s32[8]{0:T(128)S(1)} %and_select_fusion.1.target, bf16[4,208,128]{2,1,0:T(8,128)(2,1)S(1)} %all_to_all.20.gathered, bf16[4,240,128]{2,1,0:T(8,128)(2,1)S(1)} %bitcast.12), custom_call_target="tpu_custom_call" | custom-call | tf_op jit(solution)/shard_map/pallas_call | solution.py:307
  58.1 22.8 %all_to_all.21.returned = bf16[32,16,128]{2,1,0:T(8,128)(2,1)S(1)} all-to-all(bf16[32,16,128]{2,1,0:T(8,128)(2,1)S(1)} %get-tuple-element.29), channel_id=1, replica_groups={{256,496,224,464,192,432,160,400,128,368,96,336,64,304,32,272,0,240,480..., dimensions={0} | all-to-all | bytes 262144 | tf_op jit(solution)/shard_map/all_to_all | solution.py:312
  80.9 1.2 %shard_map.87 = bf16[12,16,128]{2,1,0:T(8,128)(2,1)} custom-call(s32[8]{0:T(128)S(1)} %and_select_fusion.1.target, bf16[32,16,128]{2,1,0:T(8,128)(2,1)S(1)} %all_to_all.21.returned, bf16[4,16,128]{2,1,0:T(8,128)(2,1)S(1)} %get-tuple-element.30.kept), custom_call_target="tpu_custom_call" | custom-call | tf_op jit(solution)/shard_map/pallas_call | solution.py:314
  (3 shorter events, 0.0 us)
Async XLA Ops:
  0.0 18.5 %copy-start.1 = (bf16[4,32,2048]{2,1,0:T(8,128)(2,1)S(1)}, bf16[4,32,2048]{2,1,0:T(8,128)(2,1)}, u32[]{:S(2)}) copy-start(bf16[4,32,2048]{2,1,0:T(8,128)(2,1)} %resident.1) | copy-start | bytes 1572868
  1.7 33.9 %all-to-all-start = ((bf16[32,5,4,128]{3,2,1,0:T(4,128)(2,1)}), bf16[32,5,4,128]{3,2,1,0:T(4,128)(2,1)S(1)}, u32[]{:S(2)}, u32[]{:S(2)}) async-start(bf16[32,5,4,128]{3,2,1,0:T(4,128)(2,1)} %get-tuple-element.23), calls=%async_computation | async-start | bytes 327680 | tf_op jit(solution)/shard_map/all_to_all | solution.py:257
  18.5 1.2 %copy-start = (bf16[8,32,2048]{2,1,0:T(8,128)(2,1)S(1)}, bf16[8,32,2048]{2,1,0:T(8,128)(2,1)}, u32[]{:S(2)}) copy-start(bf16[8,32,2048]{2,1,0:T(8,128)(2,1)} %moved.1) | copy-start | bytes 3145732
  20.2 21.7 %collective-permute-start = (bf16[12,32,512]{2,1,0:T(8,128)(2,1)S(1)}, bf16[12,32,512]{2,1,0:T(8,128)(2,1)S(1)}, u32[]{:S(2)}, u32[]{:S(2)}) collective-permute-start(bf16[12,32,512]{2,1,0:T(8,128)(2,1)S(1)} %get-tuple-element.26), channel_id=1, source_target_pairs={{0,7},{1,6},{2,5},{3,4},{4,3},{5,2},{6,1},{7,0},{8,15},{9,14},{10,... | collective-permute-start | bytes 1179656 | tf_op jit(solution)/shard_map/ppermute | solution.py:286
  25.6 18.1 %collective-permute-start.1 = (bf16[12,32,512]{2,1,0:T(8,128)(2,1)S(1)}, bf16[12,32,512]{2,1,0:T(8,128)(2,1)S(1)}, u32[]{:S(2)}, u32[]{:S(2)}) collective-permute-start(bf16[12,32,512]{2,1,0:T(8,128)(2,1)S(1)} %get-tuple-element.27), channel_id=1, source_target_pairs={{0,4},{1,5},{2,6},{3,7},{4,0},{5,1},{6,2},{7,3},{8,12},{9,13},{10,... | collective-permute-start | bytes 1179656 | tf_op jit(solution)/shard_map/ppermute | solution.py:286
  27.7 2.2 %copy-start.6 = (s32[128]{0:T(128)S(1)}, s32[128]{0:T(128)}, u32[]{:S(2)}) copy-start(s32[128]{0:T(128)} %param.12) | copy-start | bytes 1540
  27.7 16.0 %collective-permute-start.2 = (bf16[12,32,512]{2,1,0:T(8,128)(2,1)S(1)}, bf16[12,32,512]{2,1,0:T(8,128)(2,1)S(1)}, u32[]{:S(2)}, u32[]{:S(2)}) collective-permute-start(bf16[12,32,512]{2,1,0:T(8,128)(2,1)S(1)} %get-tuple-element.28), channel_id=1, source_target_pairs={{0,3},{1,2},{2,1},{3,0},{4,7},{5,6},{6,5},{7,4},{8,11},{9,10},{10,... | collective-permute-start | bytes 1179656 | tf_op jit(solution)/shard_map/ppermute | solution.py:286
  29.8 5.9 %copy-start.2 = (bf16[4,5,4,128]{3,2,1,0:T(4,128)(2,1)S(1)}, bf16[4,5,4,128]{3,2,1,0:T(4,128)(2,1)}, u32[]{:S(2)}) copy-start(bf16[4,5,4,128]{3,2,1,0:T(4,128)(2,1)} %get-tuple-element.24.kept) | copy-start | bytes 61444
  29.8 0.7 copy-start.4
  29.8 0.7 copy-start.5
  29.9 0.7 copy-start.3
  36.9 10.3 %all-to-all-start.1 = ((bf16[4,60,4,128]{3,2,1,0:T(4,128)(2,1)}), bf16[4,60,4,128]{3,2,1,0:T(4,128)(2,1)S(1)}, u32[]{:S(2)}, u32[]{:S(2)}) async-start(bf16[4,60,4,128]{3,2,1,0:T(4,128)(2,1)} %shard_map.83), calls=%async_computation.1 | async-start | bytes 491520 | tf_op jit(solution)/shard_map/all_to_all | solution.py:241

commit v15 on v5

--- a/solution.py
+++ b/solution.py
@@ -15,6 +15,7 @@
 RES = 4
 SLOTS = MIG + RES
 GROUPS = 32
+FIRST_G, STRIDE_G = 16, 15
 SHARDS = 16
 SIDE = 4
 STRIDE = 32
@@ -32,7 +33,7 @@
 FLOOR = -(2.0**100)
 SCALE = 1.0 / math.sqrt(HD)
 LIMIT = 48 * 1024 * 1024
-FULL = 63 * 1024 * 1024
+FULL = 60 * 1024 * 1024
 BF = jnp.bfloat16
 F32 = jnp.float32
 
@@ -41,12 +42,14 @@
 HB = pl.BlockSpec(memory_space=pltpu.HBM)
 
 
-def call(kernel, outs, specs, flops=0, moved=0, scratch=(), limit=LIMIT):
+ANY = pl.BlockSpec(memory_space=pl.ANY)
+
+def call(kernel, outs, specs, flops=0, moved=0, scratch=(), limit=LIMIT, places=None):
     return pl.pallas_call(
         kernel,
         out_shape=outs,
         in_specs=specs,
-        out_specs=jax.tree.map(lambda _: VM, outs),
+        out_specs=jax.tree.map(lambda _: VM, outs) if places is None else places,
         scratch_shapes=scratch,
         compiler_params=pltpu.CompilerParams(vmem_limit_bytes=limit),
         cost_estimate=pl.CostEstimate(flops=flops, bytes_accessed=moved, transcendentals=0),
@@ -60,6 +63,10 @@
 def place_of():
     shard = lax.axis_index("tensor")
     return shard // SIDE, shard % SIDE
+
+
+def listed(group):
+    return (group * STRIDE_G + FIRST_G) % GROUPS
 
 
 def pack_kernel(named, holders, asked, fresh, sent, kept, asked_here, fresh_here, named_here, holders_here, sems):
@@ -89,10 +96,10 @@
     groups = []
     for slot in range(RES, SLOTS):
         mine = names == lax.axis_index("group") * SLOTS + slot
-        groups.append(jnp.sum(jnp.where(mine, slots, 0.0)).astype(jnp.int32) // MIG)
+        groups.append(jnp.sum(jnp.where(mine, slots, 0.0)).astype(jnp.int32) >> 3)
     for slot, group in zip(range(RES, SLOTS), groups):
-        sent[group, :HEADS] = asked_here[slot]
-        sent[group, HEADS] = fresh_here[slot]
+        sent[listed(group), :HEADS] = asked_here[slot]
+        sent[listed(group), HEADS] = fresh_here[slot]
 
 
 def split_kernel(moved, resident, *outs):
@@ -109,7 +116,7 @@
 
 def spread_kernel(origin, arrived, kept, asking):
     for row in range(SLOTS):
-        chunk = arrived.at[origin[row]] if row < MIG else kept.at[row - MIG]
+        chunk = arrived.at[listed(origin[row])] if row < MIG else kept.at[row - MIG]
         for peer in range(PEERS):
             asking[peer, row * HEADS : (row + 1) * HEADS] = chunk[:HEADS]
             asking[peer, SLOTS * HEADS + row] = chunk[HEADS]
@@ -119,7 +126,7 @@
     return lax.dot_general(left, right, (((1,), (1,)), ((), ())), preferred_element_type=F32) * SCALE
 
 
-def partial_kernel(lengths, asking, *rest):
+def partial_kernel(lengths, target, asking, *rest):
     *blocks, payload, scores, weights, stats = rest
     y, x = place_of()
     column = lax.broadcasted_iota(jnp.int32, (1, WIDE), 1)
@@ -166,7 +173,7 @@
             payload[2 * pair + 1, span, :] = blended[QROWS:]
 
 
-def merge_kernel(origin, gathered, everyone, sent, kept):
+def merge_kernel(origin, target, gathered, everyone, sent, kept):
     y, x = place_of()
     first = 2 * y
     asked = everyone[first + x % 2, :ROWS, :]
@@ -200,7 +207,7 @@
 
     sent[...] = jnp.zeros_like(sent)
     for slot in range(MIG):
-        sent[origin[slot]] = result[slot * QROWS : (slot + 1) * QROWS]
+        sent[listed(origin[slot])] = result[slot * QROWS : (slot + 1) * QROWS]
     for slot in range(RES):
         kept[slot] = result[(MIG + slot) * QROWS : (MIG + slot + 1) * QROWS]
 
@@ -209,7 +216,7 @@
     for slot in range(RES):
         out[slot] = kept[slot]
     for slot in range(MIG):
-        out[RES + slot] = returned[target[slot]]
+        out[RES + slot] = returned[listed(target[slot])]
 
 
 def body(
@@ -224,6 +231,10 @@
 ):
     shape = jax.ShapeDtypeStruct
     peers = [[y * SIDE + 2 * half + x for y in range(SIDE) for x in range(2)] for half in range(2)]
+    turned = [[listed(place) for place in range(GROUPS)]]
+
+    def around(array):
+        return lax.all_to_all(array, "group", 0, 0, axis_index_groups=turned, tiled=True)
 
     def across(array):
         return lax.all_to_all(array, "tensor", 0, 0, axis_index_groups=peers, tiled=True)
@@ -242,11 +253,11 @@
         ],
         limit=FULL,
     )(decode_slot.reshape(2, HD), prefill_slot.reshape(2, HD), asked, new_entries)
-    arrived = lax.all_to_all(sent, "group", 0, 0, tiled=True)
-
-    later = (resident_kept, kept_tokens, prefill_slot, decode_slot, prefill_cache, resident_cache)
+    arrived = around(sent)
+
+    later = (resident_kept, kept_tokens, prefill_slot, decode_slot)
     later, kept = lax.optimization_barrier((later, kept))
-    resident_kept, kept_tokens, prefill_slot, decode_slot, prefill_cache, resident_cache = later
+    resident_kept, kept_tokens, prefill_slot, decode_slot = later
     group = lax.axis_index("group")
 
     def looked_up(names, first, values):
@@ -278,7 +289,7 @@
     payload = call(
         partial_kernel,
         shape((PEERS, PAYLOAD, HD), BF),
-        [SM] + [VM] * (1 + BLOCKS),
+        [SM, SM] + [VM] * (1 + BLOCKS),
         flops=10**8,
         moved=3 * 2**20,
         scratch=[
@@ -286,15 +297,15 @@
             pltpu.VMEM((PEERS, ROWS, WIDE), BF),
             pltpu.VMEM((2 * HD, HD), F32),
         ],
-    )(lengths, everyone, *blocks)
+    )(lengths, target, everyone, *blocks)
     gathered = across(payload)
 
     finished, here = call(
         merge_kernel,
         (shape((GROUPS, QROWS, HD), BF), shape((RES, QROWS, HD), BF)),
-        [SM, VM, VM],
-    )(origin, gathered, everyone)
-    returned = lax.all_to_all(finished, "group", 0, 0, tiled=True)
+        [SM, SM, VM, VM],
+    )(origin, target, gathered, everyone)
+    returned = around(finished)
 
     result = call(select_kernel, shape((SLOTS, QROWS, HD), BF), [SM, VM, VM])(target, returned, here)
     result = result.reshape(SLOTS, HEADS, STEPS, HD).transpose(0, 2, 1, 3)

time: 91 us -> 82.8 us (0.910)
  waiting for transfers between devices: 32.3 us -> 9.45 us
  blocking collectives: 10 us -> 32.3 us
  starting transfers between devices: 35.8 us -> 29.7 us
  Pallas kernels: 9.34 us -> 7.79 us
    all_to_all x2 -> x1, waiting for transfers between devices: 25.6 us -> 1.23 us  [around(): lax.all_to_all(array, 'group', 0, 0, axis_index_groups=turned, tiled=True)]
    all_to_all x0 -> x1, blocking collectives: none -> 20.9 us  [around(): lax.all_to_all(array, 'group', 0, 0, axis_index_groups=turned, tiled=True)]
    ppermute x1, waiting for transfers between devices: 0.36 us -> 7.98 us  [body(): blocks.append(lax.ppermute(split[step], 'tensor', steps))]
    all_to_all x1, waiting for transfers between devices: 6.3 us -> 0.24 us  [across(): lax.all_to_all(array, 'tensor', 0, 0, axis_index_groups=peers, tiled=True)]
    all_to_all x2 -> x1, starting transfers between devices: 26.1 us -> 20.2 us  [around(): lax.all_to_all(array, 'group', 0, 0, axis_index_groups=turned, tiled=True)]
    all_to_all x1, blocking collectives: 10 us -> 11.4 us  [across(): lax.all_to_all(array, 'tensor', 0, 0, axis_index_groups=peers, tiled=True)]
  transfers between devices with their start and end apart: 4 -> 3, of which waited for: 4 -> 3; matrix products, arithmetic and copies ran while one was open for 0% -> 0% of each run, Pallas kernels for 3% -> 2%
where the time goes in v15:
time: 82.8 us; the launch traced here: 82.3 us
  blocking collectives  32.3 us (39%)
  starting transfers between devices  29.7 us (36%)
  waiting for transfers between devices  9.45 us (11%)
  Pallas kernels  7.79 us (9%)
  local copies, waits for them, and re-layouts  2.62 us (3%)
    all_to_all x1, blocking collectives, around(): lax.all_to_all(array, 'group', 0, 0, axis_index_groups=turned, tiled=True)  20.9 us
    all_to_all x1, starting transfers between devices, around(): lax.all_to_all(array, 'group', 0, 0, axis_index_groups=turned, tiled=True)  20.2 us
    all_to_all x1, blocking collectives, across(): lax.all_to_all(array, 'tensor', 0, 0, axis_index_groups=peers, tiled=True)  11.4 us
    ppermute x1, waiting for transfers between devices, body(): blocks.append(lax.ppermute(split[step], 'tensor', steps))  7.98 us
    all_to_all x1, starting transfers between devices, across(): lax.all_to_all(array, 'tensor', 0, 0, axis_index_groups=peers, tiled=True)  5.12 us
    ppermute x1, starting transfers between devices, body(): blocks.append(lax.ppermute(split[step], 'tensor', steps))  4.39 us
    unnamed x14, local copies, waits for them, and re-layouts  2.54 us
    pallas_call x1, Pallas kernels, body(): call(pack_kernel, (shape((GROUPS, TILES, STEPS, HD), BF), shape((RES, TIL...  1.74 us
  transfers between devices with their start and end apart: 3, of which 3 were waited for; matrix products, arithmetic and copies ran while one was open for 0% of the time, Pallas kernels for 2%

profile of v15, /device:TPU:1, one launch (start us, length us, event | category | flops | bytes accessed | tf_op | source)
XLA Modules:
  0.0 82.3 jit_solution(11237609739846176836)
XLA Ops:
  0.0 0.0 copy-start.1
  0.0 1.7 %shard_map.82 = (bf16[32,5,4,128]{3,2,1,0:T(4,128)(2,1)}, bf16[4,5,4,128]{3,2,1,0:T(4,128)(2,1)}) custom-call(s32[2,128]{1,0:T(2,128)} %bitcast.15, s32[2,128]{1,0:T(2,128)} %bitcast.14, bf16[12,4,4,128]{3,2,1,0:T(4,128)(2,1)} %bitcast.13, bf16[12,4,2048]{2,1,0:T(4,128)(2,1)} %fresh.1), custom_call_target="tpu_custom_call" | custom-call | tf_op jit(solution)/shard_map/pallas_call | solution.py:243
  1.8 20.2 %all-to-all-start = ((bf16[32,5,4,128]{3,2,1,0:T(4,128)(2,1)}), bf16[32,5,4,128]{3,2,1,0:T(4,128)(2,1)S(1)}, u32[]{:S(2)}, u32[]{:S(2)}) async-start(bf16[32,5,4,128]{3,2,1,0:T(4,128)(2,1)} %get-tuple-element.21), calls=%async_computation | async-start | bytes 327680 | tf_op jit(solution)/shard_map/all_to_all | solution.py:237
  22.0 0.0 copy-done.1
  22.0 0.0 copy-start
  22.0 1.2 %copy-done = bf16[8,32,2048]{2,1,0:T(8,128)(2,1)S(1)} copy-done((bf16[8,32,2048]{2,1,0:T(8,128)(2,1)S(1)}, bf16[8,32,2048]{2,1,0:T(8,128)(2,1)}, u32[]{:S(2)}) %copy-start) | copy-done | bytes 1048600
  23.2 0.0 copy-start.4
  23.2 0.0 copy-start.5
  23.2 0.4 shard_map.84
  23.6 0.0 copy-start.2
  23.6 4.4 %collective-permute-start = (bf16[12,32,1024]{2,1,0:T(8,128)(2,1)S(1)}, bf16[12,32,1024]{2,1,0:T(8,128)(2,1)S(1)}, u32[]{:S(2)}, u32[]{:S(2)}) collective-permute-start(bf16[12,32,1024]{2,1,0:T(8,128)(2,1)S(1)} %get-tuple-element.24), channel_id=1, source_target_pairs={{0,3},{1,2},{2,1},{3,0},{4,7},{5,6},{6,5},{7,4},{8,11},{9,10},{10,... | collective-permute-start | bytes 2359304 | tf_op jit(solution)/shard_map/ppermute | solution.py:282
  28.1 0.0 copy-start.3
  28.1 0.0 copy-done.4
  28.1 0.0 copy-done.5
  28.1 0.7 copy-done.3
  28.8 0.2 fusion
  29.0 1.2 %all-to-all-done.arrived = bf16[32,5,4,128]{3,2,1,0:T(4,128)(2,1)S(1)} async-done(((bf16[32,5,4,128]{3,2,1,0:T(4,128)(2,1)}), bf16[32,5,4,128]{3,2,1,0:T(4,128)(2,1)S(1)}, u32[]{:S(2)}, u32[]{:S(2)}) %all-to-all-start) | async-done | bytes 163872 | tf_op jit(solution)/shard_map/all_to_all | solution.py:237
  30.2 0.0 copy-done.2
  30.2 1.4 %shard_map.83 = bf16[8,60,4,128]{3,2,1,0:T(4,128)(2,1)} custom-call(s32[8]{0:T(128)S(1)} %and_select_fusion.origin, bf16[32,5,4,128]{3,2,1,0:T(4,128)(2,1)S(1)} %all-to-all-done.arrived, bf16[4,5,4,128]{3,2,1,0:T(4,128)(2,1)S(1)} %copy-done.2), custom_call_target="tpu_custom_call" | custom-call | tf_op jit(solution)/shard_map/pallas_call | solution.py:284
  31.7 5.1 %all-to-all-start.1 = ((bf16[8,60,4,128]{3,2,1,0:T(4,128)(2,1)}), bf16[8,60,4,128]{3,2,1,0:T(4,128)(2,1)S(1)}, u32[]{:S(2)}, u32[]{:S(2)}) async-start(bf16[8,60,4,128]{3,2,1,0:T(4,128)(2,1)} %shard_map.83), calls=%async_computation.1 | async-start | bytes 983040 | tf_op jit(solution)/shard_map/all_to_all | solution.py:240
  36.8 0.0 copy-start.6
  36.8 0.7 copy-done.6
  37.4 0.1 dynamic_slice.3
  37.5 0.1 pad_add_fusion.lengths
  37.6 8.0 %collective-permute-done.rest_1_ = bf16[12,32,1024]{2,1,0:T(8,128)(2,1)S(1)} collective-permute-done((bf16[12,32,1024]{2,1,0:T(8,128)(2,1)S(1)}, bf16[12,32,1024]{2,1,0:T(8,128)(2,1)S(1)}, u32[]{:S(2)}, u32[]{:S(2)}) %collective-permute-start) | collective-permute-done | bytes 786464 | tf_op jit(solution)/shard_map/ppermute | solution.py:282
  45.6 0.2 all-to-all-done.1
  45.8 1.5 %shard_map.85 = bf16[8,208,128]{2,1,0:T(8,128)(2,1)S(1)} custom-call(s32[12]{0:T(128)S(1)} %pad_add_fusion.lengths, s32[8]{0:T(128)S(1)} %and_select_fusion.1.target, bf16[8,240,128]{2,1,0:T(8,128)(2,1)S(1)} %bitcast.11, bf16[12,32,1024]{2,1,0:T(8,128)(2,1)S(1)} %get-tuple-element.23.rest_0_, bf16[12,32,1024]{2,1,0:T(8,128)(2,1)S(1)} %collective-permute-done.rest_1_), custom_call_target="tpu_custom_call" | custom-call | flops 100000000 | bytes 3145728 | tf_op jit(solution)/shard_map/pallas_call | solution.py:289
  47.3 11.4 %all_to_all.20.gathered = bf16[8,208,128]{2,1,0:T(8,128)(2,1)S(1)} all-to-all(bf16[8,208,128]{2,1,0:T(8,128)(2,1)S(1)} %shard_map.85), channel_id=1, replica_groups={{0,1,4,5,8,9,12,13},{2,3,6,7,10,11,14,15},{16,17,20,21,24,25,28,29},{18..., dimensions={0} | all-to-all | bytes 851968 | tf_op jit(solution)/shard_map/all_to_all | solution.py:240
  58.7 1.5 %shard_map.86 = (bf16[32,16,128]{2,1,0:T(8,128)(2,1)S(1)}, bf16[4,16,128]{2,1,0:T(8,128)(2,1)S(1)}) custom-call(s32[8]{0:T(128)S(1)} %and_select_fusion.origin, s32[8]{0:T(128)S(1)} %and_select_fusion.1.target, bf16[8,208,128]{2,1,0:T(8,128)(2,1)S(1)} %all_to_all.20.gathered, bf16[8,240,128]{2,1,0:T(8,128)(2,1)S(1)} %bitcast.12), custom_call_target="tpu_custom_call" | custom-call | tf_op jit(solution)/shard_map/pallas_call | solution.py:303
  60.2 20.9 %all_to_all.21.returned = bf16[32,16,128]{2,1,0:T(8,128)(2,1)S(1)} all-to-all(bf16[32,16,128]{2,1,0:T(8,128)(2,1)S(1)} %get-tuple-element.25), channel_id=1, replica_groups={{256,496,224,464,192,432,160,400,128,368,96,336,64,304,32,272,0,240,480..., dimensions={0} | all-to-all | bytes 262144 | tf_op jit(solution)/shard_map/all_to_all | solution.py:237
  81.1 1.2 %shard_map.87 = bf16[12,16,128]{2,1,0:T(8,128)(2,1)} custom-call(s32[8]{0:T(128)S(1)} %and_select_fusion.1.target, bf16[32,16,128]{2,1,0:T(8,128)(2,1)S(1)} %all_to_all.21.returned, bf16[4,16,128]{2,1,0:T(8,128)(2,1)S(1)} %get-tuple-element.26.kept), custom_call_target="tpu_custom_call" | custom-call | tf_op jit(solution)/shard_map/pallas_call | solution.py:310
  (3 shorter events, 0.0 us)
Async XLA Ops:
  0.0 22.0 %copy-start.1 = (bf16[4,32,2048]{2,1,0:T(8,128)(2,1)S(1)}, bf16[4,32,2048]{2,1,0:T(8,128)(2,1)}, u32[]{:S(2)}) copy-start(bf16[4,32,2048]{2,1,0:T(8,128)(2,1)} %resident.1) | copy-start | bytes 1572868
  1.8 28.5 %all-to-all-start = ((bf16[32,5,4,128]{3,2,1,0:T(4,128)(2,1)}), bf16[32,5,4,128]{3,2,1,0:T(4,128)(2,1)S(1)}, u32[]{:S(2)}, u32[]{:S(2)}) async-start(bf16[32,5,4,128]{3,2,1,0:T(4,128)(2,1)} %get-tuple-element.21), calls=%async_computation | async-start | bytes 327680 | tf_op jit(solution)/shard_map/all_to_all | solution.py:237
  22.0 1.2 %copy-start = (bf16[8,32,2048]{2,1,0:T(8,128)(2,1)S(1)}, bf16[8,32,2048]{2,1,0:T(8,128)(2,1)}, u32[]{:S(2)}) copy-start(bf16[8,32,2048]{2,1,0:T(8,128)(2,1)} %moved.1) | copy-start | bytes 3145732
  23.2 4.9 %copy-start.4 = (s32[256]{0:T(256)S(1)}, s32[256]{0:T(256)}, u32[]{:S(2)}) copy-start(s32[256]{0:T(256)} %param.15) | copy-start | bytes 3076
  23.2 4.9 %copy-start.5 = (s32[256]{0:T(256)S(1)}, s32[256]{0:T(256)}, u32[]{:S(2)}) copy-start(s32[256]{0:T(256)} %param.13) | copy-start | bytes 3076
  23.6 6.6 %copy-start.2 = (bf16[4,5,4,128]{3,2,1,0:T(4,128)(2,1)S(1)}, bf16[4,5,4,128]{3,2,1,0:T(4,128)(2,1)}, u32[]{:S(2)}) copy-start(bf16[4,5,4,128]{3,2,1,0:T(4,128)(2,1)} %get-tuple-element.22.kept) | copy-start | bytes 61444
  23.6 21.9 %collective-permute-start = (bf16[12,32,1024]{2,1,0:T(8,128)(2,1)S(1)}, bf16[12,32,1024]{2,1,0:T(8,128)(2,1)S(1)}, u32[]{:S(2)}, u32[]{:S(2)}) collective-permute-start(bf16[12,32,1024]{2,1,0:T(8,128)(2,1)S(1)} %get-tuple-element.24), channel_id=1, source_target_pairs={{0,3},{1,2},{2,1},{3,0},{4,7},{5,6},{6,5},{7,4},{8,11},{9,10},{10,... | collective-permute-start | bytes 2359304 | tf_op jit(solution)/shard_map/ppermute | solution.py:282
  28.1 0.7 copy-start.3
  31.7 14.2 %all-to-all-start.1 = ((bf16[8,60,4,128]{3,2,1,0:T(4,128)(2,1)}), bf16[8,60,4,128]{3,2,1,0:T(4,128)(2,1)S(1)}, u32[]{:S(2)}, u32[]{:S(2)}) async-start(bf16[8,60,4,128]{3,2,1,0:T(4,128)(2,1)} %shard_map.83), calls=%async_computation.1 | async-start | bytes 983040 | tf_op jit(solution)/shard_map/all_to_all | solution.py:240
  36.8 0.7 copy-start.6

commit v16 on v13

--- a/solution.py
+++ b/solution.py
@@ -53,12 +53,8 @@
     )
 
 
-def swapped(step, y, x):
-    return y ^ (step % 2), x ^ (step // 2 * 3)
-
-
-def class_of(y, x):
-    return jnp.minimum(y, 3 - y), x // 2
+def shifted(y, step):
+    return (y + step) & (SIDE - 1)
 
 
 def place_of():
@@ -104,15 +100,14 @@
 
 
 def split_kernel(moved, resident, *outs):
-    y, x = place_of()
+    y, _ = place_of()
     for step, out in enumerate(outs):
-        low, half = class_of(*swapped(step, y, x))
-        for place, pair in enumerate((2 * low + half, 6 - 2 * low + half)):
-            for part in range(2):
-                lanes = pl.ds(pl.multiple_of(pair * HD + part * FEATURES, HD), HD)
-                columns = slice((part * PAIRS + place) * HD, (part * PAIRS + place + 1) * HD)
-                out[:MIG, :, columns] = moved[:, :, lanes]
-                out[MIG:, :, columns] = resident[:, :, lanes]
+        for part in range(2):
+            first = shifted(y, step) * PAIRS * HD + part * FEATURES
+            lanes = pl.ds(pl.multiple_of(first, PAIRS * HD), PAIRS * HD)
+            columns = slice(part * PAIRS * HD, (part + 1) * PAIRS * HD)
+            out[:MIG, :, columns] = moved[:, :, lanes]
+            out[MIG:, :, columns] = resident[:, :, lanes]
 
 
 def spread_kernel(origin, arrived, kept, asking):
@@ -131,7 +126,8 @@
     *blocks, payload, scores, weights, stats = rest
     column = lax.broadcasted_iota(jnp.int32, (1, HD), 1)
     block = column // STRIDE
-    y, x = swapped(jnp.where(block == 0, 0, (block + 1) % 3 + 1), *place_of())
+    y, x = place_of()
+    y = shifted(y, -jnp.where((block == 1) | (block == 2), 3 - block, block))
     position = (y * SIDE + x) * STRIDE + column % STRIDE
 
     def stored(row, place):
@@ -176,8 +172,8 @@
 
 
 def merge_kernel(origin, target, gathered, everyone, sent, kept):
-    y, x = place_of()
-    first = jnp.where(y > 1, 2, 0)
+    _, x = place_of()
+    first = x // 2 * 2
     asked = everyone[first + x % 2, :ROWS, :]
     keys = everyone[first, ROWS:, :]
     values = everyone[first + 1, ROWS:, :]
@@ -232,9 +228,7 @@
     decode_slot,
 ):
     shape = jax.ShapeDtypeStruct
-    whole = [(y, x) for y in range(SIDE) for x in range(SIDE)]
-    peers = [[y * SIDE + x for y in (low, 3 - low) for x in (2 * half, 2 * half + 1)] for low in range(2) for half in range(2)]
-
+    peers = [[y * SIDE + x for x in range(SIDE)] for y in range(SIDE)]
     turned = [[listed(place) for place in range(GROUPS)]]
 
     def around(array):
@@ -281,11 +275,8 @@
         moved=3 * 2**20,
     )(prefill_cache, resident_cache)
     blocks = [split[0]]
-    for step in (3, 1, 2):
-        steps = []
-        for y, x in whole:
-            other, side = swapped(step, y, x)
-            steps.append((y * SIDE + x, other * SIDE + side))
+    for step in (2, 1, 3):
+        steps = [(t, (t + step * SIDE) % SHARDS) for t in range(SHARDS)]
         blocks.append(lax.ppermute(split[step], "tensor", steps))
 
     asking = call(

time: 81.5 us -> 81.1 us (level)
  waiting for transfers between devices: 7.38 us -> 5.42 us
  starting transfers between devices: 33.8 us -> 35.5 us
    ppermute x3, waiting for transfers between devices: 7.38 us -> 5.03 us  [body(): blocks.append(lax.ppermute(split[step], 'tensor', steps))]
    ppermute x3, starting transfers between devices: 9.58 us -> 11.3 us  [body(): blocks.append(lax.ppermute(split[step], 'tensor', steps))]
  transfers between devices with their start and end apart: 5 -> 5, of which waited for: 1 -> 2; matrix products, arithmetic and copies ran while one was open for 0% -> 0% of each run, Pallas kernels for 2% -> 2%
where the time goes in v16:
time: 81.1 us; the launch traced here: 80.5 us
  starting transfers between devices  35.5 us (44%)
  blocking collectives  29.9 us (37%)
  Pallas kernels  7.25 us (9%)
  waiting for transfers between devices  5.42 us (7%)
  local copies, waits for them, and re-layouts  2 us (2%)
    all_to_all x1, blocking collectives, around(): lax.all_to_all(array, 'group', 0, 0, axis_index_groups=turned, tiled=True)  21.2 us
    all_to_all x1, starting transfers between devices, around(): lax.all_to_all(array, 'group', 0, 0, axis_index_groups=turned, tiled=True)  20.2 us
    ppermute x3, starting transfers between devices, body(): blocks.append(lax.ppermute(split[step], 'tensor', steps))  11.3 us
    all_to_all x1, blocking collectives, across(): lax.all_to_all(array, 'tensor', 0, 0, axis_index_groups=peers, tiled=True)  8.71 us
    ppermute x3, waiting for transfers between devices, body(): blocks.append(lax.ppermute(split[step], 'tensor', steps))  5.03 us
    all_to_all x1, starting transfers between devices, across(): lax.all_to_all(array, 'tensor', 0, 0, axis_index_groups=peers, tiled=True)  4.01 us
    unnamed x14, local copies, waits for them, and re-layouts  1.92 us
    pallas_call x1, Pallas kernels, body(): call(pack_kernel, (shape((GROUPS, TILES, STEPS, HD), BF), shape((RES, TIL...  1.75 us
  transfers between devices with their start and end apart: 5, of which 2 were waited for; matrix products, arithmetic and copies ran while one was open for 0% of the time, Pallas kernels for 2%

profile of v16, /device:TPU:1, one launch (start us, length us, event | category | flops | bytes accessed | tf_op | source)
XLA Modules:
  0.0 80.5 jit_solution(10909572242043914500)
XLA Ops:
  0.0 0.0 copy-start.1
  0.0 1.7 %shard_map.82 = (bf16[32,5,4,128]{3,2,1,0:T(4,128)(2,1)}, bf16[4,5,4,128]{3,2,1,0:T(4,128)(2,1)}) custom-call(s32[2,128]{1,0:T(2,128)} %bitcast.15, s32[2,128]{1,0:T(2,128)} %bitcast.14, bf16[12,4,4,128]{3,2,1,0:T(4,128)(2,1)} %bitcast.13, bf16[12,4,2048]{2,1,0:T(4,128)(2,1)} %fresh.1), custom_call_target="tpu_custom_call" | custom-call | tf_op jit(solution)/shard_map/pallas_call | solution.py:241
  1.8 20.2 %all-to-all-start = ((bf16[32,5,4,128]{3,2,1,0:T(4,128)(2,1)}), bf16[32,5,4,128]{3,2,1,0:T(4,128)(2,1)S(1)}, u32[]{:S(2)}, u32[]{:S(2)}) async-start(bf16[32,5,4,128]{3,2,1,0:T(4,128)(2,1)} %get-tuple-element.23), calls=%async_computation | async-start | bytes 327680 | tf_op jit(solution)/shard_map/all_to_all | solution.py:235
  22.0 0.0 copy-done.1
  22.0 0.0 copy-start
  22.0 1.2 %copy-done = bf16[8,32,2048]{2,1,0:T(8,128)(2,1)S(1)} copy-done((bf16[8,32,2048]{2,1,0:T(8,128)(2,1)S(1)}, bf16[8,32,2048]{2,1,0:T(8,128)(2,1)}, u32[]{:S(2)}) %copy-start) | copy-done | bytes 1048600
  23.2 0.2 shard_map.84
  23.4 4.8 %collective-permute-start = (bf16[12,32,512]{2,1,0:T(8,128)(2,1)S(1)}, bf16[12,32,512]{2,1,0:T(8,128)(2,1)S(1)}, u32[]{:S(2)}, u32[]{:S(2)}) collective-permute-start(bf16[12,32,512]{2,1,0:T(8,128)(2,1)S(1)} %get-tuple-element.26), channel_id=1, source_target_pairs={{0,8},{1,9},{2,10},{3,11},{4,12},{5,13},{6,14},{7,15},{8,0},{9,1},... | collective-permute-start | bytes 1179656 | tf_op jit(solution)/shard_map/ppermute | solution.py:280
  28.3 2.3 %collective-permute-start.1 = (bf16[12,32,512]{2,1,0:T(8,128)(2,1)S(1)}, bf16[12,32,512]{2,1,0:T(8,128)(2,1)S(1)}, u32[]{:S(2)}, u32[]{:S(2)}) collective-permute-start(bf16[12,32,512]{2,1,0:T(8,128)(2,1)S(1)} %get-tuple-element.27), channel_id=1, source_target_pairs={{0,4},{1,5},{2,6},{3,7},{4,8},{5,9},{6,10},{7,11},{8,12},{9,13},{1... | collective-permute-start | bytes 1179656 | tf_op jit(solution)/shard_map/ppermute | solution.py:280
  30.6 0.0 copy-start.6
  30.6 4.2 %collective-permute-start.2 = (bf16[12,32,512]{2,1,0:T(8,128)(2,1)S(1)}, bf16[12,32,512]{2,1,0:T(8,128)(2,1)S(1)}, u32[]{:S(2)}, u32[]{:S(2)}) collective-permute-start(bf16[12,32,512]{2,1,0:T(8,128)(2,1)S(1)} %get-tuple-element.28), channel_id=1, source_target_pairs={{0,12},{1,13},{2,14},{3,15},{4,0},{5,1},{6,2},{7,3},{8,4},{9,5},{1... | collective-permute-start | bytes 1179656 | tf_op jit(solution)/shard_map/ppermute | solution.py:280
  34.8 0.0 copy-start.2
  34.8 0.0 copy-start.4
  34.8 0.0 copy-start.5
  34.8 0.0 copy-done.6
  34.8 0.1 dynamic_slice.3
  34.9 0.0 copy-start.3
  34.9 0.6 copy-done.4
  35.5 0.0 copy-done.5
  35.5 0.1 copy-done.3
  35.6 0.2 fusion
  35.8 0.1 pad_add_fusion.lengths
  35.9 0.0 all-to-all-done.arrived
  35.9 0.0 copy-done.2
  35.9 1.3 %shard_map.83 = bf16[4,60,4,128]{3,2,1,0:T(4,128)(2,1)} custom-call(s32[8]{0:T(128)S(1)} %and_select_fusion.origin, bf16[32,5,4,128]{3,2,1,0:T(4,128)(2,1)S(1)} %all-to-all-done.arrived, bf16[4,5,4,128]{3,2,1,0:T(4,128)(2,1)S(1)} %copy-done.2), custom_call_target="tpu_custom_call" | custom-call | tf_op jit(solution)/shard_map/pallas_call | solution.py:282
  37.2 4.0 %all-to-all-start.1 = ((bf16[4,60,4,128]{3,2,1,0:T(4,128)(2,1)}), bf16[4,60,4,128]{3,2,1,0:T(4,128)(2,1)S(1)}, u32[]{:S(2)}, u32[]{:S(2)}) async-start(bf16[4,60,4,128]{3,2,1,0:T(4,128)(2,1)} %shard_map.83), calls=%async_computation.1 | async-start | bytes 491520 | tf_op jit(solution)/shard_map/all_to_all | solution.py:238
  41.3 0.0 collective-permute-done.rest_1_
  41.3 5.0 %collective-permute-done.1.rest_2_ = bf16[12,32,512]{2,1,0:T(8,128)(2,1)S(1)} collective-permute-done((bf16[12,32,512]{2,1,0:T(8,128)(2,1)S(1)}, bf16[12,32,512]{2,1,0:T(8,128)(2,1)S(1)}, u32[]{:S(2)}, u32[]{:S(2)}) %collective-permute-start.1) | collective-permute-done | bytes 393248 | tf_op jit(solution)/shard_map/ppermute | solution.py:280
  46.3 0.0 collective-permute-done.2.rest_3_
  46.3 0.4 all-to-all-done.1
  46.7 1.3 %shard_map.85 = bf16[4,208,128]{2,1,0:T(8,128)(2,1)S(1)} custom-call(s32[12]{0:T(128)S(1)} %pad_add_fusion.lengths, s32[8]{0:T(128)S(1)} %and_select_fusion.1.target, bf16[4,240,128]{2,1,0:T(8,128)(2,1)S(1)} %bitcast.11, bf16[12,32,512]{2,1,0:T(8,128)(2,1)S(1)} %get-tuple-element.25.rest_0_, bf16[12,32,512]{2,1,0:T(8,128)(2,1)S(1)} %collective-permute-done.rest_1_, ...), custom_call_target="tpu_custom_call" | custom-call | flops 100000000 | bytes 3145728 | tf_op jit(solution)/shard_map/pallas_call | solution.py:287
  48.0 8.7 %all_to_all.20.gathered = bf16[4,208,128]{2,1,0:T(8,128)(2,1)S(1)} all-to-all(bf16[4,208,128]{2,1,0:T(8,128)(2,1)S(1)} %shard_map.85), channel_id=1, replica_groups={{0,1,2,3},{4,5,6,7},{8,9,10,11},{12,13,14,15},{16,17,18,19},{20,21,22,2..., dimensions={0} | all-to-all | bytes 425984 | tf_op jit(solution)/shard_map/all_to_all | solution.py:238
  56.7 1.5 %shard_map.86 = (bf16[32,16,128]{2,1,0:T(8,128)(2,1)S(1)}, bf16[4,16,128]{2,1,0:T(8,128)(2,1)S(1)}) custom-call(s32[8]{0:T(128)S(1)} %and_select_fusion.origin, s32[8]{0:T(128)S(1)} %and_select_fusion.1.target, bf16[4,208,128]{2,1,0:T(8,128)(2,1)S(1)} %all_to_all.20.gathered, bf16[4,240,128]{2,1,0:T(8,128)(2,1)S(1)} %bitcast.12), custom_call_target="tpu_custom_call" | custom-call | tf_op jit(solution)/shard_map/pallas_call | solution.py:301
  58.2 21.2 %all_to_all.21.returned = bf16[32,16,128]{2,1,0:T(8,128)(2,1)S(1)} all-to-all(bf16[32,16,128]{2,1,0:T(8,128)(2,1)S(1)} %get-tuple-element.29), channel_id=1, replica_groups={{256,496,224,464,192,432,160,400,128,368,96,336,64,304,32,272,0,240,480..., dimensions={0} | all-to-all | bytes 262144 | tf_op jit(solution)/shard_map/all_to_all | solution.py:235
  79.3 1.2 %shard_map.87 = bf16[12,16,128]{2,1,0:T(8,128)(2,1)} custom-call(s32[8]{0:T(128)S(1)} %and_select_fusion.1.target, bf16[32,16,128]{2,1,0:T(8,128)(2,1)S(1)} %all_to_all.21.returned, bf16[4,16,128]{2,1,0:T(8,128)(2,1)S(1)} %get-tuple-element.30.kept), custom_call_target="tpu_custom_call" | custom-call | tf_op jit(solution)/shard_map/pallas_call | solution.py:308
  (3 shorter events, 0.0 us)
Async XLA Ops:
  0.0 22.0 %copy-start.1 = (bf16[4,32,2048]{2,1,0:T(8,128)(2,1)S(1)}, bf16[4,32,2048]{2,1,0:T(8,128)(2,1)}, u32[]{:S(2)}) copy-start(bf16[4,32,2048]{2,1,0:T(8,128)(2,1)} %resident.1) | copy-start | bytes 1572868
  1.8 34.2 %all-to-all-start = ((bf16[32,5,4,128]{3,2,1,0:T(4,128)(2,1)}), bf16[32,5,4,128]{3,2,1,0:T(4,128)(2,1)S(1)}, u32[]{:S(2)}, u32[]{:S(2)}) async-start(bf16[32,5,4,128]{3,2,1,0:T(4,128)(2,1)} %get-tuple-element.23), calls=%async_computation | async-start | bytes 327680 | tf_op jit(solution)/shard_map/all_to_all | solution.py:235
  22.0 1.2 %copy-start = (bf16[8,32,2048]{2,1,0:T(8,128)(2,1)S(1)}, bf16[8,32,2048]{2,1,0:T(8,128)(2,1)}, u32[]{:S(2)}) copy-start(bf16[8,32,2048]{2,1,0:T(8,128)(2,1)} %moved.1) | copy-start | bytes 3145732
  23.4 17.8 %collective-permute-start = (bf16[12,32,512]{2,1,0:T(8,128)(2,1)S(1)}, bf16[12,32,512]{2,1,0:T(8,128)(2,1)S(1)}, u32[]{:S(2)}, u32[]{:S(2)}) collective-permute-start(bf16[12,32,512]{2,1,0:T(8,128)(2,1)S(1)} %get-tuple-element.26), channel_id=1, source_target_pairs={{0,8},{1,9},{2,10},{3,11},{4,12},{5,13},{6,14},{7,15},{8,0},{9,1},... | collective-permute-start | bytes 1179656 | tf_op jit(solution)/shard_map/ppermute | solution.py:280
  28.3 18.0 %collective-permute-start.1 = (bf16[12,32,512]{2,1,0:T(8,128)(2,1)S(1)}, bf16[12,32,512]{2,1,0:T(8,128)(2,1)S(1)}, u32[]{:S(2)}, u32[]{:S(2)}) collective-permute-start(bf16[12,32,512]{2,1,0:T(8,128)(2,1)S(1)} %get-tuple-element.27), channel_id=1, source_target_pairs={{0,4},{1,5},{2,6},{3,7},{4,8},{5,9},{6,10},{7,11},{8,12},{9,13},{1... | collective-permute-start | bytes 1179656 | tf_op jit(solution)/shard_map/ppermute | solution.py:280
  30.6 4.3 %copy-start.6 = (s32[128]{0:T(128)S(1)}, s32[128]{0:T(128)}, u32[]{:S(2)}) copy-start(s32[128]{0:T(128)} %param.12) | copy-start | bytes 1540
  30.6 15.7 %collective-permute-start.2 = (bf16[12,32,512]{2,1,0:T(8,128)(2,1)S(1)}, bf16[12,32,512]{2,1,0:T(8,128)(2,1)S(1)}, u32[]{:S(2)}, u32[]{:S(2)}) collective-permute-start(bf16[12,32,512]{2,1,0:T(8,128)(2,1)S(1)} %get-tuple-element.28), channel_id=1, source_target_pairs={{0,12},{1,13},{2,14},{3,15},{4,0},{5,1},{6,2},{7,3},{8,4},{9,5},{1... | collective-permute-start | bytes 1179656 | tf_op jit(solution)/shard_map/ppermute | solution.py:280
  34.8 1.1 %copy-start.2 = (bf16[4,5,4,128]{3,2,1,0:T(4,128)(2,1)S(1)}, bf16[4,5,4,128]{3,2,1,0:T(4,128)(2,1)}, u32[]{:S(2)}) copy-start(bf16[4,5,4,128]{3,2,1,0:T(4,128)(2,1)} %get-tuple-element.24.kept) | copy-start | bytes 61444
  34.8 0.7 copy-start.4
  34.8 0.7 copy-start.5
  34.9 0.7 copy-start.3
  37.2 9.5 %all-to-all-start.1 = ((bf16[4,60,4,128]{3,2,1,0:T(4,128)(2,1)}), bf16[4,60,4,128]{3,2,1,0:T(4,128)(2,1)S(1)}, u32[]{:S(2)}, u32[]{:S(2)}) async-start(bf16[4,60,4,128]{3,2,1,0:T(4,128)(2,1)} %shard_map.83), calls=%async_computation.1 | async-start | bytes 491520 | tf_op jit(solution)/shard_map/all_to_all | solution.py:238

commit v17 on v16

--- a/solution.py
+++ b/solution.py
@@ -127,7 +127,7 @@
     column = lax.broadcasted_iota(jnp.int32, (1, HD), 1)
     block = column // STRIDE
     y, x = place_of()
-    y = shifted(y, -jnp.where((block == 1) | (block == 2), 3 - block, block))
+    y = shifted(y, -jnp.where(block > 1, 5 - block, block))
     position = (y * SIDE + x) * STRIDE + column % STRIDE
 
     def stored(row, place):
@@ -275,7 +275,7 @@
         moved=3 * 2**20,
     )(prefill_cache, resident_cache)
     blocks = [split[0]]
-    for step in (2, 1, 3):
+    for step in (1, 3, 2):
         steps = [(t, (t + step * SIDE) % SHARDS) for t in range(SHARDS)]
         blocks.append(lax.ppermute(split[step], "tensor", steps))
 

time: 81.1 us -> 81.9 us (level)
  starting transfers between devices: 35.5 us -> 34.3 us
  waiting for transfers between devices: 5.42 us -> 6.54 us
    ppermute x3, waiting for transfers between devices: 5.03 us -> 6.54 us  [body(): blocks.append(lax.ppermute(split[step], 'tensor', steps))]
    ppermute x3, starting transfers between devices: 11.3 us -> 10.1 us  [body(): blocks.append(lax.ppermute(split[step], 'tensor', steps))]
  transfers between devices with their start and end apart: 5 -> 5, of which waited for: 2 -> 1; matrix products, arithmetic and copies ran while one was open for 0% -> 0% of each run, Pallas kernels for 2% -> 2%
where the time goes in v17:
time: 81.9 us; the launch traced here: 80.7 us
  starting transfers between devices  34.3 us (42%)
  blocking collectives  30.1 us (37%)
  Pallas kernels  7.25 us (9%)
  waiting for transfers between devices  6.54 us (8%)
  local copies, waits for them, and re-layouts  2 us (2%)
    all_to_all x1, blocking collectives, around(): lax.all_to_all(array, 'group', 0, 0, axis_index_groups=turned, tiled=True)  21 us
    all_to_all x1, starting transfers between devices, around(): lax.all_to_all(array, 'group', 0, 0, axis_index_groups=turned, tiled=True)  20.2 us
    ppermute x3, starting transfers between devices, body(): blocks.append(lax.ppermute(split[step], 'tensor', steps))  10.1 us
    all_to_all x1, blocking collectives, across(): lax.all_to_all(array, 'tensor', 0, 0, axis_index_groups=peers, tiled=True)  9.09 us
    ppermute x3, waiting for transfers between devices, body(): blocks.append(lax.ppermute(split[step], 'tensor', steps))  6.54 us
    all_to_all x1, starting transfers between devices, across(): lax.all_to_all(array, 'tensor', 0, 0, axis_index_groups=peers, tiled=True)  4.01 us
    unnamed x14, local copies, waits for them, and re-layouts  1.92 us
    pallas_call x1, Pallas kernels, body(): call(pack_kernel, (shape((GROUPS, TILES, STEPS, HD), BF), shape((RES, TIL...  1.75 us
  transfers between devices with their start and end apart: 5, of which 1 were waited for; matrix products, arithmetic and copies ran while one was open for 0% of the time, Pallas kernels for 2%

profile of v17, /device:TPU:1, one launch (start us, length us, event | category | flops | bytes accessed | tf_op | source)
XLA Modules:
  0.0 80.7 jit_solution(4474705756341616390)
XLA Ops:
  0.0 0.0 copy-start.1
  0.0 1.7 %shard_map.82 = (bf16[32,5,4,128]{3,2,1,0:T(4,128)(2,1)}, bf16[4,5,4,128]{3,2,1,0:T(4,128)(2,1)}) custom-call(s32[2,128]{1,0:T(2,128)} %bitcast.15, s32[2,128]{1,0:T(2,128)} %bitcast.14, bf16[12,4,4,128]{3,2,1,0:T(4,128)(2,1)} %bitcast.13, bf16[12,4,2048]{2,1,0:T(4,128)(2,1)} %fresh.1), custom_call_target="tpu_custom_call" | custom-call | tf_op jit(solution)/shard_map/pallas_call | solution.py:241
  1.8 20.2 %all-to-all-start = ((bf16[32,5,4,128]{3,2,1,0:T(4,128)(2,1)}), bf16[32,5,4,128]{3,2,1,0:T(4,128)(2,1)S(1)}, u32[]{:S(2)}, u32[]{:S(2)}) async-start(bf16[32,5,4,128]{3,2,1,0:T(4,128)(2,1)} %get-tuple-element.23), calls=%async_computation | async-start | bytes 327680 | tf_op jit(solution)/shard_map/all_to_all | solution.py:235
  22.0 0.0 copy-done.1
  22.0 0.0 copy-start
  22.0 1.2 %copy-done = bf16[8,32,2048]{2,1,0:T(8,128)(2,1)S(1)} copy-done((bf16[8,32,2048]{2,1,0:T(8,128)(2,1)S(1)}, bf16[8,32,2048]{2,1,0:T(8,128)(2,1)}, u32[]{:S(2)}) %copy-start) | copy-done | bytes 1048600
  23.2 0.2 shard_map.84
  23.4 3.2 %collective-permute-start = (bf16[12,32,512]{2,1,0:T(8,128)(2,1)S(1)}, bf16[12,32,512]{2,1,0:T(8,128)(2,1)S(1)}, u32[]{:S(2)}, u32[]{:S(2)}) collective-permute-start(bf16[12,32,512]{2,1,0:T(8,128)(2,1)S(1)} %get-tuple-element.26), channel_id=1, source_target_pairs={{0,4},{1,5},{2,6},{3,7},{4,8},{5,9},{6,10},{7,11},{8,12},{9,13},{1... | collective-permute-start | bytes 1179656 | tf_op jit(solution)/shard_map/ppermute | solution.py:280
  26.6 3.4 %collective-permute-start.1 = (bf16[12,32,512]{2,1,0:T(8,128)(2,1)S(1)}, bf16[12,32,512]{2,1,0:T(8,128)(2,1)S(1)}, u32[]{:S(2)}, u32[]{:S(2)}) collective-permute-start(bf16[12,32,512]{2,1,0:T(8,128)(2,1)S(1)} %get-tuple-element.27), channel_id=1, source_target_pairs={{0,12},{1,13},{2,14},{3,15},{4,0},{5,1},{6,2},{7,3},{8,4},{9,5},{1... | collective-permute-start | bytes 1179656 | tf_op jit(solution)/shard_map/ppermute | solution.py:280
  30.0 0.0 copy-start.6
  30.0 3.5 %collective-permute-start.2 = (bf16[12,32,512]{2,1,0:T(8,128)(2,1)S(1)}, bf16[12,32,512]{2,1,0:T(8,128)(2,1)S(1)}, u32[]{:S(2)}, u32[]{:S(2)}) collective-permute-start(bf16[12,32,512]{2,1,0:T(8,128)(2,1)S(1)} %get-tuple-element.28), channel_id=1, source_target_pairs={{0,8},{1,9},{2,10},{3,11},{4,12},{5,13},{6,14},{7,15},{8,0},{9,1},... | collective-permute-start | bytes 1179656 | tf_op jit(solution)/shard_map/ppermute | solution.py:280
  33.6 0.0 copy-start.2
  33.6 0.0 copy-start.4
  33.6 0.0 copy-start.5
  33.6 0.0 copy-done.6
  33.6 0.1 dynamic_slice.3
  33.7 0.0 copy-start.3
  33.7 0.6 copy-done.4
  34.3 0.0 copy-done.5
  34.3 0.1 copy-done.3
  34.4 0.2 fusion
  34.6 0.1 pad_add_fusion.lengths
  34.7 0.0 all-to-all-done.arrived
  34.7 0.0 copy-done.2
  34.7 1.3 %shard_map.83 = bf16[4,60,4,128]{3,2,1,0:T(4,128)(2,1)} custom-call(s32[8]{0:T(128)S(1)} %and_select_fusion.origin, bf16[32,5,4,128]{3,2,1,0:T(4,128)(2,1)S(1)} %all-to-all-done.arrived, bf16[4,5,4,128]{3,2,1,0:T(4,128)(2,1)S(1)} %copy-done.2), custom_call_target="tpu_custom_call" | custom-call | tf_op jit(solution)/shard_map/pallas_call | solution.py:282
  36.0 4.0 %all-to-all-start.1 = ((bf16[4,60,4,128]{3,2,1,0:T(4,128)(2,1)}), bf16[4,60,4,128]{3,2,1,0:T(4,128)(2,1)S(1)}, u32[]{:S(2)}, u32[]{:S(2)}) async-start(bf16[4,60,4,128]{3,2,1,0:T(4,128)(2,1)} %shard_map.83), calls=%async_computation.1 | async-start | bytes 491520 | tf_op jit(solution)/shard_map/all_to_all | solution.py:238
  40.0 0.0 collective-permute-done.rest_1_
  40.1 0.0 collective-permute-done.1.rest_2_
  40.1 6.5 %collective-permute-done.2.rest_3_ = bf16[12,32,512]{2,1,0:T(8,128)(2,1)S(1)} collective-permute-done((bf16[12,32,512]{2,1,0:T(8,128)(2,1)S(1)}, bf16[12,32,512]{2,1,0:T(8,128)(2,1)S(1)}, u32[]{:S(2)}, u32[]{:S(2)}) %collective-permute-start.2) | collective-permute-done | bytes 393248 | tf_op jit(solution)/shard_map/ppermute | solution.py:280
  46.6 0.0 all-to-all-done.1
  46.6 1.3 %shard_map.85 = bf16[4,208,128]{2,1,0:T(8,128)(2,1)S(1)} custom-call(s32[12]{0:T(128)S(1)} %pad_add_fusion.lengths, s32[8]{0:T(128)S(1)} %and_select_fusion.1.target, bf16[4,240,128]{2,1,0:T(8,128)(2,1)S(1)} %bitcast.11, bf16[12,32,512]{2,1,0:T(8,128)(2,1)S(1)} %get-tuple-element.25.rest_0_, bf16[12,32,512]{2,1,0:T(8,128)(2,1)S(1)} %collective-permute-done.rest_1_, ...), custom_call_target="tpu_custom_call" | custom-call | flops 100000000 | bytes 3145728 | tf_op jit(solution)/shard_map/pallas_call | solution.py:287
  47.9 9.1 %all_to_all.20.gathered = bf16[4,208,128]{2,1,0:T(8,128)(2,1)S(1)} all-to-all(bf16[4,208,128]{2,1,0:T(8,128)(2,1)S(1)} %shard_map.85), channel_id=1, replica_groups={{0,1,2,3},{4,5,6,7},{8,9,10,11},{12,13,14,15},{16,17,18,19},{20,21,22,2..., dimensions={0} | all-to-all | bytes 425984 | tf_op jit(solution)/shard_map/all_to_all | solution.py:238
  57.0 1.5 %shard_map.86 = (bf16[32,16,128]{2,1,0:T(8,128)(2,1)S(1)}, bf16[4,16,128]{2,1,0:T(8,128)(2,1)S(1)}) custom-call(s32[8]{0:T(128)S(1)} %and_select_fusion.origin, s32[8]{0:T(128)S(1)} %and_select_fusion.1.target, bf16[4,208,128]{2,1,0:T(8,128)(2,1)S(1)} %all_to_all.20.gathered, bf16[4,240,128]{2,1,0:T(8,128)(2,1)S(1)} %bitcast.12), custom_call_target="tpu_custom_call" | custom-call | tf_op jit(solution)/shard_map/pallas_call | solution.py:301
  58.5 21.0 %all_to_all.21.returned = bf16[32,16,128]{2,1,0:T(8,128)(2,1)S(1)} all-to-all(bf16[32,16,128]{2,1,0:T(8,128)(2,1)S(1)} %get-tuple-element.29), channel_id=1, replica_groups={{256,496,224,464,192,432,160,400,128,368,96,336,64,304,32,272,0,240,480..., dimensions={0} | all-to-all | bytes 262144 | tf_op jit(solution)/shard_map/all_to_all | solution.py:235
  79.5 1.2 %shard_map.87 = bf16[12,16,128]{2,1,0:T(8,128)(2,1)} custom-call(s32[8]{0:T(128)S(1)} %and_select_fusion.1.target, bf16[32,16,128]{2,1,0:T(8,128)(2,1)S(1)} %all_to_all.21.returned, bf16[4,16,128]{2,1,0:T(8,128)(2,1)S(1)} %get-tuple-element.30.kept), custom_call_target="tpu_custom_call" | custom-call | tf_op jit(solution)/shard_map/pallas_call | solution.py:308
  (3 shorter events, 0.0 us)
Async XLA Ops:
  0.0 22.0 %copy-start.1 = (bf16[4,32,2048]{2,1,0:T(8,128)(2,1)S(1)}, bf16[4,32,2048]{2,1,0:T(8,128)(2,1)}, u32[]{:S(2)}) copy-start(bf16[4,32,2048]{2,1,0:T(8,128)(2,1)} %resident.1) | copy-start | bytes 1572868
  1.8 32.9 %all-to-all-start = ((bf16[32,5,4,128]{3,2,1,0:T(4,128)(2,1)}), bf16[32,5,4,128]{3,2,1,0:T(4,128)(2,1)S(1)}, u32[]{:S(2)}, u32[]{:S(2)}) async-start(bf16[32,5,4,128]{3,2,1,0:T(4,128)(2,1)} %get-tuple-element.23), calls=%async_computation | async-start | bytes 327680 | tf_op jit(solution)/shard_map/all_to_all | solution.py:235
  22.0 1.2 %copy-start = (bf16[8,32,2048]{2,1,0:T(8,128)(2,1)S(1)}, bf16[8,32,2048]{2,1,0:T(8,128)(2,1)}, u32[]{:S(2)}) copy-start(bf16[8,32,2048]{2,1,0:T(8,128)(2,1)} %moved.1) | copy-start | bytes 3145732
  23.4 16.6 %collective-permute-start = (bf16[12,32,512]{2,1,0:T(8,128)(2,1)S(1)}, bf16[12,32,512]{2,1,0:T(8,128)(2,1)S(1)}, u32[]{:S(2)}, u32[]{:S(2)}) collective-permute-start(bf16[12,32,512]{2,1,0:T(8,128)(2,1)S(1)} %get-tuple-element.26), channel_id=1, source_target_pairs={{0,4},{1,5},{2,6},{3,7},{4,8},{5,9},{6,10},{7,11},{8,12},{9,13},{1... | collective-permute-start | bytes 1179656 | tf_op jit(solution)/shard_map/ppermute | solution.py:280
  26.6 13.4 %collective-permute-start.1 = (bf16[12,32,512]{2,1,0:T(8,128)(2,1)S(1)}, bf16[12,32,512]{2,1,0:T(8,128)(2,1)S(1)}, u32[]{:S(2)}, u32[]{:S(2)}) collective-permute-start(bf16[12,32,512]{2,1,0:T(8,128)(2,1)S(1)} %get-tuple-element.27), channel_id=1, source_target_pairs={{0,12},{1,13},{2,14},{3,15},{4,0},{5,1},{6,2},{7,3},{8,4},{9,5},{1... | collective-permute-start | bytes 1179656 | tf_op jit(solution)/shard_map/ppermute | solution.py:280
  30.0 3.6 %copy-start.6 = (s32[128]{0:T(128)S(1)}, s32[128]{0:T(128)}, u32[]{:S(2)}) copy-start(s32[128]{0:T(128)} %param.12) | copy-start | bytes 1540
  30.0 16.6 %collective-permute-start.2 = (bf16[12,32,512]{2,1,0:T(8,128)(2,1)S(1)}, bf16[12,32,512]{2,1,0:T(8,128)(2,1)S(1)}, u32[]{:S(2)}, u32[]{:S(2)}) collective-permute-start(bf16[12,32,512]{2,1,0:T(8,128)(2,1)S(1)} %get-tuple-element.28), channel_id=1, source_target_pairs={{0,8},{1,9},{2,10},{3,11},{4,12},{5,13},{6,14},{7,15},{8,0},{9,1},... | collective-permute-start | bytes 1179656 | tf_op jit(solution)/shard_map/ppermute | solution.py:280
  33.6 1.1 %copy-start.2 = (bf16[4,5,4,128]{3,2,1,0:T(4,128)(2,1)S(1)}, bf16[4,5,4,128]{3,2,1,0:T(4,128)(2,1)}, u32[]{:S(2)}) copy-start(bf16[4,5,4,128]{3,2,1,0:T(4,128)(2,1)} %get-tuple-element.24.kept) | copy-start | bytes 61444
  33.6 0.7 copy-start.4
  33.6 0.7 copy-start.5
  33.7 0.7 copy-start.3
  36.0 10.6 %all-to-all-start.1 = ((bf16[4,60,4,128]{3,2,1,0:T(4,128)(2,1)}), bf16[4,60,4,128]{3,2,1,0:T(4,128)(2,1)S(1)}, u32[]{:S(2)}, u32[]{:S(2)}) async-start(bf16[4,60,4,128]{3,2,1,0:T(4,128)(2,1)} %shard_map.83), calls=%async_computation.1 | async-start | bytes 491520 | tf_op jit(solution)/shard_map/all_to_all | solution.py:238

commit v18 on v16

--- a/solution.py
+++ b/solution.py
@@ -210,11 +210,15 @@
         kept[slot] = result[(MIG + slot) * QROWS : (MIG + slot + 1) * QROWS]
 
 
-def select_kernel(target, returned, kept, out):
-    for slot in range(RES):
-        out[slot] = kept[slot]
-    for slot in range(MIG):
-        out[RES + slot] = returned[listed(target[slot])]
+def select_kernel(target, returned, kept, out, sems):
+    copies = []
+    for slot in range(SLOTS):
+        source = kept.at[slot] if slot < RES else returned.at[listed(target[slot - RES])]
+        copies.append(pltpu.make_async_copy(source, out.at[slot], sems.at[slot]))
+    for copy in copies:
+        copy.start()
+    for copy in copies:
+        copy.wait()
 
 
 def body(
@@ -305,7 +309,13 @@
     )(origin, target, gathered, everyone)
     returned = around(finished)
 
-    result = call(select_kernel, shape((SLOTS, QROWS, HD), BF), [SM, VM, VM])(target, returned, here)
+    result = call(
+        select_kernel,
+        shape((SLOTS, QROWS, HD), BF),
+        [SM, VM, VM],
+        scratch=[pltpu.SemaphoreType.DMA((SLOTS,))],
+        places=ANY,
+    )(target, returned, here)
     result = result.reshape(SLOTS, HEADS, STEPS, HD).transpose(0, 2, 1, 3)
     return result.reshape(SLOTS, STEPS, HEADS * HD)
 

time: 81.1 us -> 81.1 us (level)
  no operation moved by 1% of the time
where the time goes in v18:
time: 81.1 us; the launch traced here: 80.6 us
  starting transfers between devices  35.5 us (44%)
  blocking collectives  29.9 us (37%)
  Pallas kernels  7.34 us (9%)
  waiting for transfers between devices  5.42 us (7%)
  local copies, waits for them, and re-layouts  2 us (2%)
    all_to_all x1, blocking collectives, around(): lax.all_to_all(array, 'group', 0, 0, axis_index_groups=turned, tiled=True)  21.2 us
    all_to_all x1, starting transfers between devices, around(): lax.all_to_all(array, 'group', 0, 0, axis_index_groups=turned, tiled=True)  20.2 us
    ppermute x3, starting transfers between devices, body(): blocks.append(lax.ppermute(split[step], 'tensor', steps))  11.3 us
    all_to_all x1, blocking collectives, across(): lax.all_to_all(array, 'tensor', 0, 0, axis_index_groups=peers, tiled=True)  8.71 us
    ppermute x3, waiting for transfers between devices, body(): blocks.append(lax.ppermute(split[step], 'tensor', steps))  5.03 us
    all_to_all x1, starting transfers between devices, across(): lax.all_to_all(array, 'tensor', 0, 0, axis_index_groups=peers, tiled=True)  4.01 us
    unnamed x14, local copies, waits for them, and re-layouts  1.92 us
    pallas_call x1, Pallas kernels, body(): call(pack_kernel, (shape((GROUPS, TILES, STEPS, HD), BF), shape((RES, TIL...  1.75 us
  transfers between devices with their start and end apart: 5, of which 2 were waited for; matrix products, arithmetic and copies ran while one was open for 0% of the time, Pallas kernels for 2%

profile of v18, /device:TPU:1, one launch (start us, length us, event | category | flops | bytes accessed | tf_op | source)
XLA Modules:
  0.0 80.6 jit_solution(15456577786531216087)
XLA Ops:
  0.0 0.0 copy-start.1
  0.0 1.7 %shard_map.82 = (bf16[32,5,4,128]{3,2,1,0:T(4,128)(2,1)}, bf16[4,5,4,128]{3,2,1,0:T(4,128)(2,1)}) custom-call(s32[2,128]{1,0:T(2,128)} %bitcast.15, s32[2,128]{1,0:T(2,128)} %bitcast.14, bf16[12,4,4,128]{3,2,1,0:T(4,128)(2,1)} %bitcast.13, bf16[12,4,2048]{2,1,0:T(4,128)(2,1)} %fresh.1), custom_call_target="tpu_custom_call" | custom-call | tf_op jit(solution)/shard_map/pallas_call | solution.py:245
  1.8 20.2 %all-to-all-start = ((bf16[32,5,4,128]{3,2,1,0:T(4,128)(2,1)}), bf16[32,5,4,128]{3,2,1,0:T(4,128)(2,1)S(1)}, u32[]{:S(2)}, u32[]{:S(2)}) async-start(bf16[32,5,4,128]{3,2,1,0:T(4,128)(2,1)} %get-tuple-element.23), calls=%async_computation | async-start | bytes 327680 | tf_op jit(solution)/shard_map/all_to_all | solution.py:239
  22.0 0.0 copy-done.1
  22.0 0.0 copy-start
  22.0 1.2 %copy-done = bf16[8,32,2048]{2,1,0:T(8,128)(2,1)S(1)} copy-done((bf16[8,32,2048]{2,1,0:T(8,128)(2,1)S(1)}, bf16[8,32,2048]{2,1,0:T(8,128)(2,1)}, u32[]{:S(2)}) %copy-start) | copy-done | bytes 1048600
  23.2 0.2 shard_map.84
  23.4 4.8 %collective-permute-start = (bf16[12,32,512]{2,1,0:T(8,128)(2,1)S(1)}, bf16[12,32,512]{2,1,0:T(8,128)(2,1)S(1)}, u32[]{:S(2)}, u32[]{:S(2)}) collective-permute-start(bf16[12,32,512]{2,1,0:T(8,128)(2,1)S(1)} %get-tuple-element.26), channel_id=1, source_target_pairs={{0,8},{1,9},{2,10},{3,11},{4,12},{5,13},{6,14},{7,15},{8,0},{9,1},... | collective-permute-start | bytes 1179656 | tf_op jit(solution)/shard_map/ppermute | solution.py:284
  28.3 2.3 %collective-permute-start.1 = (bf16[12,32,512]{2,1,0:T(8,128)(2,1)S(1)}, bf16[12,32,512]{2,1,0:T(8,128)(2,1)S(1)}, u32[]{:S(2)}, u32[]{:S(2)}) collective-permute-start(bf16[12,32,512]{2,1,0:T(8,128)(2,1)S(1)} %get-tuple-element.27), channel_id=1, source_target_pairs={{0,4},{1,5},{2,6},{3,7},{4,8},{5,9},{6,10},{7,11},{8,12},{9,13},{1... | collective-permute-start | bytes 1179656 | tf_op jit(solution)/shard_map/ppermute | solution.py:284
  30.6 0.0 copy-start.6
  30.6 4.2 %collective-permute-start.2 = (bf16[12,32,512]{2,1,0:T(8,128)(2,1)S(1)}, bf16[12,32,512]{2,1,0:T(8,128)(2,1)S(1)}, u32[]{:S(2)}, u32[]{:S(2)}) collective-permute-start(bf16[12,32,512]{2,1,0:T(8,128)(2,1)S(1)} %get-tuple-element.28), channel_id=1, source_target_pairs={{0,12},{1,13},{2,14},{3,15},{4,0},{5,1},{6,2},{7,3},{8,4},{9,5},{1... | collective-permute-start | bytes 1179656 | tf_op jit(solution)/shard_map/ppermute | solution.py:284
  34.8 0.0 copy-start.2
  34.8 0.0 copy-start.4
  34.8 0.0 copy-start.5
  34.8 0.0 copy-done.6
  34.8 0.1 dynamic_slice.3
  34.9 0.0 copy-start.3
  34.9 0.6 copy-done.4
  35.5 0.0 copy-done.5
  35.5 0.1 copy-done.3
  35.6 0.2 fusion
  35.8 0.1 pad_add_fusion.lengths
  35.9 0.0 all-to-all-done.arrived
  35.9 0.0 copy-done.2
  35.9 1.3 %shard_map.83 = bf16[4,60,4,128]{3,2,1,0:T(4,128)(2,1)} custom-call(s32[8]{0:T(128)S(1)} %and_select_fusion.origin, bf16[32,5,4,128]{3,2,1,0:T(4,128)(2,1)S(1)} %all-to-all-done.arrived, bf16[4,5,4,128]{3,2,1,0:T(4,128)(2,1)S(1)} %copy-done.2), custom_call_target="tpu_custom_call" | custom-call | tf_op jit(solution)/shard_map/pallas_call | solution.py:286
  37.2 4.0 %all-to-all-start.1 = ((bf16[4,60,4,128]{3,2,1,0:T(4,128)(2,1)}), bf16[4,60,4,128]{3,2,1,0:T(4,128)(2,1)S(1)}, u32[]{:S(2)}, u32[]{:S(2)}) async-start(bf16[4,60,4,128]{3,2,1,0:T(4,128)(2,1)} %shard_map.83), calls=%async_computation.1 | async-start | bytes 491520 | tf_op jit(solution)/shard_map/all_to_all | solution.py:242
  41.3 0.0 collective-permute-done.rest_1_
  41.3 5.0 %collective-permute-done.1.rest_2_ = bf16[12,32,512]{2,1,0:T(8,128)(2,1)S(1)} collective-permute-done((bf16[12,32,512]{2,1,0:T(8,128)(2,1)S(1)}, bf16[12,32,512]{2,1,0:T(8,128)(2,1)S(1)}, u32[]{:S(2)}, u32[]{:S(2)}) %collective-permute-start.1) | collective-permute-done | bytes 393248 | tf_op jit(solution)/shard_map/ppermute | solution.py:284
  46.3 0.0 collective-permute-done.2.rest_3_
  46.3 0.4 all-to-all-done.1
  46.7 1.3 %shard_map.85 = bf16[4,208,128]{2,1,0:T(8,128)(2,1)S(1)} custom-call(s32[12]{0:T(128)S(1)} %pad_add_fusion.lengths, s32[8]{0:T(128)S(1)} %and_select_fusion.1.target, bf16[4,240,128]{2,1,0:T(8,128)(2,1)S(1)} %bitcast.11, bf16[12,32,512]{2,1,0:T(8,128)(2,1)S(1)} %get-tuple-element.25.rest_0_, bf16[12,32,512]{2,1,0:T(8,128)(2,1)S(1)} %collective-permute-done.rest_1_, ...), custom_call_target="tpu_custom_call" | custom-call | flops 100000000 | bytes 3145728 | tf_op jit(solution)/shard_map/pallas_call | solution.py:291
  48.0 8.7 %all_to_all.20.gathered = bf16[4,208,128]{2,1,0:T(8,128)(2,1)S(1)} all-to-all(bf16[4,208,128]{2,1,0:T(8,128)(2,1)S(1)} %shard_map.85), channel_id=1, replica_groups={{0,1,2,3},{4,5,6,7},{8,9,10,11},{12,13,14,15},{16,17,18,19},{20,21,22,2..., dimensions={0} | all-to-all | bytes 425984 | tf_op jit(solution)/shard_map/all_to_all | solution.py:242
  56.7 1.5 %shard_map.86 = (bf16[32,16,128]{2,1,0:T(8,128)(2,1)S(1)}, bf16[4,16,128]{2,1,0:T(8,128)(2,1)S(1)}) custom-call(s32[8]{0:T(128)S(1)} %and_select_fusion.origin, s32[8]{0:T(128)S(1)} %and_select_fusion.1.target, bf16[4,208,128]{2,1,0:T(8,128)(2,1)S(1)} %all_to_all.20.gathered, bf16[4,240,128]{2,1,0:T(8,128)(2,1)S(1)} %bitcast.12), custom_call_target="tpu_custom_call" | custom-call | tf_op jit(solution)/shard_map/pallas_call | solution.py:305
  58.2 21.2 %all_to_all.21.returned = bf16[32,16,128]{2,1,0:T(8,128)(2,1)S(1)} all-to-all(bf16[32,16,128]{2,1,0:T(8,128)(2,1)S(1)} %get-tuple-element.29), channel_id=1, replica_groups={{256,496,224,464,192,432,160,400,128,368,96,336,64,304,32,272,0,240,480..., dimensions={0} | all-to-all | bytes 262144 | tf_op jit(solution)/shard_map/all_to_all | solution.py:239
  79.3 1.3 %shard_map.87 = bf16[12,16,128]{2,1,0:T(8,128)(2,1)} custom-call(s32[8]{0:T(128)S(1)} %and_select_fusion.1.target, bf16[32,16,128]{2,1,0:T(8,128)(2,1)S(1)} %all_to_all.21.returned, bf16[4,16,128]{2,1,0:T(8,128)(2,1)S(1)} %get-tuple-element.30.kept), custom_call_target="tpu_custom_call" | custom-call | tf_op jit(solution)/shard_map/pallas_call | solution.py:312
  (3 shorter events, 0.0 us)
Async XLA Ops:
  0.0 22.0 %copy-start.1 = (bf16[4,32,2048]{2,1,0:T(8,128)(2,1)S(1)}, bf16[4,32,2048]{2,1,0:T(8,128)(2,1)}, u32[]{:S(2)}) copy-start(bf16[4,32,2048]{2,1,0:T(8,128)(2,1)} %resident.1) | copy-start | bytes 1572868
  1.8 34.2 %all-to-all-start = ((bf16[32,5,4,128]{3,2,1,0:T(4,128)(2,1)}), bf16[32,5,4,128]{3,2,1,0:T(4,128)(2,1)S(1)}, u32[]{:S(2)}, u32[]{:S(2)}) async-start(bf16[32,5,4,128]{3,2,1,0:T(4,128)(2,1)} %get-tuple-element.23), calls=%async_computation | async-start | bytes 327680 | tf_op jit(solution)/shard_map/all_to_all | solution.py:239
  22.0 1.2 %copy-start = (bf16[8,32,2048]{2,1,0:T(8,128)(2,1)S(1)}, bf16[8,32,2048]{2,1,0:T(8,128)(2,1)}, u32[]{:S(2)}) copy-start(bf16[8,32,2048]{2,1,0:T(8,128)(2,1)} %moved.1) | copy-start | bytes 3145732
  23.4 17.8 %collective-permute-start = (bf16[12,32,512]{2,1,0:T(8,128)(2,1)S(1)}, bf16[12,32,512]{2,1,0:T(8,128)(2,1)S(1)}, u32[]{:S(2)}, u32[]{:S(2)}) collective-permute-start(bf16[12,32,512]{2,1,0:T(8,128)(2,1)S(1)} %get-tuple-element.26), channel_id=1, source_target_pairs={{0,8},{1,9},{2,10},{3,11},{4,12},{5,13},{6,14},{7,15},{8,0},{9,1},... | collective-permute-start | bytes 1179656 | tf_op jit(solution)/shard_map/ppermute | solution.py:284
  28.3 18.0 %collective-permute-start.1 = (bf16[12,32,512]{2,1,0:T(8,128)(2,1)S(1)}, bf16[12,32,512]{2,1,0:T(8,128)(2,1)S(1)}, u32[]{:S(2)}, u32[]{:S(2)}) collective-permute-start(bf16[12,32,512]{2,1,0:T(8,128)(2,1)S(1)} %get-tuple-element.27), channel_id=1, source_target_pairs={{0,4},{1,5},{2,6},{3,7},{4,8},{5,9},{6,10},{7,11},{8,12},{9,13},{1... | collective-permute-start | bytes 1179656 | tf_op jit(solution)/shard_map/ppermute | solution.py:284
  30.6 4.3 %copy-start.6 = (s32[128]{0:T(128)S(1)}, s32[128]{0:T(128)}, u32[]{:S(2)}) copy-start(s32[128]{0:T(128)} %param.12) | copy-start | bytes 1540
  30.6 15.7 %collective-permute-start.2 = (bf16[12,32,512]{2,1,0:T(8,128)(2,1)S(1)}, bf16[12,32,512]{2,1,0:T(8,128)(2,1)S(1)}, u32[]{:S(2)}, u32[]{:S(2)}) collective-permute-start(bf16[12,32,512]{2,1,0:T(8,128)(2,1)S(1)} %get-tuple-element.28), channel_id=1, source_target_pairs={{0,12},{1,13},{2,14},{3,15},{4,0},{5,1},{6,2},{7,3},{8,4},{9,5},{1... | collective-permute-start | bytes 1179656 | tf_op jit(solution)/shard_map/ppermute | solution.py:284
  34.8 1.1 %copy-start.2 = (bf16[4,5,4,128]{3,2,1,0:T(4,128)(2,1)S(1)}, bf16[4,5,4,128]{3,2,1,0:T(4,128)(2,1)}, u32[]{:S(2)}) copy-start(bf16[4,5,4,128]{3,2,1,0:T(4,128)(2,1)} %get-tuple-element.24.kept) | copy-start | bytes 61444
  34.8 0.7 copy-start.4
  34.8 0.7 copy-start.5
  34.9 0.7 copy-start.3
  37.2 9.5 %all-to-all-start.1 = ((bf16[4,60,4,128]{3,2,1,0:T(4,128)(2,1)}), bf16[4,60,4,128]{3,2,1,0:T(4,128)(2,1)S(1)}, u32[]{:S(2)}, u32[]{:S(2)}) async-start(bf16[4,60,4,128]{3,2,1,0:T(4,128)(2,1)} %shard_map.83), calls=%async_computation.1 | async-start | bytes 491520 | tf_op jit(solution)/shard_map/all_to_all | solution.py:242
